TPU v7x, 32 devices: a whole 2x2x4 slice. The times are simulated.
32 devices in a mesh: dp: 16 (over z, y, core), fsdp: 2 (over x).
Axes of the slice: x: 2, y: 2, z: 4, core: 2. Of those that a mesh axis runs over, the one named last changes fastest.
Arguments:
- inputs: bfloat16 [16, 1024, 2048], P('dp', 'fsdp'), may hold values from -6 to 6
- cotangent: bfloat16 [16, 1024, 2048], P('dp', 'fsdp'), may hold values from -30 to 30
- segments: int32 [16, 1024], P('dp'), may hold values from 0 to 2, as said below
- w_query: float32 [2048, 2048], P(None, ('dp', 'fsdp')), may hold values from -0.125 to 0.125
- key_weight_master: float32 [2048, 1024], P(('dp', 'fsdp')), may hold values from -0.125 to 0.125
- value_weight_master: float32 [2048, 1024], P(('dp', 'fsdp')), may hold values from -0.125 to 0.125
- w_output: float32 [2048, 2048], P(('dp', 'fsdp')), may hold values from -0.75 to 0.75
- w_gate: float32 [2048, 6144], P(None, ('dp', 'fsdp')), may hold values from -0.125 to 0.125
- w_up: float32 [2048, 6144], P(None, ('dp', 'fsdp')), may hold values from -0.125 to 0.125
- w_down: float32 [6144, 2048], P(('dp', 'fsdp')), may hold values from -0.078125 to 0.078125
- moment_query: float32 [2048, 2048], P(None, ('dp', 'fsdp')), may hold values from -491520 to 491520
- moment_key: float32 [2048, 1024], P(('dp', 'fsdp')), may hold values from -491520 to 491520
- moment_value: float32 [2048, 1024], P(('dp', 'fsdp')), may hold values from -491520 to 491520
- moment_output: float32 [2048, 2048], P(('dp', 'fsdp')), may hold values from -491520 to 491520
- moment_gate: float32 [2048, 6144], P(None, ('dp', 'fsdp')), may hold values from -491520 to 491520
- moment_up: float32 [2048, 6144], P(None, ('dp', 'fsdp')), may hold values from -491520 to 491520
- moment_down: float32 [6144, 2048], P(('dp', 'fsdp')), may hold values from -491520 to 491520
- norm_gains: float32 [4352], replicated, may hold values from 0.5 to 1.5
- gain_first: float32 [4352], replicated, may hold values from -262144 to 262144
- gain_second: float32 [4352], replicated, may hold values from 0 to 262144
Outputs:
- block_out: bfloat16 [16, 1024, 2048], P('dp', 'fsdp')
- input_grad: float32 [16, 1024, 2048], P('dp', 'fsdp')
- grad_query: float32 [2048, 2048], P(None, ('dp', 'fsdp'))
- grad_key: float32 [2048, 1024], P(('dp', 'fsdp'))
- grad_value: float32 [2048, 1024], P(('dp', 'fsdp'))
- grad_output: float32 [2048, 2048], P(('dp', 'fsdp'))
- grad_gate: float32 [2048, 6144], P(None, ('dp', 'fsdp'))
- grad_up: float32 [2048, 6144], P(None, ('dp', 'fsdp'))
- grad_down: float32 [6144, 2048], P(('dp', 'fsdp'))
- moment_query_new: float32 [2048, 2048], P(None, ('dp', 'fsdp'))
- moment_key_new: float32 [2048, 1024], P(('dp', 'fsdp'))
- moment_value_new: float32 [2048, 1024], P(('dp', 'fsdp'))
- moment_output_new: float32 [2048, 2048], P(('dp', 'fsdp'))
- moment_gate_new: float32 [2048, 6144], P(None, ('dp', 'fsdp'))
- moment_up_new: float32 [2048, 6144], P(None, ('dp', 'fsdp'))
- moment_down_new: float32 [6144, 2048], P(('dp', 'fsdp'))
- weight_query_new: float32 [2048, 2048], P(None, ('dp', 'fsdp'))
- weight_key_new: float32 [2048, 1024], P(('dp', 'fsdp'))
- weight_value_new: float32 [2048, 1024], P(('dp', 'fsdp'))
- weight_output_new: float32 [2048, 2048], P(('dp', 'fsdp'))
- weight_gate_new: float32 [2048, 6144], P(None, ('dp', 'fsdp'))
- weight_up_new: float32 [2048, 6144], P(None, ('dp', 'fsdp'))
- weight_down_new: float32 [6144, 2048], P(('dp', 'fsdp'))
- gain_first_new: float32 [4352], replicated
- gain_second_new: float32 [4352], replicated
- gains_new: float32 [4352], replicated
Inputs may be any that keep to these rules, and one draw needn't show every extreme that they name: `segments`: along each row segment numbers never fall; every row holds three documents numbered 0, 1, 2; document 1 has exactly 800 tokens and reaches from the tokens of the first device of fsdp to those of the last; documents 0 and 2 have 60 tokens or more, and in every draw some row's document 0 and some row's document 2 have exactly 60.
All inputs are finite; a program needn't handle non-finite values.
Results may differ from a plain program's by a relative error of at most 0.019.
Values may be sent and summed in bfloat16 or wider, within the bound.
No kernel may reach another device: no remote copies, remote signals or barrier semaphores. Data moves between devices by JAX's collectives and lax.ppermute only.
A program may use at most 512 MiB of HBM per device.

v0:
```python
import math

import jax
import jax.numpy as jnp
from jax import lax
from jax.sharding import PartitionSpec as P

MODEL_WIDTH = 2048
QUERY_HEADS = 16
KEY_VALUE_HEADS = 8
HEAD_SIZE = 128
FF = 6144
NS_STEPS = 2
ADAM_STEP = 10


EPS_NORM = 1e-06
THETA = 1000000.0
NEG_FILL = -1e30
MOMENTUM = 0.95
NS_A = 3.4445
NS_B = -4.775
NS_C = 2.0315
NS_EPS = 1e-07
LR_MUON = 0.2
DECAY_MUON = 0.01
LR_GAIN = 0.5
BETA_ONE = 0.9
BETA_TWO = 0.95
EPS_ADAM = 1e-08
HIGH_PRECISION = lax.Precision.HIGHEST
SIDEWAYS = (True, False, False, False, True, True, False)


def rms_scale(values, gain):
    return values * lax.rsqrt(jnp.mean(values * values, axis=-1, keepdims=True) + EPS_NORM) * gain


def rope_tables(positions, head_width):
    half_width = head_width // 2
    freq = jnp.exp(
        -(2.0 * jnp.arange(half_width, dtype=jnp.float32) / head_width) * math.log(THETA)
    )
    angle = positions.astype(jnp.float32)[:, None] * freq[None, :]
    angle = jnp.concatenate([angle, angle], axis=-1)
    return (jnp.cos(angle)[:, None, :], jnp.sin(angle)[:, None, :])


def rotate(values, cosine_table, sine_table):
    half_width = values.shape[-1] // 2
    turned = jnp.concatenate([-values[..., half_width:], values[..., :half_width]], axis=-1)
    return values * cosine_table + turned * sine_table


def head_chain(projected, gain, cosine_table, sine_table):
    shaped = projected.reshape(projected.shape[0], -1, gain.shape[0])
    return rotate(rms_scale(shaped, gain), cosine_table, sine_table)


def contract_rows(left, right):
    return lax.dot_general(
        left, right, (((0,), (0,)), ((), ())), preferred_element_type=jnp.float32
    )


def contract_cols(left, right):
    return lax.dot_general(
        left, right, (((1,), (1,)), ((), ())), preferred_element_type=jnp.float32
    )


def swiglu_pass(normed_rows, out_rows, gate_mat, up_mat, down_mat):
    gate_pre = jnp.dot(normed_rows, gate_mat, preferred_element_type=jnp.float32)
    up_pre = jnp.dot(normed_rows, up_mat, preferred_element_type=jnp.float32)
    hidden = (jax.nn.silu(gate_pre) * up_pre).astype(jnp.bfloat16)
    down_part = jnp.dot(hidden, down_mat, preferred_element_type=jnp.float32)
    d_wdown = contract_rows(hidden, out_rows)
    d_hidden = contract_cols(out_rows, down_mat)
    swiglu_out, swiglu_back = jax.vjp(
        lambda gate_in, up_in: jax.nn.silu(gate_in) * up_in, gate_pre, up_pre
    )
    d_gate, d_up = swiglu_back(d_hidden)
    gate_low = d_gate.astype(jnp.bfloat16)
    up_low = d_up.astype(jnp.bfloat16)
    d_wgate = contract_rows(normed_rows, gate_low)
    d_wup = contract_rows(normed_rows, up_low)
    d_normed_part = contract_cols(gate_low, gate_mat) + contract_cols(up_low, up_mat)
    return (down_part, d_normed_part, d_wgate, d_wup, d_wdown)


def per_device(
    inputs,
    cotangent,
    segments,
    w_query,
    key_weight_master,
    value_weight_master,
    w_output,
    w_gate,
    w_up,
    w_down,
    moment_query,
    moment_key,
    moment_value,
    moment_output,
    moment_gate,
    moment_up,
    moment_down,
    norm_gains,
    gain_first,
    gain_second,
):
    sequence_count = inputs.shape[0]
    sequence_row_list = inputs.shape[1]
    complete_rows = segments.shape[1]
    token_count = sequence_count * sequence_row_list
    query_group_count = QUERY_HEADS // KEY_VALUE_HEADS
    dp_size = lax.axis_size("dp")
    first_row = lax.axis_index("fsdp") * sequence_row_list
    query_pos = first_row + jnp.arange(sequence_row_list, dtype=jnp.int32)
    row_idx = jnp.arange(complete_rows, dtype=jnp.int32)
    boundary = jnp.concatenate(
        [jnp.ones((sequence_count, 1), dtype=bool), segments[:, 1:] != segments[:, :-1]], axis=1
    )
    doc_start = lax.cummax(jnp.where(boundary, row_idx[None, :], 0), axis=1)
    positions = lax.dynamic_slice_in_dim(
        row_idx[None, :] - doc_start, first_row, sequence_row_list, 1
    ).reshape(token_count)
    own_segments = lax.dynamic_slice_in_dim(segments, first_row, sequence_row_list, 1)
    cosine_table, sine_table = rope_tables(positions, HEAD_SIZE)
    gain_attn = norm_gains[:MODEL_WIDTH]
    gain_mlp = norm_gains[MODEL_WIDTH : 2 * MODEL_WIDTH]
    gain_query = norm_gains[2 * MODEL_WIDTH : 2 * MODEL_WIDTH + HEAD_SIZE]
    gain_key = norm_gains[2 * MODEL_WIDTH + HEAD_SIZE :]
    full_query, full_key, full_value, full_output, full_gate, full_up, full_down = (
        lax.all_gather(w_query.astype(jnp.bfloat16), ("dp", "fsdp"), axis=1, tiled=True),
        lax.all_gather(key_weight_master.astype(jnp.bfloat16), ("dp", "fsdp"), axis=0, tiled=True),
        lax.all_gather(
            value_weight_master.astype(jnp.bfloat16), ("dp", "fsdp"), axis=0, tiled=True
        ),
        lax.all_gather(w_output.astype(jnp.bfloat16), ("dp", "fsdp"), axis=0, tiled=True),
        lax.all_gather(w_gate.astype(jnp.bfloat16), ("dp", "fsdp"), axis=1, tiled=True),
        lax.all_gather(w_up.astype(jnp.bfloat16), ("dp", "fsdp"), axis=1, tiled=True),
        lax.all_gather(w_down.astype(jnp.bfloat16), ("dp", "fsdp"), axis=0, tiled=True),
    )
    residual = inputs.astype(jnp.float32).reshape(token_count, MODEL_WIDTH)
    normed = rms_scale(residual, gain_attn).astype(jnp.bfloat16)
    q_proj = jnp.dot(normed, full_query, preferred_element_type=jnp.float32)
    k_proj = jnp.dot(normed, full_key, preferred_element_type=jnp.float32)
    value_projected = jnp.dot(normed, full_value, preferred_element_type=jnp.float32)
    rotated_queries = head_chain(q_proj, gain_query, cosine_table, sine_table).astype(jnp.bfloat16)
    rotated_keys = head_chain(k_proj, gain_key, cosine_table, sine_table).astype(jnp.bfloat16)
    query_block_rows = rotated_queries.reshape(
        sequence_count, sequence_row_list, KEY_VALUE_HEADS, query_group_count, HEAD_SIZE
    )
    outgoing_keys = rotated_keys.reshape(
        sequence_count, sequence_row_list, KEY_VALUE_HEADS * HEAD_SIZE
    )
    outgoing_values = value_projected.astype(jnp.bfloat16).reshape(
        sequence_count, sequence_row_list, KEY_VALUE_HEADS * HEAD_SIZE
    )
    gathered_keys, gathered_values = (
        lax.all_gather(outgoing_keys, "fsdp", axis=1, tiled=True),
        lax.all_gather(outgoing_values, "fsdp", axis=1, tiled=True),
    )
    present_keys = gathered_keys.reshape(sequence_count, complete_rows, KEY_VALUE_HEADS, HEAD_SIZE)
    present_values = gathered_values.reshape(
        sequence_count, complete_rows, KEY_VALUE_HEADS, HEAD_SIZE
    )
    allowed = (
        (row_idx[None, None, :] <= query_pos[None, :, None])
        & (segments[:, None, :] == own_segments[:, :, None])
    )[:, None, None, :, :]
    raw_scores = jnp.einsum(
        "bqhgd,bkhd->bhgqk", query_block_rows, present_keys, preferred_element_type=jnp.float32
    ) * HEAD_SIZE ** (-0.5)
    masked = jnp.where(allowed, raw_scores, NEG_FILL)
    top = jnp.max(masked, axis=-1, keepdims=True)
    expo = jnp.exp(masked - top)
    total = jnp.sum(expo, axis=-1, keepdims=True)
    log_total = top + jnp.log(total)
    attention_probability = expo / total
    head_output_rows = jnp.einsum(
        "bhgqk,bkhd->bhgqd",
        attention_probability,
        present_values.astype(jnp.float32),
        precision=HIGH_PRECISION,
    )
    att_low = (
        head_output_rows.transpose(0, 3, 1, 2, 4)
        .reshape(token_count, QUERY_HEADS * HEAD_SIZE)
        .astype(jnp.bfloat16)
    )
    middle = residual + jnp.dot(att_low, full_output, preferred_element_type=jnp.float32)
    normed_two = rms_scale(middle, gain_mlp).astype(jnp.bfloat16)
    down_part, d_normed_two, d_wgate, d_wup, d_wdown = swiglu_pass(
        normed_two, cotangent.reshape(token_count, MODEL_WIDTH), full_gate, full_up, full_down
    )
    result = middle + down_part
    block_out = result.astype(jnp.bfloat16).reshape(sequence_count, sequence_row_list, MODEL_WIDTH)
    norm_out, second_back = jax.vjp(rms_scale, middle, gain_mlp)
    d_mid_norm, d_gain_mlp = second_back(d_normed_two)
    d_middle = cotangent.reshape(token_count, MODEL_WIDTH).astype(jnp.float32) + d_mid_norm
    mid_low = d_middle.astype(jnp.bfloat16)
    d_woutput = contract_rows(att_low, mid_low)
    head_gradient_rows = contract_cols(mid_low, full_output).astype(jnp.bfloat16)
    block_gradient = head_gradient_rows.reshape(
        sequence_count, sequence_row_list, KEY_VALUE_HEADS, query_group_count, HEAD_SIZE
    )
    d_blocks_f32 = block_gradient.astype(jnp.float32)
    delta = jnp.sum(d_blocks_f32.transpose(0, 2, 3, 1, 4) * head_output_rows, axis=-1)
    again_scores = jnp.einsum(
        "bqhgd,bkhd->bhgqk", query_block_rows, present_keys, preferred_element_type=jnp.float32
    ) * HEAD_SIZE ** (-0.5)
    probs_back = jnp.exp(jnp.where(allowed, again_scores, NEG_FILL) - log_total)
    d_probs = jnp.einsum(
        "bqhgd,bkhd->bhgqk", block_gradient, present_values, preferred_element_type=jnp.float32
    )
    d_raw = (probs_back * (d_probs - delta[..., None])).astype(jnp.bfloat16)
    d_query = jnp.einsum(
        "bhgqk,bkhd->bqhgd", d_raw, present_keys, preferred_element_type=jnp.float32
    ) * HEAD_SIZE ** (-0.5)
    d_keys = jnp.einsum(
        "bhgqk,bqhgd->bkhd", d_raw, query_block_rows, preferred_element_type=jnp.float32
    ) * HEAD_SIZE ** (-0.5)
    d_values = jnp.einsum("bhgqk,bqhgd->bkhd", probs_back, d_blocks_f32, precision=HIGH_PRECISION)
    key_gradient_total, value_gradient_total = (
        lax.psum_scatter(
            d_keys.astype(jnp.bfloat16), "fsdp", scatter_dimension=1, tiled=True
        ).astype(jnp.float32),
        lax.psum_scatter(
            d_values.astype(jnp.bfloat16), "fsdp", scatter_dimension=1, tiled=True
        ).astype(jnp.float32),
    )
    q_out, query_back = jax.vjp(
        lambda proj_in, gain_in: head_chain(proj_in, gain_in, cosine_table, sine_table),
        q_proj,
        gain_query,
    )
    d_qproj, d_gain_query = query_back(d_query.reshape(token_count, QUERY_HEADS, HEAD_SIZE))
    k_out, key_cotangent = jax.vjp(
        lambda proj_in, gain_in: head_chain(proj_in, gain_in, cosine_table, sine_table),
        k_proj,
        gain_key,
    )
    key_projection_gradient, key_gain_gradient = key_cotangent(
        key_gradient_total.reshape(token_count, KEY_VALUE_HEADS, HEAD_SIZE)
    )
    q_low = d_qproj.astype(jnp.bfloat16)
    k_low = key_projection_gradient.astype(jnp.bfloat16)
    value_reduced = value_gradient_total.reshape(token_count, KEY_VALUE_HEADS * HEAD_SIZE).astype(
        jnp.bfloat16
    )
    d_wquery = contract_rows(normed, q_low)
    d_wkey = contract_rows(normed, k_low)
    d_wvalue = contract_rows(normed, value_reduced)
    d_normed = (
        contract_cols(q_low, full_query)
        + contract_cols(k_low, full_key)
        + contract_cols(value_reduced, full_value)
    )
    first_out, first_back = jax.vjp(rms_scale, residual, gain_attn)
    d_residual, d_gain_attn = first_back(d_normed)
    input_grad = (d_middle + d_residual).reshape(sequence_count, sequence_row_list, MODEL_WIDTH)
    grad_query, grad_key, grad_value, grad_output, grad_gate, grad_up, grad_down = (
        lax.psum_scatter(d_wquery, ("dp", "fsdp"), scatter_dimension=1, tiled=True),
        lax.psum_scatter(d_wkey, ("dp", "fsdp"), scatter_dimension=0, tiled=True),
        lax.psum_scatter(d_wvalue, ("dp", "fsdp"), scatter_dimension=0, tiled=True),
        lax.psum_scatter(d_woutput, ("dp", "fsdp"), scatter_dimension=0, tiled=True),
        lax.psum_scatter(d_wgate, ("dp", "fsdp"), scatter_dimension=1, tiled=True),
        lax.psum_scatter(d_wup, ("dp", "fsdp"), scatter_dimension=1, tiled=True),
        lax.psum_scatter(d_wdown, ("dp", "fsdp"), scatter_dimension=0, tiled=True),
    )
    masters = (w_query, key_weight_master, value_weight_master, w_output, w_gate, w_up, w_down)
    moments = (
        moment_query,
        moment_key,
        moment_value,
        moment_output,
        moment_gate,
        moment_up,
        moment_down,
    )
    grads = (grad_query, grad_key, grad_value, grad_output, grad_gate, grad_up, grad_down)
    full_dims = (
        (MODEL_WIDTH, QUERY_HEADS * HEAD_SIZE),
        (MODEL_WIDTH, KEY_VALUE_HEADS * HEAD_SIZE),
        (MODEL_WIDTH, KEY_VALUE_HEADS * HEAD_SIZE),
        (QUERY_HEADS * HEAD_SIZE, MODEL_WIDTH),
        (MODEL_WIDTH, FF),
        (MODEL_WIDTH, FF),
        (FF, MODEL_WIDTH),
    )
    new_moments = tuple(
        (MOMENTUM * moments[matrix_idx] + grads[matrix_idx] for matrix_idx in range(7))
    )
    updates = tuple(
        (grads[matrix_idx] + MOMENTUM * new_moments[matrix_idx] for matrix_idx in range(7))
    )
    squares = jnp.stack([jnp.sum(update_now * update_now) for update_now in updates])
    gain_part = jnp.concatenate([d_gain_attn, d_gain_mlp, d_gain_query, key_gain_gradient])
    gain_grad, totals = lax.psum((gain_part, squares), ("dp", "fsdp"))
    slot_rows = grad_gate.shape[1]
    pieces = []
    for matrix_idx in range(7):
        scaled = (updates[matrix_idx] / (jnp.sqrt(totals[matrix_idx]) + NS_EPS)).astype(
            jnp.bfloat16
        )
        form = scaled.T if SIDEWAYS[matrix_idx] else scaled
        pieces.append(
            jnp.pad(form, ((0, slot_rows - form.shape[0]), (0, MODEL_WIDTH - form.shape[1])))
        )
    for spare_idx in range(dp_size - 7):
        pieces.append(jnp.zeros((slot_rows, MODEL_WIDTH), jnp.bfloat16))
    arrived = lax.all_to_all(jnp.stack(pieces), "dp", split_axis=0, concat_axis=1, tiled=True)
    current = arrived[0]
    for ns_turn in range(NS_STEPS):
        partial_gram = contract_rows(current, current)
        gram = lax.psum(partial_gram.astype(jnp.bfloat16), "fsdp")
        product = jnp.dot(current, gram, preferred_element_type=jnp.float32)
        again = jnp.dot(product.astype(jnp.bfloat16), gram, preferred_element_type=jnp.float32)
        current = (NS_A * current.astype(jnp.float32) + NS_B * product + NS_C * again).astype(
            jnp.bfloat16
        )
    returned = lax.all_to_all(current[None], "dp", split_axis=1, concat_axis=0, tiled=True)
    new_weights = []
    for matrix_idx in range(7):
        shard_shape = masters[matrix_idx].shape
        if SIDEWAYS[matrix_idx]:
            ortho = returned[matrix_idx][: shard_shape[1], : shard_shape[0]].T
        else:
            ortho = returned[matrix_idx][: shard_shape[0], : shard_shape[1]]
        stride = LR_MUON * math.sqrt(max(full_dims[matrix_idx]))
        new_weights.append(
            masters[matrix_idx] * (1.0 - LR_MUON * DECAY_MUON) - stride * ortho.astype(jnp.float32)
        )
    first_new = BETA_ONE * gain_first + (1.0 - BETA_ONE) * gain_grad
    second_new = BETA_TWO * gain_second + (1.0 - BETA_TWO) * gain_grad * gain_grad
    corr_one = 1.0 - BETA_ONE**ADAM_STEP
    corr_two = 1.0 - BETA_TWO**ADAM_STEP
    gains_new = norm_gains - LR_GAIN * (first_new / corr_one) / (
        jnp.sqrt(second_new / corr_two) + EPS_ADAM
    )
    return (
        block_out,
        input_grad,
        grad_query,
        grad_key,
        grad_value,
        grad_output,
        grad_gate,
        grad_up,
        grad_down,
        new_moments[0],
        new_moments[1],
        new_moments[2],
        new_moments[3],
        new_moments[4],
        new_moments[5],
        new_moments[6],
        new_weights[0],
        new_weights[1],
        new_weights[2],
        new_weights[3],
        new_weights[4],
        new_weights[5],
        new_weights[6],
        first_new,
        second_new,
        gains_new,
    )


def solution(mesh):
    placed = (
        P("dp", "fsdp", None),
        P("dp", "fsdp", None),
        P("dp", None),
        P(None, ("dp", "fsdp")),
        P(("dp", "fsdp"), None),
        P(("dp", "fsdp"), None),
        P(("dp", "fsdp"), None),
        P(None, ("dp", "fsdp")),
        P(None, ("dp", "fsdp")),
        P(("dp", "fsdp"), None),
        P(None, ("dp", "fsdp")),
        P(("dp", "fsdp"), None),
        P(("dp", "fsdp"), None),
        P(("dp", "fsdp"), None),
        P(None, ("dp", "fsdp")),
        P(None, ("dp", "fsdp")),
        P(("dp", "fsdp"), None),
        P(),
        P(),
        P(),
    )
    return jax.shard_map(
        per_device,
        mesh=mesh,
        in_specs=placed,
        out_specs=(
            P("dp", "fsdp", None),
            P("dp", "fsdp", None),
            P(None, ("dp", "fsdp")),
            P(("dp", "fsdp"), None),
            P(("dp", "fsdp"), None),
            P(("dp", "fsdp"), None),
            P(None, ("dp", "fsdp")),
            P(None, ("dp", "fsdp")),
            P(("dp", "fsdp"), None),
            P(None, ("dp", "fsdp")),
            P(("dp", "fsdp"), None),
            P(("dp", "fsdp"), None),
            P(("dp", "fsdp"), None),
            P(None, ("dp", "fsdp")),
            P(None, ("dp", "fsdp")),
            P(("dp", "fsdp"), None),
            P(None, ("dp", "fsdp")),
            P(("dp", "fsdp"), None),
            P(("dp", "fsdp"), None),
            P(("dp", "fsdp"), None),
            P(None, ("dp", "fsdp")),
            P(None, ("dp", "fsdp")),
            P(("dp", "fsdp"), None),
            P(),
            P(),
            P(),
        ),
        check_vma=False,
    )
```

profile of v0, /device:TPU:0, one launch (start us, length us, event | category | flops | bytes accessed | tf_op | source)
XLA Modules:
  0.0 4815.1 jit_solution(7471540280260706934)
XLA Ops:
  14.0 62.4 %all-gather.17.cloned.1.call-done = bf16[2048,1024]{1,0:T(8,128)(2,1)} async-done(((bf16[64,1024]{1,0:T(8,128)(2,1)}), bf16[2048,1024]{1,0:T(8,128)(2,1)}) %all-gather.17.cloned.1.call-update) | async-done | bytes 4194320 | tf_op jit(solution)/shard_map/all_gather | solution.py:138
  76.4 6.2 fusion.86
  86.4 54.2 %all-gather.11.cloned.1.call-done = bf16[2048,1024]{1,0:T(8,128)(2,1)} async-done(((bf16[64,1024]{1,0:T(8,128)(2,1)}), bf16[2048,1024]{1,0:T(8,128)(2,1)}) %all-gather.11.cloned.1.call-update) | async-done | bytes 4194320 | tf_op jit(solution)/shard_map/all_gather | solution.py:137
  140.6 6.6 copy.86
  147.2 5.1 multiply_reduce_fusion.8
  164.4 10.1 all-gather.27.cloned.1.call-done
  178.0 77.2 %all-gather.15.cloned.1.call-done = bf16[2048,2048]{0,1:T(8,128)(2,1)} async-done(((bf16[2048,64]{0,1:T(8,128)(2,1)}), bf16[2048,2048]{0,1:T(8,128)(2,1)}) %all-gather.15.cloned.1.call-update) | async-done | bytes 8388624 | tf_op jit(solution)/shard_map/all_gather | solution.py:136
  255.2 7.1 multiply_reduce_fusion.5
  266.2 22.7 all-gather.13.cloned.1.call-done
  288.9 15.5 fusion.8
  304.5 14.5 fusion.7
  319.0 26.0 bitcast_convert_fusion.2
  345.0 24.6 all-gather.19.cloned.1.call-done
  369.6 7.8 multiply_reduce_fusion.4
  379.8 146.5 %all-gather.23.cloned.1.call-done = bf16[2048,6144]{0,1:T(8,128)(2,1)} async-done(((bf16[2048,192]{0,1:T(8,128)(2,1)}), bf16[2048,6144]{0,1:T(8,128)(2,1)}) %all-gather.23.cloned.1.call-update) | async-done | bytes 25165840 | tf_op jit(solution)/shard_map/all_gather | solution.py:143
  526.4 19.9 fusion.120
  546.3 136.4 %all-gather.21.cloned.1.call-done = bf16[2048,6144]{0,1:T(8,128)(2,1)} async-done(((bf16[2048,192]{0,1:T(8,128)(2,1)}), bf16[2048,6144]{0,1:T(8,128)(2,1)}) %all-gather.21.cloned.1.call-update) | async-done | bytes 25165840 | tf_op jit(solution)/shard_map/all_gather | solution.py:142
  682.7 20.1 fusion.119
  702.8 136.2 %all-gather.25.cloned.1.call-done = bf16[6144,2048]{1,0:T(8,128)(2,1)} async-done(((bf16[192,2048]{1,0:T(8,128)(2,1)}), bf16[6144,2048]{1,0:T(8,128)(2,1)}) %all-gather.25.cloned.1.call-update) | async-done | bytes 25165840 | tf_op jit(solution)/shard_map/all_gather | solution.py:144
  839.0 29.9 multiply_convert_fusion
  869.0 21.4 fusion.121
  890.3 23.1 multiply_reduce_fusion.1
  918.9 8.4 convolution_convert_fusion.1
  937.4 23.1 fusion.9
  960.5 12.5 fusion.83
  973.1 29.8 fusion.80
  1008.4 6.1 fusion.73
  1014.7 23.2 reduce-scatter.12.cloned.1.call-done
  1038.0 7.2 fusion.71
  1045.2 13.3 fusion.89
  1058.8 9.0 broadcast_multiply_fusion
  1076.2 8.6 fusion.69
  1085.3 25.5 fusion.61
  1110.9 24.0 fusion.125
  1135.0 24.0 fusion.124
  1159.2 5.1 fusion.123
  1166.8 11.2 fusion.36
  1178.0 45.8 reduce-scatter.16.cloned.1.call-done
  1226.1 184.7 %reduce-scatter.18.cloned.1.call-done = f32[64,1024]{1,0:T(8,128)} async-done(((f32[2048,1024]{1,0:T(8,128)}), f32[64,1024]{1,0:T(8,128)}) %reduce-scatter.18.cloned.1.call-update) | async-done | bytes 262160 | tf_op jit(solution)/shard_map/reduce_scatter | solution.py:268
  1413.2 358.6 %reduce-scatter.20.cloned.1.call-done = f32[64,2048]{1,0:T(8,128)} async-done(((f32[2048,2048]{1,0:T(8,128)}), f32[64,2048]{1,0:T(8,128)}) %reduce-scatter.20.cloned.1.call-update) | async-done | bytes 524304 | tf_op jit(solution)/shard_map/reduce_scatter | solution.py:269
  1774.3 358.9 %reduce-scatter.14.cloned.1.call-done = f32[2048,64]{0,1:T(8,128)} async-done(((f32[2048,2048]{0,1:T(8,128)}), f32[2048,64]{0,1:T(8,128)}) %reduce-scatter.14.cloned.1.call-update) | async-done | bytes 524304 | tf_op jit(solution)/shard_map/reduce_scatter | solution.py:266
  2135.7 437.1 %reduce-scatter.26.cloned.1.call-done = f32[192,2048]{1,0:T(8,128)} async-done(((f32[6144,2048]{1,0:T(8,128)}), f32[192,2048]{1,0:T(8,128)}) %reduce-scatter.26.cloned.1.call-update) | async-done | bytes 1572880 | tf_op jit(solution)/shard_map/reduce_scatter | solution.py:272
  2575.3 434.9 %reduce-scatter.24.cloned.1.call-done = f32[2048,192]{0,1:T(8,128)} async-done(((f32[2048,6144]{0,1:T(8,128)}), f32[2048,192]{0,1:T(8,128)}) %reduce-scatter.24.cloned.1.call-update) | async-done | bytes 1572880 | tf_op jit(solution)/shard_map/reduce_scatter | solution.py:271
  3014.3 433.3 %reduce-scatter.22.cloned.1.call-done = f32[2048,192]{0,1:T(8,128)} async-done(((f32[2048,6144]{0,1:T(8,128)}), f32[2048,192]{0,1:T(8,128)}) %reduce-scatter.22.cloned.1.call-update) | async-done | bytes 1572880 | tf_op jit(solution)/shard_map/reduce_scatter | solution.py:270
  3456.4 39.6 all-reduce.8
  3507.8 277.9 %all_to_all.21 = bf16[16,192,2048]{2,1,0:T(8,128)(2,1)S(1)} all-to-all(bf16[16,192,2048]{2,1,0:T(8,128)(2,1)S(1)} %broadcast_dynamic-update-slice_fusion), channel_id=1, replica_groups=mesh['dp'=16,'fsdp'=2] {'dp'}, dimensions={0} | all-to-all | bytes 25165824 | tf_op jit(solution)/shard_map/all_to_all | solution.py:315
  3790.3 30.2 bitcast_convert_fusion
  3820.6 198.6 %all-reduce.12.cloned.1.call-done = bf16[2048,2048]{1,0:T(8,128)(2,1)} async-done(((bf16[2048,2048]{1,0:T(8,128)(2,1)}), bf16[2048,2048]{1,0:T(8,128)(2,1)}) %all-reduce.12.cloned.1.call-update) | async-done | bytes 8388624 | tf_op jit(solution)/shard_map/psum | solution.py:319
  4019.2 33.6 fusion.126
  4052.9 40.6 add_convert_fusion.1
  4093.5 34.2 convolution_convert_fusion
  4127.8 198.5 %all-reduce.14.cloned.1.call-done = bf16[2048,2048]{1,0:T(8,128)(2,1)} async-done(((bf16[2048,2048]{1,0:T(8,128)(2,1)}), bf16[2048,2048]{1,0:T(8,128)(2,1)}) %all-reduce.14.cloned.1.call-update) | async-done | bytes 8388624 | tf_op jit(solution)/shard_map/psum | solution.py:319
  4326.3 33.6 fusion.127
  4359.9 40.9 fusion.25
  4400.8 22.4 copy.144
  4423.7 75.5 %reduce.7 = bf16[3072,2048]{1,0:T(8,128)(2,1)} reduce(bf16[3072,1,2048]{2,1,0:T(2,128)(2,1)} %bitcast.319, bf16[]{:T(256)} %broadcast.498), dimensions={1}, to_apply=%bitcast.311.reduce_sub_computation | reduce | bytes 25165826
  4499.2 17.7 reshape.660
  4516.8 6.1 all-to-all-start.1
  4523.0 21.4 fusion.51
  4548.2 198.4 %all-to-all-done.1 = bf16[16,2,196608]{2,1,0:T(2,128)(2,1)} async-done(((bf16[16,2,196608]{2,1,0:T(2,128)(2,1)}), bf16[16,2,196608]{2,1,0:T(2,128)(2,1)}, u32[]{:S(2)}, u32[]{:S(2)}) %all-to-all-start.1) | async-done | bytes 12582944 | tf_op jit(solution)/shard_map/all_to_all | solution.py:325
  4746.6 20.7 reshape.661
  4769.0 5.6 fusion.84
  4774.6 6.3 fusion.113
  4780.9 16.9 copy.120
  (301 shorter events, 117.8 us)
Async XLA Ops:
  7.2 69.2 %all-gather.17.cloned.1.call-start = ((), (), s32[]{:S(2)}) async-start(), calls=%async_computation.14 | async-start | bytes 4325376 | tf_op jit(solution)/shard_map/all_gather | solution.py:138
  8.9 131.7 %all-gather.11.cloned.1.call-start = ((), (), s32[]{:S(2)}) async-start(), calls=%async_computation.11 | async-start | bytes 4325376 | tf_op jit(solution)/shard_map/all_gather | solution.py:137
  10.6 163.9 %all-gather.27.cloned.1.call-start = ((), (), s32[]{:S(2)}) async-start(), calls=%async_computation.30 | async-start | bytes 3145728 | tf_op jit(solution)/shard_map/all_gather | solution.py:164
  13.3 241.9 %copy-start.73 = (f32[512]{0:T(512)}, f32[512]{0:T(512)S(1)}, u32[]{:S(2)}) copy-start(f32[512]{0:T(512)S(1)} %fusion.100) | copy-start | bytes 6148
  14.0 241.2 %copy-start.60 = (f32[2048]{0:T(1024)}, f32[2048]{0:T(1024)S(1)}, u32[]{:S(2)}) copy-start(f32[2048]{0:T(1024)S(1)} %get-tuple-element.73) | copy-start | bytes 24580
  76.4 6.3 copy-start.42
  76.4 7.1 copy-start.66
  82.7 172.5 %all-gather.15.cloned.1.call-start = ((), (), s32[]{:S(2)}) async-start(), calls=%async_computation.13 | async-start | bytes 8650752 | tf_op jit(solution)/shard_map/all_gather | solution.py:136
  83.5 205.4 %all-gather.13.cloned.1.call-start = ((), (), s32[]{:S(2)}) async-start(), calls=%async_computation.12 | async-start | bytes 3145728 | tf_op jit(solution)/shard_map/all_gather | solution.py:163
  85.6 179.0 %copy-start.19 = (f32[512,128]{0,1:T(8,128)}, f32[512,128]{0,1:T(8,128)S(1)}, u32[]{:S(2)}) copy-start(f32[512,128]{0,1:T(8,128)S(1)} %get-tuple-element.70) | copy-start | bytes 786436
  85.6 179.0 %copy-start.24 = (f32[512,128]{0,1:T(8,128)}, f32[512,128]{0,1:T(8,128)S(1)}, u32[]{:S(2)}) copy-start(f32[512,128]{0,1:T(8,128)S(1)} %get-tuple-element.71) | copy-start | bytes 786436
  86.4 66.8 %copy-start.76 = (f32[128]{0:T(128)}, f32[128]{0:T(128)S(1)}, u32[]{:S(2)}) copy-start(f32[128]{0:T(128)S(1)} %get-tuple-element.75) | copy-start | bytes 1540
  86.4 178.1 %copy-start.78 = (f32[128]{0:T(128)}, f32[128]{0:T(128)S(1)}, u32[]{:S(2)}) copy-start(f32[128]{0:T(128)S(1)} %get-tuple-element.74) | copy-start | bytes 1540
  140.6 6.6 copy-start.6
  155.4 214.2 %all-gather.19.cloned.1.call-start = ((), (), s32[]{:S(2)}) async-start(), calls=%async_computation.15 | async-start | bytes 8650752 | tf_op jit(solution)/shard_map/all_gather | solution.py:141
  156.2 370.1 %all-gather.23.cloned.1.call-start = ((), (), s32[]{:S(2)}) async-start(), calls=%async_computation.17 | async-start | bytes 25952256 | tf_op jit(solution)/shard_map/all_gather | solution.py:143
  158.7 524.0 %all-gather.21.cloned.1.call-start = ((), (), s32[]{:S(2)}) async-start(), calls=%async_computation.16 | async-start | bytes 25952256 | tf_op jit(solution)/shard_map/all_gather | solution.py:142
  161.2 677.9 %all-gather.25.cloned.1.call-start = ((), (), s32[]{:S(2)}) async-start(), calls=%async_computation.18 | async-start | bytes 25952256 | tf_op jit(solution)/shard_map/all_gather | solution.py:144
  163.6 839.6 %reduce-scatter.10.cloned.1.call-start = ((), (), s32[]{:S(2)}) async-start(), calls=%async_computation.19 | async-start | bytes 3145728 | tf_op jit(solution)/shard_map/reduce_scatter | solution.py:228
  164.4 154.6 %copy-start.22 = (pred[512,1024]{0,1:T(8,128)(4,1)}, pred[512,1024]{0,1:T(8,128)(4,1)S(1)}, u32[]{:S(2)}) copy-start(pred[512,1024]{0,1:T(8,128)(4,1)S(1)} %fusion.77) | copy-start | bytes 1572868
  266.1 38.3 copy-start.4
  304.4 14.5 copy-start.41
  319.0 50.6 %copy-start.7 = (bf16[1,512,2048]{2,1,0:T(8,128)(2,1)S(1)}, bf16[1,512,2048]{2,1,0:T(8,128)(2,1)}, u32[]{:S(2)}) copy-start(bf16[1,512,2048]{2,1,0:T(8,128)(2,1)} %param.20) | copy-start | bytes 6291460
  377.4 168.9 %copy-start.82 = (f32[512]{0:T(512)}, f32[512]{0:T(512)S(1)}, u32[]{:S(2)}) copy-start(f32[512]{0:T(512)S(1)} %get-tuple-element.91) | copy-start | bytes 6148
  379.8 302.9 %copy-start.36 = (bf16[512,2048]{1,0:T(8,128)(2,1)}, bf16[512,2048]{1,0:T(8,128)(2,1)S(1)}, u32[]{:S(2)}) copy-start(bf16[512,2048]{1,0:T(8,128)(2,1)S(1)} %multiply_convert_fusion.2) | copy-start | bytes 6291460
  869.0 21.4 copy-start.13
  890.3 23.1 copy-start.83
  890.3 23.2 copy-start.44
  937.4 23.1 copy-start.5
  973.0 30.2 copy-start.25
  973.1 64.9 %reduce-scatter.12.cloned.1.call-start = ((), (), s32[]{:S(2)}) async-start(), calls=%async_computation.20 | async-start | bytes 3145728 | tf_op jit(solution)/shard_map/reduce_scatter | solution.py:231
  1003.0 220.8 %reduce-scatter.16.cloned.1.call-start = ((), (), s32[]{:S(2)}) async-start(), calls=%async_computation.22 | async-start | bytes 8650752 | tf_op jit(solution)/shard_map/reduce_scatter | solution.py:267
  1014.5 23.5 copy-start.9
  1014.5 396.3 %reduce-scatter.18.cloned.1.call-start = ((), (), s32[]{:S(2)}) async-start(), calls=%async_computation.23 | async-start | bytes 8650752 | tf_op jit(solution)/shard_map/reduce_scatter | solution.py:268
  1045.2 726.6 %reduce-scatter.20.cloned.1.call-start = ((), (), s32[]{:S(2)}) async-start(), calls=%async_computation.24 | async-start | bytes 17301504 | tf_op jit(solution)/shard_map/reduce_scatter | solution.py:269
  1058.5 1074.6 %reduce-scatter.14.cloned.1.call-start = ((), (), s32[]{:S(2)}) async-start(), calls=%async_computation.21 | async-start | bytes 17301504 | tf_op jit(solution)/shard_map/reduce_scatter | solution.py:266
  1084.9 1487.9 %reduce-scatter.26.cloned.1.call-start = ((), (), s32[]{:S(2)}) async-start(), calls=%async_computation.27 | async-start | bytes 51904512 | tf_op jit(solution)/shard_map/reduce_scatter | solution.py:272
  1110.9 1899.3 %reduce-scatter.24.cloned.1.call-start = ((), (), s32[]{:S(2)}) async-start(), calls=%async_computation.26 | async-start | bytes 51904512 | tf_op jit(solution)/shard_map/reduce_scatter | solution.py:271
  1134.9 2312.7 %reduce-scatter.22.cloned.1.call-start = ((), (), s32[]{:S(2)}) async-start(), calls=%async_computation.25 | async-start | bytes 51904512 | tf_op jit(solution)/shard_map/reduce_scatter | solution.py:270
  1159.0 5.3 copy-start.50
  1159.0 2860.2 %all-reduce.12.cloned.1.call-start = ((), (), s32[]{:S(2)}) async-start(), calls=%async_computation.28 | async-start | bytes 16777216 | tf_op jit(solution)/shard_map/psum | solution.py:319
  1166.7 11.3 copy-start.81
  1166.7 11.3 copy-start.84
  1166.7 57.1 %copy-start.57 = (f32[64,1024]{1,0:T(8,128)S(1)}, f32[64,1024]{1,0:T(8,128)}, u32[]{:S(2)}) copy-start(f32[64,1024]{1,0:T(8,128)} %param.31) | copy-start | bytes 786436
  1166.8 605.0 %copy-start.53 = (f32[64,2048]{1,0:T(8,128)S(1)}, f32[64,2048]{1,0:T(8,128)}, u32[]{:S(2)}) copy-start(f32[64,2048]{1,0:T(8,128)} %param.33) | copy-start | bytes 1572868
  1166.8 966.4 %copy-start.54 = (f32[2048,64]{0,1:T(8,128)S(1)}, f32[2048,64]{0,1:T(8,128)}, u32[]{:S(2)}) copy-start(f32[2048,64]{0,1:T(8,128)} %param.30) | copy-start | bytes 1572868
  1178.0 1394.8 %copy-start.45 = (f32[192,2048]{1,0:T(8,128)S(1)}, f32[192,2048]{1,0:T(8,128)}, u32[]{:S(2)}) copy-start(f32[192,2048]{1,0:T(8,128)} %param.36) | copy-start | bytes 4718596
  2575.3 931.1 %copy-start.29 = (f32[192,2048]{1,0:T(8,128)}, f32[192,2048]{1,0:T(8,128)S(1)}, u32[]{:S(2)}) copy-start(f32[192,2048]{1,0:T(8,128)S(1)} %get-tuple-element.40) | copy-start | bytes 4718596
  3014.3 488.7 %copy-start.48 = (f32[64,1024]{1,0:T(8,128)S(1)}, f32[64,1024]{1,0:T(8,128)}, u32[]{:S(2)}) copy-start(f32[64,1024]{1,0:T(8,128)} %reduce-scatter.16.cloned.1.call-done) | copy-start | bytes 786436
  3451.7 53.9 %copy-start.28 = (f32[2048,192]{0,1:T(8,128)S(1)}, f32[2048,192]{0,1:T(8,128)}, u32[]{:S(2)}) copy-start(f32[2048,192]{0,1:T(8,128)} %reduce-scatter.22.cloned.1.call-done) | copy-start | bytes 4718596
  3496.0 9.4 copy-start.39
  3496.0 9.4 copy-start.40
  3496.0 9.6 copy-start.31
  3820.5 505.7 %all-reduce.14.cloned.1.call-start = ((), (), s32[]{:S(2)}) async-start(), calls=%async_computation.29 | async-start | bytes 16777216 | tf_op jit(solution)/shard_map/psum | solution.py:319
  4516.8 229.8 %all-to-all-start.1 = ((bf16[16,2,196608]{2,1,0:T(2,128)(2,1)}), bf16[16,2,196608]{2,1,0:T(2,128)(2,1)}, u32[]{:S(2)}, u32[]{:S(2)}) async-start(bf16[16,2,196608]{2,1,0:T(2,128)(2,1)} %reshape.660), calls=%async_computation.10 | async-start | bytes 25165824 | tf_op jit(solution)/shard_map/all_to_all | solution.py:325
  4522.9 21.5 copy-start.72
  4522.9 21.5 copy-start.80
  4522.9 21.5 copy-start.10
  4522.9 21.5 copy-start.11
  4522.9 21.5 copy-start.15
  4523.0 21.5 copy-start.62
  4523.0 21.5 copy-start.75
  4780.9 16.9 copy-start.38
  4780.9 17.9 copy-start.32
  (42 other events, 101.3 us)
Sparse Core Ops, SparseCore 0:
  11.6 64.7 all-gather.16
  80.0 60.6 all-gather.10
  142.8 31.6 all-gather.26
  177.9 77.2 all-gather.14
  257.2 31.6 all-gather.12
  292.3 77.2 all-gather.18
  373.1 153.2 all-gather.22
  529.8 152.8 all-gather.20
  686.2 152.8 all-gather.24
  973.2 29.9 reduce-scatter.9
  1006.1 31.8 reduce-scatter.11
  1040.7 183.0 reduce-scatter.15
  1226.7 184.0 reduce-scatter.17
  1413.5 358.2 reduce-scatter.19
  1774.5 358.6 reduce-scatter.13
  2140.0 432.7 reduce-scatter.25
  2579.7 430.4 reduce-scatter.23
  3017.0 430.5 reduce-scatter.21
  3820.7 198.5 all-reduce.11
  4127.9 198.3 all-reduce.13
where the time goes:
time: 4870 us; the launch traced here: 4820 us
  waiting for transfers between devices  3540 us (73%)
  matrix products  627 us (13%)
  blocking collectives  317 us (7%)
  other arithmetic  175 us (4%)
  local copies, waits for them, and re-layouts  124 us (3%)
    reduce_scatter x1, waiting for transfers between devices, per_device(): lax.psum_scatter(d_wdown, ('dp', 'fsdp'), scatter_dimension=0, tiled=True)  437 us
    reduce_scatter x1, waiting for transfers between devices, per_device(): lax.psum_scatter(d_wup, ('dp', 'fsdp'), scatter_dimension=1, tiled=True)  435 us
    reduce_scatter x1, waiting for transfers between devices, per_device(): lax.psum_scatter(d_wgate, ('dp', 'fsdp'), scatter_dimension=1, tiled=True)  433 us
    psum x2, waiting for transfers between devices, per_device(): gram = lax.psum(partial_gram.astype(jnp.bfloat16), 'fsdp')  397 us
    reduce_scatter x1, waiting for transfers between devices, per_device(): lax.psum_scatter(d_wquery, ('dp', 'fsdp'), scatter_dimension=1, tiled=True)  359 us
    reduce_scatter x1, waiting for transfers between devices, per_device(): lax.psum_scatter(d_woutput, ('dp', 'fsdp'), scatter_dimension=0, tiled=True)  359 us
    all_to_all x1, blocking collectives, per_device(): lax.all_to_all(jnp.stack(pieces), 'dp', split_axis=0, concat_axis=1, tile...  278 us
    all_to_all x1, waiting for transfers between devices, per_device(): lax.all_to_all(current[None], 'dp', split_axis=1, concat_axis=0, tiled=True)  198 us
  transfers between devices with their start and end apart: 21, of which 21 were waited for; matrix products, arithmetic and copies ran while one was open for 8% of the time, Pallas kernels for 0%

commit v1 on v0

v1 whole, which is shorter than its diff:
```python
import functools
import math

import jax
import jax.numpy as jnp
from jax import lax
from jax.experimental import pallas as pl
from jax.experimental.pallas import tpu as pltpu
from jax.sharding import Mesh
from jax.sharding import PartitionSpec as P

MODEL_WIDTH = 2048
QUERY_HEADS = 16
KEY_VALUE_HEADS = 8
HEAD_SIZE = 128
FF = 6144
ADAM_STEP = 10

EPS_NORM = 1e-06
THETA = 1000000.0
NEG_FILL = -1e30
MOMENTUM = 0.95
NS_A = 3.4445
NS_B = -4.775
NS_C = 2.0315
NS_EPS = 1e-07
LR_MUON = 0.2
DECAY_MUON = 0.01
LR_GAIN = 0.5
BETA_ONE = 0.9
BETA_TWO = 0.95
EPS_ADAM = 1e-08

CORES = 2
PLANES = 4
KV_WIDTH = KEY_VALUE_HEADS * HEAD_SIZE
BF16 = jnp.bfloat16
F32 = jnp.float32
SHARDS = ("z", "y", "fsdp")
PLANE_ROWS = ("z", "y")
EVERYWHERE = ("z", "y", "core", "fsdp")


def rms_scale(values, gain):
    return values * lax.rsqrt(jnp.mean(values * values, axis=-1, keepdims=True) + EPS_NORM) * gain


def rope_tables(positions, head_width):
    half_width = head_width // 2
    freq = jnp.exp(
        -(2.0 * jnp.arange(half_width, dtype=jnp.float32) / head_width) * math.log(THETA)
    )
    angle = positions.astype(jnp.float32)[..., None] * freq
    cosine = jnp.cos(angle)
    sine = jnp.sin(angle)
    return jnp.concatenate([cosine, cosine], -1), jnp.concatenate([-sine, sine], -1)


def dot_nn(left, right):
    return lax.dot_general(left, right, (((1,), (0,)), ((), ())), preferred_element_type=F32)


def dot_nt(left, right):
    return lax.dot_general(left, right, (((1,), (1,)), ((), ())), preferred_element_type=F32)


def dot_tn(left, right):
    return lax.dot_general(left, right, (((0,), (0,)), ((), ())), preferred_element_type=F32)


def head_chain(head, gain, cosine, sine):
    scaled = head * lax.rsqrt(jnp.mean(head * head, axis=-1, keepdims=True) + EPS_NORM) * gain
    return scaled * cosine + pltpu.roll(scaled, HEAD_SIZE // 2, 1) * sine


def head_chain_back(head, gain, cosine, sine, grad):
    grad = grad * cosine + pltpu.roll(grad * sine, HEAD_SIZE // 2, 1)
    scale = lax.rsqrt(jnp.mean(head * head, axis=-1, keepdims=True) + EPS_NORM)
    unit = head * scale
    d_gain = jnp.sum(grad * unit, axis=0, keepdims=True)
    grad = grad * gain
    return scale * (grad - unit * jnp.mean(grad * unit, axis=-1, keepdims=True)), d_gain


def key_value_kernel(near_ref, far_ref, gain_ref, cos_ref, sin_ref, proj_ref, low_ref):
    proj = near_ref[...] + far_ref[...].astype(F32)
    proj_ref[...] = proj
    is_key = pl.program_id(0) < KEY_VALUE_HEADS

    @pl.when(is_key)
    def _():
        low_ref[...] = head_chain(proj, gain_ref[...], cos_ref[...], sin_ref[...]).astype(BF16)

    @pl.when(jnp.logical_not(is_key))
    def _():
        low_ref[...] = proj.astype(BF16)


def key_value_back_kernel(grad_ref, proj_ref, gain_ref, cos_ref, sin_ref, low_ref, d_gain_ref):
    head = pl.program_id(0)

    @pl.when(head == 0)
    def _():
        d_gain_ref[...] = jnp.zeros_like(d_gain_ref)

    @pl.when(head < KEY_VALUE_HEADS)
    def _():
        d_proj, d_gain = head_chain_back(
            proj_ref[...], gain_ref[...], cos_ref[...], sin_ref[...], grad_ref[0]
        )
        low_ref[...] = d_proj.astype(BF16)
        d_gain_ref[...] += d_gain

    @pl.when(head >= KEY_VALUE_HEADS)
    def _():
        low_ref[...] = grad_ref[0].astype(BF16)


def attention_weights(q_ref, k_ref, mask_ref, gain_ref, cos_ref, sin_ref):
    query = head_chain(q_ref[...], gain_ref[...], cos_ref[0], sin_ref[0]).astype(BF16)
    scores = dot_nt(k_ref[0], query)
    weights = jnp.exp2(scores * (HEAD_SIZE ** (-0.5) * math.log2(math.e)))
    return query, weights * mask_ref[0].astype(F32)


def attention_kernel(
    q_ref, k_ref, v_ref, mask_ref, gain_ref, cos_ref, sin_ref, out_ref, out_turned_ref
):
    _, weights = attention_weights(q_ref, k_ref, mask_ref, gain_ref, cos_ref, sin_ref)
    total = jnp.sum(weights, axis=0, keepdims=True)
    out = dot_tn(v_ref[0], weights.astype(BF16)) * (1.0 / total)
    out_turned_ref[...] = out.astype(BF16)
    out_ref[...] = out.T.astype(BF16)


def attention_back_kernel(
    q_ref, k_ref, v_ref, mask_ref, gain_ref, cos_ref, sin_ref, grad_ref,
    *refs,
):
    q_low_ref, q_low_turned_ref, d_kv_ref, d_gain_ref = refs[-4:]

    @pl.when(pl.program_id(0) == 0)
    def _():
        d_gain_ref[...] = jnp.zeros_like(d_gain_ref)

    query, weights = attention_weights(q_ref, k_ref, mask_ref, gain_ref, cos_ref, sin_ref)
    grad = grad_ref[...]
    probs = weights * (1.0 / jnp.sum(weights, axis=0, keepdims=True))
    d_probs = dot_nt(v_ref[0], grad)
    delta = jnp.sum(probs * d_probs, axis=0, keepdims=True)
    d_scores = (probs * (d_probs - delta)).astype(BF16)
    d_value = dot_nn(probs.astype(BF16), grad).astype(BF16)
    d_key = (dot_nn(d_scores, query) * HEAD_SIZE ** (-0.5)).astype(BF16)

    d_kv_ref[0] = d_key
    d_kv_ref[1] = d_value
    d_query = dot_tn(k_ref[0], d_scores).T * HEAD_SIZE ** (-0.5)
    d_proj, d_gain = head_chain_back(
        q_ref[...], gain_ref[...], cos_ref[0], sin_ref[0], d_query
    )
    q_low_ref[...] = d_proj.astype(BF16)
    q_low_turned_ref[...] = d_proj.T.astype(BF16)
    d_gain_ref[...] += d_gain


def swiglu_kernel(two_ref, cot_ref, gate_ref, up_ref, down_ref, *out_refs):
    width = two_ref.shape[1]
    two = two_ref[...]
    gate = dot_nt(two, gate_ref[...].reshape(-1, width))
    up = dot_nt(two, up_ref[...].reshape(-1, width))
    d_hidden = dot_nt(cot_ref[...], down_ref[...].reshape(-1, width))
    sig = 1.0 / (1.0 + jnp.exp(-gate))
    silu = gate * sig
    results = (silu * up, d_hidden * up * sig * (1.0 + gate * (1.0 - sig)), d_hidden * silu)
    for result, out_ref, turned_ref in zip(results, out_refs[:3], out_refs[3:]):
        low = result.astype(BF16)
        out_ref[...] = low
        turned_ref[...] = low.T


def back_to_width_kernel(count, *refs):
    lefts, rights, out_ref = refs[:count], refs[count : 2 * count], refs[-1]
    width = out_ref.shape[1]
    total = 0.0
    for left, right in zip(lefts, rights):
        if split_by_y(right.shape[2]):
            half = left.shape[1] // CORES
            for y in range(CORES):
                rows = right[:, y].reshape(-1, width)
                total = total + dot_nn(left[:, y * half : (y + 1) * half], rows)
        else:
            total = total + dot_nn(left[...], right[...].reshape(-1, width))
    out_ref[...] = total.astype(BF16)


def weight_grad_kernel(place_ref, left_ref, right_ref, out_ref):
    out_ref[...] = dot_nn(left_ref[...], right_ref[...]).astype(BF16)


def chain_kernel(start_ref, gram_ref, bend_ref, out_ref, first_ref, product_ref, one_ref, two_ref):
    width = start_ref.shape[1]
    tile = 512

    def columns(body):
        @pl.loop(0, width // tile)
        def _(step):
            body(pl.ds(pl.multiple_of(step * tile, tile), tile))

    def times_p(rows_ref, cols):
        return NS_A * rows_ref[:, cols].astype(F32) + dot_nn(rows_ref[...], bend_ref[:, cols])

    def to_first(cols):
        first_ref[:, cols] = times_p(start_ref, cols).astype(BF16)

    def bent_first(cols):
        one_ref[:, cols] = times_p(first_ref, cols).astype(BF16)

    def by_gram(cols):
        two_ref[:, cols] = dot_nn(one_ref[...], gram_ref[:, cols]).astype(BF16)

    def to_product(cols):
        product_ref[:, cols] = times_p(two_ref, cols).astype(BF16)

    def bent_product(cols):
        one_ref[:, cols] = times_p(product_ref, cols).astype(BF16)

    def finish(cols):
        again = times_p(two_ref, cols)
        out_ref[:, cols] = (
            NS_A * first_ref[:, cols].astype(F32)
            + NS_B * product_ref[:, cols].astype(F32)
            + NS_C * again
        ).astype(BF16)

    for body in (to_first, bent_first, by_gram, to_product, bent_product, by_gram, finish):
        columns(body)


def shaped(shape, dtype):
    return jax.ShapeDtypeStruct(shape, dtype)


SMALL = pl.CostEstimate(flops=1, bytes_accessed=1, transcendentals=0)


def limits(mebibytes):
    return pltpu.CompilerParams(vmem_limit_bytes=mebibytes * 1024 * 1024)


def key_value_chain(near, far, gain, cosine, sine):
    rows = near.shape[0]
    block = pl.BlockSpec((rows, HEAD_SIZE), lambda head: (0, head))
    fixed = pl.BlockSpec((rows, HEAD_SIZE), lambda head: (0, 0))
    one = pl.BlockSpec((1, HEAD_SIZE), lambda head: (0, 0))
    return pl.pallas_call(
        key_value_kernel,
        grid=(2 * KEY_VALUE_HEADS,),
        in_specs=[block, block, one, fixed, fixed],
        out_specs=[block, block],
        out_shape=[shaped(near.shape, F32), shaped(near.shape, BF16)],
        compiler_params=limits(16),
        cost_estimate=SMALL,
        name="key_value_chain",
    )(near, far, gain, cosine, sine)


def key_value_back(grad, proj, gain, cosine, sine):
    rows = proj.shape[0]
    heads = KEY_VALUE_HEADS
    block = pl.BlockSpec((rows, HEAD_SIZE), lambda head: (0, head))
    split = pl.BlockSpec((1, rows, HEAD_SIZE), lambda head: (head // heads, 0, head % heads))
    fixed = pl.BlockSpec((rows, HEAD_SIZE), lambda head: (0, 0))
    one = pl.BlockSpec((1, HEAD_SIZE), lambda head: (0, 0))
    return pl.pallas_call(
        key_value_back_kernel,
        grid=(2 * heads,),
        in_specs=[split, block, one, fixed, fixed],
        out_specs=[block, one],
        out_shape=[shaped(proj.shape, BF16), shaped((1, HEAD_SIZE), F32)],
        compiler_params=limits(16),
        cost_estimate=SMALL,
        name="key_value_back",
    )(grad, proj, gain, cosine, sine)


def attention_specs(rows, keys, heads):
    return [
        pl.BlockSpec((rows, HEAD_SIZE), lambda seq, head: (seq, head)),
        pl.BlockSpec((1, keys, HEAD_SIZE), lambda seq, head: (seq, 0, head)),
        pl.BlockSpec((1, keys, HEAD_SIZE), lambda seq, head: (seq, 0, heads + head)),
        pl.BlockSpec((1, keys, rows), lambda seq, head: (seq, 0, 0)),
        pl.BlockSpec((1, HEAD_SIZE), lambda seq, head: (0, 0)),
        pl.BlockSpec((1, rows, HEAD_SIZE), lambda seq, head: (seq, 0, 0)),
        pl.BlockSpec((1, rows, HEAD_SIZE), lambda seq, head: (seq, 0, 0)),
    ]


def attention(q_proj, kv, mask, gain, cosine, sine):
    sequences, keys, rows = mask.shape
    heads = q_proj.shape[1] // HEAD_SIZE
    specs = attention_specs(rows, keys, heads)
    return pl.pallas_call(
        attention_kernel,
        grid=(sequences, heads),
        in_specs=specs,
        out_specs=[specs[0], pl.BlockSpec((HEAD_SIZE, rows), lambda seq, head: (head, seq))],
        out_shape=[shaped(q_proj.shape, BF16), shaped(q_proj.shape[::-1], BF16)],
        compiler_params=limits(40),
        cost_estimate=SMALL,
        name="attention",
    )(q_proj, kv, kv, mask, gain, cosine, sine)


def attention_back(q_proj, kv, mask, gain, cosine, sine, grad, seq, others):
    _, keys, rows = mask.shape
    heads = q_proj.shape[1] // HEAD_SIZE
    specs = [
        pl.BlockSpec((rows, HEAD_SIZE), lambda head: (seq, head)),
        pl.BlockSpec((1, keys, HEAD_SIZE), lambda head: (seq, 0, head)),
        pl.BlockSpec((1, keys, HEAD_SIZE), lambda head: (seq, 0, heads + head)),
        pl.BlockSpec((1, keys, rows), lambda head: (seq, 0, 0)),
        pl.BlockSpec((1, HEAD_SIZE), lambda head: (0, 0)),
        pl.BlockSpec((1, rows, HEAD_SIZE), lambda head: (seq, 0, 0)),
        pl.BlockSpec((1, rows, HEAD_SIZE), lambda head: (seq, 0, 0)),
    ]
    return pl.pallas_call(
        attention_back_kernel,
        grid=(heads,),
        in_specs=[*specs, specs[0]] + [pl.BlockSpec(memory_space=pl.ANY)] * len(others),
        out_specs=[
            specs[0],
            pl.BlockSpec((HEAD_SIZE, rows), lambda head: (head, seq)),
            pl.BlockSpec((2, keys, HEAD_SIZE), lambda head: (0, 0, head)),
            specs[4],
        ],
        out_shape=[
            shaped(q_proj.shape, BF16),
            shaped(q_proj.shape[::-1], BF16),
            shaped((2, keys, heads * HEAD_SIZE), BF16),
            shaped((1, HEAD_SIZE), F32),
        ],
        input_output_aliases={8 + place: place for place in range(len(others))},
        compiler_params=limits(48),
        cost_estimate=SMALL,
        name="attention_back",
    )(q_proj, kv, kv, mask, gain, cosine, sine, grad, *others)


def split_by_y(block_rows):
    return (PLANES * block_rows) % 128 == 0


def swiglu_both_ways(two, cot, ff):
    tokens, width = two.shape
    _, _, block_rows, _ = ff[0].shape
    ys = 1 if split_by_y(block_rows) else CORES
    tile = min(512, tokens)
    ff_tile = PLANES * ys * block_rows
    row_block = pl.BlockSpec((tile, width), lambda col, row: (row, 0))
    out_block = pl.BlockSpec((tile, ff_tile), lambda col, row: (row, col))
    turned_block = pl.BlockSpec((ff_tile, tile), lambda col, row: (col, row))
    weights = pl.BlockSpec((PLANES, ys, block_rows, width), lambda col, row: (0, col, 0, 0))
    columns = PLANES * CORES * block_rows
    return pl.pallas_call(
        swiglu_kernel,
        grid=(CORES // ys, tokens // tile),
        in_specs=[row_block, row_block] + [weights] * 3,
        out_specs=[out_block] * 3 + [turned_block] * 3,
        out_shape=[shaped((tokens, columns), BF16)] * 3 + [shaped((columns, tokens), BF16)] * 3,
        compiler_params=limits(60),
        cost_estimate=SMALL,
        name="swiglu_both_ways",
    )(two, cot, *ff)


def back_to_width(lefts, ff, first_row, rows):
    _, _, block_rows, width = ff[0].shape
    columns = PLANES * CORES * block_rows
    tile = min(256, rows)
    first = first_row // tile
    left_block = pl.BlockSpec((tile, columns), lambda row: (first + row, 0))
    weights = pl.BlockSpec(ff[0].shape, lambda row: (0, 0, 0, 0))
    return pl.pallas_call(
        functools.partial(back_to_width_kernel, len(lefts)),
        grid=(rows // tile,),
        in_specs=[left_block] * len(lefts) + [weights] * len(lefts),
        out_specs=pl.BlockSpec((tile, width), lambda row: (row, 0)),
        out_shape=shaped((rows, width), BF16),
        compiler_params=limits(56),
        cost_estimate=SMALL,
        name="back_to_width",
    )(*lefts, *ff)


def weight_grad(left_turned, right, place, parts):
    rows = left_turned.shape[0] // parts
    tokens, width = right.shape
    tile = min(512, width)
    return pl.pallas_call(
        weight_grad_kernel,
        grid_spec=pltpu.PrefetchScalarGridSpec(
            num_scalar_prefetch=1,
            grid=(width // tile,),
            in_specs=[
                pl.BlockSpec((rows, tokens), lambda col, place_ref: (place_ref[0], 0)),
                pl.BlockSpec((tokens, tile), lambda col, place_ref: (0, col)),
            ],
            out_specs=pl.BlockSpec((rows, tile), lambda col, place_ref: (0, col)),
        ),
        out_shape=shaped((rows, width), BF16),
        compiler_params=limits(40),
        cost_estimate=SMALL,
        name="weight_grad",
    )(jnp.asarray(place, jnp.int32).reshape(1), left_turned, right)


def times_columns_kernel(left_ref, right_ref, out_ref):
    out_ref[...] = dot_nn(left_ref[...], right_ref[...]).astype(BF16)


def times_columns(left, right, first_column, width):
    rows, depth = left.shape
    tile = min(512, width)
    first = first_column // tile
    return pl.pallas_call(
        times_columns_kernel,
        grid=(width // tile,),
        in_specs=[
            pl.BlockSpec((rows, depth), lambda col: (0, 0)),
            pl.BlockSpec((depth, tile), lambda col: (0, first + col)),
        ],
        out_specs=pl.BlockSpec((rows, tile), lambda col: (0, col)),
        out_shape=shaped((rows, width), BF16),
        compiler_params=limits(40),
        cost_estimate=SMALL,
        name="times_columns",
    )(left, right)


def bend_kernel(gram_ref, tile_ref, out_ref):
    square = dot_nn(gram_ref[...], tile_ref[...])
    out_ref[...] = (NS_B * tile_ref[...].astype(F32) + NS_C * square).astype(BF16)


def bend_of(gram):
    width = gram.shape[0]
    tile = 512
    return pl.pallas_call(
        bend_kernel,
        grid=(width // tile,),
        in_specs=[
            pl.BlockSpec((width, width), lambda col: (0, 0)),
            pl.BlockSpec((width, tile), lambda col: (0, col)),
        ],
        out_specs=pl.BlockSpec((width, tile), lambda col: (0, col)),
        out_shape=shaped(gram.shape, BF16),
        compiler_params=limits(48),
        cost_estimate=SMALL,
        name="bend_of",
    )(gram, gram)


def times_rows_kernel(left_ref, right_ref, out_ref):
    out_ref[...] = dot_nt(left_ref[...], right_ref[...]).astype(BF16)


def times_rows(left, right, place):
    rows, depth = left.shape
    columns = right.shape[0]
    tile = min(256, columns)
    return pl.pallas_call(
        times_rows_kernel,
        grid=(columns // tile,),
        in_specs=[
            pl.BlockSpec((rows, depth), lambda col: (0, 0)),
            pl.BlockSpec((tile, depth), lambda col: (col, place)),
        ],
        out_specs=pl.BlockSpec((rows, tile), lambda col: (0, col)),
        out_shape=shaped((rows, columns), BF16),
        compiler_params=limits(40),
        cost_estimate=SMALL,
        name="times_rows",
    )(left, right)


def chain(start, gram, bend):
    rows, width = start.shape
    whole = pl.BlockSpec((width, width), lambda: (0, 0), pipeline_mode=pl.Buffered(1))
    block = pl.BlockSpec((rows, width), lambda: (0, 0), pipeline_mode=pl.Buffered(1))
    return pl.pallas_call(
        chain_kernel,
        grid=(),
        in_specs=[block, whole, whole],
        out_specs=pl.BlockSpec((rows, width), lambda: (0, 0)),
        out_shape=shaped(start.shape, BF16),
        scratch_shapes=[pltpu.VMEM(start.shape, BF16)] * 4,
        compiler_params=limits(56),
        cost_estimate=SMALL,
        name="chain",
    )(start, gram, bend)


def after(value, *earlier):
    return lax.optimization_barrier((value, earlier))[0]


def shifted(step, count):
    return [(src, (src + step) % count) for src in range(count)]


def swap(value, axis_name="core"):
    return lax.ppermute(value, axis_name, shifted(1, CORES))


def with_partner(value):
    return jnp.concatenate([value, swap(value)], axis=0)


def ring_blocks(value, axis_name, count):
    return [value] + [
        lax.ppermute(value, axis_name, shifted(step, count)) for step in range(1, count)
    ]


def ring_send(blocks, axis_name, count):
    return [
        lax.ppermute(blocks[step].astype(BF16), axis_name, shifted(-step, count))
        for step in range(1, count)
    ]


def add_all(own, arrived):
    for term in arrived:
        own = own + term.astype(F32)
    return own


def pick(blocks, index, axis=0):
    return lax.dynamic_index_in_dim(blocks, index, axis, keepdims=False)


def gather_rows(shard, axes):
    return lax.all_gather(shard, axes, axis=0, tiled=True)


def scatter_blocks(blocks, axis_name):
    count = blocks.shape[0]
    here = lax.axis_index(axis_name)
    arrived = [
        lax.ppermute(pick(blocks, (here + step) % count), axis_name, shifted(step, count))
        for step in range(1, count)
    ]
    return add_all(pick(blocks, here).astype(F32), arrived)


def ordered_blocks(value, axis_name):
    count = lax.axis_size(axis_name)
    here = lax.axis_index(axis_name)
    blocks = ring_blocks(value, axis_name, count)
    if count == 2:
        first = jnp.where(here == 0, blocks[0], blocks[1])
        second = jnp.where(here == 0, blocks[1], blocks[0])
        return jnp.concatenate([first, second], axis=0)
    rows = value.shape[0]
    whole = jnp.zeros((count * rows, *value.shape[1:]), value.dtype)
    for step, block in enumerate(blocks):
        whole = lax.dynamic_update_slice_in_dim(whole, block, (here - step) % count * rows, 0)
    return whole


def sum_over_plane(partial, gain, beside):
    width = partial.shape[1]
    ring = lax.axis_size("fsdp")
    mine = scatter_blocks(partial.astype(BF16).reshape(CORES, -1, width), "core").astype(BF16)
    mine, gain = lax.optimization_barrier((mine, butterfly(gain, "core")))
    half = mine.shape[0] // 2
    one, two = mine[:half], mine[half:]
    one = scatter_blocks(one.reshape(ring, -1, width), "fsdp").astype(BF16)
    two = scatter_blocks(two.reshape(CORES, -1, width), "y").astype(BF16)
    one, two, gain, beside = lax.optimization_barrier(
        (one, two, butterfly(gain, "fsdp"), beside)
    )
    one = scatter_blocks(one.reshape(CORES, -1, width), "y").astype(BF16)
    two = scatter_blocks(two.reshape(ring, -1, width), "fsdp").astype(BF16)
    one, two, gain = lax.optimization_barrier((one, two, butterfly(gain, "y")))
    one = ordered_blocks(one, "y")
    two = ordered_blocks(two, "fsdp")
    one, two, gain = lax.optimization_barrier((one, two, butterfly(gain, "z")))
    one = ordered_blocks(one, "fsdp")
    two = ordered_blocks(two, "y")
    return ordered_blocks(jnp.concatenate([one, two], axis=0), "core"), gain, beside


def ff_grad_half(left_turned, right, block_rows, y):
    shape = (PLANES, block_rows, right.shape[1])
    if split_by_y(block_rows):
        return weight_grad(left_turned, right, y, CORES).reshape(shape)
    full = weight_grad(left_turned, right, 0, 1)
    return pick(full.reshape(PLANES, CORES, block_rows, -1), y, 1)


def halves_over_y(partials):
    here = lax.axis_index("y")
    split = [value.reshape(PLANES, CORES, -1, value.shape[-1]) for value in partials]
    sent = jnp.concatenate([pick(value, 1 - here, 1) for value in split], axis=-1)
    kept = [pick(value, here, 1) for value in split]
    return kept, swap(sent, "y"), sent


def chunks_over_z(kept, arrived):
    here = lax.axis_index("z")

    def chunk(step):
        plane = (here + step) % PLANES
        near = jnp.concatenate([pick(value, plane) for value in kept], axis=-1)
        return near.astype(F32) + pick(arrived, plane).astype(F32)

    own = chunk(0)
    sent = [chunk(step).astype(BF16) for step in range(1, PLANES)]
    return own, [
        lax.ppermute(value, "z", shifted(step + 1, PLANES)) for step, value in enumerate(sent)
    ], sent


def butterfly(value, axis_name):
    count = lax.axis_size(axis_name)
    step = 1
    while step < count:
        value = value + lax.ppermute(value, axis_name, [(src, src ^ step) for src in range(count)])
        step *= 2
    return value


def to_planes(chunks):
    here = lax.axis_index("z")
    arrived = [pick(chunks, here)]
    for step in range(1, PLANES):
        arrived.append(
            lax.ppermute(pick(chunks, (here + step) % PLANES), "z", shifted(step, PLANES))
        )
    return jnp.stack(arrived)


def from_planes(arrived):
    here = lax.axis_index("z")
    back = [arrived[0]]
    for step in range(1, PLANES):
        back.append(lax.ppermute(arrived[step], "z", shifted(-step, PLANES)))
    back = jnp.stack(back)
    return [pick(back, (chunk - here) % PLANES) for chunk in range(PLANES)]


def orthogonal_rows(update, update_gram, halves, earlier):
    width = update.shape[1]
    side = jnp.arange(width) < width // 2
    index = jnp.arange(width)
    diagonal = jnp.sum(
        jnp.where(index[:, None] == index[None, :], update_gram.astype(F32), 0.0), axis=0
    )
    low_half = jnp.sum(diagonal[: width // 2])
    high_half = jnp.sum(diagonal[width // 2 :])
    both = low_half + high_half
    squares = jnp.stack([jnp.where(halves, low_half, both), jnp.where(halves, high_half, both)])
    inverse = jnp.repeat(1.0 / (jnp.sqrt(squares) + NS_EPS), width // 2)
    kept = jnp.logical_not(halves) | (side[:, None] == side[None, :])
    start = (update.astype(F32) * inverse).astype(BF16)
    gram = jnp.where(kept, update_gram.astype(F32) * inverse[:, None] * inverse[None, :], 0.0).astype(BF16)
    return chain(start, after(gram, earlier), bend_of(gram))


def per_device(
    inputs,
    cotangent,
    segments,
    w_query,
    key_weight_master,
    value_weight_master,
    w_output,
    w_gate,
    w_up,
    w_down,
    moment_query,
    moment_key,
    moment_value,
    moment_output,
    moment_gate,
    moment_up,
    moment_down,
    norm_gains,
    gain_first,
    gain_second,
):
    rows = inputs.shape[1]
    complete_rows = segments.shape[1]
    ring = lax.axis_size("fsdp")
    place = lax.axis_index("fsdp")
    core = lax.axis_index("core")
    gain_attn = norm_gains[:MODEL_WIDTH]
    gain_mlp = norm_gains[MODEL_WIDTH : 2 * MODEL_WIDTH]
    gain_query = norm_gains[2 * MODEL_WIDTH : 2 * MODEL_WIDTH + HEAD_SIZE]
    gain_key = norm_gains[2 * MODEL_WIDTH + HEAD_SIZE :]

    attention_rows = gather_rows(
        jnp.concatenate(
            [
                key_weight_master.astype(BF16),
                value_weight_master.astype(BF16),
                w_query.astype(BF16).T,
                w_output.astype(BF16),
            ],
            axis=1,
        ),
        SHARDS,
    )
    key_value_rows = attention_rows[:, :MODEL_WIDTH]
    query_rows = attention_rows[:, MODEL_WIDTH : 2 * MODEL_WIDTH]
    output_rows = attention_rows[:, 2 * MODEL_WIDTH :]
    gate_ff, up_ff, down_ff = (
        gather_rows(shard[None], PLANE_ROWS).reshape(PLANES, CORES, *shard.shape)
        for shard in (w_gate.astype(BF16).T, w_up.astype(BF16).T, w_down.astype(BF16))
    )

    both_segments = with_partner(segments)
    row_idx = jnp.arange(complete_rows, dtype=jnp.int32)
    boundary = jnp.concatenate(
        [
            jnp.ones((CORES, 1), dtype=bool),
            both_segments[:, 1:] != both_segments[:, :-1],
        ],
        axis=1,
    )
    doc_start = lax.cummax(jnp.where(boundary, row_idx[None, :], 0), axis=1)
    first_row = place * rows
    positions = lax.dynamic_slice_in_dim(row_idx[None, :] - doc_start, first_row, rows, 1)
    cosine_table, sine_table = rope_tables(positions, HEAD_SIZE)
    query_segments = lax.dynamic_slice_in_dim(both_segments, first_row, rows, 1)
    query_pos = first_row + jnp.arange(rows, dtype=jnp.int32)
    key_starts = [((place - step) % ring) * rows for step in range(ring)]
    key_pos = jnp.concatenate([at + jnp.arange(rows, dtype=jnp.int32) for at in key_starts])
    key_segments = jnp.concatenate(
        [lax.dynamic_slice_in_dim(both_segments, at, rows, 1) for at in key_starts], axis=1
    )
    mask = (
        (key_pos[None, :, None] <= query_pos[None, None, :])
        & (key_segments[:, :, None] == query_segments[:, None, :])
    ).astype(BF16)

    residual = inputs.astype(F32).reshape(rows, MODEL_WIDTH)
    normed = rms_scale(residual, gain_attn).astype(BF16)
    both_normed = with_partner(normed)
    cotangent_rows = cotangent.reshape(rows, MODEL_WIDTH)
    pair_rows = CORES * rows

    def own_columns(values):
        split = values.reshape(values.shape[0], -1, CORES, HEAD_SIZE)
        return pick(split, core, 2).reshape(values.shape[0], MODEL_WIDTH // CORES)

    own_normed = own_columns(both_normed)
    kv_sent = dot_nn(own_normed[rows:], key_value_rows).astype(BF16)
    kv_near = dot_nn(own_normed[:rows], key_value_rows)
    q_proj = dot_nt(both_normed, query_rows)
    kv_proj, kv_low = key_value_chain(
        kv_near, swap(kv_sent), gain_key[None], cosine_table[0], sine_table[0]
    )
    own_kv = after(jnp.concatenate(ring_blocks(kv_low, "fsdp", ring), axis=0), q_proj)
    both_kv = with_partner(own_kv).reshape(CORES, complete_rows, 2 * KV_WIDTH)
    attention_inputs = (q_proj, both_kv, mask, gain_query[None], cosine_table, sine_table)
    att_low, att_turned = attention(*attention_inputs)
    team_cotangent = with_partner(
        jnp.concatenate(ring_blocks(after(cotangent_rows, own_kv), "fsdp", ring), axis=0)
    )
    out_sent = dot_nn(att_low[rows:], output_rows).astype(BF16)
    out_near = dot_nn(att_low[:rows], output_rows)
    middle = residual + out_near + swap(out_sent).astype(F32)

    normed_two = rms_scale(middle, gain_mlp).astype(BF16)
    team_two = with_partner(jnp.concatenate(ring_blocks(normed_two, "fsdp", ring), axis=0))
    hidden, d_gate, d_up, hidden_turned, d_gate_turned, d_up_turned = swiglu_both_ways(
        team_two, team_cotangent, (gate_ff, up_ff, down_ff)
    )
    block_rows = gate_ff.shape[2]
    own_rows = ring * rows
    other_y = 1 - lax.axis_index("y")
    own_y = lax.axis_index("y")
    down_sent = ff_grad_half(hidden_turned, team_cotangent, block_rows, other_y)
    down_passed = swap(down_sent, "y")
    down_kept = ff_grad_half(
        after(hidden_turned, down_sent), team_cotangent, block_rows, own_y
    )
    back_grads = after((d_gate, d_up), down_kept)
    back_far = back_to_width(back_grads, (gate_ff, up_ff), own_rows, own_rows)
    back_near = back_to_width(after(back_grads, back_far), (gate_ff, up_ff), 0, own_rows)
    gate_turned = after(d_gate_turned, back_near)
    gate_sent = ff_grad_half(gate_turned, team_two, block_rows, other_y)
    gate_passed = swap(gate_sent, "y")
    down_own, down_chunks, down_chunks_sent = chunks_over_z(
        [down_kept], after(down_passed, gate_sent)
    )
    back_half = back_near.astype(F32) + swap(after(back_far, down_chunks_sent)).astype(F32)
    back_half = back_half.reshape(ring, rows, MODEL_WIDTH)
    back_arrived = ring_send([back_half[step] for step in range(ring)], "fsdp", ring)
    gate_kept = ff_grad_half(after(gate_turned, back_half), team_two, block_rows, own_y)
    up_turned = after(d_up_turned, gate_kept)
    up_sent = ff_grad_half(up_turned, team_two, block_rows, other_y)
    up_passed = swap(up_sent, "y")
    up_kept = ff_grad_half(after(up_turned, up_sent), team_two, block_rows, own_y)
    back_arrived, down_chunks, gate_passed = after(
        (back_arrived, down_chunks, gate_passed), up_kept
    )
    gate_own, gate_chunks, gate_chunks_sent = chunks_over_z([gate_kept], gate_passed)
    d_normed_two = add_all(after(back_half[0], gate_chunks_sent), back_arrived)
    second_back = jax.vjp(rms_scale, middle, gain_mlp)[1]
    d_mid_norm, d_gain_mlp = second_back(d_normed_two)
    d_middle = cotangent_rows.astype(F32) + d_mid_norm

    both_mid = with_partner(d_middle.astype(BF16))
    d_head = times_rows(both_mid, attention_rows, 2)
    output_grad = weight_grad(att_turned, after(both_mid, d_head), 0, 1)
    output_blocks = jnp.moveaxis(output_grad.reshape(PLANES * CORES, ring, -1, MODEL_WIDTH), 1, 0)
    output_half = scatter_blocks(output_blocks, "fsdp").astype(BF16)
    d_head = after(d_head, output_grad)
    *far_parts, d_kv_far, far_gain = attention_back(*attention_inputs, d_head, 1, ())
    q_low, q_low_turned, d_kv_near, near_gain = attention_back(
        *attention_inputs, d_head, 0, far_parts
    )
    d_gain_query = (far_gain + near_gain)[0]
    query_grad = weight_grad(q_low_turned, both_normed, 0, 1)
    from_query = times_columns(after(q_low, query_grad), attention_rows, MODEL_WIDTH, MODEL_WIDTH)
    up_passed, gate_chunks = after((up_passed, gate_chunks), from_query)
    up_own, up_chunks, up_chunks_sent = chunks_over_z([up_kept], up_passed)
    d_kv_half = d_kv_near.astype(F32) + swap(after(d_kv_far, up_chunks_sent)).astype(F32)
    d_kv_half = d_kv_half.reshape(2, ring, rows, KV_WIDTH)
    d_kv_arrived = ring_send([d_kv_half[:, step] for step in range(ring)], "fsdp", ring)
    hidden = after(hidden, d_kv_half)
    down_far = back_to_width((hidden,), (down_ff,), own_rows, own_rows)
    down_near = back_to_width((after(hidden, down_far),), (down_ff,), 0, own_rows)
    up_chunks, d_kv_arrived, output_half = after(
        (up_chunks, d_kv_arrived, output_half), down_near
    )
    query_blocks = jnp.moveaxis(
        after(query_grad, *d_kv_arrived).reshape(PLANES * CORES, ring, -1, MODEL_WIDTH), 1, 0
    )
    query_half = scatter_blocks(query_blocks, "fsdp").astype(BF16)
    d_kv_total = add_all(d_kv_half[:, 0], d_kv_arrived)
    kv_low_grad, d_gain_key = key_value_back(
        d_kv_total, kv_proj, gain_key[None], cosine_table[0], sine_table[0]
    )
    d_gain_key = d_gain_key[0]
    both_kv_low = with_partner(kv_low_grad)
    key_value_grad = dot_tn(own_normed, both_kv_low).astype(BF16)
    key_value_blocks = jnp.moveaxis(
        key_value_grad.reshape(PLANES * CORES, ring, -1, MODEL_WIDTH), 1, 0
    )
    key_value_half = scatter_blocks(key_value_blocks, "fsdp").astype(BF16)
    from_kv = times_rows(after(both_kv_low, key_value_blocks), attention_rows, 0)
    down_shard = add_all(down_own, down_chunks)
    gate_shard = add_all(gate_own, gate_chunks)
    up_shard = add_all(up_own, up_chunks)
    masters = (w_query, key_weight_master, value_weight_master, w_output, w_gate, w_up, w_down)
    moments = (
        moment_query,
        moment_key,
        moment_value,
        moment_output,
        moment_gate,
        moment_up,
        moment_down,
    )
    full_sides = (MODEL_WIDTH,) * 4 + (FF,) * 3
    sideways = (True, False, False, False, True, True, False)

    def updated(shard, idx):
        grad = shard.T if sideways[idx] else shard
        moment = MOMENTUM * moments[idx] + grad
        update = grad + MOMENTUM * moment
        return grad, moment, (update.T if sideways[idx] else update).astype(BF16)

    plane = lax.axis_index("z")
    in_plane = ("y", "core", "fsdp")
    big = [updated(gate_shard, 4), updated(up_shard, 5), updated(down_shard, 6)]
    slots = jnp.stack([form for _, _, form in big] + [jnp.zeros_like(big[0][2])])
    big_mine = to_planes(slots).reshape(-1, MODEL_WIDTH)
    big_mine, query_half, key_value_half = after(
        (big_mine, query_half, key_value_half), from_kv
    )
    kept, arrived, attention_passed = halves_over_y([output_half, query_half, key_value_half])
    big_gram = dot_tn(after(big_mine, attention_passed), big_mine)

    from_query = from_query[:rows].astype(F32) + swap(from_query[rows:]).astype(F32)
    kv_here = from_kv[:rows].reshape(rows, -1, HEAD_SIZE)
    kv_there = swap(from_kv[rows:]).reshape(rows, -1, HEAD_SIZE)
    from_kv_full = jnp.stack(
        [jnp.where(core == 0, kv_here, kv_there), jnp.where(core == 0, kv_there, kv_here)], axis=2
    ).reshape(rows, MODEL_WIDTH)
    d_normed = from_query + from_kv_full.astype(F32)
    first_back = jax.vjp(rms_scale, residual, gain_attn)[1]
    d_residual, d_gain_attn = first_back(d_normed)
    input_grad = (d_middle + d_residual).reshape(inputs.shape)
    down_half = (down_near.astype(F32) + swap(after(down_far, big_gram)).astype(F32)).reshape(
        ring, rows, MODEL_WIDTH
    )
    down_arrived = ring_send([down_half[step] for step in range(ring)], "fsdp", ring)
    block_out = (middle + add_all(down_half[0], down_arrived)).astype(BF16).reshape(inputs.shape)
    gain_grad = jnp.concatenate([d_gain_attn, d_gain_mlp, d_gain_query, d_gain_key])

    big_gram, gain_grad, arrived = sum_over_plane(big_gram, gain_grad, arrived)
    attention_own, attention_chunks, _ = chunks_over_z(kept, arrived)
    attention_total = add_all(attention_own, attention_chunks)
    output_shard = attention_total[:, :MODEL_WIDTH]
    query_shard = attention_total[:, MODEL_WIDTH : 2 * MODEL_WIDTH]
    key_value_shard = attention_total[:, 2 * MODEL_WIDTH :]
    small = [
        updated(query_shard, 0),
        updated(key_value_shard[:, :KV_WIDTH], 1),
        updated(key_value_shard[:, KV_WIDTH:], 2),
        updated(output_shard, 3),
    ]
    small_slots = jnp.stack(
        [
            small[0][2],
            jnp.concatenate([small[1][2], small[2][2]], axis=1),
            small[3][2],
            jnp.zeros_like(small[3][2]),
        ]
    )
    small_mine = to_planes(small_slots).reshape(-1, MODEL_WIDTH)
    whole = gather_rows(small_mine, in_plane)
    turned = orthogonal_rows(big_mine, big_gram, jnp.bool_(False), small_mine)
    turned, whole = lax.optimization_barrier((turned, whole))
    returned = from_planes(turned.reshape(slots.shape))
    turned = orthogonal_rows(small_mine, dot_tn(whole, whole), plane == 1, small_mine)
    turned, returned = lax.optimization_barrier((turned, returned))
    small_returned = from_planes(turned.reshape(small_slots.shape))
    ortho = (
        small_returned[0],
        small_returned[1][:, :KV_WIDTH],
        small_returned[1][:, KV_WIDTH:],
        small_returned[2],
        *returned[:3],
    )
    new_weights = tuple(
        master * (1.0 - LR_MUON * DECAY_MUON)
        - LR_MUON * math.sqrt(side) * (rows_now.T if turn else rows_now).astype(F32)
        for master, rows_now, turn, side in zip(masters, ortho, sideways, full_sides)
    )

    first_new = BETA_ONE * gain_first + (1.0 - BETA_ONE) * gain_grad
    second_new = BETA_TWO * gain_second + (1.0 - BETA_TWO) * gain_grad * gain_grad
    corr_one = 1.0 - BETA_ONE**ADAM_STEP
    corr_two = 1.0 - BETA_TWO**ADAM_STEP
    gains_new = norm_gains - LR_GAIN * (first_new / corr_one) / (
        jnp.sqrt(second_new / corr_two) + EPS_ADAM
    )
    return (
        block_out,
        input_grad,
        *(grad for grad, _, _ in small + big),
        *(moment for _, moment, _ in small + big),
        *new_weights,
        first_new,
        second_new,
        gains_new,
    )


def solution(mesh):
    dp_size, fsdp_size = mesh.devices.shape
    fine_mesh = Mesh(
        mesh.devices.reshape(PLANES, dp_size // (PLANES * CORES), CORES, fsdp_size),
        ("z", "y", "core", "fsdp"),
    )
    dp = ("z", "y", "core")
    tokens = P(dp, "fsdp", None)
    by_row = P(EVERYWHERE, None)
    by_col = P(None, EVERYWHERE)
    matrices = (by_col, by_row, by_row, by_row, by_col, by_col, by_row)
    return jax.shard_map(
        per_device,
        mesh=fine_mesh,
        in_specs=(tokens, tokens, P(dp, None), *matrices, *matrices, P(), P(), P()),
        out_specs=(tokens, tokens, *matrices, *matrices, *matrices, P(), P(), P()),
        check_vma=False,
    )
```

time: 4870 us -> 1640 us (0.34)
  waiting for transfers between devices: 3540 us -> 708 us
  matrix products: 627 us -> 70.6 us
  Pallas kernels: 0 us -> 415 us
  blocking collectives: 317 us -> 0 us
  starting transfers between devices: 8.05 us -> 112 us
    reduce_scatter x9 -> x0, waiting for transfers between devices: 2280 us -> none  [the longest x1 437 us: per_device(): lax.psum_scatter(d_wdown, ('dp', 'fsdp'), scatter_dimension=0, tiled=True)]
    dot_general x33 -> x8, matrix products: 627 us -> 70.6 us  [the longest x3 36.6 us: dot_tn(): lax.dot_general(left, right, (((0,), (0,)), ((), ())), preferred_element_...]
    ppermute x0 -> x66, waiting for transfers between devices: none -> 521 us  [the longest x8 160 us: ring_blocks(): lax.ppermute(value, axis_name, shifted(step, count))]
    all_gather x9 -> x5, waiting for transfers between devices: 670 us -> 186 us  [gather_rows(): return lax.all_gather(shard, axes, axis=0, tiled=True)]
    pallas_call x0 -> x25, Pallas kernels: none -> 415 us  [the longest x2 87.5 us: chain(): pl.pallas_call(chain_kernel, grid=(), in_specs=[block, whole, whole], out...]
    psum x2 -> x0, waiting for transfers between devices: 397 us -> none  [per_device(): gram = lax.psum(partial_gram.astype(jnp.bfloat16), 'fsdp')]
    all_to_all x1 -> x0, blocking collectives: 278 us -> none  [per_device(): lax.all_to_all(jnp.stack(pieces), 'dp', split_axis=0, concat_axis=1, tile...]
    all_to_all x1 -> x0, waiting for transfers between devices: 198 us -> none  [per_device(): lax.all_to_all(current[None], 'dp', split_axis=1, concat_axis=0, tiled=True)]
  transfers between devices with their start and end apart: 21 -> 71, of which waited for: 21 -> 37; matrix products, arithmetic and copies ran while one was open for 8% -> 16% of each run, Pallas kernels for 0% -> 21%
where the time goes in v1:
time: 1640 us; the launch traced here: 1630 us
  waiting for transfers between devices  708 us (43%)
  Pallas kernels  415 us (25%)
  other arithmetic  189 us (12%)
  local copies, waits for them, and re-layouts  112 us (7%)
  starting transfers between devices  112 us (7%)
  matrix products  70.6 us (4%)
  between operations  19.7 us (1%)
    all_gather x5, waiting for transfers between devices, gather_rows(): return lax.all_gather(shard, axes, axis=0, tiled=True)  186 us
    ppermute x8, waiting for transfers between devices, ring_blocks(): lax.ppermute(value, axis_name, shifted(step, count))  160 us
    ppermute x8, waiting for transfers between devices, scatter_blocks(): lax.ppermute(pick(blocks, (here + step) % count), axis_name, shifted(step...  94.5 us
    pallas_call x2, Pallas kernels, chain(): pl.pallas_call(chain_kernel, grid=(), in_specs=[block, whole, whole], out...  87.5 us
    pallas_call x8, Pallas kernels, weight_grad(): pl.pallas_call(weight_grad_kernel, grid_spec=pltpu.PrefetchScalarGridSpec...  68.4 us
    ppermute x6, waiting for transfers between devices, to_planes(): lax.ppermute(pick(chunks, (here + step) % PLANES), 'z', shifted(step, PLA...  64.8 us
    pallas_call x4, Pallas kernels, back_to_width(): pl.pallas_call(functools.partial(back_to_width_kernel, len(lefts)), grid=...  62.3 us
    pallas_call x1, Pallas kernels, swiglu_both_ways(): pl.pallas_call(swiglu_kernel, grid=(CORES // ys, tokens // tile), in_spec...  53.5 us
  transfers between devices with their start and end apart: 71, of which 37 were waited for; matrix products, arithmetic and copies ran while one was open for 16% of the time, Pallas kernels for 21%

profile of v1, /device:TPU:0, one launch (start us, length us, event | category | flops | bytes accessed | tf_op | source)
XLA Modules:
  0.0 1626.6 jit_solution(2711099838084454618)
XLA Ops:
  27.0 7.7 reshape.448
  34.7 8.5 constant_dynamic-slice_fusion.9
  43.2 9.1 copy.53
  53.6 113.7 %all-gather.9.cloned.1.call-done.right_ref = bf16[1024,6144]{1,0:T(8,128)(2,1)} async-done(((bf16[64,6144]{1,0:T(8,128)(2,1)}), bf16[1024,6144]{1,0:T(8,128)(2,1)}) %all-gather.9.cloned.1.call-update) | async-done | bytes 12582928 | tf_op jit(solution)/shard_map/all_gather | solution.py:543
  167.4 5.9 fusion.30
  191.1 9.4 fusion.17.q_ref
  200.5 37.0 %collective-permute-done.3 = bf16[512,2048]{1,0:T(8,128)(2,1)S(1)} collective-permute-done((bf16[512,2048]{1,0:T(8,128)(2,1)S(1)}, bf16[512,2048]{1,0:T(8,128)(2,1)S(1)}, u32[]{:S(2)}, u32[]{:S(2)}) %collective-permute-start.3) | collective-permute-done | bytes 2097184 | tf_op jit(solution)/shard_map/ppermute | solution.py:521
  245.4 8.6 pad_maximum_fusion
  256.2 19.0 %attention.1 = (bf16[1024,1024]{1,0:T(8,128)(2,1)S(1)}, bf16[1024,1024]{1,0:T(8,128)(2,1)S(1)}) custom-call(f32[1024,1024]{1,0:T(8,128)S(1)} %copy-done.1, bf16[2,1024,2048]{2,1,0:T(8,128)(2,1)} %bitcast.327, bf16[2,1024,2048]{2,1,0:T(8,128)(2,1)} %bitcast.328, bf16[2,1024,512]{2,1,0:T(8,128)(2,1)S(1)} %and_convert_fusion.mask_ref, ...), custom_call_target="tpu_custom_call" | custom-call | flops 1 | bytes 1 | tf_op jit(solution)/shard_map/attention/pallas_call | solution.py:302
  275.2 7.6 fusion.33
  287.3 6.0 multiply_reduce_fusion.2
  297.6 35.2 %collective-permute-done.8 = bf16[512,2048]{1,0:T(8,128)(2,1)S(1)} collective-permute-done((bf16[512,2048]{1,0:T(8,128)(2,1)}, bf16[512,2048]{1,0:T(8,128)(2,1)S(1)}, u32[]{:S(2)}, u32[]{:S(2)}) %collective-permute-start.8) | collective-permute-done | bytes 2097184 | tf_op jit(solution)/shard_map/ppermute | solution.py:521
  335.5 41.7 %collective-permute-done.6 = bf16[512,2048]{1,0:T(8,128)(2,1)S(1)} collective-permute-done((bf16[512,2048]{1,0:T(8,128)(2,1)S(1)}, bf16[512,2048]{1,0:T(8,128)(2,1)S(1)}, u32[]{:S(2)}, u32[]{:S(2)}) %collective-permute-start.6) | collective-permute-done | bytes 2097184 | tf_op jit(solution)/shard_map/ppermute | solution.py:521
  388.7 6.2 pad_maximum_fusion.1.two_ref.right_ref
  394.9 72.3 %all-gather.17.cloned.1.call-done = bf16[1536,2048]{1,0:T(8,128)(2,1)} async-done(((bf16[192,2048]{1,0:T(8,128)(2,1)}), bf16[1536,2048]{1,0:T(8,128)(2,1)}) %all-gather.17.cloned.1.call-update) | async-done | bytes 6291472 | tf_op jit(solution)/shard_map/all_gather | solution.py:543
  467.2 53.5 %swiglu_both_ways.1 = (bf16[2048,1536]{1,0:T(8,128)(2,1)}, bf16[2048,1536]{1,0:T(8,128)(2,1)}, bf16[2048,1536]{1,0:T(8,128)(2,1)}, bf16[1536,2048]{1,0:T(8,128)(...) custom-call(bf16[2048,2048]{1,0:T(8,128)(2,1)} %pad_maximum_fusion.1.two_ref.right_ref, ...), custom_call_target="tpu_custom_call" | custom-call | flops 1 | bytes 1 | tf_op jit(solution)/shard_map/swiglu_both_ways/pallas_call | solution.py:364
  523.5 9.8 weight_grad.8
  536.7 9.0 weight_grad.9
  547.3 19.9 %back_to_width.4 = bf16[1024,2048]{1,0:T(8,128)(2,1)} custom-call(bf16[2048,1536]{1,0:T(8,128)(2,1)} %get-tuple-element.116.refs_0_, bf16[2048,1536]{1,0:T(8,128)(2,1)} %get-tuple-element.117.refs_1_, bf16[4,2,192,2048]{3,2,1,0:T(8,128)(2,1)} %bitcast.334, bf16[4,2,192,2048]{3,2,1,0:T(8,128)(2,1)} %bitcast.337), custom_call_target="tpu_custom_call" | custom-call | flops 1 | bytes 1 | tf_op jit(solution)/shard_map/back_to_width/pallas_call | solution.py:383
  567.1 19.9 %back_to_width.5 = bf16[1024,2048]{1,0:T(8,128)(2,1)} custom-call(bf16[2048,1536]{1,0:T(8,128)(2,1)} %get-tuple-element.116.refs_0_, bf16[2048,1536]{1,0:T(8,128)(2,1)} %get-tuple-element.117.refs_1_, bf16[4,2,192,2048]{3,2,1,0:T(8,128)(2,1)} %bitcast.335, bf16[4,2,192,2048]{3,2,1,0:T(8,128)(2,1)} %bitcast.338), custom_call_target="tpu_custom_call" | custom-call | flops 1 | bytes 1 | tf_op jit(solution)/shard_map/back_to_width/pallas_call | solution.py:383
  587.1 9.6 weight_grad.10
  596.7 6.3 collective-permute-done.10
  607.1 6.7 collective-permute-done.11
  630.1 9.0 weight_grad.11
  639.1 10.9 weight_grad.12
  650.0 9.0 weight_grad.13
  661.7 15.5 collective-permute-done.16
  692.2 16.4 %collective-permute-start.19 = (bf16[192,2048]{1,0:T(8,128)(2,1)}, bf16[192,2048]{1,0:T(8,128)(2,1)}, u32[]{:S(2)}, u32[]{:S(2)}) collective-permute-start(bf16[192,2048]{1,0:T(8,128)(2,1)} %get-tuple-element.225), channel_id=1, source_target_pairs={{0,8},{8,16},{16,24},{24,0},{1,9},{9,17},{17,25},{25,1},{2,10},{10... | collective-permute-start | bytes 2359304 | tf_op jit(solution)/shard_map/ppermute | solution.py:621
  711.6 6.9 times_rows.2.grad_ref
  727.5 21.8 %attention_back.2 = (bf16[1024,1024]{1,0:T(8,128)(2,1)S(1)}, bf16[1024,1024]{1,0:T(8,128)(2,1)S(1)}, bf16[2,1024,1024]{2,1,0:T(8,128)(2,1)}, f32[1,128]{1,0:T(1,128)S(1)}) custom-call(f32[1024,1024]{1,0:T(8,128)} %fusion.17.q_ref, bf16[2,1024,2048]{2,1,0:T(8,128)(2,1)} %bitcast.329, bf16[2,1024,2048]{2,1,0:T(8,128)(2,1)} %bitcast.330, ...), custom_call_target="tpu_custom_call" | custom-call | flops 1 | bytes 1 | tf_op jit(solution)/shard_map/attention_back/pallas_call | solution.py:326
  749.3 22.1 %attention_back.3 = (bf16[1024,1024]{1,0:T(8,128)(2,1)S(1)}, bf16[1024,1024]{1,0:T(8,128)(2,1)S(1)}, bf16[2,1024,1024]{2,1,0:T(8,128)(2,1)}, f32[1,128]{1,0:T(1,128)S(1)}) custom-call(f32[1024,1024]{1,0:T(8,128)} %fusion.17.q_ref, bf16[2,1024,2048]{2,1,0:T(8,128)(2,1)} %bitcast.331, ...), custom_call_target="tpu_custom_call", output_to_operand_aliasing={{0}: (8, {}), {1}: (9, {})} | custom-call | flops 1 | bytes 1 | tf_op jit(solution)/shard_map/attention_back/pallas_call | solution.py:326
  779.1 6.5 times_columns.1
  812.7 30.6 %collective-permute-done.27 = bf16[8,64,2048]{2,1,0:T(8,128)(2,1)} collective-permute-done((bf16[8,64,2048]{2,1,0:T(8,128)(2,1)}, bf16[8,64,2048]{2,1,0:T(8,128)(2,1)}, u32[]{:S(2)}, u32[]{:S(2)}) %collective-permute-start.27) | collective-permute-done | bytes 2097184 | tf_op jit(solution)/shard_map/ppermute | solution.py:550
  847.7 11.3 back_to_width.6
  859.0 11.3 back_to_width.7
  870.3 17.5 %collective-permute-done.26 = bf16[2,512,1024]{2,1,0:T(8,128)(2,1)} collective-permute-done((bf16[2,512,1024]{2,1,0:T(8,128)(2,1)}, bf16[2,512,1024]{2,1,0:T(8,128)(2,1)}, u32[]{:S(2)}, u32[]{:S(2)}) %collective-permute-start.26) | collective-permute-done | bytes 2097184 | tf_op jit(solution)/shard_map/ppermute | solution.py:527
  929.7 18.1 %collective-permute-done.28 = bf16[192,2048]{1,0:T(8,128)(2,1)} collective-permute-done((bf16[192,2048]{1,0:T(8,128)(2,1)}, bf16[192,2048]{1,0:T(8,128)(2,1)}, u32[]{:S(2)}, u32[]{:S(2)}) %collective-permute-start.28) | collective-permute-done | bytes 786464 | tf_op jit(solution)/shard_map/ppermute | solution.py:639
  947.8 32.5 %collective-permute-done.29 = bf16[192,2048]{1,0:T(8,128)(2,1)} collective-permute-done((bf16[192,2048]{1,0:T(8,128)(2,1)}, bf16[192,2048]{1,0:T(8,128)(2,1)}, u32[]{:S(2)}, u32[]{:S(2)}) %collective-permute-start.29) | collective-permute-done | bytes 786464 | tf_op jit(solution)/shard_map/ppermute | solution.py:639
  982.4 7.6 times_rows.3
  992.6 8.1 collective-permute-done.33
  1005.6 7.0 fusion.105
  1020.3 8.1 collective-permute-done.37
  1035.9 6.7 reshape.486
  1064.2 21.5 %collective-permute-done.42 = f32[4352]{0:T(1024)S(1)} collective-permute-done((f32[4352]{0:T(1024)S(1)}, f32[4352]{0:T(1024)S(1)}, u32[]{:S(2)}, u32[]{:S(2)}) %collective-permute-start.42) | collective-permute-done | bytes 17440 | tf_op jit(solution)/shard_map/ppermute | solution.py:629
  1085.7 55.8 %collective-permute-done.41 = bf16[256,2048]{1,0:T(8,128)(2,1)} collective-permute-done((bf16[256,2048]{1,0:T(8,128)(2,1)S(1)}, bf16[256,2048]{1,0:T(8,128)(2,1)}, u32[]{:S(2)}, u32[]{:S(2)}) %collective-permute-start.41) | collective-permute-done | bytes 1048608 | tf_op jit(solution)/shard_map/ppermute | solution.py:550
  1146.0 10.0 collective-permute-start.44
  1158.5 16.1 collective-permute-done.44
  1174.6 32.3 %collective-permute-done.45 = bf16[64,6144]{1,0:T(8,128)(2,1)S(1)} collective-permute-done((bf16[64,6144]{1,0:T(8,128)(2,1)S(1)}, bf16[64,6144]{1,0:T(8,128)(2,1)S(1)}, u32[]{:S(2)}, u32[]{:S(2)}) %collective-permute-start.45) | collective-permute-done | bytes 786464 | tf_op jit(solution)/shard_map/ppermute | solution.py:621
  1212.0 17.4 %collective-permute-start.47 = (bf16[64,2048]{1,0:T(8,128)(2,1)S(1)}, bf16[64,2048]{1,0:T(8,128)(2,1)S(1)}, u32[]{:S(2)}, u32[]{:S(2)}) collective-permute-start(bf16[64,2048]{1,0:T(8,128)(2,1)S(1)} %get-tuple-element.275), channel_id=1, source_target_pairs={{0,8},{8,16},{16,24},{24,0},{1,9},{9,17},{17,25},{25,1},{2,10},{10... | collective-permute-start | bytes 786440 | tf_op jit(solution)/shard_map/ppermute | solution.py:639
  1238.5 9.2 collective-permute-done.48
  1250.9 12.2 collective-permute-done.52
  1267.1 10.8 collective-permute-start.55
  1286.6 16.5 %collective-permute-done.53 = bf16[128,2048]{1,0:T(8,128)(2,1)S(1)} collective-permute-done((bf16[128,2048]{1,0:T(8,128)(2,1)}, bf16[128,2048]{1,0:T(8,128)(2,1)S(1)}, u32[]{:S(2)}, u32[]{:S(2)}) %collective-permute-start.53) | collective-permute-done | bytes 524320 | tf_op jit(solution)/shard_map/ppermute | solution.py:521
  1306.3 24.3 %collective-permute-done.57 = bf16[256,2048]{1,0:T(8,128)(2,1)S(1)} collective-permute-done((bf16[256,2048]{1,0:T(8,128)(2,1)S(1)}, bf16[256,2048]{1,0:T(8,128)(2,1)S(1)}, u32[]{:S(2)}, u32[]{:S(2)}) %collective-permute-start.57) | collective-permute-done | bytes 1048608 | tf_op jit(solution)/shard_map/ppermute | solution.py:521
  1338.4 7.2 fusion.10
  1363.2 8.2 fusion.2.gram_ref.tile_ref
  1371.4 26.7 %collective-permute-done.35 = bf16[512,2048]{1,0:T(8,128)(2,1)} collective-permute-done((bf16[512,2048]{1,0:T(8,128)(2,1)S(1)}, bf16[512,2048]{1,0:T(8,128)(2,1)}, u32[]{:S(2)}, u32[]{:S(2)}) %collective-permute-start.35) | collective-permute-done | bytes 2097184 | tf_op jit(solution)/shard_map/ppermute | solution.py:527
  1403.4 25.1 %bend_of.2.bend_ref = bf16[2048,2048]{1,0:T(8,128)(2,1)} custom-call(bf16[2048,2048]{1,0:T(8,128)(2,1)} %fusion.2.gram_ref.tile_ref, bf16[2048,2048]{1,0:T(8,128)(2,1)} %fusion.2.gram_ref.tile_ref), custom_call_target="tpu_custom_call" | custom-call | flops 1 | bytes 1 | tf_op jit(solution)/shard_map/bend_of/pallas_call | solution.py:448
  1431.1 59.8 %chain.2 = bf16[768,2048]{1,0:T(8,128)(2,1)} custom-call(bf16[768,2048]{1,0:T(8,128)(2,1)} %multiply_convert_fusion.start_ref, bf16[2048,2048]{1,0:T(8,128)(2,1)} %fusion.2.gram_ref.tile_ref, bf16[2048,2048]{1,0:T(8,128)(2,1)} %bend_of.2.bend_ref), custom_call_target="tpu_custom_call" | custom-call | flops 1 | bytes 1 | tf_op jit(solution)/shard_map/chain/pallas_call | solution.py:490
  1490.9 24.9 %select_reduce_fusion = (f32[2048]{0:T(1024)S(1)}, f32[2048,2048]{1,0:T(8,128)}) fusion(bf16[2048,2048]{1,0:T(8,128)(2,1)} %all-gather.11.cloned.1.call-done), kind=kOutput, calls=%fused_computation.6 | convolution fusion | flops 17192450048 | bytes 25174016 | tf_op jit(solution)/shard_map/dot_general | solution.py:68
  1524.1 11.1 select_convert_fusion.gram_ref.tile_ref
  1535.9 24.8 %bend_of.3.bend_ref = bf16[2048,2048]{1,0:T(8,128)(2,1)} custom-call(bf16[2048,2048]{1,0:T(8,128)(2,1)} %select_convert_fusion.gram_ref.tile_ref, bf16[2048,2048]{1,0:T(8,128)(2,1)} %select_convert_fusion.gram_ref.tile_ref), custom_call_target="tpu_custom_call" | custom-call | flops 1 | bytes 1 | tf_op jit(solution)/shard_map/bend_of/pallas_call | solution.py:448
  1561.9 27.7 %chain.3 = bf16[256,2048]{1,0:T(8,128)(2,1)} custom-call(bf16[256,2048]{1,0:T(8,128)(2,1)} %multiply_convert_fusion.2.start_ref, bf16[2048,2048]{1,0:T(8,128)(2,1)} %select_convert_fusion.gram_ref.tile_ref, bf16[2048,2048]{1,0:T(8,128)(2,1)} %bend_of.3.bend_ref), custom_call_target="tpu_custom_call" | custom-call | flops 1 | bytes 1 | tf_op jit(solution)/shard_map/chain/pallas_call | solution.py:490
  1600.9 16.1 collective-permute-done.64
  (506 shorter events, 350.0 us)
Async XLA Ops:
  7.2 160.1 %all-gather.9.cloned.1.call-start = ((), (), s32[]{:S(2)}) async-start(), calls=%async_computation | async-start | bytes 13369344 | tf_op jit(solution)/shard_map/all_gather | solution.py:543
  12.5 382.4 %all-gather.13.cloned.1.call-start = ((), (), s32[]{:S(2)}) async-start(), calls=%async_computation.2 | async-start | bytes 7077888 | tf_op jit(solution)/shard_map/all_gather | solution.py:543
  15.0 380.0 %all-gather.15.cloned.1.call-start = ((), (), s32[]{:S(2)}) async-start(), calls=%async_computation.3 | async-start | bytes 7077888 | tf_op jit(solution)/shard_map/all_gather | solution.py:543
  17.9 155.4 %collective-permute-start.2 = (s32[1,1024]{1,0:T(1,128)S(1)}, s32[1,1024]{1,0:T(1,128)S(1)}, u32[]{:S(2)}, u32[]{:S(2)}) collective-permute-start(s32[1,1024]{1,0:T(1,128)S(1)} %copy-done.109), channel_id=1, source_target_pairs={{0,2},{2,0},{1,3},{3,1},{4,6},{6,4},{5,7},{7,5},{8,10},{10,8},{9,1... | collective-permute-start | bytes 12296 | tf_op jit(solution)/shard_map/ppermute | solution.py:512
  19.0 448.2 %all-gather.17.cloned.1.call-start = ((), (), s32[]{:S(2)}) async-start(), calls=%async_computation.4 | async-start | bytes 7077888 | tf_op jit(solution)/shard_map/all_gather | solution.py:543
  173.2 9.3 collective-permute-start.1
  189.5 48.0 %collective-permute-start.3 = (bf16[512,2048]{1,0:T(8,128)(2,1)S(1)}, bf16[512,2048]{1,0:T(8,128)(2,1)S(1)}, u32[]{:S(2)}, u32[]{:S(2)}) collective-permute-start(bf16[512,2048]{1,0:T(8,128)(2,1)S(1)} %get-tuple-element.105), channel_id=1, source_target_pairs={{0,1},{1,0},{2,3},{3,2},{4,5},{5,4},{6,7},{7,6},{8,9},{9,8},{10,11... | collective-permute-start | bytes 6291464 | tf_op jit(solution)/shard_map/ppermute | solution.py:521
  284.1 1206.9 %all-gather.11.cloned.1.call-start = ((), (), s32[]{:S(2)}) async-start(), calls=%async_computation.1 | async-start | bytes 9437184 | tf_op jit(solution)/shard_map/all_gather | solution.py:543
  284.1 48.7 %collective-permute-start.8 = (bf16[512,2048]{1,0:T(8,128)(2,1)}, bf16[512,2048]{1,0:T(8,128)(2,1)S(1)}, u32[]{:S(2)}, u32[]{:S(2)}) collective-permute-start(bf16[512,2048]{1,0:T(8,128)(2,1)} %bitcast.344), channel_id=1, source_target_pairs={{0,1},{1,0},{2,3},{3,2},{4,5},{5,4},{6,7},{7,6},{8,9},{9,8},{10,11... | collective-permute-start | bytes 6291464 | tf_op jit(solution)/shard_map/ppermute | solution.py:521
  295.9 81.3 %collective-permute-start.6 = (bf16[512,2048]{1,0:T(8,128)(2,1)S(1)}, bf16[512,2048]{1,0:T(8,128)(2,1)S(1)}, u32[]{:S(2)}, u32[]{:S(2)}) collective-permute-start(bf16[512,2048]{1,0:T(8,128)(2,1)S(1)} %multiply_convert_fusion.1), channel_id=1, source_target_pairs={{0,1},{1,0},{2,3},{3,2},{4,5},{5,4},{6,7},{7,6},{8,9},{9,8},{10,11... | collective-permute-start | bytes 6291464 | tf_op jit(solution)/shard_map/ppermute | solution.py:521
  335.5 48.3 %collective-permute-start.9 = (bf16[1024,2048]{1,0:T(8,128)(2,1)}, bf16[1024,2048]{1,0:T(8,128)(2,1)}, u32[]{:S(2)}, u32[]{:S(2)}) collective-permute-start(bf16[1024,2048]{1,0:T(8,128)(2,1)} %pad_maximum_fusion.6), channel_id=1, source_target_pairs={{0,2},{2,0},{1,3},{3,1},{4,6},{6,4},{5,7},{7,5},{8,10},{10,8},{9,1... | collective-permute-start | bytes 12582920 | tf_op jit(solution)/shard_map/ppermute | solution.py:512
  379.9 8.7 collective-permute-start.7
  533.3 69.7 %collective-permute-start.10 = (bf16[4,192,2048]{2,1,0:T(8,128)(2,1)}, bf16[4,192,2048]{2,1,0:T(8,128)(2,1)}, u32[]{:S(2)}, u32[]{:S(2)}) collective-permute-start(bf16[4,192,2048]{2,1,0:T(8,128)(2,1)} %bitcast.18), channel_id=1, source_target_pairs={{0,4},{4,0},{1,5},{5,1},{2,6},{6,2},{3,7},{7,3},{8,12},{12,8},{9,1... | collective-permute-start | bytes 9437192 | tf_op jit(solution)/shard_map/ppermute | solution.py:512
  606.6 70.6 %collective-permute-start.16 = (bf16[4,192,2048]{2,1,0:T(8,128)(2,1)S(1)}, bf16[4,192,2048]{2,1,0:T(8,128)(2,1)}, u32[]{:S(2)}, u32[]{:S(2)}) collective-permute-start(bf16[4,192,2048]{2,1,0:T(8,128)(2,1)S(1)} %bitcast.324), channel_id=1, source_target_pairs={{0,4},{4,0},{1,5},{5,1},{2,6},{6,2},{3,7},{7,3},{8,12},{12,8},{9,1... | collective-permute-start | bytes 9437192 | tf_op jit(solution)/shard_map/ppermute | solution.py:512
  624.2 56.8 %collective-permute-start.12 = (bf16[512,2048]{1,0:T(8,128)(2,1)}, bf16[512,2048]{1,0:T(8,128)(2,1)}, u32[]{:S(2)}, u32[]{:S(2)}) collective-permute-start(bf16[512,2048]{1,0:T(8,128)(2,1)} %slice.339), channel_id=1, source_target_pairs={{0,1},{1,0},{2,3},{3,2},{4,5},{5,4},{6,7},{7,6},{8,9},{9,8},{10,11... | collective-permute-start | bytes 6291464 | tf_op jit(solution)/shard_map/ppermute | solution.py:527
  625.6 52.1 %collective-permute-start.13 = (bf16[192,2048]{1,0:T(8,128)(2,1)}, bf16[192,2048]{1,0:T(8,128)(2,1)}, u32[]{:S(2)}, u32[]{:S(2)}) collective-permute-start(bf16[192,2048]{1,0:T(8,128)(2,1)} %get-tuple-element.228), channel_id=1, source_target_pairs={{0,8},{8,16},{16,24},{24,0},{1,9},{9,17},{17,25},{25,1},{2,10},{10... | collective-permute-start | bytes 2359304 | tf_op jit(solution)/shard_map/ppermute | solution.py:621
  625.6 55.3 %collective-permute-start.14 = (bf16[192,2048]{1,0:T(8,128)(2,1)}, bf16[192,2048]{1,0:T(8,128)(2,1)}, u32[]{:S(2)}, u32[]{:S(2)}) collective-permute-start(bf16[192,2048]{1,0:T(8,128)(2,1)} %get-tuple-element.227), channel_id=1, source_target_pairs={{0,16},{8,24},{16,0},{24,8},{1,17},{9,25},{17,1},{25,9},{2,18},{10... | collective-permute-start | bytes 2359304 | tf_op jit(solution)/shard_map/ppermute | solution.py:621
  628.3 52.6 %collective-permute-start.15 = (bf16[192,2048]{1,0:T(8,128)(2,1)}, bf16[192,2048]{1,0:T(8,128)(2,1)}, u32[]{:S(2)}, u32[]{:S(2)}) collective-permute-start(bf16[192,2048]{1,0:T(8,128)(2,1)} %get-tuple-element.226), channel_id=1, source_target_pairs={{0,24},{8,0},{16,8},{24,16},{1,25},{9,1},{17,9},{25,17},{2,26},{10... | collective-permute-start | bytes 2359304 | tf_op jit(solution)/shard_map/ppermute | solution.py:621
  677.2 110.4 %collective-permute-start.18 = (bf16[4,192,2048]{2,1,0:T(8,128)(2,1)}, bf16[4,192,2048]{2,1,0:T(8,128)(2,1)}, u32[]{:S(2)}, u32[]{:S(2)}) collective-permute-start(bf16[4,192,2048]{2,1,0:T(8,128)(2,1)} %bitcast.25), channel_id=1, source_target_pairs={{0,4},{4,0},{1,5},{5,1},{2,6},{6,2},{3,7},{7,3},{8,12},{12,8},{9,1... | collective-permute-start | bytes 9437192 | tf_op jit(solution)/shard_map/ppermute | solution.py:512
  692.2 18.8 %collective-permute-start.17 = (bf16[512,2048]{1,0:T(8,128)(2,1)S(1)}, bf16[512,2048]{1,0:T(8,128)(2,1)S(1)}, u32[]{:S(2)}, u32[]{:S(2)}) collective-permute-start(bf16[512,2048]{1,0:T(8,128)(2,1)S(1)} %get-tuple-element.216), channel_id=1, source_target_pairs={{0,2},{2,0},{1,3},{3,1},{4,6},{6,4},{5,7},{7,5},{8,10},{10,8},{9,1... | collective-permute-start | bytes 6291464 | tf_op jit(solution)/shard_map/ppermute | solution.py:512
  692.2 95.4 %collective-permute-start.19 = (bf16[192,2048]{1,0:T(8,128)(2,1)}, bf16[192,2048]{1,0:T(8,128)(2,1)}, u32[]{:S(2)}, u32[]{:S(2)}) collective-permute-start(bf16[192,2048]{1,0:T(8,128)(2,1)} %get-tuple-element.225), channel_id=1, source_target_pairs={{0,8},{8,16},{16,24},{24,0},{1,9},{9,17},{17,25},{25,1},{2,10},{10... | collective-permute-start | bytes 2359304 | tf_op jit(solution)/shard_map/ppermute | solution.py:621
  708.6 79.0 %collective-permute-start.20 = (bf16[192,2048]{1,0:T(8,128)(2,1)S(1)}, bf16[192,2048]{1,0:T(8,128)(2,1)}, u32[]{:S(2)}, u32[]{:S(2)}) collective-permute-start(bf16[192,2048]{1,0:T(8,128)(2,1)S(1)} %get-tuple-element.224), channel_id=1, source_target_pairs={{0,16},{8,24},{16,0},{24,8},{1,17},{9,25},{17,1},{25,9},{2,18},{10... | collective-permute-start | bytes 2359304 | tf_op jit(solution)/shard_map/ppermute | solution.py:621
  710.2 77.4 %collective-permute-start.21 = (bf16[192,2048]{1,0:T(8,128)(2,1)S(1)}, bf16[192,2048]{1,0:T(8,128)(2,1)}, u32[]{:S(2)}, u32[]{:S(2)}) collective-permute-start(bf16[192,2048]{1,0:T(8,128)(2,1)S(1)} %get-tuple-element.223), channel_id=1, source_target_pairs={{0,24},{8,0},{16,8},{24,16},{1,25},{9,1},{17,9},{25,17},{2,26},{10... | collective-permute-start | bytes 2359304 | tf_op jit(solution)/shard_map/ppermute | solution.py:621
  794.5 48.7 %collective-permute-start.27 = (bf16[8,64,2048]{2,1,0:T(8,128)(2,1)}, bf16[8,64,2048]{2,1,0:T(8,128)(2,1)}, u32[]{:S(2)}, u32[]{:S(2)}) collective-permute-start(bf16[8,64,2048]{2,1,0:T(8,128)(2,1)} %dynamic-slice_bitcast_fusion.3), channel_id=1, source_target_pairs={{0,1},{1,0},{2,3},{3,2},{4,5},{5,4},{6,7},{7,6},{8,9},{9,8},{10,11... | collective-permute-start | bytes 6291464 | tf_op jit(solution)/shard_map/ppermute | solution.py:550
  807.8 80.1 %collective-permute-start.26 = (bf16[2,512,1024]{2,1,0:T(8,128)(2,1)}, bf16[2,512,1024]{2,1,0:T(8,128)(2,1)}, u32[]{:S(2)}, u32[]{:S(2)}) collective-permute-start(bf16[2,512,1024]{2,1,0:T(8,128)(2,1)} %fusion.39), channel_id=1, source_target_pairs={{0,1},{1,0},{2,3},{3,2},{4,5},{5,4},{6,7},{7,6},{8,9},{9,8},{10,11... | collective-permute-start | bytes 6291464 | tf_op jit(solution)/shard_map/ppermute | solution.py:527
  808.3 62.0 %collective-permute-start.23 = (bf16[192,2048]{1,0:T(8,128)(2,1)}, bf16[192,2048]{1,0:T(8,128)(2,1)}, u32[]{:S(2)}, u32[]{:S(2)}) collective-permute-start(bf16[192,2048]{1,0:T(8,128)(2,1)} %get-tuple-element.222), channel_id=1, source_target_pairs={{0,8},{8,16},{16,24},{24,0},{1,9},{9,17},{17,25},{25,1},{2,10},{10... | collective-permute-start | bytes 2359304 | tf_op jit(solution)/shard_map/ppermute | solution.py:621
  810.1 60.2 %collective-permute-start.24 = (bf16[192,2048]{1,0:T(8,128)(2,1)}, bf16[192,2048]{1,0:T(8,128)(2,1)}, u32[]{:S(2)}, u32[]{:S(2)}) collective-permute-start(bf16[192,2048]{1,0:T(8,128)(2,1)} %get-tuple-element.221), channel_id=1, source_target_pairs={{0,16},{8,24},{16,0},{24,8},{1,17},{9,25},{17,1},{25,9},{2,18},{10... | collective-permute-start | bytes 2359304 | tf_op jit(solution)/shard_map/ppermute | solution.py:621
  811.7 58.7 %collective-permute-start.25 = (bf16[192,2048]{1,0:T(8,128)(2,1)}, bf16[192,2048]{1,0:T(8,128)(2,1)}, u32[]{:S(2)}, u32[]{:S(2)}) collective-permute-start(bf16[192,2048]{1,0:T(8,128)(2,1)} %get-tuple-element.220), channel_id=1, source_target_pairs={{0,24},{8,0},{16,8},{24,16},{1,25},{9,1},{17,9},{25,17},{2,26},{10... | collective-permute-start | bytes 2359304 | tf_op jit(solution)/shard_map/ppermute | solution.py:621
  896.4 16.3 %collective-permute-start.32 = (bf16[512,2048]{1,0:T(8,128)(2,1)S(1)}, bf16[512,2048]{1,0:T(8,128)(2,1)S(1)}, u32[]{:S(2)}, u32[]{:S(2)}) collective-permute-start(bf16[512,2048]{1,0:T(8,128)(2,1)S(1)} %get-tuple-element.154), channel_id=1, source_target_pairs={{0,2},{2,0},{1,3},{3,1},{4,6},{6,4},{5,7},{7,5},{8,10},{10,8},{9,1... | collective-permute-start | bytes 6291464 | tf_op jit(solution)/shard_map/ppermute | solution.py:512
  907.6 82.4 %collective-permute-start.31 = (bf16[8,64,2048]{2,1,0:T(8,128)(2,1)}, bf16[8,64,2048]{2,1,0:T(8,128)(2,1)}, u32[]{:S(2)}, u32[]{:S(2)}) collective-permute-start(bf16[8,64,2048]{2,1,0:T(8,128)(2,1)} %dynamic-slice_bitcast_fusion.2), channel_id=1, source_target_pairs={{0,1},{1,0},{2,3},{3,2},{4,5},{5,4},{6,7},{7,6},{8,9},{9,8},{10,11... | collective-permute-start | bytes 6291464 | tf_op jit(solution)/shard_map/ppermute | solution.py:550
  921.5 79.3 %collective-permute-start.33 = (bf16[8,64,2048]{2,1,0:T(8,128)(2,1)}, bf16[8,64,2048]{2,1,0:T(8,128)(2,1)}, u32[]{:S(2)}, u32[]{:S(2)}) collective-permute-start(bf16[8,64,2048]{2,1,0:T(8,128)(2,1)} %dynamic-slice_bitcast_fusion.1), channel_id=1, source_target_pairs={{0,1},{1,0},{2,3},{3,2},{4,5},{5,4},{6,7},{7,6},{8,9},{9,8},{10,11... | collective-permute-start | bytes 6291464 | tf_op jit(solution)/shard_map/ppermute | solution.py:550
  925.1 22.7 %collective-permute-start.28 = (bf16[192,2048]{1,0:T(8,128)(2,1)}, bf16[192,2048]{1,0:T(8,128)(2,1)}, u32[]{:S(2)}, u32[]{:S(2)}) collective-permute-start(bf16[192,2048]{1,0:T(8,128)(2,1)} %get-tuple-element.246), channel_id=1, source_target_pairs={{0,8},{8,16},{16,24},{24,0},{1,9},{9,17},{17,25},{25,1},{2,10},{10... | collective-permute-start | bytes 2359304 | tf_op jit(solution)/shard_map/ppermute | solution.py:639
  926.8 53.5 %collective-permute-start.29 = (bf16[192,2048]{1,0:T(8,128)(2,1)}, bf16[192,2048]{1,0:T(8,128)(2,1)}, u32[]{:S(2)}, u32[]{:S(2)}) collective-permute-start(bf16[192,2048]{1,0:T(8,128)(2,1)} %get-tuple-element.245), channel_id=1, source_target_pairs={{0,16},{8,24},{16,0},{24,8},{1,17},{9,25},{17,1},{25,9},{2,18},{10... | collective-permute-start | bytes 2359304 | tf_op jit(solution)/shard_map/ppermute | solution.py:639
  928.4 51.9 %collective-permute-start.30 = (bf16[192,2048]{1,0:T(8,128)(2,1)}, bf16[192,2048]{1,0:T(8,128)(2,1)}, u32[]{:S(2)}, u32[]{:S(2)}) collective-permute-start(bf16[192,2048]{1,0:T(8,128)(2,1)} %get-tuple-element.244), channel_id=1, source_target_pairs={{0,24},{8,0},{16,8},{24,16},{1,25},{9,1},{17,9},{25,17},{2,26},{10... | collective-permute-start | bytes 2359304 | tf_op jit(solution)/shard_map/ppermute | solution.py:639
  1018.1 31.0 %collective-permute-start.38 = (bf16[1024,2048]{1,0:T(8,128)(2,1)}, bf16[1024,2048]{1,0:T(8,128)(2,1)}, u32[]{:S(2)}, u32[]{:S(2)}) collective-permute-start(bf16[1024,2048]{1,0:T(8,128)(2,1)} %dynamic-slice_bitcast_fusion), channel_id=1, source_target_pairs={{0,2},{2,0},{1,3},{3,1},{4,6},{6,4},{5,7},{7,5},{8,10},{10,8},{9,1... | collective-permute-start | bytes 12582920 | tf_op jit(solution)/shard_map/ppermute | solution.py:550
  1019.6 23.0 %collective-permute-start.36 = (bf16[512,2048]{1,0:T(8,128)(2,1)}, bf16[512,2048]{1,0:T(8,128)(2,1)}, u32[]{:S(2)}, u32[]{:S(2)}) collective-permute-start(bf16[512,2048]{1,0:T(8,128)(2,1)} %slice.243), channel_id=1, source_target_pairs={{0,2},{2,0},{1,3},{3,1},{4,6},{6,4},{5,7},{7,5},{8,10},{10,8},{9,1... | collective-permute-start | bytes 6291464 | tf_op jit(solution)/shard_map/ppermute | solution.py:512
  1020.2 8.2 collective-permute-start.37
  1048.6 95.1 %collective-permute-start.43 = (bf16[4,64,6144]{2,1,0:T(8,128)(2,1)}, bf16[4,64,6144]{2,1,0:T(8,128)(2,1)}, u32[]{:S(2)}, u32[]{:S(2)}) collective-permute-start(bf16[4,64,6144]{2,1,0:T(8,128)(2,1)} %pad_maximum_fusion.10), channel_id=1, source_target_pairs={{0,4},{4,0},{1,5},{5,1},{2,6},{6,2},{3,7},{7,3},{8,12},{12,8},{9,1... | collective-permute-start | bytes 9437192 | tf_op jit(solution)/shard_map/ppermute | solution.py:512
  1057.6 84.0 %collective-permute-start.41 = (bf16[256,2048]{1,0:T(8,128)(2,1)S(1)}, bf16[256,2048]{1,0:T(8,128)(2,1)}, u32[]{:S(2)}, u32[]{:S(2)}) collective-permute-start(bf16[256,2048]{1,0:T(8,128)(2,1)S(1)} %dynamic-slice_bitcast_fusion.4), channel_id=1, source_target_pairs={{0,4},{4,0},{1,5},{5,1},{2,6},{6,2},{3,7},{7,3},{8,12},{12,8},{9,1... | collective-permute-start | bytes 3145736 | tf_op jit(solution)/shard_map/ppermute | solution.py:550
  1060.6 82.6 %collective-permute-start.40 = (bf16[256,2048]{1,0:T(8,128)(2,1)S(1)}, bf16[256,2048]{1,0:T(8,128)(2,1)S(1)}, u32[]{:S(2)}, u32[]{:S(2)}) collective-permute-start(bf16[256,2048]{1,0:T(8,128)(2,1)S(1)} %dynamic-slice_bitcast_fusion.5), channel_id=1, source_target_pairs={{0,1},{1,0},{2,3},{3,2},{4,5},{5,4},{6,7},{7,6},{8,9},{9,8},{10,11... | collective-permute-start | bytes 3145736 | tf_op jit(solution)/shard_map/ppermute | solution.py:550
  1062.7 23.0 %collective-permute-start.42 = (f32[4352]{0:T(1024)S(1)}, f32[4352]{0:T(1024)S(1)}, u32[]{:S(2)}, u32[]{:S(2)}) collective-permute-start(f32[4352]{0:T(1024)S(1)} %fusion.95), channel_id=1, source_target_pairs={{0,1},{1,0},{2,3},{3,2},{4,5},{5,4},{6,7},{7,6},{8,9},{9,8},{10,11... | collective-permute-start | bytes 52232 | tf_op jit(solution)/shard_map/ppermute | solution.py:629
  1146.0 28.5 %collective-permute-start.44 = (bf16[64,6144]{1,0:T(8,128)(2,1)S(1)}, bf16[64,6144]{1,0:T(8,128)(2,1)S(1)}, u32[]{:S(2)}, u32[]{:S(2)}) collective-permute-start(bf16[64,6144]{1,0:T(8,128)(2,1)S(1)} %get-tuple-element.238), channel_id=1, source_target_pairs={{0,8},{8,16},{16,24},{24,0},{1,9},{9,17},{17,25},{25,1},{2,10},{10... | collective-permute-start | bytes 2359304 | tf_op jit(solution)/shard_map/ppermute | solution.py:621
  1156.0 50.8 %collective-permute-start.45 = (bf16[64,6144]{1,0:T(8,128)(2,1)S(1)}, bf16[64,6144]{1,0:T(8,128)(2,1)S(1)}, u32[]{:S(2)}, u32[]{:S(2)}) collective-permute-start(bf16[64,6144]{1,0:T(8,128)(2,1)S(1)} %get-tuple-element.240), channel_id=1, source_target_pairs={{0,16},{8,24},{16,0},{24,8},{1,17},{9,25},{17,1},{25,9},{2,18},{10... | collective-permute-start | bytes 2359304 | tf_op jit(solution)/shard_map/ppermute | solution.py:621
  1156.5 50.3 %collective-permute-start.46 = (bf16[64,6144]{1,0:T(8,128)(2,1)S(1)}, bf16[64,6144]{1,0:T(8,128)(2,1)S(1)}, u32[]{:S(2)}, u32[]{:S(2)}) collective-permute-start(bf16[64,6144]{1,0:T(8,128)(2,1)S(1)} %get-tuple-element.239), channel_id=1, source_target_pairs={{0,24},{8,0},{16,8},{24,16},{1,25},{9,1},{17,9},{25,17},{2,26},{10... | collective-permute-start | bytes 2359304 | tf_op jit(solution)/shard_map/ppermute | solution.py:621
  1212.0 26.5 %collective-permute-start.47 = (bf16[64,2048]{1,0:T(8,128)(2,1)S(1)}, bf16[64,2048]{1,0:T(8,128)(2,1)S(1)}, u32[]{:S(2)}, u32[]{:S(2)}) collective-permute-start(bf16[64,2048]{1,0:T(8,128)(2,1)S(1)} %get-tuple-element.275), channel_id=1, source_target_pairs={{0,8},{8,16},{16,24},{24,0},{1,9},{9,17},{17,25},{25,1},{2,10},{10... | collective-permute-start | bytes 786440 | tf_op jit(solution)/shard_map/ppermute | solution.py:639
  1229.3 18.3 %collective-permute-start.48 = (bf16[64,2048]{1,0:T(8,128)(2,1)S(1)}, bf16[64,2048]{1,0:T(8,128)(2,1)S(1)}, u32[]{:S(2)}, u32[]{:S(2)}) collective-permute-start(bf16[64,2048]{1,0:T(8,128)(2,1)S(1)} %get-tuple-element.274), channel_id=1, source_target_pairs={{0,16},{8,24},{16,0},{24,8},{1,17},{9,25},{17,1},{25,9},{2,18},{10... | collective-permute-start | bytes 786440 | tf_op jit(solution)/shard_map/ppermute | solution.py:639
  1231.7 16.0 collective-permute-start.49
  1232.6 30.5 %collective-permute-start.51 = (bf16[128,2048]{1,0:T(8,128)(2,1)}, bf16[128,2048]{1,0:T(8,128)(2,1)}, u32[]{:S(2)}, u32[]{:S(2)}) collective-permute-start(bf16[128,2048]{1,0:T(8,128)(2,1)} %dynamic-slice_bitcast_fusion.15), channel_id=1, source_target_pairs={{0,1},{1,0},{2,3},{3,2},{4,5},{5,4},{6,7},{7,6},{8,9},{9,8},{10,11... | collective-permute-start | bytes 1572872 | tf_op jit(solution)/shard_map/ppermute | solution.py:550
  1248.8 16.4 %collective-permute-start.50 = (bf16[128,2048]{1,0:T(8,128)(2,1)S(1)}, bf16[128,2048]{1,0:T(8,128)(2,1)S(1)}, u32[]{:S(2)}, u32[]{:S(2)}) collective-permute-start(bf16[128,2048]{1,0:T(8,128)(2,1)S(1)} %dynamic-slice_bitcast_fusion.16), channel_id=1, source_target_pairs={{0,4},{4,0},{1,5},{5,1},{2,6},{6,2},{3,7},{7,3},{8,12},{12,8},{9,1... | collective-permute-start | bytes 1572872 | tf_op jit(solution)/shard_map/ppermute | solution.py:550
  1249.5 13.6 collective-permute-start.52
  1266.2 19.2 %collective-permute-start.54 = (bf16[128,2048]{1,0:T(8,128)(2,1)}, bf16[128,2048]{1,0:T(8,128)(2,1)S(1)}, u32[]{:S(2)}, u32[]{:S(2)}) collective-permute-start(bf16[128,2048]{1,0:T(8,128)(2,1)} %fusion.56), channel_id=1, source_target_pairs={{0,1},{1,0},{2,3},{3,2},{4,5},{5,4},{6,7},{7,6},{8,9},{9,8},{10,11... | collective-permute-start | bytes 1572872 | tf_op jit(solution)/shard_map/ppermute | solution.py:521
  1267.1 12.5 collective-permute-start.55
  1280.4 22.7 %collective-permute-start.53 = (bf16[128,2048]{1,0:T(8,128)(2,1)}, bf16[128,2048]{1,0:T(8,128)(2,1)S(1)}, u32[]{:S(2)}, u32[]{:S(2)}) collective-permute-start(bf16[128,2048]{1,0:T(8,128)(2,1)} %fusion.57), channel_id=1, source_target_pairs={{0,4},{4,0},{1,5},{5,1},{2,6},{6,2},{3,7},{7,3},{8,12},{12,8},{9,1... | collective-permute-start | bytes 1572872 | tf_op jit(solution)/shard_map/ppermute | solution.py:521
  1303.3 27.3 %collective-permute-start.57 = (bf16[256,2048]{1,0:T(8,128)(2,1)S(1)}, bf16[256,2048]{1,0:T(8,128)(2,1)S(1)}, u32[]{:S(2)}, u32[]{:S(2)}) collective-permute-start(bf16[256,2048]{1,0:T(8,128)(2,1)S(1)} %pad_maximum_fusion.13), channel_id=1, source_target_pairs={{0,1},{1,0},{2,3},{3,2},{4,5},{5,4},{6,7},{7,6},{8,9},{9,8},{10,11... | collective-permute-start | bytes 3145736 | tf_op jit(solution)/shard_map/ppermute | solution.py:521
  1306.2 29.1 %collective-permute-start.58 = (bf16[256,2048]{1,0:T(8,128)(2,1)S(1)}, bf16[256,2048]{1,0:T(8,128)(2,1)S(1)}, u32[]{:S(2)}, u32[]{:S(2)}) collective-permute-start(bf16[256,2048]{1,0:T(8,128)(2,1)S(1)} %pad_maximum_fusion.14), channel_id=1, source_target_pairs={{0,4},{4,0},{1,5},{5,1},{2,6},{6,2},{3,7},{7,3},{8,12},{12,8},{9,1... | collective-permute-start | bytes 3145736 | tf_op jit(solution)/shard_map/ppermute | solution.py:521
  1306.3 39.3 %collective-permute-start.34 = (bf16[1024,2048]{1,0:T(8,128)(2,1)}, bf16[1024,2048]{1,0:T(8,128)(2,1)}, u32[]{:S(2)}, u32[]{:S(2)}) collective-permute-start(bf16[1024,2048]{1,0:T(8,128)(2,1)} %back_to_width.6), channel_id=1, source_target_pairs={{0,2},{2,0},{1,3},{3,1},{4,6},{6,4},{5,7},{7,5},{8,10},{10,8},{9,1... | collective-permute-start | bytes 12582920 | tf_op jit(solution)/shard_map/ppermute | solution.py:512
  1338.2 15.3 collective-permute-start.59
  1349.9 48.1 %collective-permute-start.35 = (bf16[512,2048]{1,0:T(8,128)(2,1)S(1)}, bf16[512,2048]{1,0:T(8,128)(2,1)}, u32[]{:S(2)}, u32[]{:S(2)}) collective-permute-start(bf16[512,2048]{1,0:T(8,128)(2,1)S(1)} %slice.338), channel_id=1, source_target_pairs={{0,1},{1,0},{2,3},{3,2},{4,5},{5,4},{6,7},{7,6},{8,9},{9,8},{10,11... | collective-permute-start | bytes 6291464 | tf_op jit(solution)/shard_map/ppermute | solution.py:527
  1519.3 70.4 %collective-permute-start.60 = (bf16[192,2048]{1,0:T(8,128)(2,1)S(1)}, bf16[192,2048]{1,0:T(8,128)(2,1)S(1)}, u32[]{:S(2)}, u32[]{:S(2)}) collective-permute-start(bf16[192,2048]{1,0:T(8,128)(2,1)S(1)} %get-tuple-element.237), channel_id=1, source_target_pairs={{0,24},{8,0},{16,8},{24,16},{1,25},{9,1},{17,9},{25,17},{2,26},{10... | collective-permute-start | bytes 2359304 | tf_op jit(solution)/shard_map/ppermute | solution.py:648
  1523.1 67.1 %collective-permute-start.61 = (bf16[192,2048]{1,0:T(8,128)(2,1)S(1)}, bf16[192,2048]{1,0:T(8,128)(2,1)S(1)}, u32[]{:S(2)}, u32[]{:S(2)}) collective-permute-start(bf16[192,2048]{1,0:T(8,128)(2,1)S(1)} %get-tuple-element.236), channel_id=1, source_target_pairs={{0,16},{8,24},{16,0},{24,8},{1,17},{9,25},{17,1},{25,9},{2,18},{10... | collective-permute-start | bytes 2359304 | tf_op jit(solution)/shard_map/ppermute | solution.py:648
  1523.1 67.1 %collective-permute-start.62 = (bf16[192,2048]{1,0:T(8,128)(2,1)S(1)}, bf16[192,2048]{1,0:T(8,128)(2,1)S(1)}, u32[]{:S(2)}, u32[]{:S(2)}) collective-permute-start(bf16[192,2048]{1,0:T(8,128)(2,1)S(1)} %get-tuple-element.235), channel_id=1, source_target_pairs={{0,8},{8,16},{16,24},{24,0},{1,9},{9,17},{17,25},{25,1},{2,10},{10... | collective-permute-start | bytes 2359304 | tf_op jit(solution)/shard_map/ppermute | solution.py:648
  1591.5 9.4 collective-permute-start.63
  1594.0 23.0 %collective-permute-start.64 = (bf16[64,2048]{1,0:T(8,128)(2,1)S(1)}, bf16[64,2048]{1,0:T(8,128)(2,1)S(1)}, u32[]{:S(2)}, u32[]{:S(2)}) collective-permute-start(bf16[64,2048]{1,0:T(8,128)(2,1)S(1)} %get-tuple-element.270), channel_id=1, source_target_pairs={{0,16},{8,24},{16,0},{24,8},{1,17},{9,25},{17,1},{25,9},{2,18},{10... | collective-permute-start | bytes 786440 | tf_op jit(solution)/shard_map/ppermute | solution.py:648
  1595.2 21.8 %collective-permute-start.65 = (bf16[64,2048]{1,0:T(8,128)(2,1)S(1)}, bf16[64,2048]{1,0:T(8,128)(2,1)S(1)}, u32[]{:S(2)}, u32[]{:S(2)}) collective-permute-start(bf16[64,2048]{1,0:T(8,128)(2,1)S(1)} %get-tuple-element.269), channel_id=1, source_target_pairs={{0,8},{8,16},{16,24},{24,0},{1,9},{9,17},{17,25},{25,1},{2,10},{10... | collective-permute-start | bytes 786440 | tf_op jit(solution)/shard_map/ppermute | solution.py:648
  (121 other events, 1697.0 us)
Sparse Core Ops, SparseCore 0:
  12.6 154.7 all-gather.8
  170.1 97.2 all-gather.12
  270.2 97.1 all-gather.14
  370.0 97.1 all-gather.16
  1248.9 80.0 all-gather.10

commit v2 on v1

--- a/solution.py
+++ b/solution.py
@@ -550,45 +550,7 @@
         lax.ppermute(pick(blocks, (here + step) % count), axis_name, shifted(step, count))
         for step in range(1, count)
     ]
-    return add_all(pick(blocks, here).astype(F32), arrived)
-
-
-def ordered_blocks(value, axis_name):
-    count = lax.axis_size(axis_name)
-    here = lax.axis_index(axis_name)
-    blocks = ring_blocks(value, axis_name, count)
-    if count == 2:
-        first = jnp.where(here == 0, blocks[0], blocks[1])
-        second = jnp.where(here == 0, blocks[1], blocks[0])
-        return jnp.concatenate([first, second], axis=0)
-    rows = value.shape[0]
-    whole = jnp.zeros((count * rows, *value.shape[1:]), value.dtype)
-    for step, block in enumerate(blocks):
-        whole = lax.dynamic_update_slice_in_dim(whole, block, (here - step) % count * rows, 0)
-    return whole
-
-
-def sum_over_plane(partial, gain, beside):
-    width = partial.shape[1]
-    ring = lax.axis_size("fsdp")
-    mine = scatter_blocks(partial.astype(BF16).reshape(CORES, -1, width), "core").astype(BF16)
-    mine, gain = lax.optimization_barrier((mine, butterfly(gain, "core")))
-    half = mine.shape[0] // 2
-    one, two = mine[:half], mine[half:]
-    one = scatter_blocks(one.reshape(ring, -1, width), "fsdp").astype(BF16)
-    two = scatter_blocks(two.reshape(CORES, -1, width), "y").astype(BF16)
-    one, two, gain, beside = lax.optimization_barrier(
-        (one, two, butterfly(gain, "fsdp"), beside)
-    )
-    one = scatter_blocks(one.reshape(CORES, -1, width), "y").astype(BF16)
-    two = scatter_blocks(two.reshape(ring, -1, width), "fsdp").astype(BF16)
-    one, two, gain = lax.optimization_barrier((one, two, butterfly(gain, "y")))
-    one = ordered_blocks(one, "y")
-    two = ordered_blocks(two, "fsdp")
-    one, two, gain = lax.optimization_barrier((one, two, butterfly(gain, "z")))
-    one = ordered_blocks(one, "fsdp")
-    two = ordered_blocks(two, "y")
-    return ordered_blocks(jnp.concatenate([one, two], axis=0), "core"), gain, beside
+    return pick(blocks, here), arrived
 
 
 def ff_grad_half(left_turned, right, block_rows, y):
@@ -622,13 +584,8 @@
     ], sent
 
 
-def butterfly(value, axis_name):
-    count = lax.axis_size(axis_name)
-    step = 1
-    while step < count:
-        value = value + lax.ppermute(value, axis_name, [(src, src ^ step) for src in range(count)])
-        step *= 2
-    return value
+def sum_everywhere(value):
+    return jnp.sum(lax.all_gather(value, EVERYWHERE, axis=0, tiled=False), axis=0)
 
 
 def to_planes(chunks):
@@ -650,22 +607,29 @@
     return [pick(back, (chunk - here) % PLANES) for chunk in range(PLANES)]
 
 
-def orthogonal_rows(update, update_gram, halves, earlier):
+def normalized(update, update_gram, halves):
     width = update.shape[1]
-    side = jnp.arange(width) < width // 2
-    index = jnp.arange(width)
+    block = 128
+    index = jnp.arange(block)
+    diagonal = jnp.stack(
+        [
+            update_gram[at : at + block, at : at + block].astype(F32)
+            for at in range(0, width, block)
+        ]
+    )
     diagonal = jnp.sum(
-        jnp.where(index[:, None] == index[None, :], update_gram.astype(F32), 0.0), axis=0
-    )
-    low_half = jnp.sum(diagonal[: width // 2])
-    high_half = jnp.sum(diagonal[width // 2 :])
+        jnp.where(index[:, None] == index[None, :], diagonal, 0.0), axis=(1, 2)
+    )
+    low_half = jnp.sum(diagonal[: width // block // 2])
+    high_half = jnp.sum(diagonal[width // block // 2 :])
     both = low_half + high_half
     squares = jnp.stack([jnp.where(halves, low_half, both), jnp.where(halves, high_half, both)])
     inverse = jnp.repeat(1.0 / (jnp.sqrt(squares) + NS_EPS), width // 2)
+    side = jnp.arange(width) < width // 2
     kept = jnp.logical_not(halves) | (side[:, None] == side[None, :])
     start = (update.astype(F32) * inverse).astype(BF16)
-    gram = jnp.where(kept, update_gram.astype(F32) * inverse[:, None] * inverse[None, :], 0.0).astype(BF16)
-    return chain(start, after(gram, earlier), bend_of(gram))
+    gram = update_gram.astype(F32) * inverse[:, None] * inverse[None, :]
+    return start, jnp.where(kept, gram, 0.0).astype(BF16)
 
 
 def per_device(
@@ -720,6 +684,25 @@
         for shard in (w_gate.astype(BF16).T, w_up.astype(BF16).T, w_down.astype(BF16))
     )
 
+    masters = (w_query, key_weight_master, value_weight_master, w_output, w_gate, w_up, w_down)
+    moments = (
+        moment_query,
+        moment_key,
+        moment_value,
+        moment_output,
+        moment_gate,
+        moment_up,
+        moment_down,
+    )
+    full_sides = (MODEL_WIDTH,) * 4 + (FF,) * 3
+    sideways = (True, False, False, False, True, True, False)
+
+    def updated(shard, idx):
+        grad = shard.T if sideways[idx] else shard
+        moment = MOMENTUM * moments[idx] + grad
+        update = grad + MOMENTUM * moment
+        return grad, moment, (update.T if sideways[idx] else update).astype(BF16)
+
     both_segments = with_partner(segments)
     row_idx = jnp.arange(complete_rows, dtype=jnp.int32)
     boundary = jnp.concatenate(
@@ -817,7 +800,7 @@
     d_head = times_rows(both_mid, attention_rows, 2)
     output_grad = weight_grad(att_turned, after(both_mid, d_head), 0, 1)
     output_blocks = jnp.moveaxis(output_grad.reshape(PLANES * CORES, ring, -1, MODEL_WIDTH), 1, 0)
-    output_half = scatter_blocks(output_blocks, "fsdp").astype(BF16)
+    output_own, output_arrived = scatter_blocks(output_blocks, "fsdp")
     d_head = after(d_head, output_grad)
     *far_parts, d_kv_far, far_gain = attention_back(*attention_inputs, d_head, 1, ())
     q_low, q_low_turned, d_kv_near, near_gain = attention_back(
@@ -826,7 +809,11 @@
     d_gain_query = (far_gain + near_gain)[0]
     query_grad = weight_grad(q_low_turned, both_normed, 0, 1)
     from_query = times_columns(after(q_low, query_grad), attention_rows, MODEL_WIDTH, MODEL_WIDTH)
-    up_passed, gate_chunks = after((up_passed, gate_chunks), from_query)
+    query_blocks = jnp.moveaxis(query_grad.reshape(PLANES * CORES, ring, -1, MODEL_WIDTH), 1, 0)
+    query_own, query_arrived = scatter_blocks(query_blocks, "fsdp")
+    up_passed, gate_chunks, output_arrived = after(
+        (up_passed, gate_chunks, output_arrived), from_query
+    )
     up_own, up_chunks, up_chunks_sent = chunks_over_z([up_kept], up_passed)
     d_kv_half = d_kv_near.astype(F32) + swap(after(d_kv_far, up_chunks_sent)).astype(F32)
     d_kv_half = d_kv_half.reshape(2, ring, rows, KV_WIDTH)
@@ -834,13 +821,20 @@
     hidden = after(hidden, d_kv_half)
     down_far = back_to_width((hidden,), (down_ff,), own_rows, own_rows)
     down_near = back_to_width((after(hidden, down_far),), (down_ff,), 0, own_rows)
-    up_chunks, d_kv_arrived, output_half = after(
-        (up_chunks, d_kv_arrived, output_half), down_near
-    )
-    query_blocks = jnp.moveaxis(
-        after(query_grad, *d_kv_arrived).reshape(PLANES * CORES, ring, -1, MODEL_WIDTH), 1, 0
-    )
-    query_half = scatter_blocks(query_blocks, "fsdp").astype(BF16)
+    gate_new = updated(add_all(gate_own, gate_chunks), 4)
+    down_new = updated(add_all(down_own, down_chunks), 6)
+    up_chunks, d_kv_arrived, query_arrived = after(
+        (up_chunks, d_kv_arrived, query_arrived), down_near
+    )
+    big = [gate_new, updated(add_all(up_own, up_chunks), 5), down_new]
+    slots = jnp.stack([new[2] for new in big] + [jnp.zeros_like(down_new[2])])
+    big_mine = to_planes(slots).reshape(-1, MODEL_WIDTH)
+    first_kept, first_passed, first_sent = halves_over_y(
+        [
+            add_all(output_own.astype(F32), output_arrived).astype(BF16),
+            add_all(query_own.astype(F32), query_arrived).astype(BF16),
+        ]
+    )
     d_kv_total = add_all(d_kv_half[:, 0], d_kv_arrived)
     kv_low_grad, d_gain_key = key_value_back(
         d_kv_total, kv_proj, gain_key[None], cosine_table[0], sine_table[0]
@@ -851,40 +845,22 @@
     key_value_blocks = jnp.moveaxis(
         key_value_grad.reshape(PLANES * CORES, ring, -1, MODEL_WIDTH), 1, 0
     )
-    key_value_half = scatter_blocks(key_value_blocks, "fsdp").astype(BF16)
-    from_kv = times_rows(after(both_kv_low, key_value_blocks), attention_rows, 0)
-    down_shard = add_all(down_own, down_chunks)
-    gate_shard = add_all(gate_own, gate_chunks)
-    up_shard = add_all(up_own, up_chunks)
-    masters = (w_query, key_weight_master, value_weight_master, w_output, w_gate, w_up, w_down)
-    moments = (
-        moment_query,
-        moment_key,
-        moment_value,
-        moment_output,
-        moment_gate,
-        moment_up,
-        moment_down,
-    )
-    full_sides = (MODEL_WIDTH,) * 4 + (FF,) * 3
-    sideways = (True, False, False, False, True, True, False)
-
-    def updated(shard, idx):
-        grad = shard.T if sideways[idx] else shard
-        moment = MOMENTUM * moments[idx] + grad
-        update = grad + MOMENTUM * moment
-        return grad, moment, (update.T if sideways[idx] else update).astype(BF16)
-
+    key_value_own, key_value_arrived = scatter_blocks(key_value_blocks, "fsdp")
     plane = lax.axis_index("z")
     in_plane = ("y", "core", "fsdp")
-    big = [updated(gate_shard, 4), updated(up_shard, 5), updated(down_shard, 6)]
-    slots = jnp.stack([form for _, _, form in big] + [jnp.zeros_like(big[0][2])])
-    big_mine = to_planes(slots).reshape(-1, MODEL_WIDTH)
-    big_mine, query_half, key_value_half = after(
-        (big_mine, query_half, key_value_half), from_kv
-    )
-    kept, arrived, attention_passed = halves_over_y([output_half, query_half, key_value_half])
-    big_gram = dot_tn(after(big_mine, attention_passed), big_mine)
+    big_mine, key_value_arrived, first_passed = lax.optimization_barrier(
+        (big_mine, key_value_arrived, first_passed)
+    )
+    first_own, first_chunks, first_chunks_sent = chunks_over_z(first_kept, first_passed)
+    kept, arrived, attention_passed = halves_over_y(
+        [add_all(key_value_own.astype(F32), key_value_arrived).astype(BF16)]
+    )
+    big_gram = dot_tn(after(big_mine, attention_passed, first_chunks_sent), big_mine).astype(BF16)
+    from_kv = times_rows(after(both_kv_low, big_gram), attention_rows, 0)
+    big_gram = lax.psum(big_gram, in_plane)
+    arrived, first_chunks = after((arrived, first_chunks), from_kv)
+    last_own, last_chunks, last_chunks_sent = chunks_over_z(kept, arrived)
+    from_kv = after(from_kv, last_chunks_sent)
 
     from_query = from_query[:rows].astype(F32) + swap(from_query[rows:]).astype(F32)
     kv_here = from_kv[:rows].reshape(rows, -1, HEAD_SIZE)
@@ -896,19 +872,17 @@
     first_back = jax.vjp(rms_scale, residual, gain_attn)[1]
     d_residual, d_gain_attn = first_back(d_normed)
     input_grad = (d_middle + d_residual).reshape(inputs.shape)
-    down_half = (down_near.astype(F32) + swap(after(down_far, big_gram)).astype(F32)).reshape(
+    down_half = (down_near.astype(F32) + swap(after(down_far, d_normed)).astype(F32)).reshape(
         ring, rows, MODEL_WIDTH
     )
     down_arrived = ring_send([down_half[step] for step in range(ring)], "fsdp", ring)
-    block_out = (middle + add_all(down_half[0], down_arrived)).astype(BF16).reshape(inputs.shape)
     gain_grad = jnp.concatenate([d_gain_attn, d_gain_mlp, d_gain_query, d_gain_key])
 
-    big_gram, gain_grad, arrived = sum_over_plane(big_gram, gain_grad, arrived)
-    attention_own, attention_chunks, _ = chunks_over_z(kept, arrived)
-    attention_total = add_all(attention_own, attention_chunks)
-    output_shard = attention_total[:, :MODEL_WIDTH]
-    query_shard = attention_total[:, MODEL_WIDTH : 2 * MODEL_WIDTH]
-    key_value_shard = attention_total[:, 2 * MODEL_WIDTH :]
+    last_chunks = after(last_chunks, input_grad)
+    first_total = add_all(first_own, first_chunks)
+    output_shard = first_total[:, :MODEL_WIDTH]
+    query_shard = first_total[:, MODEL_WIDTH:]
+    key_value_shard = add_all(last_own, last_chunks)
     small = [
         updated(query_shard, 0),
         updated(key_value_shard[:, :KV_WIDTH], 1),
@@ -925,12 +899,17 @@
     )
     small_mine = to_planes(small_slots).reshape(-1, MODEL_WIDTH)
     whole = gather_rows(small_mine, in_plane)
-    turned = orthogonal_rows(big_mine, big_gram, jnp.bool_(False), small_mine)
+    start, gram = normalized(big_mine, big_gram, jnp.bool_(False))
+    turned = chain(start, after(gram, small_mine), bend_of(gram))
     turned, whole = lax.optimization_barrier((turned, whole))
-    returned = from_planes(turned.reshape(slots.shape))
-    turned = orthogonal_rows(small_mine, dot_tn(whole, whole), plane == 1, small_mine)
-    turned, returned = lax.optimization_barrier((turned, returned))
+    returned = from_planes(turned.reshape(PLANES, -1, MODEL_WIDTH))
+    small_gram = dot_tn(whole, whole).astype(BF16)
+    start, gram = normalized(small_mine, small_gram, plane == 1)
+    turned, returned, down_arrived, gain_grad = lax.optimization_barrier(
+        (chain(start, gram, bend_of(gram)), returned, down_arrived, sum_everywhere(gain_grad))
+    )
     small_returned = from_planes(turned.reshape(small_slots.shape))
+    block_out = (middle + add_all(down_half[0], down_arrived)).astype(BF16).reshape(inputs.shape)
     ortho = (
         small_returned[0],
         small_returned[1][:, :KV_WIDTH],

time: 1640 us -> 1540 us (0.939)
  waiting for transfers between devices: 708 us -> 517 us
  blocking collectives: 0 us -> 105 us
  other arithmetic: 189 us -> 170 us
    all_gather x0 -> x1, blocking collectives: none -> 105 us  [sum_everywhere(): lax.all_gather(value, EVERYWHERE, axis=0, tiled=False)]
    ppermute x8 -> x3, waiting for transfers between devices: 94.5 us -> 0.01 us  [scatter_blocks(): lax.ppermute(pick(blocks, (here + step) % count), axis_name, shifted(step...]
    ppermute x8 -> x3, waiting for transfers between devices: 160 us -> 114 us  [ring_blocks(): lax.ppermute(value, axis_name, shifted(step, count))]
    ppermute x5 -> x0, waiting for transfers between devices: 39.8 us -> none  [butterfly(): lax.ppermute(value, axis_name, [(src, src ^ step) for src in range(count)])]
    psum x0 -> x1, waiting for transfers between devices: none -> 36.4 us  [per_device(): big_gram = lax.psum(big_gram, in_plane)]
    ppermute x3, waiting for transfers between devices: 44.2 us -> 12.1 us  [ring_send(): lax.ppermute(blocks[step].astype(BF16), axis_name, shifted(-step, count))]
    ppermute x12 -> x15, starting transfers between devices: 40.1 us -> 68.4 us  [chunks_over_z(): lax.ppermute(value, 'z', shifted(step + 1, PLANES))]
    convert_element_type x12 -> x7, other arithmetic: 43.1 us -> 28.9 us  [the longest x2 18.1 us: normalized(): return (start, jnp.where(kept, gram, 0.0).astype(BF16))]
  transfers between devices with their start and end apart: 71 -> 61, of which waited for: 37 -> 25; matrix products, arithmetic and copies ran while one was open for 16% -> 19% of each run, Pallas kernels for 21% -> 23%
where the time goes in v2:
time: 1540 us; the launch traced here: 1530 us
  waiting for transfers between devices  517 us (34%)
  Pallas kernels  417 us (27%)
  other arithmetic  170 us (11%)
  local copies, waits for them, and re-layouts  121 us (8%)
  starting transfers between devices  108 us (7%)
  blocking collectives  105 us (7%)
  matrix products  70.3 us (5%)
  between operations  20.1 us (1%)
    all_gather x5, waiting for transfers between devices, gather_rows(): return lax.all_gather(shard, axes, axis=0, tiled=True)  186 us
    ppermute x3, waiting for transfers between devices, ring_blocks(): lax.ppermute(value, axis_name, shifted(step, count))  114 us
    all_gather x1, blocking collectives, sum_everywhere(): lax.all_gather(value, EVERYWHERE, axis=0, tiled=False)  105 us
    pallas_call x2, Pallas kernels, chain(): pl.pallas_call(chain_kernel, grid=(), in_specs=[block, whole, whole], out...  88.3 us
    ppermute x6, waiting for transfers between devices, to_planes(): lax.ppermute(pick(chunks, (here + step) % PLANES), 'z', shifted(step, PLA...  70.2 us
    ppermute x15, starting transfers between devices, chunks_over_z(): lax.ppermute(value, 'z', shifted(step + 1, PLANES))  68.4 us
    pallas_call x8, Pallas kernels, weight_grad(): pl.pallas_call(weight_grad_kernel, grid_spec=pltpu.PrefetchScalarGridSpec...  68.4 us
    pallas_call x4, Pallas kernels, back_to_width(): pl.pallas_call(functools.partial(back_to_width_kernel, len(lefts)), grid=...  62.8 us
  transfers between devices with their start and end apart: 61, of which 25 were waited for; matrix products, arithmetic and copies ran while one was open for 19% of the time, Pallas kernels for 23%

profile of v2, /device:TPU:0, one launch (start us, length us, event | category | flops | bytes accessed | tf_op | source)
XLA Modules:
  0.0 1528.3 jit_solution(11529335332494359862)
XLA Ops:
  27.0 7.7 reshape.439
  34.7 8.5 constant_dynamic-slice_fusion.9
  43.2 9.1 copy.57
  53.7 113.7 %all-gather.11.cloned.1.call-done.right_ref = bf16[1024,6144]{1,0:T(8,128)(2,1)} async-done(((bf16[64,6144]{1,0:T(8,128)(2,1)}), bf16[1024,6144]{1,0:T(8,128)(2,1)}) %all-gather.11.cloned.1.call-update) | async-done | bytes 12582928 | tf_op jit(solution)/shard_map/all_gather | solution.py:543
  167.4 5.9 fusion.26
  191.1 9.4 fusion.13.q_ref
  200.5 37.0 %collective-permute-done.3 = bf16[512,2048]{1,0:T(8,128)(2,1)S(1)} collective-permute-done((bf16[512,2048]{1,0:T(8,128)(2,1)S(1)}, bf16[512,2048]{1,0:T(8,128)(2,1)S(1)}, u32[]{:S(2)}, u32[]{:S(2)}) %collective-permute-start.3) | collective-permute-done | bytes 2097184 | tf_op jit(solution)/shard_map/ppermute | solution.py:521
  245.4 8.7 pad_maximum_fusion
  256.3 19.0 %attention.1 = (bf16[1024,1024]{1,0:T(8,128)(2,1)S(1)}, bf16[1024,1024]{1,0:T(8,128)(2,1)S(1)}) custom-call(f32[1024,1024]{1,0:T(8,128)S(1)} %copy-done.2, bf16[2,1024,2048]{2,1,0:T(8,128)(2,1)} %bitcast.440, bf16[2,1024,2048]{2,1,0:T(8,128)(2,1)} %bitcast.441, bf16[2,1024,512]{2,1,0:T(8,128)(2,1)S(1)} %and_convert_fusion.mask_ref, ...), custom_call_target="tpu_custom_call" | custom-call | flops 1 | bytes 1 | tf_op jit(solution)/shard_map/attention/pallas_call | solution.py:302
  275.3 7.6 fusion.29
  287.4 6.0 multiply_reduce_fusion.2
  297.7 35.2 %collective-permute-done.8 = bf16[512,2048]{1,0:T(8,128)(2,1)S(1)} collective-permute-done((bf16[512,2048]{1,0:T(8,128)(2,1)}, bf16[512,2048]{1,0:T(8,128)(2,1)S(1)}, u32[]{:S(2)}, u32[]{:S(2)}) %collective-permute-start.8) | collective-permute-done | bytes 2097184 | tf_op jit(solution)/shard_map/ppermute | solution.py:521
  335.5 41.7 %collective-permute-done.6 = bf16[512,2048]{1,0:T(8,128)(2,1)S(1)} collective-permute-done((bf16[512,2048]{1,0:T(8,128)(2,1)S(1)}, bf16[512,2048]{1,0:T(8,128)(2,1)S(1)}, u32[]{:S(2)}, u32[]{:S(2)}) %collective-permute-start.6) | collective-permute-done | bytes 2097184 | tf_op jit(solution)/shard_map/ppermute | solution.py:521
  388.8 6.3 pad_maximum_fusion.1.two_ref.right_ref
  395.1 72.2 %all-gather.19.cloned.1.call-done = bf16[1536,2048]{1,0:T(8,128)(2,1)} async-done(((bf16[192,2048]{1,0:T(8,128)(2,1)}), bf16[1536,2048]{1,0:T(8,128)(2,1)}) %all-gather.19.cloned.1.call-update) | async-done | bytes 6291472 | tf_op jit(solution)/shard_map/all_gather | solution.py:543
  467.3 53.6 %swiglu_both_ways.1 = (bf16[2048,1536]{1,0:T(8,128)(2,1)}, bf16[2048,1536]{1,0:T(8,128)(2,1)}, bf16[2048,1536]{1,0:T(8,128)(2,1)}, bf16[1536,2048]{1,0:T(8,128)(...) custom-call(bf16[2048,2048]{1,0:T(8,128)(2,1)} %pad_maximum_fusion.1.two_ref.right_ref, ...), custom_call_target="tpu_custom_call" | custom-call | flops 1 | bytes 1 | tf_op jit(solution)/shard_map/swiglu_both_ways/pallas_call | solution.py:364
  523.6 9.8 weight_grad.8
  536.8 9.0 weight_grad.9
  547.5 19.9 %back_to_width.4 = bf16[1024,2048]{1,0:T(8,128)(2,1)} custom-call(bf16[2048,1536]{1,0:T(8,128)(2,1)} %get-tuple-element.114.refs_0_, bf16[2048,1536]{1,0:T(8,128)(2,1)} %get-tuple-element.115.refs_1_, bf16[4,2,192,2048]{3,2,1,0:T(8,128)(2,1)} %bitcast.447, bf16[4,2,192,2048]{3,2,1,0:T(8,128)(2,1)} %bitcast.450), custom_call_target="tpu_custom_call" | custom-call | flops 1 | bytes 1 | tf_op jit(solution)/shard_map/back_to_width/pallas_call | solution.py:383
  567.3 19.9 %back_to_width.5 = bf16[1024,2048]{1,0:T(8,128)(2,1)} custom-call(bf16[2048,1536]{1,0:T(8,128)(2,1)} %get-tuple-element.114.refs_0_, bf16[2048,1536]{1,0:T(8,128)(2,1)} %get-tuple-element.115.refs_1_, bf16[4,2,192,2048]{3,2,1,0:T(8,128)(2,1)} %bitcast.448, bf16[4,2,192,2048]{3,2,1,0:T(8,128)(2,1)} %bitcast.451), custom_call_target="tpu_custom_call" | custom-call | flops 1 | bytes 1 | tf_op jit(solution)/shard_map/back_to_width/pallas_call | solution.py:383
  587.3 9.6 weight_grad.10
  596.9 6.2 collective-permute-done.10
  607.3 6.9 collective-permute-done.11
  614.2 7.2 convert_add_fusion.3
  631.4 9.0 weight_grad.11
  640.4 10.9 weight_grad.12
  651.3 9.0 weight_grad.13
  663.0 14.4 collective-permute-done.16
  705.5 6.8 times_rows.2.grad_ref
  713.6 5.6 weight_grad.14
  723.3 16.4 %collective-permute-start.19 = (bf16[192,2048]{1,0:T(8,128)(2,1)}, bf16[192,2048]{1,0:T(8,128)(2,1)S(1)}, u32[]{:S(2)}, u32[]{:S(2)}) collective-permute-start(bf16[192,2048]{1,0:T(8,128)(2,1)} %get-tuple-element.220), channel_id=1, source_target_pairs={{0,8},{8,16},{16,24},{24,0},{1,9},{9,17},{17,25},{25,1},{2,10},{10... | collective-permute-start | bytes 2359304 | tf_op jit(solution)/shard_map/ppermute | solution.py:583
  742.1 22.0 %attention_back.2 = (bf16[1024,1024]{1,0:T(8,128)(2,1)S(1)}, bf16[1024,1024]{1,0:T(8,128)(2,1)S(1)}, bf16[2,1024,1024]{2,1,0:T(8,128)(2,1)}, f32[1,128]{1,0:T(1,128)S(1)}) custom-call(f32[1024,1024]{1,0:T(8,128)} %fusion.13.q_ref, bf16[2,1024,2048]{2,1,0:T(8,128)(2,1)} %bitcast.442, bf16[2,1024,2048]{2,1,0:T(8,128)(2,1)} %bitcast.443, ...), custom_call_target="tpu_custom_call" | custom-call | flops 1 | bytes 1 | tf_op jit(solution)/shard_map/attention_back/pallas_call | solution.py:326
  764.1 22.1 %attention_back.3 = (bf16[1024,1024]{1,0:T(8,128)(2,1)S(1)}, bf16[1024,1024]{1,0:T(8,128)(2,1)S(1)}, bf16[2,1024,1024]{2,1,0:T(8,128)(2,1)}, f32[1,128]{1,0:T(1,128)S(1)}) custom-call(f32[1024,1024]{1,0:T(8,128)} %fusion.13.q_ref, bf16[2,1024,2048]{2,1,0:T(8,128)(2,1)} %bitcast.444, ...), custom_call_target="tpu_custom_call", output_to_operand_aliasing={{0}: (8, {}), {1}: (9, {})} | custom-call | flops 1 | bytes 1 | tf_op jit(solution)/shard_map/attention_back/pallas_call | solution.py:326
  786.2 5.6 weight_grad.15
  791.8 7.4 times_columns.1
  799.3 5.8 fusion.60
  826.2 9.1 collective-permute-start.25
  840.1 11.7 back_to_width.6
  851.8 11.3 back_to_width.7
  863.2 24.7 %collective-permute-done.26 = bf16[192,2048]{1,0:T(8,128)(2,1)S(1)} collective-permute-done((bf16[192,2048]{1,0:T(8,128)(2,1)}, bf16[192,2048]{1,0:T(8,128)(2,1)S(1)}, u32[]{:S(2)}, u32[]{:S(2)}) %collective-permute-start.26) | collective-permute-done | bytes 786464 | tf_op jit(solution)/shard_map/ppermute | solution.py:583
  887.9 12.1 collective-permute-done.28
  933.7 9.1 collective-permute-start.31
  949.3 13.2 collective-permute-done.31
  962.5 33.7 %collective-permute-done.32 = bf16[192,2048]{1,0:T(8,128)(2,1)} collective-permute-done((bf16[192,2048]{1,0:T(8,128)(2,1)}, bf16[192,2048]{1,0:T(8,128)(2,1)}, u32[]{:S(2)}, u32[]{:S(2)}) %collective-permute-start.32) | collective-permute-done | bytes 786464 | tf_op jit(solution)/shard_map/ppermute | solution.py:596
  1005.0 17.4 %collective-permute-start.37 = (bf16[64,4096]{1,0:T(8,128)(2,1)}, bf16[64,4096]{1,0:T(8,128)(2,1)}, u32[]{:S(2)}, u32[]{:S(2)}) collective-permute-start(bf16[64,4096]{1,0:T(8,128)(2,1)} %get-tuple-element.250), channel_id=1, source_target_pairs={{0,8},{8,16},{16,24},{24,0},{1,9},{9,17},{17,25},{25,1},{2,10},{10... | collective-permute-start | bytes 1572872 | tf_op jit(solution)/shard_map/ppermute | solution.py:583
  1025.3 9.0 convolution_convert_fusion.1
  1036.6 6.7 times_rows.3
  1043.3 15.0 collective-permute-done.38
  1060.7 11.4 collective-permute-start.42
  1085.0 6.7 reshape.481
  1105.7 6.1 collective-permute-done.47
  1111.8 5.9 collective-permute-done.45
  1117.7 11.4 collective-permute-done.46
  1130.5 36.4 %all-reduce.3.cloned.1.call-done = bf16[2048,2048]{1,0:T(8,128)(2,1)} async-done(((bf16[2048,2048]{1,0:T(8,128)(2,1)}), bf16[2048,2048]{1,0:T(8,128)(2,1)}) %all-reduce.3.cloned.1.call-update) | async-done | bytes 8388624 | tf_op jit(solution)/shard_map/psum | solution.py:860
  1181.6 8.7 multiply_convert_fusion.gram_ref.tile_ref
  1190.3 25.0 %bend_of.2.bend_ref = bf16[2048,2048]{1,0:T(8,128)(2,1)} custom-call(bf16[2048,2048]{1,0:T(8,128)(2,1)} %multiply_convert_fusion.gram_ref.tile_ref, bf16[2048,2048]{1,0:T(8,128)(2,1)} %multiply_convert_fusion.gram_ref.tile_ref), custom_call_target="tpu_custom_call" | custom-call | flops 1 | bytes 1 | tf_op jit(solution)/shard_map/bend_of/pallas_call | solution.py:448
  1217.8 60.6 %chain.2 = bf16[768,2048]{1,0:T(8,128)(2,1)} custom-call(bf16[768,2048]{1,0:T(8,128)(2,1)} %multiply_convert_fusion.1.start_ref, bf16[2048,2048]{1,0:T(8,128)(2,1)} %multiply_convert_fusion.gram_ref.tile_ref, bf16[2048,2048]{1,0:T(8,128)(2,1)} %bend_of.2.bend_ref), custom_call_target="tpu_custom_call" | custom-call | flops 1 | bytes 1 | tf_op jit(solution)/shard_map/chain/pallas_call | solution.py:490
  1288.8 22.5 %convolution_convert_fusion = bf16[2048,2048]{1,0:T(8,128)(2,1)S(1)} fusion(bf16[2048,2048]{1,0:T(8,128)(2,1)} %all-gather.13.cloned.1.call-done), kind=kOutput, calls=%fused_computation.12 | convolution fusion | flops 17184063488 | bytes 16777216 | tf_op jit(solution)/shard_map/dot_general | solution.py:68
  1324.9 9.5 select_convert_fusion.gram_ref.tile_ref
  1334.3 105.1 %all-gather.4 = f32[32,1,4352]{2,1,0:T(1,128)S(1)} all-gather(f32[1,1,4352]{2,1,0:T(1,128)S(1)} %reshape.492), channel_id=5, replica_groups=mesh['z'=4,'y'=2,'core'=2,'fsdp'=2] {'z','y','core','fsdp'}, dimensions={0}, use_global_device_ids=true | all-gather | bytes 574464 | tf_op jit(solution)/shard_map/all_gather | solution.py:588
  1439.4 25.0 %bend_of.3.bend_ref = bf16[2048,2048]{1,0:T(8,128)(2,1)} custom-call(bf16[2048,2048]{1,0:T(8,128)(2,1)} %select_convert_fusion.gram_ref.tile_ref, bf16[2048,2048]{1,0:T(8,128)(2,1)} %select_convert_fusion.gram_ref.tile_ref), custom_call_target="tpu_custom_call" | custom-call | flops 1 | bytes 1 | tf_op jit(solution)/shard_map/bend_of/pallas_call | solution.py:448
  1466.0 27.8 %chain.3 = bf16[256,2048]{1,0:T(8,128)(2,1)} custom-call(bf16[256,2048]{1,0:T(8,128)(2,1)} %multiply_convert_fusion.3.start_ref, bf16[2048,2048]{1,0:T(8,128)(2,1)} %select_convert_fusion.gram_ref.tile_ref, bf16[2048,2048]{1,0:T(8,128)(2,1)} %bend_of.3.bend_ref), custom_call_target="tpu_custom_call" | custom-call | flops 1 | bytes 1 | tf_op jit(solution)/shard_map/chain/pallas_call | solution.py:490
  1498.4 5.4 fusion.34
  1509.2 9.2 collective-permute-done.53
  (501 shorter events, 294.0 us)
Async XLA Ops:
  7.2 160.2 %all-gather.11.cloned.1.call-start = ((), (), s32[]{:S(2)}) async-start(), calls=%async_computation | async-start | bytes 13369344 | tf_op jit(solution)/shard_map/all_gather | solution.py:543
  12.5 382.6 %all-gather.15.cloned.1.call-start = ((), (), s32[]{:S(2)}) async-start(), calls=%async_computation.3 | async-start | bytes 7077888 | tf_op jit(solution)/shard_map/all_gather | solution.py:543
  15.0 380.1 %all-gather.17.cloned.1.call-start = ((), (), s32[]{:S(2)}) async-start(), calls=%async_computation.4 | async-start | bytes 7077888 | tf_op jit(solution)/shard_map/all_gather | solution.py:543
  17.4 4.5 collective-permute-start
  17.9 155.4 %collective-permute-start.2 = (s32[1,1024]{1,0:T(1,128)S(1)}, s32[1,1024]{1,0:T(1,128)S(1)}, u32[]{:S(2)}, u32[]{:S(2)}) collective-permute-start(s32[1,1024]{1,0:T(1,128)S(1)} %copy-done.109), channel_id=1, source_target_pairs={{0,2},{2,0},{1,3},{3,1},{4,6},{6,4},{5,7},{7,5},{8,10},{10,8},{9,1... | collective-permute-start | bytes 12296 | tf_op jit(solution)/shard_map/ppermute | solution.py:512
  19.0 448.3 %all-gather.19.cloned.1.call-start = ((), (), s32[]{:S(2)}) async-start(), calls=%async_computation.5 | async-start | bytes 7077888 | tf_op jit(solution)/shard_map/all_gather | solution.py:543
  52.3 115.1 %copy-start.57 = (bf16[1024,8,1,128]{0,3,1,2:T(8,128)(2,1)}, bf16[1024,8,1,128]{0,3,1,2:T(8,128)(2,1)S(1)}, u32[]{:S(2)}) copy-start(bf16[1024,8,1,128]{0,3,1,2:T(8,128)(2,1)S(1)} %copy.57) | copy-start | bytes 6291460
  173.3 9.3 collective-permute-start.1
  189.5 48.0 %collective-permute-start.3 = (bf16[512,2048]{1,0:T(8,128)(2,1)S(1)}, bf16[512,2048]{1,0:T(8,128)(2,1)S(1)}, u32[]{:S(2)}, u32[]{:S(2)}) collective-permute-start(bf16[512,2048]{1,0:T(8,128)(2,1)S(1)} %get-tuple-element.103), channel_id=1, source_target_pairs={{0,1},{1,0},{2,3},{3,2},{4,5},{5,4},{6,7},{7,6},{8,9},{9,8},{10,11... | collective-permute-start | bytes 6291464 | tf_op jit(solution)/shard_map/ppermute | solution.py:521
  238.1 7.4 collective-permute-start.4
  282.9 4.5 collective-permute-start.5
  284.1 882.8 %all-reduce.3.cloned.1.call-start = ((), (), s32[]{:S(2)}) async-start(), calls=%async_computation.1 | async-start | bytes 16777216 | tf_op jit(solution)/shard_map/psum | solution.py:860
  284.2 48.7 %collective-permute-start.8 = (bf16[512,2048]{1,0:T(8,128)(2,1)}, bf16[512,2048]{1,0:T(8,128)(2,1)S(1)}, u32[]{:S(2)}, u32[]{:S(2)}) collective-permute-start(bf16[512,2048]{1,0:T(8,128)(2,1)} %bitcast.457), channel_id=1, source_target_pairs={{0,1},{1,0},{2,3},{3,2},{4,5},{5,4},{6,7},{7,6},{8,9},{9,8},{10,11... | collective-permute-start | bytes 6291464 | tf_op jit(solution)/shard_map/ppermute | solution.py:521
  295.9 81.3 %copy-start.42 = (bf16[512,2048]{1,0:T(8,128)(2,1)}, bf16[512,2048]{1,0:T(8,128)(2,1)S(1)}, u32[]{:S(2)}) copy-start(bf16[512,2048]{1,0:T(8,128)(2,1)S(1)} %multiply_convert_fusion.2) | copy-start | bytes 6291460
  296.0 81.3 %collective-permute-start.6 = (bf16[512,2048]{1,0:T(8,128)(2,1)S(1)}, bf16[512,2048]{1,0:T(8,128)(2,1)S(1)}, u32[]{:S(2)}, u32[]{:S(2)}) collective-permute-start(bf16[512,2048]{1,0:T(8,128)(2,1)S(1)} %multiply_convert_fusion.2), channel_id=1, source_target_pairs={{0,1},{1,0},{2,3},{3,2},{4,5},{5,4},{6,7},{7,6},{8,9},{9,8},{10,11... | collective-permute-start | bytes 6291464 | tf_op jit(solution)/shard_map/ppermute | solution.py:521
  335.5 48.3 %collective-permute-start.9 = (bf16[1024,2048]{1,0:T(8,128)(2,1)}, bf16[1024,2048]{1,0:T(8,128)(2,1)}, u32[]{:S(2)}, u32[]{:S(2)}) collective-permute-start(bf16[1024,2048]{1,0:T(8,128)(2,1)} %pad_maximum_fusion.5), channel_id=1, source_target_pairs={{0,2},{2,0},{1,3},{3,1},{4,6},{6,4},{5,7},{7,5},{8,10},{10,8},{9,1... | collective-permute-start | bytes 12582920 | tf_op jit(solution)/shard_map/ppermute | solution.py:512
  380.0 8.8 collective-permute-start.7
  533.4 69.7 %collective-permute-start.10 = (bf16[4,192,2048]{2,1,0:T(8,128)(2,1)}, bf16[4,192,2048]{2,1,0:T(8,128)(2,1)}, u32[]{:S(2)}, u32[]{:S(2)}) collective-permute-start(bf16[4,192,2048]{2,1,0:T(8,128)(2,1)} %bitcast.18), channel_id=1, source_target_pairs={{0,4},{4,0},{1,5},{5,1},{2,6},{6,2},{3,7},{7,3},{8,12},{12,8},{9,1... | collective-permute-start | bytes 9437192 | tf_op jit(solution)/shard_map/ppermute | solution.py:512
  606.7 7.5 collective-permute-start.11
  606.7 70.6 %collective-permute-start.16 = (bf16[4,192,2048]{2,1,0:T(8,128)(2,1)S(1)}, bf16[4,192,2048]{2,1,0:T(8,128)(2,1)}, u32[]{:S(2)}, u32[]{:S(2)}) collective-permute-start(bf16[4,192,2048]{2,1,0:T(8,128)(2,1)S(1)} %bitcast.438), channel_id=1, source_target_pairs={{0,4},{4,0},{1,5},{5,1},{2,6},{6,2},{3,7},{7,3},{8,12},{12,8},{9,1... | collective-permute-start | bytes 9437192 | tf_op jit(solution)/shard_map/ppermute | solution.py:512
  625.4 56.7 %collective-permute-start.12 = (bf16[512,2048]{1,0:T(8,128)(2,1)}, bf16[512,2048]{1,0:T(8,128)(2,1)}, u32[]{:S(2)}, u32[]{:S(2)}) collective-permute-start(bf16[512,2048]{1,0:T(8,128)(2,1)} %slice.572), channel_id=1, source_target_pairs={{0,1},{1,0},{2,3},{3,2},{4,5},{5,4},{6,7},{7,6},{8,9},{9,8},{10,11... | collective-permute-start | bytes 6291464 | tf_op jit(solution)/shard_map/ppermute | solution.py:527
  626.9 50.5 %collective-permute-start.13 = (bf16[192,2048]{1,0:T(8,128)(2,1)}, bf16[192,2048]{1,0:T(8,128)(2,1)}, u32[]{:S(2)}, u32[]{:S(2)}) collective-permute-start(bf16[192,2048]{1,0:T(8,128)(2,1)} %get-tuple-element.223), channel_id=1, source_target_pairs={{0,8},{8,16},{16,24},{24,0},{1,9},{9,17},{17,25},{25,1},{2,10},{10... | collective-permute-start | bytes 2359304 | tf_op jit(solution)/shard_map/ppermute | solution.py:583
  626.9 55.3 %collective-permute-start.14 = (bf16[192,2048]{1,0:T(8,128)(2,1)}, bf16[192,2048]{1,0:T(8,128)(2,1)}, u32[]{:S(2)}, u32[]{:S(2)}) collective-permute-start(bf16[192,2048]{1,0:T(8,128)(2,1)} %get-tuple-element.222), channel_id=1, source_target_pairs={{0,16},{8,24},{16,0},{24,8},{1,17},{9,25},{17,1},{25,9},{2,18},{10... | collective-permute-start | bytes 2359304 | tf_op jit(solution)/shard_map/ppermute | solution.py:583
  629.6 52.6 %collective-permute-start.15 = (bf16[192,2048]{1,0:T(8,128)(2,1)}, bf16[192,2048]{1,0:T(8,128)(2,1)}, u32[]{:S(2)}, u32[]{:S(2)}) collective-permute-start(bf16[192,2048]{1,0:T(8,128)(2,1)} %get-tuple-element.221), channel_id=1, source_target_pairs={{0,24},{8,0},{16,8},{24,16},{1,25},{9,1},{17,9},{25,17},{2,26},{10... | collective-permute-start | bytes 2359304 | tf_op jit(solution)/shard_map/ppermute | solution.py:583
  694.0 4.5 collective-permute-start.17
  694.0 105.2 %collective-permute-start.18 = (bf16[4,192,2048]{2,1,0:T(8,128)(2,1)}, bf16[4,192,2048]{2,1,0:T(8,128)(2,1)}, u32[]{:S(2)}, u32[]{:S(2)}) collective-permute-start(bf16[4,192,2048]{2,1,0:T(8,128)(2,1)} %bitcast.25), channel_id=1, source_target_pairs={{0,4},{4,0},{1,5},{5,1},{2,6},{6,2},{3,7},{7,3},{8,12},{12,8},{9,1... | collective-permute-start | bytes 9437192 | tf_op jit(solution)/shard_map/ppermute | solution.py:512
  722.8 76.5 %collective-permute-start.22 = (bf16[8,64,2048]{2,1,0:T(8,128)(2,1)}, bf16[8,64,2048]{2,1,0:T(8,128)(2,1)S(1)}, u32[]{:S(2)}, u32[]{:S(2)}) collective-permute-start(bf16[8,64,2048]{2,1,0:T(8,128)(2,1)} %dynamic-slice_bitcast_fusion.2), channel_id=1, source_target_pairs={{0,1},{1,0},{2,3},{3,2},{4,5},{5,4},{6,7},{7,6},{8,9},{9,8},{10,11... | collective-permute-start | bytes 6291464 | tf_op jit(solution)/shard_map/ppermute | solution.py:550
  723.3 75.9 %collective-permute-start.19 = (bf16[192,2048]{1,0:T(8,128)(2,1)}, bf16[192,2048]{1,0:T(8,128)(2,1)S(1)}, u32[]{:S(2)}, u32[]{:S(2)}) collective-permute-start(bf16[192,2048]{1,0:T(8,128)(2,1)} %get-tuple-element.220), channel_id=1, source_target_pairs={{0,8},{8,16},{16,24},{24,0},{1,9},{9,17},{17,25},{25,1},{2,10},{10... | collective-permute-start | bytes 2359304 | tf_op jit(solution)/shard_map/ppermute | solution.py:583
  739.7 59.5 %collective-permute-start.20 = (bf16[192,2048]{1,0:T(8,128)(2,1)}, bf16[192,2048]{1,0:T(8,128)(2,1)S(1)}, u32[]{:S(2)}, u32[]{:S(2)}) collective-permute-start(bf16[192,2048]{1,0:T(8,128)(2,1)} %get-tuple-element.219), channel_id=1, source_target_pairs={{0,16},{8,24},{16,0},{24,8},{1,17},{9,25},{17,1},{25,9},{2,18},{10... | collective-permute-start | bytes 2359304 | tf_op jit(solution)/shard_map/ppermute | solution.py:583
  741.3 57.9 %collective-permute-start.21 = (bf16[192,2048]{1,0:T(8,128)(2,1)}, bf16[192,2048]{1,0:T(8,128)(2,1)}, u32[]{:S(2)}, u32[]{:S(2)}) collective-permute-start(bf16[192,2048]{1,0:T(8,128)(2,1)} %get-tuple-element.218), channel_id=1, source_target_pairs={{0,24},{8,0},{16,8},{24,16},{1,25},{9,1},{17,9},{25,17},{2,26},{10... | collective-permute-start | bytes 2359304 | tf_op jit(solution)/shard_map/ppermute | solution.py:583
  805.1 7.4 collective-permute-start.23
  806.7 56.5 %collective-permute-start.29 = (bf16[8,64,2048]{2,1,0:T(8,128)(2,1)}, bf16[8,64,2048]{2,1,0:T(8,128)(2,1)}, u32[]{:S(2)}, u32[]{:S(2)}) collective-permute-start(bf16[8,64,2048]{2,1,0:T(8,128)(2,1)} %dynamic-slice_bitcast_fusion.1), channel_id=1, source_target_pairs={{0,1},{1,0},{2,3},{3,2},{4,5},{5,4},{6,7},{7,6},{8,9},{9,8},{10,11... | collective-permute-start | bytes 6291464 | tf_op jit(solution)/shard_map/ppermute | solution.py:550
  819.4 80.6 %collective-permute-start.28 = (bf16[2,512,1024]{2,1,0:T(8,128)(2,1)}, bf16[2,512,1024]{2,1,0:T(8,128)(2,1)}, u32[]{:S(2)}, u32[]{:S(2)}) collective-permute-start(bf16[2,512,1024]{2,1,0:T(8,128)(2,1)} %fusion.35), channel_id=1, source_target_pairs={{0,1},{1,0},{2,3},{3,2},{4,5},{5,4},{6,7},{7,6},{8,9},{9,8},{10,11... | collective-permute-start | bytes 6291464 | tf_op jit(solution)/shard_map/ppermute | solution.py:527
  826.2 36.9 %collective-permute-start.25 = (bf16[192,2048]{1,0:T(8,128)(2,1)}, bf16[192,2048]{1,0:T(8,128)(2,1)S(1)}, u32[]{:S(2)}, u32[]{:S(2)}) collective-permute-start(bf16[192,2048]{1,0:T(8,128)(2,1)} %get-tuple-element.217), channel_id=1, source_target_pairs={{0,8},{8,16},{16,24},{24,0},{1,9},{9,17},{17,25},{25,1},{2,10},{10... | collective-permute-start | bytes 2359304 | tf_op jit(solution)/shard_map/ppermute | solution.py:583
  835.3 52.5 %collective-permute-start.26 = (bf16[192,2048]{1,0:T(8,128)(2,1)}, bf16[192,2048]{1,0:T(8,128)(2,1)S(1)}, u32[]{:S(2)}, u32[]{:S(2)}) collective-permute-start(bf16[192,2048]{1,0:T(8,128)(2,1)} %get-tuple-element.216), channel_id=1, source_target_pairs={{0,16},{8,24},{16,0},{24,8},{1,17},{9,25},{17,1},{25,9},{2,18},{10... | collective-permute-start | bytes 2359304 | tf_op jit(solution)/shard_map/ppermute | solution.py:583
  836.8 51.1 %collective-permute-start.27 = (bf16[192,2048]{1,0:T(8,128)(2,1)}, bf16[192,2048]{1,0:T(8,128)(2,1)S(1)}, u32[]{:S(2)}, u32[]{:S(2)}) collective-permute-start(bf16[192,2048]{1,0:T(8,128)(2,1)} %get-tuple-element.215), channel_id=1, source_target_pairs={{0,24},{8,0},{16,8},{24,16},{1,25},{9,1},{17,9},{25,17},{2,26},{10... | collective-permute-start | bytes 2359304 | tf_op jit(solution)/shard_map/ppermute | solution.py:583
  908.6 9.6 collective-permute-start.30
  917.5 80.5 %collective-permute-start.35 = (bf16[4,64,4096]{2,1,0:T(8,128)(2,1)}, bf16[4,64,4096]{2,1,0:T(8,128)(2,1)}, u32[]{:S(2)}, u32[]{:S(2)}) collective-permute-start(bf16[4,64,4096]{2,1,0:T(8,128)(2,1)} %pad_maximum_fusion.9), channel_id=1, source_target_pairs={{0,4},{4,0},{1,5},{5,1},{2,6},{6,2},{3,7},{7,3},{8,12},{12,8},{9,1... | collective-permute-start | bytes 6291464 | tf_op jit(solution)/shard_map/ppermute | solution.py:512
  925.5 72.5 %collective-permute-start.34 = (bf16[8,64,2048]{2,1,0:T(8,128)(2,1)}, bf16[8,64,2048]{2,1,0:T(8,128)(2,1)}, u32[]{:S(2)}, u32[]{:S(2)}) collective-permute-start(bf16[8,64,2048]{2,1,0:T(8,128)(2,1)} %dynamic-slice_bitcast_fusion), channel_id=1, source_target_pairs={{0,1},{1,0},{2,3},{3,2},{4,5},{5,4},{6,7},{7,6},{8,9},{9,8},{10,11... | collective-permute-start | bytes 6291464 | tf_op jit(solution)/shard_map/ppermute | solution.py:550
  933.7 28.8 %collective-permute-start.31 = (bf16[192,2048]{1,0:T(8,128)(2,1)}, bf16[192,2048]{1,0:T(8,128)(2,1)}, u32[]{:S(2)}, u32[]{:S(2)}) collective-permute-start(bf16[192,2048]{1,0:T(8,128)(2,1)} %get-tuple-element.239), channel_id=1, source_target_pairs={{0,8},{8,16},{16,24},{24,0},{1,9},{9,17},{17,25},{25,1},{2,10},{10... | collective-permute-start | bytes 2359304 | tf_op jit(solution)/shard_map/ppermute | solution.py:596
  942.8 53.4 %collective-permute-start.32 = (bf16[192,2048]{1,0:T(8,128)(2,1)}, bf16[192,2048]{1,0:T(8,128)(2,1)}, u32[]{:S(2)}, u32[]{:S(2)}) collective-permute-start(bf16[192,2048]{1,0:T(8,128)(2,1)} %get-tuple-element.238), channel_id=1, source_target_pairs={{0,16},{8,24},{16,0},{24,8},{1,17},{9,25},{17,1},{25,9},{2,18},{10... | collective-permute-start | bytes 2359304 | tf_op jit(solution)/shard_map/ppermute | solution.py:596
  944.3 51.9 %collective-permute-start.33 = (bf16[192,2048]{1,0:T(8,128)(2,1)}, bf16[192,2048]{1,0:T(8,128)(2,1)}, u32[]{:S(2)}, u32[]{:S(2)}) collective-permute-start(bf16[192,2048]{1,0:T(8,128)(2,1)} %get-tuple-element.237), channel_id=1, source_target_pairs={{0,24},{8,0},{16,8},{24,16},{1,25},{9,1},{17,9},{25,17},{2,26},{10... | collective-permute-start | bytes 2359304 | tf_op jit(solution)/shard_map/ppermute | solution.py:596
  962.5 129.2 %collective-permute-start.24 = (bf16[512,2048]{1,0:T(8,128)(2,1)}, bf16[512,2048]{1,0:T(8,128)(2,1)}, u32[]{:S(2)}, u32[]{:S(2)}) collective-permute-start(bf16[512,2048]{1,0:T(8,128)(2,1)} %slice.356), channel_id=1, source_target_pairs={{0,2},{2,0},{1,3},{3,1},{4,6},{6,4},{5,7},{7,5},{8,10},{10,8},{9,1... | collective-permute-start | bytes 6291464 | tf_op jit(solution)/shard_map/ppermute | solution.py:512
  1005.0 38.3 %collective-permute-start.37 = (bf16[64,4096]{1,0:T(8,128)(2,1)}, bf16[64,4096]{1,0:T(8,128)(2,1)}, u32[]{:S(2)}, u32[]{:S(2)}) collective-permute-start(bf16[64,4096]{1,0:T(8,128)(2,1)} %get-tuple-element.250), channel_id=1, source_target_pairs={{0,8},{8,16},{16,24},{24,0},{1,9},{9,17},{17,25},{25,1},{2,10},{10... | collective-permute-start | bytes 1572872 | tf_op jit(solution)/shard_map/ppermute | solution.py:583
  1022.4 35.9 %collective-permute-start.38 = (bf16[64,4096]{1,0:T(8,128)(2,1)}, bf16[64,4096]{1,0:T(8,128)(2,1)}, u32[]{:S(2)}, u32[]{:S(2)}) collective-permute-start(bf16[64,4096]{1,0:T(8,128)(2,1)} %get-tuple-element.249), channel_id=1, source_target_pairs={{0,16},{8,24},{16,0},{24,8},{1,17},{9,25},{17,1},{25,9},{2,18},{10... | collective-permute-start | bytes 1572872 | tf_op jit(solution)/shard_map/ppermute | solution.py:583
  1023.7 34.6 %collective-permute-start.39 = (bf16[64,4096]{1,0:T(8,128)(2,1)}, bf16[64,4096]{1,0:T(8,128)(2,1)}, u32[]{:S(2)}, u32[]{:S(2)}) collective-permute-start(bf16[64,4096]{1,0:T(8,128)(2,1)} %get-tuple-element.248), channel_id=1, source_target_pairs={{0,24},{8,0},{16,8},{24,16},{1,25},{9,1},{17,9},{25,17},{2,26},{10... | collective-permute-start | bytes 1572872 | tf_op jit(solution)/shard_map/ppermute | solution.py:583
  1024.7 33.8 %collective-permute-start.36 = (bf16[4,64,2048]{2,1,0:T(8,128)(2,1)S(1)}, bf16[4,64,2048]{2,1,0:T(8,128)(2,1)}, u32[]{:S(2)}, u32[]{:S(2)}) collective-permute-start(bf16[4,64,2048]{2,1,0:T(8,128)(2,1)S(1)} %dynamic-slice_bitcast_fusion.3), channel_id=1, source_target_pairs={{0,4},{4,0},{1,5},{5,1},{2,6},{6,2},{3,7},{7,3},{8,12},{12,8},{9,1... | collective-permute-start | bytes 3145736 | tf_op jit(solution)/shard_map/ppermute | solution.py:512
  1034.4 254.4 %all-gather.13.cloned.1.call-start = ((), (), s32[]{:S(2)}) async-start(), calls=%async_computation.2 | async-start | bytes 9437184 | tf_op jit(solution)/shard_map/all_gather | solution.py:543
  1060.7 39.4 %collective-permute-start.42 = (bf16[64,2048]{1,0:T(8,128)(2,1)}, bf16[64,2048]{1,0:T(8,128)(2,1)}, u32[]{:S(2)}, u32[]{:S(2)}) collective-permute-start(bf16[64,2048]{1,0:T(8,128)(2,1)} %get-tuple-element.235), channel_id=1, source_target_pairs={{0,8},{8,16},{16,24},{24,0},{1,9},{9,17},{17,25},{25,1},{2,10},{10... | collective-permute-start | bytes 786440 | tf_op jit(solution)/shard_map/ppermute | solution.py:583
  1072.1 28.1 %collective-permute-start.43 = (bf16[64,2048]{1,0:T(8,128)(2,1)}, bf16[64,2048]{1,0:T(8,128)(2,1)}, u32[]{:S(2)}, u32[]{:S(2)}) collective-permute-start(bf16[64,2048]{1,0:T(8,128)(2,1)} %get-tuple-element.234), channel_id=1, source_target_pairs={{0,16},{8,24},{16,0},{24,8},{1,17},{9,25},{17,1},{25,9},{2,18},{10... | collective-permute-start | bytes 786440 | tf_op jit(solution)/shard_map/ppermute | solution.py:583
  1073.6 26.5 %collective-permute-start.44 = (bf16[64,2048]{1,0:T(8,128)(2,1)}, bf16[64,2048]{1,0:T(8,128)(2,1)}, u32[]{:S(2)}, u32[]{:S(2)}) collective-permute-start(bf16[64,2048]{1,0:T(8,128)(2,1)} %get-tuple-element.233), channel_id=1, source_target_pairs={{0,24},{8,0},{16,8},{24,16},{1,25},{9,1},{17,9},{25,17},{2,26},{10... | collective-permute-start | bytes 786440 | tf_op jit(solution)/shard_map/ppermute | solution.py:583
  1074.7 4.1 collective-permute-start.40
  1102.9 8.9 collective-permute-start.47
  1104.8 12.9 collective-permute-start.45
  1105.0 24.2 %collective-permute-start.46 = (bf16[64,2048]{1,0:T(8,128)(2,1)S(1)}, bf16[64,2048]{1,0:T(8,128)(2,1)S(1)}, u32[]{:S(2)}, u32[]{:S(2)}) collective-permute-start(bf16[64,2048]{1,0:T(8,128)(2,1)S(1)} %get-tuple-element.259), channel_id=1, source_target_pairs={{0,16},{8,24},{16,0},{24,8},{1,17},{9,25},{17,1},{25,9},{2,18},{10... | collective-permute-start | bytes 786440 | tf_op jit(solution)/shard_map/ppermute | solution.py:596
  1130.4 148.0 %collective-permute-start.41 = (bf16[1024,2048]{1,0:T(8,128)(2,1)}, bf16[1024,2048]{1,0:T(8,128)(2,1)}, u32[]{:S(2)}, u32[]{:S(2)}) collective-permute-start(bf16[1024,2048]{1,0:T(8,128)(2,1)} %back_to_width.6), channel_id=1, source_target_pairs={{0,2},{2,0},{1,3},{3,1},{4,6},{6,4},{5,7},{7,5},{8,10},{10,8},{9,1... | collective-permute-start | bytes 12582920 | tf_op jit(solution)/shard_map/ppermute | solution.py:512
  1217.8 60.6 %copy-start.47 = (bf16[1024,2048]{1,0:T(8,128)(2,1)S(1)}, bf16[1024,2048]{1,0:T(8,128)(2,1)}, u32[]{:S(2)}) copy-start(bf16[1024,2048]{1,0:T(8,128)(2,1)} %back_to_width.7) | copy-start | bytes 12582916
  1287.5 207.0 %collective-permute-start.51 = (bf16[512,2048]{1,0:T(8,128)(2,1)}, bf16[512,2048]{1,0:T(8,128)(2,1)}, u32[]{:S(2)}, u32[]{:S(2)}) collective-permute-start(bf16[512,2048]{1,0:T(8,128)(2,1)} %slice.571), channel_id=1, source_target_pairs={{0,1},{1,0},{2,3},{3,2},{4,5},{5,4},{6,7},{7,6},{8,9},{9,8},{10,11... | collective-permute-start | bytes 6291464 | tf_op jit(solution)/shard_map/ppermute | solution.py:527
  1319.9 173.9 %collective-permute-start.48 = (bf16[192,2048]{1,0:T(8,128)(2,1)}, bf16[192,2048]{1,0:T(8,128)(2,1)S(1)}, u32[]{:S(2)}, u32[]{:S(2)}) collective-permute-start(bf16[192,2048]{1,0:T(8,128)(2,1)} %get-tuple-element.230), channel_id=1, source_target_pairs={{0,24},{8,0},{16,8},{24,16},{1,25},{9,1},{17,9},{25,17},{2,26},{10... | collective-permute-start | bytes 2359304 | tf_op jit(solution)/shard_map/ppermute | solution.py:605
  1324.1 169.7 %collective-permute-start.49 = (bf16[192,2048]{1,0:T(8,128)(2,1)}, bf16[192,2048]{1,0:T(8,128)(2,1)S(1)}, u32[]{:S(2)}, u32[]{:S(2)}) collective-permute-start(bf16[192,2048]{1,0:T(8,128)(2,1)} %get-tuple-element.229), channel_id=1, source_target_pairs={{0,16},{8,24},{16,0},{24,8},{1,17},{9,25},{17,1},{25,9},{2,18},{10... | collective-permute-start | bytes 2359304 | tf_op jit(solution)/shard_map/ppermute | solution.py:605
  1324.1 169.7 %collective-permute-start.50 = (bf16[192,2048]{1,0:T(8,128)(2,1)}, bf16[192,2048]{1,0:T(8,128)(2,1)S(1)}, u32[]{:S(2)}, u32[]{:S(2)}) collective-permute-start(bf16[192,2048]{1,0:T(8,128)(2,1)} %get-tuple-element.228), channel_id=1, source_target_pairs={{0,8},{8,16},{16,24},{24,0},{1,9},{9,17},{17,25},{25,1},{2,10},{10... | collective-permute-start | bytes 2359304 | tf_op jit(solution)/shard_map/ppermute | solution.py:605
  1495.1 14.1 collective-permute-start.52
  1495.2 23.2 %collective-permute-start.53 = (bf16[64,2048]{1,0:T(8,128)(2,1)S(1)}, bf16[64,2048]{1,0:T(8,128)(2,1)S(1)}, u32[]{:S(2)}, u32[]{:S(2)}) collective-permute-start(bf16[64,2048]{1,0:T(8,128)(2,1)S(1)} %get-tuple-element.255), channel_id=1, source_target_pairs={{0,16},{8,24},{16,0},{24,8},{1,17},{9,25},{17,1},{25,9},{2,18},{10... | collective-permute-start | bytes 786440 | tf_op jit(solution)/shard_map/ppermute | solution.py:605
  1496.4 21.9 %collective-permute-start.54 = (bf16[64,2048]{1,0:T(8,128)(2,1)S(1)}, bf16[64,2048]{1,0:T(8,128)(2,1)S(1)}, u32[]{:S(2)}, u32[]{:S(2)}) collective-permute-start(bf16[64,2048]{1,0:T(8,128)(2,1)S(1)} %get-tuple-element.254), channel_id=1, source_target_pairs={{0,8},{8,16},{16,24},{24,0},{1,9},{9,17},{17,25},{25,1},{2,10},{10... | collective-permute-start | bytes 786440 | tf_op jit(solution)/shard_map/ppermute | solution.py:605
  (111 other events, 1362.4 us)
Sparse Core Ops, SparseCore 0:
  12.6 154.7 all-gather.10
  170.1 97.2 all-gather.14
  270.1 97.2 all-gather.16
  370.0 97.1 all-gather.18
  1034.5 132.3 all-reduce.2
  1169.4 55.3 all-gather.12

commit v3 on v2

--- a/solution.py
+++ b/solution.py
@@ -33,11 +33,11 @@
 
 CORES = 2
 PLANES = 4
+GRAM_TILE = 512
 KV_WIDTH = KEY_VALUE_HEADS * HEAD_SIZE
 BF16 = jnp.bfloat16
 F32 = jnp.float32
 SHARDS = ("z", "y", "fsdp")
-PLANE_ROWS = ("z", "y")
 EVERYWHERE = ("z", "y", "core", "fsdp")
 
 
@@ -66,6 +66,11 @@
 
 def dot_tn(left, right):
     return lax.dot_general(left, right, (((0,), (0,)), ((), ())), preferred_element_type=F32)
+
+
+def gram_pairs(width):
+    count = width // GRAM_TILE
+    return [(i, j) for i in range(count) for j in range(i, count)]
 
 
 def head_chain(head, gain, cosine, sine):
@@ -164,11 +169,10 @@
 
 
 def swiglu_kernel(two_ref, cot_ref, gate_ref, up_ref, down_ref, *out_refs):
-    width = two_ref.shape[1]
     two = two_ref[...]
-    gate = dot_nt(two, gate_ref[...].reshape(-1, width))
-    up = dot_nt(two, up_ref[...].reshape(-1, width))
-    d_hidden = dot_nt(cot_ref[...], down_ref[...].reshape(-1, width))
+    gate = dot_nt(two, gate_ref[...])
+    up = dot_nt(two, up_ref[...])
+    d_hidden = dot_nt(cot_ref[...], down_ref[...])
     sig = 1.0 / (1.0 + jnp.exp(-gate))
     silu = gate * sig
     results = (silu * up, d_hidden * up * sig * (1.0 + gate * (1.0 - sig)), d_hidden * silu)
@@ -180,29 +184,48 @@
 
 def back_to_width_kernel(count, *refs):
     lefts, rights, out_ref = refs[:count], refs[count : 2 * count], refs[-1]
-    width = out_ref.shape[1]
     total = 0.0
     for left, right in zip(lefts, rights):
-        if split_by_y(right.shape[2]):
-            half = left.shape[1] // CORES
-            for y in range(CORES):
-                rows = right[:, y].reshape(-1, width)
-                total = total + dot_nn(left[:, y * half : (y + 1) * half], rows)
-        else:
-            total = total + dot_nn(left[...], right[...].reshape(-1, width))
+        total = total + dot_nn(left[...], right[...])
     out_ref[...] = total.astype(BF16)
 
 
-def weight_grad_kernel(place_ref, left_ref, right_ref, out_ref):
+def weight_grad_kernel(left_ref, right_ref, out_ref):
     out_ref[...] = dot_nn(left_ref[...], right_ref[...]).astype(BF16)
 
 
-def chain_kernel(start_ref, gram_ref, bend_ref, out_ref, first_ref, product_ref, one_ref, two_ref):
-    width = start_ref.shape[1]
-    tile = 512
+def gram_kernel(first_ref, second_ref, left_ref, right_ref, out_ref):
+    out_ref[0] = dot_tn(left_ref[...], right_ref[...]).astype(BF16)
+
+
+def muon_kernel(
+    halves_ref, update_ref, packed_ref, row_ref, col_ref, out_ref,
+    start_ref, gram_ref, bend_ref, first_ref, product_ref, one_ref, two_ref,
+):
+    width = update_ref.shape[1]
+    tile = GRAM_TILE
+    count = width // tile
+    start_ref[...] = (update_ref[...].astype(F32) * row_ref[...]).astype(BF16)
+    one_matrix = (1 - halves_ref[0]).astype(F32)
+
+    def put(ref, i, j, value):
+        ref[i * tile : (i + 1) * tile, j * tile : (j + 1) * tile] = value
+        if i != j:
+            ref[j * tile : (j + 1) * tile, i * tile : (i + 1) * tile] = value.T
+
+    for place, (i, j) in enumerate(gram_pairs(width)):
+        block = packed_ref[place].astype(F32) * col_ref[i * tile : (i + 1) * tile, :]
+        block = block * row_ref[:, j * tile : (j + 1) * tile]
+        if 2 * i < count <= 2 * j:
+            block = block * one_matrix
+        put(gram_ref, i, j, block.astype(BF16))
+    for i, j in gram_pairs(width):
+        rows, cols = slice(i * tile, (i + 1) * tile), slice(j * tile, (j + 1) * tile)
+        square = dot_nn(gram_ref[rows, :], gram_ref[:, cols])
+        put(bend_ref, i, j, (NS_B * gram_ref[rows, cols].astype(F32) + NS_C * square).astype(BF16))
 
     def columns(body):
-        @pl.loop(0, width // tile)
+        @pl.loop(0, count)
         def _(step):
             body(pl.ds(pl.multiple_of(step * tile, tile), tile))
 
@@ -346,72 +369,61 @@
     )(q_proj, kv, kv, mask, gain, cosine, sine, grad, *others)
 
 
-def split_by_y(block_rows):
-    return (PLANES * block_rows) % 128 == 0
-
-
-def swiglu_both_ways(two, cot, ff):
+def swiglu_both_ways(two, cot, gate, up, down):
     tokens, width = two.shape
-    _, _, block_rows, _ = ff[0].shape
-    ys = 1 if split_by_y(block_rows) else CORES
+    columns = gate.shape[0]
     tile = min(512, tokens)
-    ff_tile = PLANES * ys * block_rows
-    row_block = pl.BlockSpec((tile, width), lambda col, row: (row, 0))
-    out_block = pl.BlockSpec((tile, ff_tile), lambda col, row: (row, col))
-    turned_block = pl.BlockSpec((ff_tile, tile), lambda col, row: (col, row))
-    weights = pl.BlockSpec((PLANES, ys, block_rows, width), lambda col, row: (0, col, 0, 0))
-    columns = PLANES * CORES * block_rows
+    row_block = pl.BlockSpec((tile, width), lambda row: (row, 0))
+    weights = pl.BlockSpec((columns, width), lambda row: (0, 0))
     return pl.pallas_call(
         swiglu_kernel,
-        grid=(CORES // ys, tokens // tile),
+        grid=(tokens // tile,),
         in_specs=[row_block, row_block] + [weights] * 3,
-        out_specs=[out_block] * 3 + [turned_block] * 3,
+        out_specs=[pl.BlockSpec((tile, columns), lambda row: (row, 0))] * 3
+        + [pl.BlockSpec((columns, tile), lambda row: (0, row))] * 3,
         out_shape=[shaped((tokens, columns), BF16)] * 3 + [shaped((columns, tokens), BF16)] * 3,
         compiler_params=limits(60),
         cost_estimate=SMALL,
         name="swiglu_both_ways",
-    )(two, cot, *ff)
-
-
-def back_to_width(lefts, ff, first_row, rows):
-    _, _, block_rows, width = ff[0].shape
-    columns = PLANES * CORES * block_rows
+    )(two, cot, gate, up, down)
+
+
+def back_to_width(lefts, rights, first_row, rows):
+    width = rights[0].shape[1]
     tile = min(256, rows)
     first = first_row // tile
-    left_block = pl.BlockSpec((tile, columns), lambda row: (first + row, 0))
-    weights = pl.BlockSpec(ff[0].shape, lambda row: (0, 0, 0, 0))
     return pl.pallas_call(
         functools.partial(back_to_width_kernel, len(lefts)),
         grid=(rows // tile,),
-        in_specs=[left_block] * len(lefts) + [weights] * len(lefts),
+        in_specs=[
+            pl.BlockSpec((tile, left.shape[1]), lambda row: (first + row, 0)) for left in lefts
+        ]
+        + [pl.BlockSpec(right.shape, lambda row: (0, 0)) for right in rights],
         out_specs=pl.BlockSpec((tile, width), lambda row: (row, 0)),
         out_shape=shaped((rows, width), BF16),
         compiler_params=limits(56),
         cost_estimate=SMALL,
         name="back_to_width",
-    )(*lefts, *ff)
-
-
-def weight_grad(left_turned, right, place, parts):
-    rows = left_turned.shape[0] // parts
-    tokens, width = right.shape
+    )(*lefts, *rights)
+
+
+def weight_grad(left_turned, right):
+    rows, tokens = left_turned.shape
+    width = right.shape[1]
     tile = min(512, width)
     return pl.pallas_call(
         weight_grad_kernel,
-        grid_spec=pltpu.PrefetchScalarGridSpec(
-            num_scalar_prefetch=1,
-            grid=(width // tile,),
-            in_specs=[
-                pl.BlockSpec((rows, tokens), lambda col, place_ref: (place_ref[0], 0)),
-                pl.BlockSpec((tokens, tile), lambda col, place_ref: (0, col)),
-            ],
-            out_specs=pl.BlockSpec((rows, tile), lambda col, place_ref: (0, col)),
-        ),
+        grid=(width // tile,),
+        in_specs=[
+            pl.BlockSpec((rows, tokens), lambda col: (0, 0)),
+            pl.BlockSpec((tokens, tile), lambda col: (0, col)),
+        ],
+        out_specs=pl.BlockSpec((rows, tile), lambda col: (0, col)),
         out_shape=shaped((rows, width), BF16),
         compiler_params=limits(40),
         cost_estimate=SMALL,
         name="weight_grad",
-    )(jnp.asarray(place, jnp.int32).reshape(1), left_turned, right)
+    )(left_turned, right)
 
 
 def times_columns_kernel(left_ref, right_ref, out_ref):
@@ -437,29 +449,6 @@
     )(left, right)
 
 
-def bend_kernel(gram_ref, tile_ref, out_ref):
-    square = dot_nn(gram_ref[...], tile_ref[...])
-    out_ref[...] = (NS_B * tile_ref[...].astype(F32) + NS_C * square).astype(BF16)
-
-
-def bend_of(gram):
-    width = gram.shape[0]
-    tile = 512
-    return pl.pallas_call(
-        bend_kernel,
-        grid=(width // tile,),
-        in_specs=[
-            pl.BlockSpec((width, width), lambda col: (0, 0)),
-            pl.BlockSpec((width, tile), lambda col: (0, col)),
-        ],
-        out_specs=pl.BlockSpec((width, tile), lambda col: (0, col)),
-        out_shape=shaped(gram.shape, BF16),
-        compiler_params=limits(48),
-        cost_estimate=SMALL,
-        name="bend_of",
-    )(gram, gram)
-
-
 def times_rows_kernel(left_ref, right_ref, out_ref):
     out_ref[...] = dot_nt(left_ref[...], right_ref[...]).astype(BF16)
 
@@ -483,21 +472,72 @@
     )(left, right)
 
 
-def chain(start, gram, bend):
-    rows, width = start.shape
-    whole = pl.BlockSpec((width, width), lambda: (0, 0), pipeline_mode=pl.Buffered(1))
-    block = pl.BlockSpec((rows, width), lambda: (0, 0), pipeline_mode=pl.Buffered(1))
+def gram_blocks(rows):
+    depth, width = rows.shape
+    pairs = gram_pairs(width)
+    first = jnp.asarray([i for i, _ in pairs], jnp.int32)
+    second = jnp.asarray([j for _, j in pairs], jnp.int32)
+    shape = (len(pairs), GRAM_TILE, GRAM_TILE)
     return pl.pallas_call(
-        chain_kernel,
+        gram_kernel,
+        grid_spec=pltpu.PrefetchScalarGridSpec(
+            num_scalar_prefetch=2,
+            grid=(len(pairs),),
+            in_specs=[
+                pl.BlockSpec((depth, GRAM_TILE), lambda step, one, two: (0, one[step])),
+                pl.BlockSpec((depth, GRAM_TILE), lambda step, one, two: (0, two[step])),
+            ],
+            out_specs=pl.BlockSpec((1, *shape[1:]), lambda step, one, two: (step, 0, 0)),
+        ),
+        out_shape=shaped(shape, BF16),
+        compiler_params=limits(40),
+        cost_estimate=SMALL,
+        name="gram_blocks",
+    )(first, second, rows, rows)
+
+
+def muon(update, packed, halves):
+    rows, width = update.shape
+    index = jnp.arange(GRAM_TILE)
+    pairs = gram_pairs(width)
+    squares = jnp.stack(
+        [
+            jnp.sum(jnp.where(index[:, None] == index[None, :], packed[at].astype(F32), 0.0))
+            for at, (i, j) in enumerate(pairs)
+            if i == j
+        ]
+    )
+    count = squares.shape[0]
+    low_half, high_half = jnp.sum(squares[: count // 2]), jnp.sum(squares[count // 2 :])
+    both = low_half + high_half
+    squares = jnp.stack([jnp.where(halves, low_half, both), jnp.where(halves, high_half, both)])
+    inverse = jnp.repeat(1.0 / (jnp.sqrt(squares) + NS_EPS), width // 2)
+    once = dict(pipeline_mode=pl.Buffered(1))
+    return pl.pallas_call(
+        muon_kernel,
         grid=(),
-        in_specs=[block, whole, whole],
-        out_specs=pl.BlockSpec((rows, width), lambda: (0, 0)),
-        out_shape=shaped(start.shape, BF16),
-        scratch_shapes=[pltpu.VMEM(start.shape, BF16)] * 4,
-        compiler_params=limits(56),
+        in_specs=[
+            pl.BlockSpec(memory_space=pltpu.SMEM),
+            pl.BlockSpec(update.shape, lambda: (0, 0), **once),
+            pl.BlockSpec(packed.shape, lambda: (0, 0, 0), **once),
+            pl.BlockSpec((1, width), lambda: (0, 0)),
+            pl.BlockSpec((width, 1), lambda: (0, 0)),
+        ],
+        out_specs=pl.BlockSpec(update.shape, lambda: (0, 0)),
+        out_shape=shaped(update.shape, BF16),
+        scratch_shapes=[pltpu.VMEM(update.shape, BF16)]
+        + [pltpu.VMEM((width, width), BF16)] * 2
+        + [pltpu.VMEM(update.shape, BF16)] * 4,
+        compiler_params=limits(58),
         cost_estimate=SMALL,
-        name="chain",
-    )(start, gram, bend)
+        name="muon",
+    )(
+        jnp.asarray(halves, jnp.int32).reshape(1),
+        update,
+        packed,
+        inverse[None],
+        inverse[:, None],
+    )
 
 
 def after(value, *earlier):
@@ -553,12 +593,8 @@
     return pick(blocks, here), arrived
 
 
-def ff_grad_half(left_turned, right, block_rows, y):
-    shape = (PLANES, block_rows, right.shape[1])
-    if split_by_y(block_rows):
-        return weight_grad(left_turned, right, y, CORES).reshape(shape)
-    full = weight_grad(left_turned, right, 0, 1)
-    return pick(full.reshape(PLANES, CORES, block_rows, -1), y, 1)
+def ff_grad(left_turned, right):
+    return weight_grad(left_turned, right).reshape(PLANES, -1, right.shape[1])
 
 
 def halves_over_y(partials):
@@ -584,8 +620,22 @@
     ], sent
 
 
-def sum_everywhere(value):
-    return jnp.sum(lax.all_gather(value, EVERYWHERE, axis=0, tiled=False), axis=0)
+def butterfly(value, axis_name):
+    count = lax.axis_size(axis_name)
+    step = 1
+    while step < count:
+        value = value + lax.ppermute(value, axis_name, [(src, src ^ step) for src in range(count)])
+        step *= 2
+    return value
+
+
+def sum_in_order(value, arrived):
+    here = lax.axis_index("z")
+    values = jnp.stack([value, *arrived])
+    total = pick(values, here)
+    for plane in range(1, PLANES):
+        total = total + pick(values, (here - plane) % PLANES)
+    return total
 
 
 def to_planes(chunks):
@@ -605,31 +655,6 @@
         back.append(lax.ppermute(arrived[step], "z", shifted(-step, PLANES)))
     back = jnp.stack(back)
     return [pick(back, (chunk - here) % PLANES) for chunk in range(PLANES)]
-
-
-def normalized(update, update_gram, halves):
-    width = update.shape[1]
-    block = 128
-    index = jnp.arange(block)
-    diagonal = jnp.stack(
-        [
-            update_gram[at : at + block, at : at + block].astype(F32)
-            for at in range(0, width, block)
-        ]
-    )
-    diagonal = jnp.sum(
-        jnp.where(index[:, None] == index[None, :], diagonal, 0.0), axis=(1, 2)
-    )
-    low_half = jnp.sum(diagonal[: width // block // 2])
-    high_half = jnp.sum(diagonal[width // block // 2 :])
-    both = low_half + high_half
-    squares = jnp.stack([jnp.where(halves, low_half, both), jnp.where(halves, high_half, both)])
-    inverse = jnp.repeat(1.0 / (jnp.sqrt(squares) + NS_EPS), width // 2)
-    side = jnp.arange(width) < width // 2
-    kept = jnp.logical_not(halves) | (side[:, None] == side[None, :])
-    start = (update.astype(F32) * inverse).astype(BF16)
-    gram = update_gram.astype(F32) * inverse[:, None] * inverse[None, :]
-    return start, jnp.where(kept, gram, 0.0).astype(BF16)
 
 
 def per_device(
@@ -679,8 +704,8 @@
     key_value_rows = attention_rows[:, :MODEL_WIDTH]
     query_rows = attention_rows[:, MODEL_WIDTH : 2 * MODEL_WIDTH]
     output_rows = attention_rows[:, 2 * MODEL_WIDTH :]
-    gate_ff, up_ff, down_ff = (
-        gather_rows(shard[None], PLANE_ROWS).reshape(PLANES, CORES, *shard.shape)
+    gate_own, up_own_rows, down_own_rows = (
+        gather_rows(shard, ("z",))
         for shard in (w_gate.astype(BF16).T, w_up.astype(BF16).T, w_down.astype(BF16))
     )
 
@@ -745,69 +770,81 @@
     kv_proj, kv_low = key_value_chain(
         kv_near, swap(kv_sent), gain_key[None], cosine_table[0], sine_table[0]
     )
-    own_kv = after(jnp.concatenate(ring_blocks(kv_low, "fsdp", ring), axis=0), q_proj)
+    kv_blocks, gate_own = after((ring_blocks(kv_low, "fsdp", ring), gate_own), q_proj)
+    gate_other = swap(gate_own, "y")
+    own_kv = jnp.concatenate(kv_blocks, axis=0)
     both_kv = with_partner(own_kv).reshape(CORES, complete_rows, 2 * KV_WIDTH)
     attention_inputs = (q_proj, both_kv, mask, gain_query[None], cosine_table, sine_table)
     att_low, att_turned = attention(*attention_inputs)
-    team_cotangent = with_partner(
-        jnp.concatenate(ring_blocks(after(cotangent_rows, own_kv), "fsdp", ring), axis=0)
-    )
+    cotangent_blocks = ring_blocks(after(cotangent_rows, own_kv), "fsdp", ring)
+    att_low, cotangent_blocks = lax.optimization_barrier((att_low, cotangent_blocks))
+    team_cotangent = with_partner(jnp.concatenate(cotangent_blocks, axis=0))
     out_sent = dot_nn(att_low[rows:], output_rows).astype(BF16)
     out_near = dot_nn(att_low[:rows], output_rows)
+    out_sent, out_near, gate_other, up_own_rows = lax.optimization_barrier(
+        (out_sent, out_near, gate_other, up_own_rows)
+    )
+    up_other = swap(up_own_rows, "y")
     middle = residual + out_near + swap(out_sent).astype(F32)
 
     normed_two = rms_scale(middle, gain_mlp).astype(BF16)
-    team_two = with_partner(jnp.concatenate(ring_blocks(normed_two, "fsdp", ring), axis=0))
+    two_blocks, down_own_rows, up_other = after(
+        (ring_blocks(normed_two, "fsdp", ring), down_own_rows, up_other), team_cotangent
+    )
+    down_other = swap(down_own_rows, "y")
+    team_two = with_partner(jnp.concatenate(two_blocks, axis=0))
+    own_rows = ring * rows
     hidden, d_gate, d_up, hidden_turned, d_gate_turned, d_up_turned = swiglu_both_ways(
-        team_two, team_cotangent, (gate_ff, up_ff, down_ff)
-    )
-    block_rows = gate_ff.shape[2]
-    own_rows = ring * rows
-    other_y = 1 - lax.axis_index("y")
-    own_y = lax.axis_index("y")
-    down_sent = ff_grad_half(hidden_turned, team_cotangent, block_rows, other_y)
+        team_two, team_cotangent, gate_own, up_own_rows, down_own_rows
+    )
+    down_kept = ff_grad(hidden_turned, team_cotangent)
+    gate_kept = ff_grad(after(d_gate_turned, down_kept), team_two)
+    up_kept = ff_grad(after(d_up_turned, gate_kept), team_two)
+    (
+        far_hidden,
+        far_d_gate,
+        far_d_up,
+        far_hidden_turned,
+        far_d_gate_turned,
+        far_d_up_turned,
+    ) = swiglu_both_ways(
+        team_two, team_cotangent, gate_other, up_other, after(down_other, up_kept)
+    )
+    down_sent = ff_grad(far_hidden_turned, team_cotangent)
     down_passed = swap(down_sent, "y")
-    down_kept = ff_grad_half(
-        after(hidden_turned, down_sent), team_cotangent, block_rows, own_y
-    )
-    back_grads = after((d_gate, d_up), down_kept)
-    back_far = back_to_width(back_grads, (gate_ff, up_ff), own_rows, own_rows)
-    back_near = back_to_width(after(back_grads, back_far), (gate_ff, up_ff), 0, own_rows)
-    gate_turned = after(d_gate_turned, back_near)
-    gate_sent = ff_grad_half(gate_turned, team_two, block_rows, other_y)
+    gate_sent = ff_grad(after(far_d_gate_turned, down_sent), team_two)
     gate_passed = swap(gate_sent, "y")
+    back_lefts = after((d_gate, d_up, far_d_gate, far_d_up), gate_sent)
+    back_rights = (gate_own, up_own_rows, gate_other, up_other)
+    back_far = back_to_width(back_lefts, back_rights, own_rows, own_rows)
+    back_near = back_to_width(after(back_lefts, back_far), back_rights, 0, own_rows)
     down_own, down_chunks, down_chunks_sent = chunks_over_z(
-        [down_kept], after(down_passed, gate_sent)
+        [down_kept], after(down_passed, back_near)
     )
     back_half = back_near.astype(F32) + swap(after(back_far, down_chunks_sent)).astype(F32)
     back_half = back_half.reshape(ring, rows, MODEL_WIDTH)
     back_arrived = ring_send([back_half[step] for step in range(ring)], "fsdp", ring)
-    gate_kept = ff_grad_half(after(gate_turned, back_half), team_two, block_rows, own_y)
-    up_turned = after(d_up_turned, gate_kept)
-    up_sent = ff_grad_half(up_turned, team_two, block_rows, other_y)
+    up_sent = ff_grad(after(far_d_up_turned, back_half), team_two)
     up_passed = swap(up_sent, "y")
-    up_kept = ff_grad_half(after(up_turned, up_sent), team_two, block_rows, own_y)
-    back_arrived, down_chunks, gate_passed = after(
-        (back_arrived, down_chunks, gate_passed), up_kept
-    )
-    gate_own, gate_chunks, gate_chunks_sent = chunks_over_z([gate_kept], gate_passed)
-    d_normed_two = add_all(after(back_half[0], gate_chunks_sent), back_arrived)
+    back_arrived, down_chunks = after((back_arrived, down_chunks), up_sent)
+    d_normed_two = add_all(after(back_half[0], down_chunks), back_arrived)
     second_back = jax.vjp(rms_scale, middle, gain_mlp)[1]
     d_mid_norm, d_gain_mlp = second_back(d_normed_two)
     d_middle = cotangent_rows.astype(F32) + d_mid_norm
+    d_middle, gate_passed = lax.optimization_barrier((d_middle, gate_passed))
 
     both_mid = with_partner(d_middle.astype(BF16))
-    d_head = times_rows(both_mid, attention_rows, 2)
-    output_grad = weight_grad(att_turned, after(both_mid, d_head), 0, 1)
+    gate_own, gate_chunks, gate_chunks_sent = chunks_over_z([gate_kept], gate_passed)
+    output_grad = weight_grad(att_turned, after(both_mid, gate_chunks_sent))
     output_blocks = jnp.moveaxis(output_grad.reshape(PLANES * CORES, ring, -1, MODEL_WIDTH), 1, 0)
     output_own, output_arrived = scatter_blocks(output_blocks, "fsdp")
-    d_head = after(d_head, output_grad)
+    d_head = times_rows(after(both_mid, output_grad), attention_rows, 2)
     *far_parts, d_kv_far, far_gain = attention_back(*attention_inputs, d_head, 1, ())
     q_low, q_low_turned, d_kv_near, near_gain = attention_back(
         *attention_inputs, d_head, 0, far_parts
     )
     d_gain_query = (far_gain + near_gain)[0]
-    query_grad = weight_grad(q_low_turned, both_normed, 0, 1)
+    query_grad = weight_grad(q_low_turned, both_normed)
     from_query = times_columns(after(q_low, query_grad), attention_rows, MODEL_WIDTH, MODEL_WIDTH)
     query_blocks = jnp.moveaxis(query_grad.reshape(PLANES * CORES, ring, -1, MODEL_WIDTH), 1, 0)
     query_own, query_arrived = scatter_blocks(query_blocks, "fsdp")
@@ -818,9 +855,10 @@
     d_kv_half = d_kv_near.astype(F32) + swap(after(d_kv_far, up_chunks_sent)).astype(F32)
     d_kv_half = d_kv_half.reshape(2, ring, rows, KV_WIDTH)
     d_kv_arrived = ring_send([d_kv_half[:, step] for step in range(ring)], "fsdp", ring)
-    hidden = after(hidden, d_kv_half)
-    down_far = back_to_width((hidden,), (down_ff,), own_rows, own_rows)
-    down_near = back_to_width((after(hidden, down_far),), (down_ff,), 0, own_rows)
+    hiddens = after((hidden, far_hidden), d_kv_half)
+    down_rights = (down_own_rows, down_other)
+    down_far = back_to_width(hiddens, down_rights, own_rows, own_rows)
+    down_near = back_to_width(after(hiddens, down_far), down_rights, 0, own_rows)
     gate_new = updated(add_all(gate_own, gate_chunks), 4)
     down_new = updated(add_all(down_own, down_chunks), 6)
     up_chunks, d_kv_arrived, query_arrived = after(
@@ -848,19 +886,21 @@
     key_value_own, key_value_arrived = scatter_blocks(key_value_blocks, "fsdp")
     plane = lax.axis_index("z")
     in_plane = ("y", "core", "fsdp")
-    big_mine, key_value_arrived, first_passed = lax.optimization_barrier(
-        (big_mine, key_value_arrived, first_passed)
-    )
-    first_own, first_chunks, first_chunks_sent = chunks_over_z(first_kept, first_passed)
-    kept, arrived, attention_passed = halves_over_y(
-        [add_all(key_value_own.astype(F32), key_value_arrived).astype(BF16)]
-    )
-    big_gram = dot_tn(after(big_mine, attention_passed, first_chunks_sent), big_mine).astype(BF16)
-    from_kv = times_rows(after(both_kv_low, big_gram), attention_rows, 0)
+    big_mine, first_passed, key_value_grad = lax.optimization_barrier(
+        (big_mine, first_passed, key_value_grad)
+    )
+    big_gram = gram_blocks(big_mine)
+    from_query, down_far = after((from_query, down_far), big_gram)
+    down_half = (down_near.astype(F32) + swap(down_far).astype(F32)).reshape(
+        ring, rows, MODEL_WIDTH
+    )
+    first_own, first_chunks, first_chunks_sent = chunks_over_z(
+        first_kept, after(first_passed, big_gram)
+    )
+    from_kv = times_rows(
+        after(both_kv_low, key_value_grad, first_chunks_sent), attention_rows, 0
+    )
     big_gram = lax.psum(big_gram, in_plane)
-    arrived, first_chunks = after((arrived, first_chunks), from_kv)
-    last_own, last_chunks, last_chunks_sent = chunks_over_z(kept, arrived)
-    from_kv = after(from_kv, last_chunks_sent)
 
     from_query = from_query[:rows].astype(F32) + swap(from_query[rows:]).astype(F32)
     kv_here = from_kv[:rows].reshape(rows, -1, HEAD_SIZE)
@@ -872,13 +912,16 @@
     first_back = jax.vjp(rms_scale, residual, gain_attn)[1]
     d_residual, d_gain_attn = first_back(d_normed)
     input_grad = (d_middle + d_residual).reshape(inputs.shape)
-    down_half = (down_near.astype(F32) + swap(after(down_far, d_normed)).astype(F32)).reshape(
-        ring, rows, MODEL_WIDTH
-    )
-    down_arrived = ring_send([down_half[step] for step in range(ring)], "fsdp", ring)
     gain_grad = jnp.concatenate([d_gain_attn, d_gain_mlp, d_gain_query, d_gain_key])
 
-    last_chunks = after(last_chunks, input_grad)
+    key_value_arrived, first_chunks = after((key_value_arrived, first_chunks), input_grad)
+    kept, arrived, _ = halves_over_y(
+        [add_all(key_value_own.astype(F32), key_value_arrived).astype(BF16)]
+    )
+    last_own, last_chunks, _ = chunks_over_z(kept, arrived)
+    last_chunks, big_gram, gain_grad, down_half = lax.optimization_barrier(
+        (last_chunks, big_gram, butterfly(butterfly(gain_grad, "core"), "fsdp"), down_half)
+    )
     first_total = add_all(first_own, first_chunks)
     output_shard = first_total[:, :MODEL_WIDTH]
     query_shard = first_total[:, MODEL_WIDTH:]
@@ -898,15 +941,20 @@
         ]
     )
     small_mine = to_planes(small_slots).reshape(-1, MODEL_WIDTH)
+    small_mine, gain_grad = lax.optimization_barrier((small_mine, butterfly(gain_grad, "y")))
     whole = gather_rows(small_mine, in_plane)
-    start, gram = normalized(big_mine, big_gram, jnp.bool_(False))
-    turned = chain(start, after(gram, small_mine), bend_of(gram))
-    turned, whole = lax.optimization_barrier((turned, whole))
+    turned = muon(after(big_mine, small_mine), big_gram, jnp.bool_(False))
+    turned, whole, gain_arrived = lax.optimization_barrier(
+        (turned, whole, ring_blocks(gain_grad, "z", PLANES)[1:])
+    )
+    gain_grad = sum_in_order(gain_grad, gain_arrived)
     returned = from_planes(turned.reshape(PLANES, -1, MODEL_WIDTH))
-    small_gram = dot_tn(whole, whole).astype(BF16)
-    start, gram = normalized(small_mine, small_gram, plane == 1)
-    turned, returned, down_arrived, gain_grad = lax.optimization_barrier(
-        (chain(start, gram, bend_of(gram)), returned, down_arrived, sum_everywhere(gain_grad))
+    small_gram = gram_blocks(whole)
+    down_arrived = ring_send(
+        [after(down_half, small_gram)[step] for step in range(ring)], "fsdp", ring
+    )
+    turned, returned, down_arrived = lax.optimization_barrier(
+        (muon(small_mine, small_gram, plane == 1), returned, down_arrived)
     )
     small_returned = from_planes(turned.reshape(small_slots.shape))
     block_out = (middle + add_all(down_half[0], down_arrived)).astype(BF16).reshape(inputs.shape)

time: 1540 us -> 1390 us (0.903)
  blocking collectives: 105 us -> 0 us
  matrix products: 70.3 us -> 34.4 us
  waiting for transfers between devices: 517 us -> 539 us
  other arithmetic: 170 us -> 149 us
    all_gather x1 -> x0, blocking collectives: 105 us -> none  [sum_everywhere(): lax.all_gather(value, EVERYWHERE, axis=0, tiled=False)]
    ppermute x3 -> x6, waiting for transfers between devices: 114 us -> 22.9 us  [ring_blocks(): lax.ppermute(value, axis_name, shifted(step, count))]
    ppermute x3, waiting for transfers between devices: 0.01 us -> 45.8 us  [scatter_blocks(): lax.ppermute(pick(blocks, (here + step) % count), axis_name, shifted(step...]
    ppermute x19 -> x22, waiting for transfers between devices: 44.9 us -> 89.3 us  [swap(): return lax.ppermute(value, axis_name, shifted(1, CORES))]
    psum x1, waiting for transfers between devices: 36.4 us -> 2.75 us  [per_device(): big_gram = lax.psum(big_gram, in_plane)]
    dot_general x3 -> x1, matrix products: 36.3 us -> 6.06 us  [dot_tn(): lax.dot_general(left, right, (((0,), (0,)), ((), ())), preferred_element_...]
    ppermute x6, waiting for transfers between devices: 9.22 us -> 36.4 us  [from_planes(): back.append(lax.ppermute(arrived[step], 'z', shifted(-step, PLANES)))]
    ppermute x15, waiting for transfers between devices: 44.5 us -> 69.6 us  [chunks_over_z(): lax.ppermute(value, 'z', shifted(step + 1, PLANES))]
  transfers between devices with their start and end apart: 61 -> 70, of which waited for: 25 -> 32; matrix products, arithmetic and copies ran while one was open for 19% -> 16% of each run, Pallas kernels for 23% -> 26%
where the time goes in v3:
time: 1390 us; the launch traced here: 1380 us
  waiting for transfers between devices  539 us (39%)
  Pallas kernels  417 us (30%)
  other arithmetic  149 us (11%)
  local copies, waits for them, and re-layouts  124 us (9%)
  starting transfers between devices  93.1 us (7%)
  matrix products  34.4 us (2%)
  between operations  21.6 us (2%)
    all_gather x5, waiting for transfers between devices, gather_rows(): return lax.all_gather(shard, axes, axis=0, tiled=True)  194 us
    pallas_call x2, Pallas kernels, muon(): pl.pallas_call(muon_kernel, grid=(), in_specs=[pl.BlockSpec(memory_space=...  108 us
    ppermute x22, waiting for transfers between devices, swap(): return lax.ppermute(value, axis_name, shifted(1, CORES))  89.3 us
    ppermute x15, waiting for transfers between devices, chunks_over_z(): lax.ppermute(value, 'z', shifted(step + 1, PLANES))  69.6 us
    pallas_call x8, Pallas kernels, weight_grad(): pl.pallas_call(weight_grad_kernel, grid=(width // tile,), in_specs=[pl.Bl...  68.1 us
    pallas_call x4, Pallas kernels, back_to_width(): pl.pallas_call(functools.partial(back_to_width_kernel, len(lefts)), grid=...  63.2 us
    pallas_call x2, Pallas kernels, swiglu_both_ways(): pl.pallas_call(swiglu_kernel, grid=(tokens // tile,), in_specs=[row_block...  59.9 us
    unnamed x267, local copies, waits for them, and re-layouts  55.9 us
  transfers between devices with their start and end apart: 70, of which 32 were waited for; matrix products, arithmetic and copies ran while one was open for 16% of the time, Pallas kernels for 26%

profile of v3, /device:TPU:0, one launch (start us, length us, event | category | flops | bytes accessed | tf_op | source)
XLA Modules:
  0.0 1378.9 jit_solution(13278200441752494223)
XLA Ops:
  24.2 7.7 reshape.447
  32.0 8.5 constant_dynamic-slice_fusion.13
  40.4 9.0 copy.59
  50.8 116.6 %all-gather.6.cloned.1.call-done.right_ref = bf16[1024,6144]{1,0:T(8,128)(2,1)} async-done(((bf16[64,6144]{1,0:T(8,128)(2,1)}), bf16[1024,6144]{1,0:T(8,128)(2,1)}) %all-gather.6.cloned.1.call-update) | async-done | bytes 12582928 | tf_op jit(solution)/shard_map/all_gather | solution.py:583
  167.4 5.9 fusion.26
  194.2 9.4 fusion.11.q_ref
  203.6 27.7 %all-gather.8.cloned.1.call-done.gate_ref.refs_4_ = bf16[768,2048]{1,0:T(8,128)(2,1)} async-done(((bf16[192,2048]{1,0:T(8,128)(2,1)}), bf16[768,2048]{1,0:T(8,128)(2,1)}) %all-gather.8.cloned.1.call-update) | async-done | bytes 3145744 | tf_op jit(solution)/shard_map/all_gather | solution.py:583
  231.3 9.6 collective-permute-done.3
  253.6 8.5 pad_maximum_fusion
  262.1 19.7 %attention.1 = (bf16[1024,1024]{1,0:T(8,128)(2,1)S(1)}, bf16[1024,1024]{1,0:T(8,128)(2,1)S(1)}) custom-call(f32[1024,1024]{1,0:T(8,128)S(1)} %copy-done.2, bf16[2,1024,2048]{2,1,0:T(8,128)(2,1)} %bitcast.352, bf16[2,1024,2048]{2,1,0:T(8,128)(2,1)} %bitcast.353, bf16[2,1024,512]{2,1,0:T(8,128)(2,1)S(1)} %and_convert_fusion.mask_ref, ...), custom_call_target="tpu_custom_call" | custom-call | flops 1 | bytes 1 | tf_op jit(solution)/shard_map/attention/pallas_call | solution.py:325
  281.8 13.3 collective-permute-done.5
  303.2 5.7 all-gather.10.cloned.1.call-done.up_ref.refs_5_
  308.9 9.9 collective-permute-done.6.gate_ref.refs_6_
  338.8 44.5 %all-gather.12.cloned.1.call-done.down_ref.refs_2_ = bf16[768,2048]{1,0:T(8,128)(2,1)} async-done(((bf16[192,2048]{1,0:T(8,128)(2,1)}), bf16[768,2048]{1,0:T(8,128)(2,1)}) %all-gather.12.cloned.1.call-update) | async-done | bytes 3145744 | tf_op jit(solution)/shard_map/all_gather | solution.py:583
  383.3 11.8 collective-permute-done.9.up_ref.refs_7_
  406.7 29.9 %swiglu_both_ways.2 = (bf16[2048,768]{1,0:T(8,128)(2,1)}, bf16[2048,768]{1,0:T(8,128)(2,1)}, bf16[2048,768]{1,0:T(8,128)(2,1)}, bf16[768,2048]{1,0:T(8,128)(2,1)...) custom-call(bf16[2048,2048]{1,0:T(8,128)(2,1)} %constant_dynamic-update-slice_fusion.5.two_ref.right_ref, ...), custom_call_target="tpu_custom_call" | custom-call | flops 1 | bytes 1 | tf_op jit(solution)/shard_map/swiglu_both_ways/pallas_call | solution.py:378
  438.6 9.1 weight_grad.8
  449.5 9.1 weight_grad.9
  458.6 10.1 weight_grad.10
  468.8 30.0 %swiglu_both_ways.3 = (bf16[2048,768]{1,0:T(8,128)(2,1)}, bf16[2048,768]{1,0:T(8,128)(2,1)}, bf16[2048,768]{1,0:T(8,128)(2,1)}, bf16[768,2048]{1,0:T(8,128)(2,1)...) custom-call(bf16[2048,2048]{1,0:T(8,128)(2,1)} %constant_dynamic-update-slice_fusion.5.two_ref.right_ref, ...), custom_call_target="tpu_custom_call" | custom-call | flops 1 | bytes 1 | tf_op jit(solution)/shard_map/swiglu_both_ways/pallas_call | solution.py:378
  500.7 9.8 weight_grad.11
  513.0 9.0 weight_grad.12
  523.7 20.0 %back_to_width.4 = bf16[1024,2048]{1,0:T(8,128)(2,1)} custom-call(bf16[2048,768]{1,0:T(8,128)(2,1)} %get-tuple-element.170.refs_0_, bf16[2048,768]{1,0:T(8,128)(2,1)} %get-tuple-element.171.refs_1_, bf16[2048,768]{1,0:T(8,128)(2,1)} %get-tuple-element.172.refs_2_, bf16[2048,768]{1,0:T(8,128)(2,1)} %get-tuple-element.173.refs_3_, ...), custom_call_target="tpu_custom_call" | custom-call | flops 1 | bytes 1 | tf_op jit(solution)/shard_map/back_to_width/pallas_call | solution.py:395
  543.7 20.5 %back_to_width.5 = bf16[1024,2048]{1,0:T(8,128)(2,1)} custom-call(bf16[2048,768]{1,0:T(8,128)(2,1)} %get-tuple-element.170.refs_0_, bf16[2048,768]{1,0:T(8,128)(2,1)} %get-tuple-element.171.refs_1_, bf16[2048,768]{1,0:T(8,128)(2,1)} %get-tuple-element.172.refs_2_, bf16[2048,768]{1,0:T(8,128)(2,1)} %get-tuple-element.173.refs_3_, ...), custom_call_target="tpu_custom_call" | custom-call | flops 1 | bytes 1 | tf_op jit(solution)/shard_map/back_to_width/pallas_call | solution.py:395
  564.2 16.7 %collective-permute-done.13 = bf16[4,192,2048]{2,1,0:T(8,128)(2,1)} collective-permute-done((bf16[4,192,2048]{2,1,0:T(8,128)(2,1)}, bf16[4,192,2048]{2,1,0:T(8,128)(2,1)}, u32[]{:S(2)}, u32[]{:S(2)}) %collective-permute-start.13) | collective-permute-done | bytes 3145760 | tf_op jit(solution)/shard_map/ppermute | solution.py:552
  584.6 7.3 collective-permute-done.14
  591.9 5.5 convert_add_fusion.3
  605.6 9.8 weight_grad.13
  618.3 5.4 collective-permute-done.16
  623.7 32.4 %collective-permute-done.17 = bf16[192,2048]{1,0:T(8,128)(2,1)S(1)} collective-permute-done((bf16[192,2048]{1,0:T(8,128)(2,1)}, bf16[192,2048]{1,0:T(8,128)(2,1)S(1)}, u32[]{:S(2)}, u32[]{:S(2)}) %collective-permute-start.17) | collective-permute-done | bytes 786464 | tf_op jit(solution)/shard_map/ppermute | solution.py:619
  664.2 5.4 collective-permute-done.19
  680.1 5.6 weight_grad.14
  688.2 11.9 collective-permute-start.22
  702.5 6.8 times_rows.2.grad_ref
  710.6 21.8 %attention_back.2 = (bf16[1024,1024]{1,0:T(8,128)(2,1)S(1)}, bf16[1024,1024]{1,0:T(8,128)(2,1)S(1)}, bf16[2,1024,1024]{2,1,0:T(8,128)(2,1)}, f32[1,128]{1,0:T(1,128)S(1)}) custom-call(f32[1024,1024]{1,0:T(8,128)} %fusion.11.q_ref, bf16[2,1024,2048]{2,1,0:T(8,128)(2,1)} %bitcast.354, bf16[2,1024,2048]{2,1,0:T(8,128)(2,1)} %bitcast.355, ...), custom_call_target="tpu_custom_call" | custom-call | flops 1 | bytes 1 | tf_op jit(solution)/shard_map/attention_back/pallas_call | solution.py:349
  732.4 22.1 %attention_back.3 = (bf16[1024,1024]{1,0:T(8,128)(2,1)S(1)}, bf16[1024,1024]{1,0:T(8,128)(2,1)S(1)}, bf16[2,1024,1024]{2,1,0:T(8,128)(2,1)}, f32[1,128]{1,0:T(1,128)S(1)}) custom-call(f32[1024,1024]{1,0:T(8,128)} %fusion.11.q_ref, bf16[2,1024,2048]{2,1,0:T(8,128)(2,1)} %bitcast.356, ...), custom_call_target="tpu_custom_call", output_to_operand_aliasing={{0}: (8, {}), {1}: (9, {})} | custom-call | flops 1 | bytes 1 | tf_op jit(solution)/shard_map/attention_back/pallas_call | solution.py:349
  754.5 5.6 weight_grad.15
  760.1 7.4 times_columns.1
  767.6 5.8 fusion.67
  788.7 5.3 fusion.70
  805.1 11.3 back_to_width.6
  816.4 11.4 back_to_width.7
  827.8 21.5 %collective-permute-done.28 = bf16[192,2048]{1,0:T(8,128)(2,1)} collective-permute-done((bf16[192,2048]{1,0:T(8,128)(2,1)}, bf16[192,2048]{1,0:T(8,128)(2,1)}, u32[]{:S(2)}, u32[]{:S(2)}) %collective-permute-start.28) | collective-permute-done | bytes 786464 | tf_op jit(solution)/shard_map/ppermute | solution.py:619
  849.3 19.6 %collective-permute-done.30 = bf16[2,512,1024]{2,1,0:T(8,128)(2,1)} collective-permute-done((bf16[2,512,1024]{2,1,0:T(8,128)(2,1)}, bf16[2,512,1024]{2,1,0:T(8,128)(2,1)}, u32[]{:S(2)}, u32[]{:S(2)}) %collective-permute-start.30) | collective-permute-done | bytes 2097184 | tf_op jit(solution)/shard_map/ppermute | solution.py:567
  898.4 32.4 %collective-permute-done.35 = bf16[192,2048]{1,0:T(8,128)(2,1)} collective-permute-done((bf16[192,2048]{1,0:T(8,128)(2,1)}, bf16[192,2048]{1,0:T(8,128)(2,1)}, u32[]{:S(2)}, u32[]{:S(2)}) %collective-permute-start.35) | collective-permute-done | bytes 786464 | tf_op jit(solution)/shard_map/ppermute | solution.py:646
  936.0 6.1 convolution_convert_fusion
  942.1 7.5 gram_blocks.2
  959.3 6.6 times_rows.3
  967.0 17.4 %collective-permute-start.38 = (bf16[64,4096]{1,0:T(8,128)(2,1)}, bf16[64,4096]{1,0:T(8,128)(2,1)S(1)}, u32[]{:S(2)}, u32[]{:S(2)}) collective-permute-start(bf16[64,4096]{1,0:T(8,128)(2,1)} %get-tuple-element.319), channel_id=1, source_target_pairs={{0,8},{8,16},{16,24},{24,0},{1,9},{9,17},{17,25},{25,1},{2,10},{10... | collective-permute-start | bytes 1572872 | tf_op jit(solution)/shard_map/ppermute | solution.py:619
  993.2 5.2 copy.56
  998.5 6.6 reshape.481
  1005.2 5.6 fusion.3
  1011.2 5.7 fusion.6
  1020.2 45.8 %collective-permute-done.33 = bf16[8,64,2048]{2,1,0:T(8,128)(2,1)} collective-permute-done((bf16[8,64,2048]{2,1,0:T(8,128)(2,1)}, bf16[8,64,2048]{2,1,0:T(8,128)(2,1)}, u32[]{:S(2)}, u32[]{:S(2)}) %collective-permute-start.33) | collective-permute-done | bytes 2097184 | tf_op jit(solution)/shard_map/ppermute | solution.py:590
  1075.8 28.6 %collective-permute-done.43 = bf16[4,64,2048]{2,1,0:T(8,128)(2,1)S(1)} collective-permute-done((bf16[4,64,2048]{2,1,0:T(8,128)(2,1)S(1)}, bf16[4,64,2048]{2,1,0:T(8,128)(2,1)S(1)}, u32[]{:S(2)}, u32[]{:S(2)}) %collective-permute-start.43) | collective-permute-done | bytes 1048608 | tf_op jit(solution)/shard_map/ppermute | solution.py:552
  1111.3 5.3 convert_add_fusion.1
  1119.3 7.1 collective-permute-done.45
  1129.1 6.4 collective-permute-start.52
  1148.4 10.1 collective-permute-done.51
  1170.1 70.9 %muon.2 = bf16[768,2048]{1,0:T(8,128)(2,1)} custom-call(s32[1]{0:T(128)} %constant.618.clone.1.halves_ref, bf16[768,2048]{1,0:T(8,128)(2,1)} %bitcast.338, bf16[10,512,512]{2,1,0:T(8,128)(2,1)} %all-reduce.3.cloned.1.call-done.packed_ref, f32[1,2048]{1,0:T(1,128)} %bitcast.399, f32[2048,1]{1,0:T(8,128)} %bitcast.386), custom_call_target="tpu_custom_call" | custom-call | flops 1 | bytes 1 | tf_op jit(solution)/shard_map/muon/pallas_call | solution.py:516
  1244.5 15.6 %gram_blocks.3.packed_ref = bf16[10,512,512]{2,1,0:T(8,128)(2,1)S(1)} custom-call(s32[10]{0:T(128)S(1)} %copy-done.43, s32[10]{0:T(128)S(1)} %copy-done.44, bf16[2048,2048]{1,0:T(8,128)(2,1)S(1)} %copy-done.3, bf16[2048,2048]{1,0:T(8,128)(2,1)S(1)} %copy-done.3), custom_call_target="tpu_custom_call" | custom-call | flops 1 | bytes 1 | tf_op jit(solution)/shard_map/gram_blocks/pallas_call | solution.py:481
  1279.1 37.5 %muon.3 = bf16[256,2048]{1,0:T(8,128)(2,1)} custom-call(s32[1]{0:T(128)} %bitcast.84.halves_ref, bf16[256,2048]{1,0:T(8,128)(2,1)} %bitcast.372, bf16[10,512,512]{2,1,0:T(8,128)(2,1)} %copy-done.5, f32[1,2048]{1,0:T(1,128)} %bitcast.397, f32[2048,1]{1,0:T(8,128)} %bitcast.383), custom_call_target="tpu_custom_call" | custom-call | flops 1 | bytes 1 | tf_op jit(solution)/shard_map/muon/pallas_call | solution.py:516
  1317.5 23.9 %collective-permute-done.58 = bf16[192,2048]{1,0:T(8,128)(2,1)} collective-permute-done((bf16[192,2048]{1,0:T(8,128)(2,1)}, bf16[192,2048]{1,0:T(8,128)(2,1)}, u32[]{:S(2)}, u32[]{:S(2)}) %collective-permute-start.58) | collective-permute-done | bytes 786464 | tf_op jit(solution)/shard_map/ppermute | solution.py:655
  1356.5 12.5 collective-permute-done.62
  (514 shorter events, 306.7 us)
Async XLA Ops:
  7.2 160.2 %all-gather.6.cloned.1.call-start = ((), (), s32[]{:S(2)}) async-start(), calls=%async_computation | async-start | bytes 13369344 | tf_op jit(solution)/shard_map/all_gather | solution.py:583
  12.5 218.8 %all-gather.8.cloned.1.call-start = ((), (), s32[]{:S(2)}) async-start(), calls=%async_computation.1 | async-start | bytes 3932160 | tf_op jit(solution)/shard_map/all_gather | solution.py:583
  15.4 157.9 %collective-permute-start.2 = (s32[1,1024]{1,0:T(1,128)S(1)}, s32[1,1024]{1,0:T(1,128)S(1)}, u32[]{:S(2)}, u32[]{:S(2)}) collective-permute-start(s32[1,1024]{1,0:T(1,128)S(1)} %copy-done.116), channel_id=1, source_target_pairs={{0,2},{2,0},{1,3},{3,1},{4,6},{6,4},{5,7},{7,5},{8,10},{10,8},{9,1... | collective-permute-start | bytes 12296 | tf_op jit(solution)/shard_map/ppermute | solution.py:552
  16.5 292.3 %all-gather.10.cloned.1.call-start = ((), (), s32[]{:S(2)}) async-start(), calls=%async_computation.2 | async-start | bytes 3932160 | tf_op jit(solution)/shard_map/all_gather | solution.py:583
  173.3 9.6 collective-permute-start.1
  192.7 48.2 %collective-permute-start.3 = (bf16[512,2048]{1,0:T(8,128)(2,1)S(1)}, bf16[512,2048]{1,0:T(8,128)(2,1)}, u32[]{:S(2)}, u32[]{:S(2)}) collective-permute-start(bf16[512,2048]{1,0:T(8,128)(2,1)S(1)} %get-tuple-element.137), channel_id=1, source_target_pairs={{0,1},{1,0},{2,3},{3,2},{4,5},{5,4},{6,7},{7,6},{8,9},{9,8},{10,11... | collective-permute-start | bytes 6291464 | tf_op jit(solution)/shard_map/ppermute | solution.py:561
  245.6 7.9 collective-permute-start.4
  246.6 136.7 %all-gather.12.cloned.1.call-start = ((), (), s32[]{:S(2)}) async-start(), calls=%async_computation.3 | async-start | bytes 3932160 | tf_op jit(solution)/shard_map/all_gather | solution.py:583
  246.7 48.4 %collective-permute-start.5 = (bf16[512,2048]{1,0:T(8,128)(2,1)}, bf16[512,2048]{1,0:T(8,128)(2,1)}, u32[]{:S(2)}, u32[]{:S(2)}) collective-permute-start(bf16[512,2048]{1,0:T(8,128)(2,1)} %bitcast.368), channel_id=1, source_target_pairs={{0,1},{1,0},{2,3},{3,2},{4,5},{5,4},{6,7},{7,6},{8,9},{9,8},{10,11... | collective-permute-start | bytes 6291464 | tf_op jit(solution)/shard_map/ppermute | solution.py:561
  248.2 70.5 %collective-permute-start.6 = (bf16[768,2048]{1,0:T(8,128)(2,1)}, bf16[768,2048]{1,0:T(8,128)(2,1)}, u32[]{:S(2)}, u32[]{:S(2)}) collective-permute-start(bf16[768,2048]{1,0:T(8,128)(2,1)} %all-gather.8.cloned.1.call-done.gate_ref.refs_4_), channel_id=1, source_target_pairs={{0,4},{4,0},{1,5},{5,1},{2,6},{6,2},{3,7},{7,3},{8,12},{12,8},{9,1... | collective-permute-start | bytes 9437192 | tf_op jit(solution)/shard_map/ppermute | solution.py:552
  321.2 798.2 %all-reduce.3.cloned.1.call-start = ((), (), s32[]{:S(2)}) async-start(), calls=%async_computation.4 | async-start | bytes 10485760 | tf_op jit(solution)/shard_map/psum | solution.py:903
  324.1 12.1 collective-permute-start.10
  324.7 70.4 %collective-permute-start.9 = (bf16[768,2048]{1,0:T(8,128)(2,1)}, bf16[768,2048]{1,0:T(8,128)(2,1)}, u32[]{:S(2)}, u32[]{:S(2)}) collective-permute-start(bf16[768,2048]{1,0:T(8,128)(2,1)} %all-gather.10.cloned.1.call-done.up_ref.refs_5_), channel_id=1, source_target_pairs={{0,4},{4,0},{1,5},{5,1},{2,6},{6,2},{3,7},{7,3},{8,12},{12,8},{9,1... | collective-permute-start | bytes 9437192 | tf_op jit(solution)/shard_map/ppermute | solution.py:552
  330.2 64.9 %collective-permute-start.8 = (bf16[512,2048]{1,0:T(8,128)(2,1)S(1)}, bf16[512,2048]{1,0:T(8,128)(2,1)}, u32[]{:S(2)}, u32[]{:S(2)}) collective-permute-start(bf16[512,2048]{1,0:T(8,128)(2,1)S(1)} %multiply_convert_fusion), channel_id=1, source_target_pairs={{0,1},{1,0},{2,3},{3,2},{4,5},{5,4},{6,7},{7,6},{8,9},{9,8},{10,11... | collective-permute-start | bytes 6291464 | tf_op jit(solution)/shard_map/ppermute | solution.py:561
  397.2 7.2 collective-permute-start.11
  397.3 71.4 %collective-permute-start.12 = (bf16[768,2048]{1,0:T(8,128)(2,1)}, bf16[768,2048]{1,0:T(8,128)(2,1)}, u32[]{:S(2)}, u32[]{:S(2)}) collective-permute-start(bf16[768,2048]{1,0:T(8,128)(2,1)} %all-gather.12.cloned.1.call-done.down_ref.refs_2_), channel_id=1, source_target_pairs={{0,4},{4,0},{1,5},{5,1},{2,6},{6,2},{3,7},{7,3},{8,12},{12,8},{9,1... | collective-permute-start | bytes 9437192 | tf_op jit(solution)/shard_map/ppermute | solution.py:552
  510.5 70.4 %collective-permute-start.13 = (bf16[4,192,2048]{2,1,0:T(8,128)(2,1)}, bf16[4,192,2048]{2,1,0:T(8,128)(2,1)}, u32[]{:S(2)}, u32[]{:S(2)}) collective-permute-start(bf16[4,192,2048]{2,1,0:T(8,128)(2,1)} %bitcast.17), channel_id=1, source_target_pairs={{0,4},{4,0},{1,5},{5,1},{2,6},{6,2},{3,7},{7,3},{8,12},{12,8},{9,1... | collective-permute-start | bytes 9437192 | tf_op jit(solution)/shard_map/ppermute | solution.py:552
  584.6 7.3 collective-permute-start.14
  599.1 57.0 %collective-permute-start.15 = (bf16[512,2048]{1,0:T(8,128)(2,1)}, bf16[512,2048]{1,0:T(8,128)(2,1)S(1)}, u32[]{:S(2)}, u32[]{:S(2)}) collective-permute-start(bf16[512,2048]{1,0:T(8,128)(2,1)} %slice.354), channel_id=1, source_target_pairs={{0,1},{1,0},{2,3},{3,2},{4,5},{5,4},{6,7},{7,6},{8,9},{9,8},{10,11... | collective-permute-start | bytes 6291464 | tf_op jit(solution)/shard_map/ppermute | solution.py:567
  599.6 70.0 %collective-permute-start.19 = (bf16[4,192,2048]{2,1,0:T(8,128)(2,1)S(1)}, bf16[4,192,2048]{2,1,0:T(8,128)(2,1)}, u32[]{:S(2)}, u32[]{:S(2)}) collective-permute-start(bf16[4,192,2048]{2,1,0:T(8,128)(2,1)S(1)} %bitcast.349), channel_id=1, source_target_pairs={{0,4},{4,0},{1,5},{5,1},{2,6},{6,2},{3,7},{7,3},{8,12},{12,8},{9,1... | collective-permute-start | bytes 9437192 | tf_op jit(solution)/shard_map/ppermute | solution.py:552
  601.1 22.6 %collective-permute-start.16 = (bf16[192,2048]{1,0:T(8,128)(2,1)}, bf16[192,2048]{1,0:T(8,128)(2,1)S(1)}, u32[]{:S(2)}, u32[]{:S(2)}) collective-permute-start(bf16[192,2048]{1,0:T(8,128)(2,1)} %get-tuple-element.292), channel_id=1, source_target_pairs={{0,8},{8,16},{16,24},{24,0},{1,9},{9,17},{17,25},{25,1},{2,10},{10... | collective-permute-start | bytes 2359304 | tf_op jit(solution)/shard_map/ppermute | solution.py:619
  601.1 54.9 %collective-permute-start.17 = (bf16[192,2048]{1,0:T(8,128)(2,1)}, bf16[192,2048]{1,0:T(8,128)(2,1)S(1)}, u32[]{:S(2)}, u32[]{:S(2)}) collective-permute-start(bf16[192,2048]{1,0:T(8,128)(2,1)} %get-tuple-element.291), channel_id=1, source_target_pairs={{0,16},{8,24},{16,0},{24,8},{1,17},{9,25},{17,1},{25,9},{2,18},{10... | collective-permute-start | bytes 2359304 | tf_op jit(solution)/shard_map/ppermute | solution.py:619
  603.4 52.7 %collective-permute-start.18 = (bf16[192,2048]{1,0:T(8,128)(2,1)}, bf16[192,2048]{1,0:T(8,128)(2,1)}, u32[]{:S(2)}, u32[]{:S(2)}) collective-permute-start(bf16[192,2048]{1,0:T(8,128)(2,1)} %get-tuple-element.290), channel_id=1, source_target_pairs={{0,24},{8,0},{16,8},{24,16},{1,25},{9,1},{17,9},{25,17},{2,26},{10... | collective-permute-start | bytes 2359304 | tf_op jit(solution)/shard_map/ppermute | solution.py:619
  671.3 96.2 %collective-permute-start.21 = (bf16[4,192,2048]{2,1,0:T(8,128)(2,1)}, bf16[4,192,2048]{2,1,0:T(8,128)(2,1)}, u32[]{:S(2)}, u32[]{:S(2)}) collective-permute-start(bf16[4,192,2048]{2,1,0:T(8,128)(2,1)} %bitcast.22), channel_id=1, source_target_pairs={{0,4},{4,0},{1,5},{5,1},{2,6},{6,2},{3,7},{7,3},{8,12},{12,8},{9,1... | collective-permute-start | bytes 9437192 | tf_op jit(solution)/shard_map/ppermute | solution.py:552
  687.6 80.0 %collective-permute-start.25 = (bf16[8,64,2048]{2,1,0:T(8,128)(2,1)}, bf16[8,64,2048]{2,1,0:T(8,128)(2,1)S(1)}, u32[]{:S(2)}, u32[]{:S(2)}) collective-permute-start(bf16[8,64,2048]{2,1,0:T(8,128)(2,1)} %dynamic-slice_bitcast_fusion.2), channel_id=1, source_target_pairs={{0,1},{1,0},{2,3},{3,2},{4,5},{5,4},{6,7},{7,6},{8,9},{9,8},{10,11... | collective-permute-start | bytes 6291464 | tf_op jit(solution)/shard_map/ppermute | solution.py:590
  688.2 79.3 %collective-permute-start.22 = (bf16[192,2048]{1,0:T(8,128)(2,1)}, bf16[192,2048]{1,0:T(8,128)(2,1)S(1)}, u32[]{:S(2)}, u32[]{:S(2)}) collective-permute-start(bf16[192,2048]{1,0:T(8,128)(2,1)} %get-tuple-element.289), channel_id=1, source_target_pairs={{0,8},{8,16},{16,24},{24,0},{1,9},{9,17},{17,25},{25,1},{2,10},{10... | collective-permute-start | bytes 2359304 | tf_op jit(solution)/shard_map/ppermute | solution.py:619
  700.1 67.4 %collective-permute-start.23 = (bf16[192,2048]{1,0:T(8,128)(2,1)}, bf16[192,2048]{1,0:T(8,128)(2,1)S(1)}, u32[]{:S(2)}, u32[]{:S(2)}) collective-permute-start(bf16[192,2048]{1,0:T(8,128)(2,1)} %get-tuple-element.288), channel_id=1, source_target_pairs={{0,16},{8,24},{16,0},{24,8},{1,17},{9,25},{17,1},{25,9},{2,18},{10... | collective-permute-start | bytes 2359304 | tf_op jit(solution)/shard_map/ppermute | solution.py:619
  701.6 66.0 %collective-permute-start.24 = (bf16[192,2048]{1,0:T(8,128)(2,1)}, bf16[192,2048]{1,0:T(8,128)(2,1)}, u32[]{:S(2)}, u32[]{:S(2)}) collective-permute-start(bf16[192,2048]{1,0:T(8,128)(2,1)} %get-tuple-element.287), channel_id=1, source_target_pairs={{0,24},{8,0},{16,8},{24,16},{1,25},{9,1},{17,9},{25,17},{2,26},{10... | collective-permute-start | bytes 2359304 | tf_op jit(solution)/shard_map/ppermute | solution.py:619
  775.6 52.2 %collective-permute-start.31 = (bf16[8,64,2048]{2,1,0:T(8,128)(2,1)}, bf16[8,64,2048]{2,1,0:T(8,128)(2,1)}, u32[]{:S(2)}, u32[]{:S(2)}) collective-permute-start(bf16[8,64,2048]{2,1,0:T(8,128)(2,1)} %dynamic-slice_bitcast_fusion.1), channel_id=1, source_target_pairs={{0,1},{1,0},{2,3},{3,2},{4,5},{5,4},{6,7},{7,6},{8,9},{9,8},{10,11... | collective-permute-start | bytes 6291464 | tf_op jit(solution)/shard_map/ppermute | solution.py:590
  788.0 80.9 %collective-permute-start.30 = (bf16[2,512,1024]{2,1,0:T(8,128)(2,1)}, bf16[2,512,1024]{2,1,0:T(8,128)(2,1)}, u32[]{:S(2)}, u32[]{:S(2)}) collective-permute-start(bf16[2,512,1024]{2,1,0:T(8,128)(2,1)} %fusion.34), channel_id=1, source_target_pairs={{0,1},{1,0},{2,3},{3,2},{4,5},{5,4},{6,7},{7,6},{8,9},{9,8},{10,11... | collective-permute-start | bytes 6291464 | tf_op jit(solution)/shard_map/ppermute | solution.py:567
  794.0 33.8 %collective-permute-start.27 = (bf16[192,2048]{1,0:T(8,128)(2,1)}, bf16[192,2048]{1,0:T(8,128)(2,1)}, u32[]{:S(2)}, u32[]{:S(2)}) collective-permute-start(bf16[192,2048]{1,0:T(8,128)(2,1)} %get-tuple-element.286), channel_id=1, source_target_pairs={{0,8},{8,16},{16,24},{24,0},{1,9},{9,17},{17,25},{25,1},{2,10},{10... | collective-permute-start | bytes 2359304 | tf_op jit(solution)/shard_map/ppermute | solution.py:619
  796.4 52.9 %collective-permute-start.28 = (bf16[192,2048]{1,0:T(8,128)(2,1)}, bf16[192,2048]{1,0:T(8,128)(2,1)}, u32[]{:S(2)}, u32[]{:S(2)}) collective-permute-start(bf16[192,2048]{1,0:T(8,128)(2,1)} %get-tuple-element.285), channel_id=1, source_target_pairs={{0,16},{8,24},{16,0},{24,8},{1,17},{9,25},{17,1},{25,9},{2,18},{10... | collective-permute-start | bytes 2359304 | tf_op jit(solution)/shard_map/ppermute | solution.py:619
  797.8 51.5 %collective-permute-start.29 = (bf16[192,2048]{1,0:T(8,128)(2,1)}, bf16[192,2048]{1,0:T(8,128)(2,1)}, u32[]{:S(2)}, u32[]{:S(2)}) collective-permute-start(bf16[192,2048]{1,0:T(8,128)(2,1)} %get-tuple-element.284), channel_id=1, source_target_pairs={{0,24},{8,0},{16,8},{24,16},{1,25},{9,1},{17,9},{25,17},{2,26},{10... | collective-permute-start | bytes 2359304 | tf_op jit(solution)/shard_map/ppermute | solution.py:619
  875.7 22.7 %collective-permute-start.34 = (bf16[192,2048]{1,0:T(8,128)(2,1)}, bf16[192,2048]{1,0:T(8,128)(2,1)}, u32[]{:S(2)}, u32[]{:S(2)}) collective-permute-start(bf16[192,2048]{1,0:T(8,128)(2,1)} %get-tuple-element.308), channel_id=1, source_target_pairs={{0,8},{8,16},{16,24},{24,0},{1,9},{9,17},{17,25},{25,1},{2,10},{10... | collective-permute-start | bytes 2359304 | tf_op jit(solution)/shard_map/ppermute | solution.py:646
  878.0 52.8 %collective-permute-start.35 = (bf16[192,2048]{1,0:T(8,128)(2,1)}, bf16[192,2048]{1,0:T(8,128)(2,1)}, u32[]{:S(2)}, u32[]{:S(2)}) collective-permute-start(bf16[192,2048]{1,0:T(8,128)(2,1)} %get-tuple-element.307), channel_id=1, source_target_pairs={{0,16},{8,24},{16,0},{24,8},{1,17},{9,25},{17,1},{25,9},{2,18},{10... | collective-permute-start | bytes 2359304 | tf_op jit(solution)/shard_map/ppermute | solution.py:646
  879.5 51.4 %collective-permute-start.36 = (bf16[192,2048]{1,0:T(8,128)(2,1)}, bf16[192,2048]{1,0:T(8,128)(2,1)}, u32[]{:S(2)}, u32[]{:S(2)}) collective-permute-start(bf16[192,2048]{1,0:T(8,128)(2,1)} %get-tuple-element.306), channel_id=1, source_target_pairs={{0,24},{8,0},{16,8},{24,16},{1,25},{9,1},{17,9},{25,17},{2,26},{10... | collective-permute-start | bytes 2359304 | tf_op jit(solution)/shard_map/ppermute | solution.py:646
  888.2 44.5 %collective-permute-start.32 = (bf16[512,2048]{1,0:T(8,128)(2,1)S(1)}, bf16[512,2048]{1,0:T(8,128)(2,1)}, u32[]{:S(2)}, u32[]{:S(2)}) collective-permute-start(bf16[512,2048]{1,0:T(8,128)(2,1)S(1)} %get-tuple-element.204), channel_id=1, source_target_pairs={{0,2},{2,0},{1,3},{3,1},{4,6},{6,4},{5,7},{7,5},{8,10},{10,8},{9,1... | collective-permute-start | bytes 6291464 | tf_op jit(solution)/shard_map/ppermute | solution.py:552
  892.7 49.4 %collective-permute-start.37 = (bf16[4,64,4096]{2,1,0:T(8,128)(2,1)}, bf16[4,64,4096]{2,1,0:T(8,128)(2,1)}, u32[]{:S(2)}, u32[]{:S(2)}) collective-permute-start(bf16[4,64,4096]{2,1,0:T(8,128)(2,1)} %pad_maximum_fusion.7), channel_id=1, source_target_pairs={{0,4},{4,0},{1,5},{5,1},{2,6},{6,2},{3,7},{7,3},{8,12},{12,8},{9,1... | collective-permute-start | bytes 6291464 | tf_op jit(solution)/shard_map/ppermute | solution.py:552
  955.3 49.8 %collective-permute-start.41 = (bf16[512,2048]{1,0:T(8,128)(2,1)}, bf16[512,2048]{1,0:T(8,128)(2,1)}, u32[]{:S(2)}, u32[]{:S(2)}) collective-permute-start(bf16[512,2048]{1,0:T(8,128)(2,1)} %slice.204), channel_id=1, source_target_pairs={{0,2},{2,0},{1,3},{3,1},{4,6},{6,4},{5,7},{7,5},{8,10},{10,8},{9,1... | collective-permute-start | bytes 6291464 | tf_op jit(solution)/shard_map/ppermute | solution.py:552
  967.0 23.2 %collective-permute-start.42 = (bf16[512,1024]{1,0:T(8,128)(2,1)}, bf16[512,1024]{1,0:T(8,128)(2,1)}, u32[]{:S(2)}, u32[]{:S(2)}) collective-permute-start(bf16[512,1024]{1,0:T(8,128)(2,1)} %slice.252), channel_id=1, source_target_pairs={{0,2},{2,0},{1,3},{3,1},{4,6},{6,4},{5,7},{7,5},{8,10},{10,8},{9,1... | collective-permute-start | bytes 3145736 | tf_op jit(solution)/shard_map/ppermute | solution.py:552
  967.0 49.9 %collective-permute-start.38 = (bf16[64,4096]{1,0:T(8,128)(2,1)}, bf16[64,4096]{1,0:T(8,128)(2,1)S(1)}, u32[]{:S(2)}, u32[]{:S(2)}) collective-permute-start(bf16[64,4096]{1,0:T(8,128)(2,1)} %get-tuple-element.319), channel_id=1, source_target_pairs={{0,8},{8,16},{16,24},{24,0},{1,9},{9,17},{17,25},{25,1},{2,10},{10... | collective-permute-start | bytes 1572872 | tf_op jit(solution)/shard_map/ppermute | solution.py:619
  984.4 35.8 %collective-permute-start.39 = (bf16[64,4096]{1,0:T(8,128)(2,1)}, bf16[64,4096]{1,0:T(8,128)(2,1)S(1)}, u32[]{:S(2)}, u32[]{:S(2)}) collective-permute-start(bf16[64,4096]{1,0:T(8,128)(2,1)} %get-tuple-element.318), channel_id=1, source_target_pairs={{0,16},{8,24},{16,0},{24,8},{1,17},{9,25},{17,1},{25,9},{2,18},{10... | collective-permute-start | bytes 1572872 | tf_op jit(solution)/shard_map/ppermute | solution.py:619
  985.4 34.8 %collective-permute-start.40 = (bf16[64,4096]{1,0:T(8,128)(2,1)}, bf16[64,4096]{1,0:T(8,128)(2,1)}, u32[]{:S(2)}, u32[]{:S(2)}) collective-permute-start(bf16[64,4096]{1,0:T(8,128)(2,1)} %get-tuple-element.317), channel_id=1, source_target_pairs={{0,24},{8,0},{16,8},{24,16},{1,25},{9,1},{17,9},{25,17},{2,26},{10... | collective-permute-start | bytes 1572872 | tf_op jit(solution)/shard_map/ppermute | solution.py:619
  986.8 254.3 %all-gather.14.cloned.1.call-start = ((), (), s32[]{:S(2)}) async-start(), calls=%async_computation.5 | async-start | bytes 9437184 | tf_op jit(solution)/shard_map/all_gather | solution.py:583
  990.2 75.8 %collective-permute-start.33 = (bf16[8,64,2048]{2,1,0:T(8,128)(2,1)}, bf16[8,64,2048]{2,1,0:T(8,128)(2,1)}, u32[]{:S(2)}, u32[]{:S(2)}) collective-permute-start(bf16[8,64,2048]{2,1,0:T(8,128)(2,1)} %dynamic-slice_bitcast_fusion), channel_id=1, source_target_pairs={{0,1},{1,0},{2,3},{3,2},{4,5},{5,4},{6,7},{7,6},{8,9},{9,8},{10,11... | collective-permute-start | bytes 6291464 | tf_op jit(solution)/shard_map/ppermute | solution.py:590
  1005.1 106.2 %collective-permute-start.49 = (bf16[1024,2048]{1,0:T(8,128)(2,1)}, bf16[1024,2048]{1,0:T(8,128)(2,1)S(1)}, u32[]{:S(2)}, u32[]{:S(2)}) collective-permute-start(bf16[1024,2048]{1,0:T(8,128)(2,1)} %back_to_width.6), channel_id=1, source_target_pairs={{0,2},{2,0},{1,3},{3,1},{4,6},{6,4},{5,7},{7,5},{8,10},{10,8},{9,1... | collective-permute-start | bytes 12582920 | tf_op jit(solution)/shard_map/ppermute | solution.py:552
  1016.9 55.1 %collective-permute-start.47 = (f32[4352]{0:T(1024)S(1)}, f32[4352]{0:T(1024)S(1)}, u32[]{:S(2)}, u32[]{:S(2)}) collective-permute-start(f32[4352]{0:T(1024)S(1)} %pad_maximum_fusion.14), channel_id=1, source_target_pairs={{0,2},{2,0},{1,3},{3,1},{4,6},{6,4},{5,7},{7,5},{8,10},{10,8},{9,1... | collective-permute-start | bytes 52232 | tf_op jit(solution)/shard_map/ppermute | solution.py:627
  1068.7 35.7 %collective-permute-start.43 = (bf16[4,64,2048]{2,1,0:T(8,128)(2,1)S(1)}, bf16[4,64,2048]{2,1,0:T(8,128)(2,1)S(1)}, u32[]{:S(2)}, u32[]{:S(2)}) collective-permute-start(bf16[4,64,2048]{2,1,0:T(8,128)(2,1)S(1)} %dynamic-slice_bitcast_fusion.3), channel_id=1, source_target_pairs={{0,4},{4,0},{1,5},{5,1},{2,6},{6,2},{3,7},{7,3},{8,12},{12,8},{9,1... | collective-permute-start | bytes 3145736 | tf_op jit(solution)/shard_map/ppermute | solution.py:552
  1105.6 13.7 collective-permute-start.44
  1107.6 18.9 %collective-permute-start.45 = (bf16[64,2048]{1,0:T(8,128)(2,1)}, bf16[64,2048]{1,0:T(8,128)(2,1)}, u32[]{:S(2)}, u32[]{:S(2)}) collective-permute-start(bf16[64,2048]{1,0:T(8,128)(2,1)} %get-tuple-element.301), channel_id=1, source_target_pairs={{0,16},{8,24},{16,0},{24,8},{1,17},{9,25},{17,1},{25,9},{2,18},{10... | collective-permute-start | bytes 786440 | tf_op jit(solution)/shard_map/ppermute | solution.py:619
  1109.9 16.5 %collective-permute-start.46 = (bf16[64,2048]{1,0:T(8,128)(2,1)}, bf16[64,2048]{1,0:T(8,128)(2,1)}, u32[]{:S(2)}, u32[]{:S(2)}) collective-permute-start(bf16[64,2048]{1,0:T(8,128)(2,1)} %get-tuple-element.300), channel_id=1, source_target_pairs={{0,24},{8,0},{16,8},{24,16},{1,25},{9,1},{17,9},{25,17},{2,26},{10... | collective-permute-start | bytes 786440 | tf_op jit(solution)/shard_map/ppermute | solution.py:619
  1129.1 15.4 %collective-permute-start.52 = (bf16[64,2048]{1,0:T(8,128)(2,1)S(1)}, bf16[64,2048]{1,0:T(8,128)(2,1)S(1)}, u32[]{:S(2)}, u32[]{:S(2)}) collective-permute-start(bf16[64,2048]{1,0:T(8,128)(2,1)S(1)} %get-tuple-element.327), channel_id=1, source_target_pairs={{0,24},{8,0},{16,8},{24,16},{1,25},{9,1},{17,9},{25,17},{2,26},{10... | collective-permute-start | bytes 786440 | tf_op jit(solution)/shard_map/ppermute | solution.py:646
  1135.4 12.9 collective-permute-start.50
  1135.4 23.0 %collective-permute-start.51 = (bf16[64,2048]{1,0:T(8,128)(2,1)S(1)}, bf16[64,2048]{1,0:T(8,128)(2,1)S(1)}, u32[]{:S(2)}, u32[]{:S(2)}) collective-permute-start(bf16[64,2048]{1,0:T(8,128)(2,1)S(1)} %get-tuple-element.328), channel_id=1, source_target_pairs={{0,16},{8,24},{16,0},{24,8},{1,17},{9,25},{17,1},{25,9},{2,18},{10... | collective-permute-start | bytes 786440 | tf_op jit(solution)/shard_map/ppermute | solution.py:646
  1164.6 76.4 %collective-permute-start.54 = (f32[4352]{0:T(1024)S(1)}, f32[4352]{0:T(1024)S(1)}, u32[]{:S(2)}, u32[]{:S(2)}) collective-permute-start(f32[4352]{0:T(1024)S(1)} %add.688), channel_id=1, source_target_pairs={{0,8},{8,16},{16,24},{24,0},{1,9},{9,17},{17,25},{25,1},{2,10},{10... | collective-permute-start | bytes 52232 | tf_op jit(solution)/shard_map/ppermute | solution.py:561
  1164.6 76.4 %collective-permute-start.55 = (f32[4352]{0:T(1024)S(1)}, f32[4352]{0:T(1024)S(1)}, u32[]{:S(2)}, u32[]{:S(2)}) collective-permute-start(f32[4352]{0:T(1024)S(1)} %add.688), channel_id=1, source_target_pairs={{0,16},{8,24},{16,0},{24,8},{1,17},{9,25},{17,1},{25,9},{2,18},{10... | collective-permute-start | bytes 52232 | tf_op jit(solution)/shard_map/ppermute | solution.py:561
  1166.5 74.6 %collective-permute-start.56 = (f32[4352]{0:T(1024)S(1)}, f32[4352]{0:T(1024)S(1)}, u32[]{:S(2)}, u32[]{:S(2)}) collective-permute-start(f32[4352]{0:T(1024)S(1)} %add.688), channel_id=1, source_target_pairs={{0,24},{8,0},{16,8},{24,16},{1,25},{9,1},{17,9},{25,17},{2,26},{10... | collective-permute-start | bytes 52232 | tf_op jit(solution)/shard_map/ppermute | solution.py:561
  1269.8 73.7 %collective-permute-start.60 = (bf16[512,2048]{1,0:T(8,128)(2,1)}, bf16[512,2048]{1,0:T(8,128)(2,1)}, u32[]{:S(2)}, u32[]{:S(2)}) collective-permute-start(bf16[512,2048]{1,0:T(8,128)(2,1)} %fusion.33), channel_id=1, source_target_pairs={{0,1},{1,0},{2,3},{3,2},{4,5},{5,4},{6,7},{7,6},{8,9},{9,8},{10,11... | collective-permute-start | bytes 6291464 | tf_op jit(solution)/shard_map/ppermute | solution.py:567
  1273.3 44.2 %collective-permute-start.57 = (bf16[192,2048]{1,0:T(8,128)(2,1)}, bf16[192,2048]{1,0:T(8,128)(2,1)S(1)}, u32[]{:S(2)}, u32[]{:S(2)}) collective-permute-start(bf16[192,2048]{1,0:T(8,128)(2,1)} %get-tuple-element.299), channel_id=1, source_target_pairs={{0,24},{8,0},{16,8},{24,16},{1,25},{9,1},{17,9},{25,17},{2,26},{10... | collective-permute-start | bytes 2359304 | tf_op jit(solution)/shard_map/ppermute | solution.py:655
  1273.9 67.5 %collective-permute-start.58 = (bf16[192,2048]{1,0:T(8,128)(2,1)}, bf16[192,2048]{1,0:T(8,128)(2,1)}, u32[]{:S(2)}, u32[]{:S(2)}) collective-permute-start(bf16[192,2048]{1,0:T(8,128)(2,1)} %get-tuple-element.298), channel_id=1, source_target_pairs={{0,16},{8,24},{16,0},{24,8},{1,17},{9,25},{17,1},{25,9},{2,18},{10... | collective-permute-start | bytes 2359304 | tf_op jit(solution)/shard_map/ppermute | solution.py:655
  1275.3 66.1 %collective-permute-start.59 = (bf16[192,2048]{1,0:T(8,128)(2,1)}, bf16[192,2048]{1,0:T(8,128)(2,1)}, u32[]{:S(2)}, u32[]{:S(2)}) collective-permute-start(bf16[192,2048]{1,0:T(8,128)(2,1)} %get-tuple-element.297), channel_id=1, source_target_pairs={{0,8},{8,16},{16,24},{24,0},{1,9},{9,17},{17,25},{25,1},{2,10},{10... | collective-permute-start | bytes 2359304 | tf_op jit(solution)/shard_map/ppermute | solution.py:655
  1343.6 12.8 collective-permute-start.61
  1343.7 25.3 %collective-permute-start.62 = (bf16[64,2048]{1,0:T(8,128)(2,1)S(1)}, bf16[64,2048]{1,0:T(8,128)(2,1)S(1)}, u32[]{:S(2)}, u32[]{:S(2)}) collective-permute-start(bf16[64,2048]{1,0:T(8,128)(2,1)S(1)} %get-tuple-element.324), channel_id=1, source_target_pairs={{0,16},{8,24},{16,0},{24,8},{1,17},{9,25},{17,1},{25,9},{2,18},{10... | collective-permute-start | bytes 786440 | tf_op jit(solution)/shard_map/ppermute | solution.py:655
  1345.7 23.3 %collective-permute-start.63 = (bf16[64,2048]{1,0:T(8,128)(2,1)S(1)}, bf16[64,2048]{1,0:T(8,128)(2,1)S(1)}, u32[]{:S(2)}, u32[]{:S(2)}) collective-permute-start(bf16[64,2048]{1,0:T(8,128)(2,1)S(1)} %get-tuple-element.323), channel_id=1, source_target_pairs={{0,8},{8,16},{16,24},{24,0},{1,9},{9,17},{17,25},{25,1},{2,10},{10... | collective-permute-start | bytes 786440 | tf_op jit(solution)/shard_map/ppermute | solution.py:655
  (131 other events, 1596.0 us)
Sparse Core Ops, SparseCore 0:
  12.6 154.7 all-gather.5
  169.5 61.6 all-gather.7
  246.7 62.0 all-gather.9
  321.3 62.0 all-gather.11
  986.9 132.3 all-reduce.2
  1159.7 52.1 all-gather.13

commit v4 on v3

--- a/solution.py
+++ b/solution.py
@@ -199,14 +199,27 @@
 
 
 def muon_kernel(
-    halves_ref, update_ref, packed_ref, row_ref, col_ref, out_ref,
+    halves_ref, update_ref, packed_ref, out_ref,
     start_ref, gram_ref, bend_ref, first_ref, product_ref, one_ref, two_ref,
 ):
     width = update_ref.shape[1]
     tile = GRAM_TILE
     count = width // tile
-    start_ref[...] = (update_ref[...].astype(F32) * row_ref[...]).astype(BF16)
     one_matrix = (1 - halves_ref[0]).astype(F32)
+    index = lax.broadcasted_iota(jnp.int32, (tile, tile), 0)
+    on_diagonal = index == lax.broadcasted_iota(jnp.int32, (tile, tile), 1)
+    traces = [0.0, 0.0]
+    for place, (i, j) in enumerate(gram_pairs(width)):
+        if i == j:
+            block = jnp.where(on_diagonal, packed_ref[place].astype(F32), 0.0)
+            block = jnp.sum(jnp.sum(block, axis=0, keepdims=True), axis=1, keepdims=True)
+            traces[2 * i // count] = traces[2 * i // count] + block
+    inverse = [
+        1.0 / (jnp.sqrt(traces[half] + one_matrix * traces[1 - half]) + NS_EPS) for half in range(2)
+    ]
+    middle = width // 2
+    start_ref[:, :middle] = (update_ref[:, :middle].astype(F32) * inverse[0]).astype(BF16)
+    start_ref[:, middle:] = (update_ref[:, middle:].astype(F32) * inverse[1]).astype(BF16)
 
     def put(ref, i, j, value):
         ref[i * tile : (i + 1) * tile, j * tile : (j + 1) * tile] = value
@@ -214,8 +227,7 @@
             ref[j * tile : (j + 1) * tile, i * tile : (i + 1) * tile] = value.T
 
     for place, (i, j) in enumerate(gram_pairs(width)):
-        block = packed_ref[place].astype(F32) * col_ref[i * tile : (i + 1) * tile, :]
-        block = block * row_ref[:, j * tile : (j + 1) * tile]
+        block = packed_ref[place].astype(F32) * inverse[2 * i // count] * inverse[2 * j // count]
         if 2 * i < count <= 2 * j:
             block = block * one_matrix
         put(gram_ref, i, j, block.astype(BF16))
@@ -497,21 +509,7 @@
 
 
 def muon(update, packed, halves):
-    rows, width = update.shape
-    index = jnp.arange(GRAM_TILE)
-    pairs = gram_pairs(width)
-    squares = jnp.stack(
-        [
-            jnp.sum(jnp.where(index[:, None] == index[None, :], packed[at].astype(F32), 0.0))
-            for at, (i, j) in enumerate(pairs)
-            if i == j
-        ]
-    )
-    count = squares.shape[0]
-    low_half, high_half = jnp.sum(squares[: count // 2]), jnp.sum(squares[count // 2 :])
-    both = low_half + high_half
-    squares = jnp.stack([jnp.where(halves, low_half, both), jnp.where(halves, high_half, both)])
-    inverse = jnp.repeat(1.0 / (jnp.sqrt(squares) + NS_EPS), width // 2)
+    width = update.shape[1]
     once = dict(pipeline_mode=pl.Buffered(1))
     return pl.pallas_call(
         muon_kernel,
@@ -520,8 +518,6 @@
             pl.BlockSpec(memory_space=pltpu.SMEM),
             pl.BlockSpec(update.shape, lambda: (0, 0), **once),
             pl.BlockSpec(packed.shape, lambda: (0, 0, 0), **once),
-            pl.BlockSpec((1, width), lambda: (0, 0)),
-            pl.BlockSpec((width, 1), lambda: (0, 0)),
         ],
         out_specs=pl.BlockSpec(update.shape, lambda: (0, 0)),
         out_shape=shaped(update.shape, BF16),
@@ -531,13 +527,7 @@
         compiler_params=limits(58),
         cost_estimate=SMALL,
         name="muon",
-    )(
-        jnp.asarray(halves, jnp.int32).reshape(1),
-        update,
-        packed,
-        inverse[None],
-        inverse[:, None],
-    )
+    )(jnp.asarray(halves, jnp.int32).reshape(1), update, packed)
 
 
 def after(value, *earlier):
@@ -886,21 +876,27 @@
     key_value_own, key_value_arrived = scatter_blocks(key_value_blocks, "fsdp")
     plane = lax.axis_index("z")
     in_plane = ("y", "core", "fsdp")
-    big_mine, first_passed, key_value_grad = lax.optimization_barrier(
-        (big_mine, first_passed, key_value_grad)
+    big_mine, key_value_arrived, first_passed = lax.optimization_barrier(
+        (big_mine, key_value_arrived, first_passed)
     )
     big_gram = gram_blocks(big_mine)
-    from_query, down_far = after((from_query, down_far), big_gram)
+    from_query, down_far, first_passed, key_value_arrived = after(
+        (from_query, down_far, first_passed, key_value_arrived), big_gram
+    )
     down_half = (down_near.astype(F32) + swap(down_far).astype(F32)).reshape(
         ring, rows, MODEL_WIDTH
     )
-    first_own, first_chunks, first_chunks_sent = chunks_over_z(
-        first_kept, after(first_passed, big_gram)
-    )
+    kept, arrived, attention_passed = halves_over_y(
+        [add_all(key_value_own.astype(F32), key_value_arrived).astype(BF16)]
+    )
+    first_own, first_chunks, first_chunks_sent = chunks_over_z(first_kept, first_passed)
     from_kv = times_rows(
-        after(both_kv_low, key_value_grad, first_chunks_sent), attention_rows, 0
+        after(both_kv_low, attention_passed, first_chunks_sent), attention_rows, 0
     )
     big_gram = lax.psum(big_gram, in_plane)
+    arrived, first_chunks = after((arrived, first_chunks), from_kv)
+    last_own, last_chunks, last_chunks_sent = chunks_over_z(kept, arrived)
+    from_kv = after(from_kv, last_chunks_sent)
 
     from_query = from_query[:rows].astype(F32) + swap(from_query[rows:]).astype(F32)
     kv_here = from_kv[:rows].reshape(rows, -1, HEAD_SIZE)
@@ -914,23 +910,26 @@
     input_grad = (d_middle + d_residual).reshape(inputs.shape)
     gain_grad = jnp.concatenate([d_gain_attn, d_gain_mlp, d_gain_query, d_gain_key])
 
-    key_value_arrived, first_chunks = after((key_value_arrived, first_chunks), input_grad)
-    kept, arrived, _ = halves_over_y(
-        [add_all(key_value_own.astype(F32), key_value_arrived).astype(BF16)]
-    )
-    last_own, last_chunks, _ = chunks_over_z(kept, arrived)
-    last_chunks, big_gram, gain_grad, down_half = lax.optimization_barrier(
-        (last_chunks, big_gram, butterfly(butterfly(gain_grad, "core"), "fsdp"), down_half)
-    )
     first_total = add_all(first_own, first_chunks)
-    output_shard = first_total[:, :MODEL_WIDTH]
-    query_shard = first_total[:, MODEL_WIDTH:]
+    output_new = updated(first_total[:, :MODEL_WIDTH], 3)
+    query_new = updated(first_total[:, MODEL_WIDTH:], 0)
+    last_chunks, big_gram, gain_grad, down_half, output_new, query_new = after(
+        (
+            last_chunks,
+            big_gram,
+            butterfly(butterfly(gain_grad, "core"), "fsdp"),
+            down_half,
+            output_new,
+            query_new,
+        ),
+        input_grad,
+    )
     key_value_shard = add_all(last_own, last_chunks)
     small = [
-        updated(query_shard, 0),
+        query_new,
         updated(key_value_shard[:, :KV_WIDTH], 1),
         updated(key_value_shard[:, KV_WIDTH:], 2),
-        updated(output_shard, 3),
+        output_new,
     ]
     small_slots = jnp.stack(
         [
@@ -951,7 +950,7 @@
     returned = from_planes(turned.reshape(PLANES, -1, MODEL_WIDTH))
     small_gram = gram_blocks(whole)
     down_arrived = ring_send(
-        [after(down_half, small_gram)[step] for step in range(ring)], "fsdp", ring
+        [after(down_half, turned)[step] for step in range(ring)], "fsdp", ring
     )
     turned, returned, down_arrived = lax.optimization_barrier(
         (muon(small_mine, small_gram, plane == 1), returned, down_arrived)

time: 1390 us -> 1330 us (0.957)
  waiting for transfers between devices: 539 us -> 483 us
    ppermute x3, waiting for transfers between devices: 45.8 us -> 0.11 us  [scatter_blocks(): lax.ppermute(pick(blocks, (here + step) % count), axis_name, shifted(step...]
    ppermute x22, waiting for transfers between devices: 89.3 us -> 60.9 us  [swap(): return lax.ppermute(value, axis_name, shifted(1, CORES))]
    ppermute x6, waiting for transfers between devices: 36.4 us -> 17.3 us  [from_planes(): back.append(lax.ppermute(arrived[step], 'z', shifted(-step, PLANES)))]
    ppermute x15, waiting for transfers between devices: 69.6 us -> 84.9 us  [chunks_over_z(): lax.ppermute(value, 'z', shifted(step + 1, PLANES))]
    unnamed x267 -> x271, local copies, waits for them, and re-layouts: 55.9 us -> 57 us
  transfers between devices with their start and end apart: 70 -> 70, of which waited for: 32 -> 31; matrix products, arithmetic and copies ran while one was open for 16% -> 16% of each run, Pallas kernels for 26% -> 28%
where the time goes in v4:
time: 1330 us; the launch traced here: 1320 us
  waiting for transfers between devices  483 us (36%)
  Pallas kernels  418 us (31%)
  other arithmetic  148 us (11%)
  local copies, waits for them, and re-layouts  119 us (9%)
  starting transfers between devices  99.7 us (7%)
  matrix products  33 us (2%)
  between operations  16.3 us (1%)
    all_gather x5, waiting for transfers between devices, gather_rows(): return lax.all_gather(shard, axes, axis=0, tiled=True)  195 us
    pallas_call x2, Pallas kernels, muon(): pl.pallas_call(muon_kernel, grid=(), in_specs=[pl.BlockSpec(memory_space=...  108 us
    ppermute x15, waiting for transfers between devices, chunks_over_z(): lax.ppermute(value, 'z', shifted(step + 1, PLANES))  84.9 us
    pallas_call x8, Pallas kernels, weight_grad(): pl.pallas_call(weight_grad_kernel, grid=(width // tile,), in_specs=[pl.Bl...  68.2 us
    ppermute x6, waiting for transfers between devices, to_planes(): lax.ppermute(pick(chunks, (here + step) % PLANES), 'z', shifted(step, PLA...  67.6 us
    pallas_call x4, Pallas kernels, back_to_width(): pl.pallas_call(functools.partial(back_to_width_kernel, len(lefts)), grid=...  63.2 us
    ppermute x22, waiting for transfers between devices, swap(): return lax.ppermute(value, axis_name, shifted(1, CORES))  60.9 us
    pallas_call x2, Pallas kernels, swiglu_both_ways(): pl.pallas_call(swiglu_kernel, grid=(tokens // tile,), in_specs=[row_block...  60 us
  transfers between devices with their start and end apart: 70, of which 31 were waited for; matrix products, arithmetic and copies ran while one was open for 16% of the time, Pallas kernels for 28%

profile of v4, /device:TPU:0, one launch (start us, length us, event | category | flops | bytes accessed | tf_op | source)
XLA Modules:
  0.0 1316.9 jit_solution(14802994158876661396)
XLA Ops:
  24.3 7.7 reshape.415
  32.0 8.5 constant_dynamic-slice_fusion.13
  40.4 9.0 copy.57
  50.8 116.6 %all-gather.6.cloned.1.call-done.right_ref = bf16[1024,6144]{1,0:T(8,128)(2,1)} async-done(((bf16[64,6144]{1,0:T(8,128)(2,1)}), bf16[1024,6144]{1,0:T(8,128)(2,1)}) %all-gather.6.cloned.1.call-update) | async-done | bytes 12582928 | tf_op jit(solution)/shard_map/all_gather | solution.py:573
  167.4 5.9 fusion.26
  194.1 9.4 fusion.11.q_ref
  203.6 27.7 %all-gather.8.cloned.1.call-done.gate_ref.refs_4_ = bf16[768,2048]{1,0:T(8,128)(2,1)} async-done(((bf16[192,2048]{1,0:T(8,128)(2,1)}), bf16[768,2048]{1,0:T(8,128)(2,1)}) %all-gather.8.cloned.1.call-update) | async-done | bytes 3145744 | tf_op jit(solution)/shard_map/all_gather | solution.py:573
  231.3 9.6 collective-permute-done.3
  253.5 8.5 pad_maximum_fusion
  262.0 19.7 %attention.1 = (bf16[1024,1024]{1,0:T(8,128)(2,1)S(1)}, bf16[1024,1024]{1,0:T(8,128)(2,1)S(1)}) custom-call(f32[1024,1024]{1,0:T(8,128)S(1)} %copy-done.2, bf16[2,1024,2048]{2,1,0:T(8,128)(2,1)} %bitcast.302, bf16[2,1024,2048]{2,1,0:T(8,128)(2,1)} %bitcast.303, bf16[2,1024,512]{2,1,0:T(8,128)(2,1)S(1)} %and_convert_fusion.mask_ref, ...), custom_call_target="tpu_custom_call" | custom-call | flops 1 | bytes 1 | tf_op jit(solution)/shard_map/attention/pallas_call | solution.py:337
  281.7 13.3 %collective-permute-done.5 = bf16[512,2048]{1,0:T(8,128)(2,1)} collective-permute-done((bf16[512,2048]{1,0:T(8,128)(2,1)}, bf16[512,2048]{1,0:T(8,128)(2,1)}, u32[]{:S(2)}, u32[]{:S(2)}) %collective-permute-start.5) | collective-permute-done | bytes 2097184 | tf_op jit(solution)/shard_map/ppermute | solution.py:551
  303.1 5.7 all-gather.10.cloned.1.call-done.up_ref.refs_5_
  308.8 9.9 collective-permute-done.6.gate_ref.refs_6_
  338.7 44.6 %all-gather.12.cloned.1.call-done.down_ref.refs_2_ = bf16[768,2048]{1,0:T(8,128)(2,1)} async-done(((bf16[192,2048]{1,0:T(8,128)(2,1)}), bf16[768,2048]{1,0:T(8,128)(2,1)}) %all-gather.12.cloned.1.call-update) | async-done | bytes 3145744 | tf_op jit(solution)/shard_map/all_gather | solution.py:573
  383.3 11.8 collective-permute-done.9.up_ref.refs_7_
  406.7 30.0 %swiglu_both_ways.2 = (bf16[2048,768]{1,0:T(8,128)(2,1)}, bf16[2048,768]{1,0:T(8,128)(2,1)}, bf16[2048,768]{1,0:T(8,128)(2,1)}, bf16[768,2048]{1,0:T(8,128)(2,1)...) custom-call(bf16[2048,2048]{1,0:T(8,128)(2,1)} %constant_dynamic-update-slice_fusion.5.two_ref.right_ref, ...), custom_call_target="tpu_custom_call" | custom-call | flops 1 | bytes 1 | tf_op jit(solution)/shard_map/swiglu_both_ways/pallas_call | solution.py:390
  438.6 9.1 weight_grad.8
  449.5 9.1 weight_grad.9
  458.7 10.1 weight_grad.10
  468.8 30.0 %swiglu_both_ways.3 = (bf16[2048,768]{1,0:T(8,128)(2,1)}, bf16[2048,768]{1,0:T(8,128)(2,1)}, bf16[2048,768]{1,0:T(8,128)(2,1)}, bf16[768,2048]{1,0:T(8,128)(2,1)...) custom-call(bf16[2048,2048]{1,0:T(8,128)(2,1)} %constant_dynamic-update-slice_fusion.5.two_ref.right_ref, ...), custom_call_target="tpu_custom_call" | custom-call | flops 1 | bytes 1 | tf_op jit(solution)/shard_map/swiglu_both_ways/pallas_call | solution.py:390
  500.7 9.8 weight_grad.11
  513.0 9.0 weight_grad.12
  523.7 20.0 %back_to_width.4 = bf16[1024,2048]{1,0:T(8,128)(2,1)} custom-call(bf16[2048,768]{1,0:T(8,128)(2,1)} %get-tuple-element.179.refs_0_, bf16[2048,768]{1,0:T(8,128)(2,1)} %get-tuple-element.180.refs_1_, bf16[2048,768]{1,0:T(8,128)(2,1)} %get-tuple-element.181.refs_2_, bf16[2048,768]{1,0:T(8,128)(2,1)} %get-tuple-element.182.refs_3_, ...), custom_call_target="tpu_custom_call" | custom-call | flops 1 | bytes 1 | tf_op jit(solution)/shard_map/back_to_width/pallas_call | solution.py:407
  543.7 20.5 %back_to_width.5 = bf16[1024,2048]{1,0:T(8,128)(2,1)} custom-call(bf16[2048,768]{1,0:T(8,128)(2,1)} %get-tuple-element.179.refs_0_, bf16[2048,768]{1,0:T(8,128)(2,1)} %get-tuple-element.180.refs_1_, bf16[2048,768]{1,0:T(8,128)(2,1)} %get-tuple-element.181.refs_2_, bf16[2048,768]{1,0:T(8,128)(2,1)} %get-tuple-element.182.refs_3_, ...), custom_call_target="tpu_custom_call" | custom-call | flops 1 | bytes 1 | tf_op jit(solution)/shard_map/back_to_width/pallas_call | solution.py:407
  564.2 16.8 %collective-permute-done.13 = bf16[4,192,2048]{2,1,0:T(8,128)(2,1)} collective-permute-done((bf16[4,192,2048]{2,1,0:T(8,128)(2,1)}, bf16[4,192,2048]{2,1,0:T(8,128)(2,1)}, u32[]{:S(2)}, u32[]{:S(2)}) %collective-permute-start.13) | collective-permute-done | bytes 3145760 | tf_op jit(solution)/shard_map/ppermute | solution.py:542
  584.7 7.3 collective-permute-done.14
  592.0 5.5 convert_add_fusion.3
  605.7 9.8 weight_grad.13
  618.4 5.4 collective-permute-done.16
  623.8 32.4 %collective-permute-done.17 = bf16[192,2048]{1,0:T(8,128)(2,1)S(1)} collective-permute-done((bf16[192,2048]{1,0:T(8,128)(2,1)}, bf16[192,2048]{1,0:T(8,128)(2,1)S(1)}, u32[]{:S(2)}, u32[]{:S(2)}) %collective-permute-start.17) | collective-permute-done | bytes 786464 | tf_op jit(solution)/shard_map/ppermute | solution.py:609
  664.3 5.4 collective-permute-done.19
  680.2 5.6 weight_grad.14
  688.3 12.0 collective-permute-start.22
  702.7 6.8 times_rows.2.grad_ref
  710.8 21.8 %attention_back.2 = (bf16[1024,1024]{1,0:T(8,128)(2,1)S(1)}, bf16[1024,1024]{1,0:T(8,128)(2,1)S(1)}, bf16[2,1024,1024]{2,1,0:T(8,128)(2,1)}, f32[1,128]{1,0:T(1,128)S(1)}) custom-call(f32[1024,1024]{1,0:T(8,128)} %fusion.11.q_ref, bf16[2,1024,2048]{2,1,0:T(8,128)(2,1)} %bitcast.304, bf16[2,1024,2048]{2,1,0:T(8,128)(2,1)} %bitcast.305, ...), custom_call_target="tpu_custom_call" | custom-call | flops 1 | bytes 1 | tf_op jit(solution)/shard_map/attention_back/pallas_call | solution.py:361
  732.6 22.1 %attention_back.3 = (bf16[1024,1024]{1,0:T(8,128)(2,1)S(1)}, bf16[1024,1024]{1,0:T(8,128)(2,1)S(1)}, bf16[2,1024,1024]{2,1,0:T(8,128)(2,1)}, f32[1,128]{1,0:T(1,128)S(1)}) custom-call(f32[1024,1024]{1,0:T(8,128)} %fusion.11.q_ref, bf16[2,1024,2048]{2,1,0:T(8,128)(2,1)} %bitcast.306, ...), custom_call_target="tpu_custom_call", output_to_operand_aliasing={{0}: (8, {}), {1}: (9, {})} | custom-call | flops 1 | bytes 1 | tf_op jit(solution)/shard_map/attention_back/pallas_call | solution.py:361
  754.7 5.6 weight_grad.15
  760.3 7.4 times_columns.1
  767.8 5.8 fusion.59
  776.4 5.0 collective-permute-done.26
  788.9 5.3 fusion.62
  801.6 11.4 back_to_width.6
  813.0 11.4 back_to_width.7
  824.5 24.8 %collective-permute-done.28 = bf16[192,2048]{1,0:T(8,128)(2,1)S(1)} collective-permute-done((bf16[192,2048]{1,0:T(8,128)(2,1)}, bf16[192,2048]{1,0:T(8,128)(2,1)S(1)}, u32[]{:S(2)}, u32[]{:S(2)}) %collective-permute-start.28) | collective-permute-done | bytes 786464 | tf_op jit(solution)/shard_map/ppermute | solution.py:609
  849.3 19.7 %collective-permute-done.30 = bf16[2,512,1024]{2,1,0:T(8,128)(2,1)} collective-permute-done((bf16[2,512,1024]{2,1,0:T(8,128)(2,1)}, bf16[2,512,1024]{2,1,0:T(8,128)(2,1)}, u32[]{:S(2)}, u32[]{:S(2)}) %collective-permute-start.30) | collective-permute-done | bytes 2097184 | tf_op jit(solution)/shard_map/ppermute | solution.py:557
  910.4 16.7 %collective-permute-done.33 = bf16[192,2048]{1,0:T(8,128)(2,1)S(1)} collective-permute-done((bf16[192,2048]{1,0:T(8,128)(2,1)}, bf16[192,2048]{1,0:T(8,128)(2,1)S(1)}, u32[]{:S(2)}, u32[]{:S(2)}) %collective-permute-start.33) | collective-permute-done | bytes 786464 | tf_op jit(solution)/shard_map/ppermute | solution.py:636
  927.1 33.3 %collective-permute-done.34 = bf16[192,2048]{1,0:T(8,128)(2,1)} collective-permute-done((bf16[192,2048]{1,0:T(8,128)(2,1)}, bf16[192,2048]{1,0:T(8,128)(2,1)}, u32[]{:S(2)}, u32[]{:S(2)}) %collective-permute-start.34) | collective-permute-done | bytes 786464 | tf_op jit(solution)/shard_map/ppermute | solution.py:636
  962.6 7.5 gram_blocks.2
  980.7 17.3 %collective-permute-start.39 = (bf16[64,4096]{1,0:T(8,128)(2,1)}, bf16[64,4096]{1,0:T(8,128)(2,1)}, u32[]{:S(2)}, u32[]{:S(2)}) collective-permute-start(bf16[64,4096]{1,0:T(8,128)(2,1)} %get-tuple-element.323), channel_id=1, source_target_pairs={{0,8},{8,16},{16,24},{24,0},{1,9},{9,17},{17,25},{25,1},{2,10},{10... | collective-permute-start | bytes 1572872 | tf_op jit(solution)/shard_map/ppermute | solution.py:609
  1003.8 6.9 times_rows.3
  1011.7 21.3 %collective-permute-done.40 = bf16[64,4096]{1,0:T(8,128)(2,1)} collective-permute-done((bf16[64,4096]{1,0:T(8,128)(2,1)}, bf16[64,4096]{1,0:T(8,128)(2,1)}, u32[]{:S(2)}, u32[]{:S(2)}) %collective-permute-start.40) | collective-permute-done | bytes 524320 | tf_op jit(solution)/shard_map/ppermute | solution.py:609
  1035.1 11.7 collective-permute-start.42
  1054.6 5.2 copy.56
  1059.8 6.7 reshape.455
  1066.5 5.6 fusion.9
  1074.5 6.5 fusion.6
  1081.1 7.4 convert_add_fusion.1
  1088.5 11.7 all-reduce.3.cloned.1.call-done.packed_ref
  1112.9 6.7 collective-permute-done.50
  1119.6 9.0 collective-permute-done.51
  1133.7 71.1 %muon.2 = bf16[768,2048]{1,0:T(8,128)(2,1)} custom-call(s32[1]{0:T(128)} %constant.615.clone.1.halves_ref, bf16[768,2048]{1,0:T(8,128)(2,1)} %bitcast.288, bf16[10,512,512]{2,1,0:T(8,128)(2,1)} %all-reduce.3.cloned.1.call-done.packed_ref), custom_call_target="tpu_custom_call" | custom-call | flops 1 | bytes 1 | tf_op jit(solution)/shard_map/muon/pallas_call | solution.py:514
  1219.2 15.8 %gram_blocks.3.packed_ref = bf16[10,512,512]{2,1,0:T(8,128)(2,1)S(1)} custom-call(s32[10]{0:T(128)S(1)} %copy-done.43, s32[10]{0:T(128)S(1)} %copy-done.44, bf16[2048,2048]{1,0:T(8,128)(2,1)S(1)} %copy-done.3, bf16[2048,2048]{1,0:T(8,128)(2,1)S(1)} %copy-done.3), custom_call_target="tpu_custom_call" | custom-call | flops 1 | bytes 1 | tf_op jit(solution)/shard_map/gram_blocks/pallas_call | solution.py:493
  1237.2 37.2 %muon.3 = bf16[256,2048]{1,0:T(8,128)(2,1)} custom-call(s32[1]{0:T(128)} %bitcast.89.halves_ref, bf16[256,2048]{1,0:T(8,128)(2,1)} %bitcast.320, bf16[10,512,512]{2,1,0:T(8,128)(2,1)} %copy-done.8), custom_call_target="tpu_custom_call" | custom-call | flops 1 | bytes 1 | tf_op jit(solution)/shard_map/muon/pallas_call | solution.py:514
  1294.5 12.5 collective-permute-done.62
  (513 shorter events, 288.0 us)
Async XLA Ops:
  7.2 160.2 %all-gather.6.cloned.1.call-start = ((), (), s32[]{:S(2)}) async-start(), calls=%async_computation | async-start | bytes 13369344 | tf_op jit(solution)/shard_map/all_gather | solution.py:573
  12.5 218.8 %all-gather.8.cloned.1.call-start = ((), (), s32[]{:S(2)}) async-start(), calls=%async_computation.1 | async-start | bytes 3932160 | tf_op jit(solution)/shard_map/all_gather | solution.py:573
  15.4 157.9 %collective-permute-start.2 = (s32[1,1024]{1,0:T(1,128)S(1)}, s32[1,1024]{1,0:T(1,128)S(1)}, u32[]{:S(2)}, u32[]{:S(2)}) collective-permute-start(s32[1,1024]{1,0:T(1,128)S(1)} %copy-done.123), channel_id=1, source_target_pairs={{0,2},{2,0},{1,3},{3,1},{4,6},{6,4},{5,7},{7,5},{8,10},{10,8},{9,1... | collective-permute-start | bytes 12296 | tf_op jit(solution)/shard_map/ppermute | solution.py:542
  16.5 292.3 %all-gather.10.cloned.1.call-start = ((), (), s32[]{:S(2)}) async-start(), calls=%async_computation.2 | async-start | bytes 3932160 | tf_op jit(solution)/shard_map/all_gather | solution.py:573
  173.3 9.6 collective-permute-start.1
  192.7 48.2 %collective-permute-start.3 = (bf16[512,2048]{1,0:T(8,128)(2,1)S(1)}, bf16[512,2048]{1,0:T(8,128)(2,1)}, u32[]{:S(2)}, u32[]{:S(2)}) collective-permute-start(bf16[512,2048]{1,0:T(8,128)(2,1)S(1)} %get-tuple-element.146), channel_id=1, source_target_pairs={{0,1},{1,0},{2,3},{3,2},{4,5},{5,4},{6,7},{7,6},{8,9},{9,8},{10,11... | collective-permute-start | bytes 6291464 | tf_op jit(solution)/shard_map/ppermute | solution.py:551
  245.6 7.9 collective-permute-start.4
  246.6 136.7 %all-gather.12.cloned.1.call-start = ((), (), s32[]{:S(2)}) async-start(), calls=%async_computation.3 | async-start | bytes 3932160 | tf_op jit(solution)/shard_map/all_gather | solution.py:573
  246.6 48.4 %collective-permute-start.5 = (bf16[512,2048]{1,0:T(8,128)(2,1)}, bf16[512,2048]{1,0:T(8,128)(2,1)}, u32[]{:S(2)}, u32[]{:S(2)}) collective-permute-start(bf16[512,2048]{1,0:T(8,128)(2,1)} %bitcast.316), channel_id=1, source_target_pairs={{0,1},{1,0},{2,3},{3,2},{4,5},{5,4},{6,7},{7,6},{8,9},{9,8},{10,11... | collective-permute-start | bytes 6291464 | tf_op jit(solution)/shard_map/ppermute | solution.py:551
  248.1 70.5 %collective-permute-start.6 = (bf16[768,2048]{1,0:T(8,128)(2,1)}, bf16[768,2048]{1,0:T(8,128)(2,1)}, u32[]{:S(2)}, u32[]{:S(2)}) collective-permute-start(bf16[768,2048]{1,0:T(8,128)(2,1)} %all-gather.8.cloned.1.call-done.gate_ref.refs_4_), channel_id=1, source_target_pairs={{0,4},{4,0},{1,5},{5,1},{2,6},{6,2},{3,7},{7,3},{8,12},{12,8},{9,1... | collective-permute-start | bytes 9437192 | tf_op jit(solution)/shard_map/ppermute | solution.py:542
  321.1 779.0 %all-reduce.3.cloned.1.call-start = ((), (), s32[]{:S(2)}) async-start(), calls=%async_computation.4 | async-start | bytes 10485760 | tf_op jit(solution)/shard_map/psum | solution.py:896
  324.1 12.2 collective-permute-start.10
  324.7 70.4 %collective-permute-start.9 = (bf16[768,2048]{1,0:T(8,128)(2,1)}, bf16[768,2048]{1,0:T(8,128)(2,1)}, u32[]{:S(2)}, u32[]{:S(2)}) collective-permute-start(bf16[768,2048]{1,0:T(8,128)(2,1)} %all-gather.10.cloned.1.call-done.up_ref.refs_5_), channel_id=1, source_target_pairs={{0,4},{4,0},{1,5},{5,1},{2,6},{6,2},{3,7},{7,3},{8,12},{12,8},{9,1... | collective-permute-start | bytes 9437192 | tf_op jit(solution)/shard_map/ppermute | solution.py:542
  330.2 64.9 %collective-permute-start.8 = (bf16[512,2048]{1,0:T(8,128)(2,1)S(1)}, bf16[512,2048]{1,0:T(8,128)(2,1)}, u32[]{:S(2)}, u32[]{:S(2)}) collective-permute-start(bf16[512,2048]{1,0:T(8,128)(2,1)S(1)} %multiply_convert_fusion), channel_id=1, source_target_pairs={{0,1},{1,0},{2,3},{3,2},{4,5},{5,4},{6,7},{7,6},{8,9},{9,8},{10,11... | collective-permute-start | bytes 6291464 | tf_op jit(solution)/shard_map/ppermute | solution.py:551
  397.2 7.2 collective-permute-start.11
  397.3 71.5 %collective-permute-start.12 = (bf16[768,2048]{1,0:T(8,128)(2,1)}, bf16[768,2048]{1,0:T(8,128)(2,1)}, u32[]{:S(2)}, u32[]{:S(2)}) collective-permute-start(bf16[768,2048]{1,0:T(8,128)(2,1)} %all-gather.12.cloned.1.call-done.down_ref.refs_2_), channel_id=1, source_target_pairs={{0,4},{4,0},{1,5},{5,1},{2,6},{6,2},{3,7},{7,3},{8,12},{12,8},{9,1... | collective-permute-start | bytes 9437192 | tf_op jit(solution)/shard_map/ppermute | solution.py:542
  510.5 70.5 %collective-permute-start.13 = (bf16[4,192,2048]{2,1,0:T(8,128)(2,1)}, bf16[4,192,2048]{2,1,0:T(8,128)(2,1)}, u32[]{:S(2)}, u32[]{:S(2)}) collective-permute-start(bf16[4,192,2048]{2,1,0:T(8,128)(2,1)} %bitcast.17), channel_id=1, source_target_pairs={{0,4},{4,0},{1,5},{5,1},{2,6},{6,2},{3,7},{7,3},{8,12},{12,8},{9,1... | collective-permute-start | bytes 9437192 | tf_op jit(solution)/shard_map/ppermute | solution.py:542
  584.7 7.3 collective-permute-start.14
  599.2 57.0 %collective-permute-start.15 = (bf16[512,2048]{1,0:T(8,128)(2,1)}, bf16[512,2048]{1,0:T(8,128)(2,1)S(1)}, u32[]{:S(2)}, u32[]{:S(2)}) collective-permute-start(bf16[512,2048]{1,0:T(8,128)(2,1)} %slice.298), channel_id=1, source_target_pairs={{0,1},{1,0},{2,3},{3,2},{4,5},{5,4},{6,7},{7,6},{8,9},{9,8},{10,11... | collective-permute-start | bytes 6291464 | tf_op jit(solution)/shard_map/ppermute | solution.py:557
  599.7 70.0 %collective-permute-start.19 = (bf16[4,192,2048]{2,1,0:T(8,128)(2,1)S(1)}, bf16[4,192,2048]{2,1,0:T(8,128)(2,1)}, u32[]{:S(2)}, u32[]{:S(2)}) collective-permute-start(bf16[4,192,2048]{2,1,0:T(8,128)(2,1)S(1)} %bitcast.299), channel_id=1, source_target_pairs={{0,4},{4,0},{1,5},{5,1},{2,6},{6,2},{3,7},{7,3},{8,12},{12,8},{9,1... | collective-permute-start | bytes 9437192 | tf_op jit(solution)/shard_map/ppermute | solution.py:542
  601.2 22.6 %collective-permute-start.16 = (bf16[192,2048]{1,0:T(8,128)(2,1)}, bf16[192,2048]{1,0:T(8,128)(2,1)S(1)}, u32[]{:S(2)}, u32[]{:S(2)}) collective-permute-start(bf16[192,2048]{1,0:T(8,128)(2,1)} %get-tuple-element.296), channel_id=1, source_target_pairs={{0,8},{8,16},{16,24},{24,0},{1,9},{9,17},{17,25},{25,1},{2,10},{10... | collective-permute-start | bytes 2359304 | tf_op jit(solution)/shard_map/ppermute | solution.py:609
  601.2 54.9 %collective-permute-start.17 = (bf16[192,2048]{1,0:T(8,128)(2,1)}, bf16[192,2048]{1,0:T(8,128)(2,1)S(1)}, u32[]{:S(2)}, u32[]{:S(2)}) collective-permute-start(bf16[192,2048]{1,0:T(8,128)(2,1)} %get-tuple-element.295), channel_id=1, source_target_pairs={{0,16},{8,24},{16,0},{24,8},{1,17},{9,25},{17,1},{25,9},{2,18},{10... | collective-permute-start | bytes 2359304 | tf_op jit(solution)/shard_map/ppermute | solution.py:609
  603.4 52.7 %collective-permute-start.18 = (bf16[192,2048]{1,0:T(8,128)(2,1)}, bf16[192,2048]{1,0:T(8,128)(2,1)}, u32[]{:S(2)}, u32[]{:S(2)}) collective-permute-start(bf16[192,2048]{1,0:T(8,128)(2,1)} %get-tuple-element.294), channel_id=1, source_target_pairs={{0,24},{8,0},{16,8},{24,16},{1,25},{9,1},{17,9},{25,17},{2,26},{10... | collective-permute-start | bytes 2359304 | tf_op jit(solution)/shard_map/ppermute | solution.py:609
  671.4 96.4 %collective-permute-start.21 = (bf16[4,192,2048]{2,1,0:T(8,128)(2,1)}, bf16[4,192,2048]{2,1,0:T(8,128)(2,1)}, u32[]{:S(2)}, u32[]{:S(2)}) collective-permute-start(bf16[4,192,2048]{2,1,0:T(8,128)(2,1)} %bitcast.22), channel_id=1, source_target_pairs={{0,4},{4,0},{1,5},{5,1},{2,6},{6,2},{3,7},{7,3},{8,12},{12,8},{9,1... | collective-permute-start | bytes 9437192 | tf_op jit(solution)/shard_map/ppermute | solution.py:542
  687.7 80.1 %collective-permute-start.25 = (bf16[8,64,2048]{2,1,0:T(8,128)(2,1)}, bf16[8,64,2048]{2,1,0:T(8,128)(2,1)S(1)}, u32[]{:S(2)}, u32[]{:S(2)}) collective-permute-start(bf16[8,64,2048]{2,1,0:T(8,128)(2,1)} %dynamic-slice_bitcast_fusion.2), channel_id=1, source_target_pairs={{0,1},{1,0},{2,3},{3,2},{4,5},{5,4},{6,7},{7,6},{8,9},{9,8},{10,11... | collective-permute-start | bytes 6291464 | tf_op jit(solution)/shard_map/ppermute | solution.py:580
  688.3 79.5 %collective-permute-start.22 = (bf16[192,2048]{1,0:T(8,128)(2,1)}, bf16[192,2048]{1,0:T(8,128)(2,1)S(1)}, u32[]{:S(2)}, u32[]{:S(2)}) collective-permute-start(bf16[192,2048]{1,0:T(8,128)(2,1)} %get-tuple-element.293), channel_id=1, source_target_pairs={{0,8},{8,16},{16,24},{24,0},{1,9},{9,17},{17,25},{25,1},{2,10},{10... | collective-permute-start | bytes 2359304 | tf_op jit(solution)/shard_map/ppermute | solution.py:609
  700.3 67.5 %collective-permute-start.23 = (bf16[192,2048]{1,0:T(8,128)(2,1)}, bf16[192,2048]{1,0:T(8,128)(2,1)S(1)}, u32[]{:S(2)}, u32[]{:S(2)}) collective-permute-start(bf16[192,2048]{1,0:T(8,128)(2,1)} %get-tuple-element.292), channel_id=1, source_target_pairs={{0,16},{8,24},{16,0},{24,8},{1,17},{9,25},{17,1},{25,9},{2,18},{10... | collective-permute-start | bytes 2359304 | tf_op jit(solution)/shard_map/ppermute | solution.py:609
  701.7 66.1 %collective-permute-start.24 = (bf16[192,2048]{1,0:T(8,128)(2,1)}, bf16[192,2048]{1,0:T(8,128)(2,1)}, u32[]{:S(2)}, u32[]{:S(2)}) collective-permute-start(bf16[192,2048]{1,0:T(8,128)(2,1)} %get-tuple-element.291), channel_id=1, source_target_pairs={{0,24},{8,0},{16,8},{24,16},{1,25},{9,1},{17,9},{25,17},{2,26},{10... | collective-permute-start | bytes 2359304 | tf_op jit(solution)/shard_map/ppermute | solution.py:609
  774.2 7.2 collective-permute-start.26
  775.8 48.7 %collective-permute-start.31 = (bf16[8,64,2048]{2,1,0:T(8,128)(2,1)}, bf16[8,64,2048]{2,1,0:T(8,128)(2,1)}, u32[]{:S(2)}, u32[]{:S(2)}) collective-permute-start(bf16[8,64,2048]{2,1,0:T(8,128)(2,1)} %dynamic-slice_bitcast_fusion.1), channel_id=1, source_target_pairs={{0,1},{1,0},{2,3},{3,2},{4,5},{5,4},{6,7},{7,6},{8,9},{9,8},{10,11... | collective-permute-start | bytes 6291464 | tf_op jit(solution)/shard_map/ppermute | solution.py:580
  788.2 80.9 %collective-permute-start.30 = (bf16[2,512,1024]{2,1,0:T(8,128)(2,1)}, bf16[2,512,1024]{2,1,0:T(8,128)(2,1)}, u32[]{:S(2)}, u32[]{:S(2)}) collective-permute-start(bf16[2,512,1024]{2,1,0:T(8,128)(2,1)} %fusion.34), channel_id=1, source_target_pairs={{0,1},{1,0},{2,3},{3,2},{4,5},{5,4},{6,7},{7,6},{8,9},{9,8},{10,11... | collective-permute-start | bytes 6291464 | tf_op jit(solution)/shard_map/ppermute | solution.py:557
  794.2 30.3 %collective-permute-start.27 = (bf16[192,2048]{1,0:T(8,128)(2,1)}, bf16[192,2048]{1,0:T(8,128)(2,1)S(1)}, u32[]{:S(2)}, u32[]{:S(2)}) collective-permute-start(bf16[192,2048]{1,0:T(8,128)(2,1)} %get-tuple-element.290), channel_id=1, source_target_pairs={{0,8},{8,16},{16,24},{24,0},{1,9},{9,17},{17,25},{25,1},{2,10},{10... | collective-permute-start | bytes 2359304 | tf_op jit(solution)/shard_map/ppermute | solution.py:609
  796.5 52.9 %collective-permute-start.28 = (bf16[192,2048]{1,0:T(8,128)(2,1)}, bf16[192,2048]{1,0:T(8,128)(2,1)S(1)}, u32[]{:S(2)}, u32[]{:S(2)}) collective-permute-start(bf16[192,2048]{1,0:T(8,128)(2,1)} %get-tuple-element.289), channel_id=1, source_target_pairs={{0,16},{8,24},{16,0},{24,8},{1,17},{9,25},{17,1},{25,9},{2,18},{10... | collective-permute-start | bytes 2359304 | tf_op jit(solution)/shard_map/ppermute | solution.py:609
  797.9 51.4 %collective-permute-start.29 = (bf16[192,2048]{1,0:T(8,128)(2,1)}, bf16[192,2048]{1,0:T(8,128)(2,1)S(1)}, u32[]{:S(2)}, u32[]{:S(2)}) collective-permute-start(bf16[192,2048]{1,0:T(8,128)(2,1)} %get-tuple-element.288), channel_id=1, source_target_pairs={{0,24},{8,0},{16,8},{24,16},{1,25},{9,1},{17,9},{25,17},{2,26},{10... | collective-permute-start | bytes 2359304 | tf_op jit(solution)/shard_map/ppermute | solution.py:609
  877.7 9.7 collective-permute-start.32
  886.6 76.0 %collective-permute-start.37 = (bf16[4,64,4096]{2,1,0:T(8,128)(2,1)}, bf16[4,64,4096]{2,1,0:T(8,128)(2,1)}, u32[]{:S(2)}, u32[]{:S(2)}) collective-permute-start(bf16[4,64,4096]{2,1,0:T(8,128)(2,1)} %pad_maximum_fusion.7), channel_id=1, source_target_pairs={{0,4},{4,0},{1,5},{5,1},{2,6},{6,2},{3,7},{7,3},{8,12},{12,8},{9,1... | collective-permute-start | bytes 6291464 | tf_op jit(solution)/shard_map/ppermute | solution.py:542
  896.1 66.5 %collective-permute-start.36 = (bf16[8,64,2048]{2,1,0:T(8,128)(2,1)}, bf16[8,64,2048]{2,1,0:T(8,128)(2,1)}, u32[]{:S(2)}, u32[]{:S(2)}) collective-permute-start(bf16[8,64,2048]{2,1,0:T(8,128)(2,1)} %dynamic-slice_bitcast_fusion), channel_id=1, source_target_pairs={{0,1},{1,0},{2,3},{3,2},{4,5},{5,4},{6,7},{7,6},{8,9},{9,8},{10,11... | collective-permute-start | bytes 6291464 | tf_op jit(solution)/shard_map/ppermute | solution.py:580
  904.6 22.5 %collective-permute-start.33 = (bf16[192,2048]{1,0:T(8,128)(2,1)}, bf16[192,2048]{1,0:T(8,128)(2,1)S(1)}, u32[]{:S(2)}, u32[]{:S(2)}) collective-permute-start(bf16[192,2048]{1,0:T(8,128)(2,1)} %get-tuple-element.312), channel_id=1, source_target_pairs={{0,8},{8,16},{16,24},{24,0},{1,9},{9,17},{17,25},{25,1},{2,10},{10... | collective-permute-start | bytes 2359304 | tf_op jit(solution)/shard_map/ppermute | solution.py:636
  907.2 53.3 %collective-permute-start.34 = (bf16[192,2048]{1,0:T(8,128)(2,1)}, bf16[192,2048]{1,0:T(8,128)(2,1)}, u32[]{:S(2)}, u32[]{:S(2)}) collective-permute-start(bf16[192,2048]{1,0:T(8,128)(2,1)} %get-tuple-element.311), channel_id=1, source_target_pairs={{0,16},{8,24},{16,0},{24,8},{1,17},{9,25},{17,1},{25,9},{2,18},{10... | collective-permute-start | bytes 2359304 | tf_op jit(solution)/shard_map/ppermute | solution.py:636
  908.4 52.0 %collective-permute-start.35 = (bf16[192,2048]{1,0:T(8,128)(2,1)}, bf16[192,2048]{1,0:T(8,128)(2,1)}, u32[]{:S(2)}, u32[]{:S(2)}) collective-permute-start(bf16[192,2048]{1,0:T(8,128)(2,1)} %get-tuple-element.310), channel_id=1, source_target_pairs={{0,24},{8,0},{16,8},{24,16},{1,25},{9,1},{17,9},{25,17},{2,26},{10... | collective-permute-start | bytes 2359304 | tf_op jit(solution)/shard_map/ppermute | solution.py:636
  975.7 57.3 %collective-permute-start.38 = (bf16[4,64,2048]{2,1,0:T(8,128)(2,1)S(1)}, bf16[4,64,2048]{2,1,0:T(8,128)(2,1)}, u32[]{:S(2)}, u32[]{:S(2)}) collective-permute-start(bf16[4,64,2048]{2,1,0:T(8,128)(2,1)S(1)} %dynamic-slice_bitcast_fusion.3), channel_id=1, source_target_pairs={{0,4},{4,0},{1,5},{5,1},{2,6},{6,2},{3,7},{7,3},{8,12},{12,8},{9,1... | collective-permute-start | bytes 3145736 | tf_op jit(solution)/shard_map/ppermute | solution.py:542
  980.7 31.1 %collective-permute-start.39 = (bf16[64,4096]{1,0:T(8,128)(2,1)}, bf16[64,4096]{1,0:T(8,128)(2,1)}, u32[]{:S(2)}, u32[]{:S(2)}) collective-permute-start(bf16[64,4096]{1,0:T(8,128)(2,1)} %get-tuple-element.323), channel_id=1, source_target_pairs={{0,8},{8,16},{16,24},{24,0},{1,9},{9,17},{17,25},{25,1},{2,10},{10... | collective-permute-start | bytes 1572872 | tf_op jit(solution)/shard_map/ppermute | solution.py:609
  998.0 35.0 %collective-permute-start.40 = (bf16[64,4096]{1,0:T(8,128)(2,1)}, bf16[64,4096]{1,0:T(8,128)(2,1)}, u32[]{:S(2)}, u32[]{:S(2)}) collective-permute-start(bf16[64,4096]{1,0:T(8,128)(2,1)} %get-tuple-element.322), channel_id=1, source_target_pairs={{0,16},{8,24},{16,0},{24,8},{1,17},{9,25},{17,1},{25,9},{2,18},{10... | collective-permute-start | bytes 1572872 | tf_op jit(solution)/shard_map/ppermute | solution.py:609
  999.0 34.0 %collective-permute-start.41 = (bf16[64,4096]{1,0:T(8,128)(2,1)}, bf16[64,4096]{1,0:T(8,128)(2,1)}, u32[]{:S(2)}, u32[]{:S(2)}) collective-permute-start(bf16[64,4096]{1,0:T(8,128)(2,1)} %get-tuple-element.321), channel_id=1, source_target_pairs={{0,24},{8,0},{16,8},{24,16},{1,25},{9,1},{17,9},{25,17},{2,26},{10... | collective-permute-start | bytes 1572872 | tf_op jit(solution)/shard_map/ppermute | solution.py:609
  1000.4 204.5 %all-gather.14.cloned.1.call-start = ((), (), s32[]{:S(2)}) async-start(), calls=%async_computation.5 | async-start | bytes 9437184 | tf_op jit(solution)/shard_map/all_gather | solution.py:573
  1003.8 62.7 %collective-permute-start.45 = (bf16[512,2048]{1,0:T(8,128)(2,1)}, bf16[512,2048]{1,0:T(8,128)(2,1)}, u32[]{:S(2)}, u32[]{:S(2)}) collective-permute-start(bf16[512,2048]{1,0:T(8,128)(2,1)} %slice.172), channel_id=1, source_target_pairs={{0,2},{2,0},{1,3},{3,1},{4,6},{6,4},{5,7},{7,5},{8,10},{10,8},{9,1... | collective-permute-start | bytes 6291464 | tf_op jit(solution)/shard_map/ppermute | solution.py:542
  1011.7 69.3 %collective-permute-start.49 = (bf16[1024,2048]{1,0:T(8,128)(2,1)}, bf16[1024,2048]{1,0:T(8,128)(2,1)}, u32[]{:S(2)}, u32[]{:S(2)}) collective-permute-start(bf16[1024,2048]{1,0:T(8,128)(2,1)} %back_to_width.6), channel_id=1, source_target_pairs={{0,2},{2,0},{1,3},{3,1},{4,6},{6,4},{5,7},{7,5},{8,10},{10,8},{9,1... | collective-permute-start | bytes 12582920 | tf_op jit(solution)/shard_map/ppermute | solution.py:542
  1035.1 53.3 %collective-permute-start.42 = (bf16[64,2048]{1,0:T(8,128)(2,1)}, bf16[64,2048]{1,0:T(8,128)(2,1)S(1)}, u32[]{:S(2)}, u32[]{:S(2)}) collective-permute-start(bf16[64,2048]{1,0:T(8,128)(2,1)} %get-tuple-element.308), channel_id=1, source_target_pairs={{0,8},{8,16},{16,24},{24,0},{1,9},{9,17},{17,25},{25,1},{2,10},{10... | collective-permute-start | bytes 786440 | tf_op jit(solution)/shard_map/ppermute | solution.py:609
  1046.8 41.6 %collective-permute-start.43 = (bf16[64,2048]{1,0:T(8,128)(2,1)}, bf16[64,2048]{1,0:T(8,128)(2,1)S(1)}, u32[]{:S(2)}, u32[]{:S(2)}) collective-permute-start(bf16[64,2048]{1,0:T(8,128)(2,1)} %get-tuple-element.307), channel_id=1, source_target_pairs={{0,16},{8,24},{16,0},{24,8},{1,17},{9,25},{17,1},{25,9},{2,18},{10... | collective-permute-start | bytes 786440 | tf_op jit(solution)/shard_map/ppermute | solution.py:609
  1053.3 35.2 %collective-permute-start.44 = (bf16[64,2048]{1,0:T(8,128)(2,1)}, bf16[64,2048]{1,0:T(8,128)(2,1)}, u32[]{:S(2)}, u32[]{:S(2)}) collective-permute-start(bf16[64,2048]{1,0:T(8,128)(2,1)} %get-tuple-element.306), channel_id=1, source_target_pairs={{0,24},{8,0},{16,8},{24,16},{1,25},{9,1},{17,9},{25,17},{2,26},{10... | collective-permute-start | bytes 786440 | tf_op jit(solution)/shard_map/ppermute | solution.py:609
  1073.5 7.5 collective-permute-start.48
  1102.7 10.1 collective-permute-start.52
  1106.1 13.4 %collective-permute-start.50 = (bf16[64,2048]{1,0:T(8,128)(2,1)S(1)}, bf16[64,2048]{1,0:T(8,128)(2,1)S(1)}, u32[]{:S(2)}, u32[]{:S(2)}) collective-permute-start(bf16[64,2048]{1,0:T(8,128)(2,1)S(1)} %get-tuple-element.337), channel_id=1, source_target_pairs={{0,8},{8,16},{16,24},{24,0},{1,9},{9,17},{17,25},{25,1},{2,10},{10... | collective-permute-start | bytes 786440 | tf_op jit(solution)/shard_map/ppermute | solution.py:636
  1106.1 22.4 %collective-permute-start.51 = (bf16[64,2048]{1,0:T(8,128)(2,1)S(1)}, bf16[64,2048]{1,0:T(8,128)(2,1)S(1)}, u32[]{:S(2)}, u32[]{:S(2)}) collective-permute-start(bf16[64,2048]{1,0:T(8,128)(2,1)S(1)} %get-tuple-element.336), channel_id=1, source_target_pairs={{0,16},{8,24},{16,0},{24,8},{1,17},{9,25},{17,1},{25,9},{2,18},{10... | collective-permute-start | bytes 786440 | tf_op jit(solution)/shard_map/ppermute | solution.py:636
  1129.7 75.2 %collective-permute-start.54 = (f32[4352]{0:T(1024)S(1)}, f32[4352]{0:T(1024)S(1)}, u32[]{:S(2)}, u32[]{:S(2)}) collective-permute-start(f32[4352]{0:T(1024)S(1)} %add.676), channel_id=1, source_target_pairs={{0,8},{8,16},{16,24},{24,0},{1,9},{9,17},{17,25},{25,1},{2,10},{10... | collective-permute-start | bytes 52232 | tf_op jit(solution)/shard_map/ppermute | solution.py:551
  1129.7 75.1 %collective-permute-start.55 = (f32[4352]{0:T(1024)S(1)}, f32[4352]{0:T(1024)S(1)}, u32[]{:S(2)}, u32[]{:S(2)}) collective-permute-start(f32[4352]{0:T(1024)S(1)} %add.676), channel_id=1, source_target_pairs={{0,16},{8,24},{16,0},{24,8},{1,17},{9,25},{17,1},{25,9},{2,18},{10... | collective-permute-start | bytes 52232 | tf_op jit(solution)/shard_map/ppermute | solution.py:551
  1132.9 71.9 %collective-permute-start.56 = (f32[4352]{0:T(1024)S(1)}, f32[4352]{0:T(1024)S(1)}, u32[]{:S(2)}, u32[]{:S(2)}) collective-permute-start(f32[4352]{0:T(1024)S(1)} %add.676), channel_id=1, source_target_pairs={{0,24},{8,0},{16,8},{24,16},{1,25},{9,1},{17,9},{25,17},{2,26},{10... | collective-permute-start | bytes 52232 | tf_op jit(solution)/shard_map/ppermute | solution.py:551
  1208.9 73.3 %collective-permute-start.60 = (bf16[512,2048]{1,0:T(8,128)(2,1)}, bf16[512,2048]{1,0:T(8,128)(2,1)}, u32[]{:S(2)}, u32[]{:S(2)}) collective-permute-start(bf16[512,2048]{1,0:T(8,128)(2,1)} %fusion.33), channel_id=1, source_target_pairs={{0,1},{1,0},{2,3},{3,2},{4,5},{5,4},{6,7},{7,6},{8,9},{9,8},{10,11... | collective-permute-start | bytes 6291464 | tf_op jit(solution)/shard_map/ppermute | solution.py:557
  1211.9 63.4 %collective-permute-start.57 = (bf16[192,2048]{1,0:T(8,128)(2,1)}, bf16[192,2048]{1,0:T(8,128)(2,1)S(1)}, u32[]{:S(2)}, u32[]{:S(2)}) collective-permute-start(bf16[192,2048]{1,0:T(8,128)(2,1)} %get-tuple-element.303), channel_id=1, source_target_pairs={{0,24},{8,0},{16,8},{24,16},{1,25},{9,1},{17,9},{25,17},{2,26},{10... | collective-permute-start | bytes 2359304 | tf_op jit(solution)/shard_map/ppermute | solution.py:645
  1212.4 67.7 %collective-permute-start.58 = (bf16[192,2048]{1,0:T(8,128)(2,1)}, bf16[192,2048]{1,0:T(8,128)(2,1)}, u32[]{:S(2)}, u32[]{:S(2)}) collective-permute-start(bf16[192,2048]{1,0:T(8,128)(2,1)} %get-tuple-element.302), channel_id=1, source_target_pairs={{0,16},{8,24},{16,0},{24,8},{1,17},{9,25},{17,1},{25,9},{2,18},{10... | collective-permute-start | bytes 2359304 | tf_op jit(solution)/shard_map/ppermute | solution.py:645
  1214.7 65.4 %collective-permute-start.59 = (bf16[192,2048]{1,0:T(8,128)(2,1)}, bf16[192,2048]{1,0:T(8,128)(2,1)}, u32[]{:S(2)}, u32[]{:S(2)}) collective-permute-start(bf16[192,2048]{1,0:T(8,128)(2,1)} %get-tuple-element.301), channel_id=1, source_target_pairs={{0,8},{8,16},{16,24},{24,0},{1,9},{9,17},{17,25},{25,1},{2,10},{10... | collective-permute-start | bytes 2359304 | tf_op jit(solution)/shard_map/ppermute | solution.py:645
  1282.3 12.2 collective-permute-start.61
  1282.4 24.6 %collective-permute-start.62 = (bf16[64,2048]{1,0:T(8,128)(2,1)S(1)}, bf16[64,2048]{1,0:T(8,128)(2,1)S(1)}, u32[]{:S(2)}, u32[]{:S(2)}) collective-permute-start(bf16[64,2048]{1,0:T(8,128)(2,1)S(1)} %get-tuple-element.332), channel_id=1, source_target_pairs={{0,16},{8,24},{16,0},{24,8},{1,17},{9,25},{17,1},{25,9},{2,18},{10... | collective-permute-start | bytes 786440 | tf_op jit(solution)/shard_map/ppermute | solution.py:645
  1283.7 23.3 %collective-permute-start.63 = (bf16[64,2048]{1,0:T(8,128)(2,1)S(1)}, bf16[64,2048]{1,0:T(8,128)(2,1)S(1)}, u32[]{:S(2)}, u32[]{:S(2)}) collective-permute-start(bf16[64,2048]{1,0:T(8,128)(2,1)S(1)} %get-tuple-element.331), channel_id=1, source_target_pairs={{0,8},{8,16},{16,24},{24,0},{1,9},{9,17},{17,25},{25,1},{2,10},{10... | collective-permute-start | bytes 786440 | tf_op jit(solution)/shard_map/ppermute | solution.py:645
  (136 other events, 1794.1 us)
Sparse Core Ops, SparseCore 0:
  12.6 154.7 all-gather.5
  169.5 61.6 all-gather.7
  246.7 62.0 all-gather.9
  321.2 62.0 all-gather.11
  1000.5 99.6 all-reduce.2
  1129.8 53.9 all-gather.13

commit v5 on v4

--- a/solution.py
+++ b/solution.py
@@ -837,7 +837,6 @@
     query_grad = weight_grad(q_low_turned, both_normed)
     from_query = times_columns(after(q_low, query_grad), attention_rows, MODEL_WIDTH, MODEL_WIDTH)
     query_blocks = jnp.moveaxis(query_grad.reshape(PLANES * CORES, ring, -1, MODEL_WIDTH), 1, 0)
-    query_own, query_arrived = scatter_blocks(query_blocks, "fsdp")
     up_passed, gate_chunks, output_arrived = after(
         (up_passed, gate_chunks, output_arrived), from_query
     )
@@ -849,20 +848,18 @@
     down_rights = (down_own_rows, down_other)
     down_far = back_to_width(hiddens, down_rights, own_rows, own_rows)
     down_near = back_to_width(after(hiddens, down_far), down_rights, 0, own_rows)
-    gate_new = updated(add_all(gate_own, gate_chunks), 4)
-    down_new = updated(add_all(down_own, down_chunks), 6)
-    up_chunks, d_kv_arrived, query_arrived = after(
-        (up_chunks, d_kv_arrived, query_arrived), down_near
-    )
-    big = [gate_new, updated(add_all(up_own, up_chunks), 5), down_new]
-    slots = jnp.stack([new[2] for new in big] + [jnp.zeros_like(down_new[2])])
+    gate_shard = add_all(gate_own, gate_chunks)
+    down_shard = add_all(down_own, down_chunks)
+    gate_form = updated(gate_shard, 4)[2]
+    down_form = updated(down_shard, 6)[2]
+    first_kept, first_passed, _ = halves_over_y(
+        [add_all(output_own.astype(F32), output_arrived).astype(BF16)]
+    )
+    up_chunks, d_kv_arrived, first_passed = after((up_chunks, d_kv_arrived, first_passed), down_near)
+    query_own, query_arrived = scatter_blocks(after(query_blocks, *d_kv_arrived), "fsdp")
+    up_shard = add_all(up_own, up_chunks)
+    slots = jnp.stack([gate_form, updated(up_shard, 5)[2], down_form, jnp.zeros_like(down_form)])
     big_mine = to_planes(slots).reshape(-1, MODEL_WIDTH)
-    first_kept, first_passed, first_sent = halves_over_y(
-        [
-            add_all(output_own.astype(F32), output_arrived).astype(BF16),
-            add_all(query_own.astype(F32), query_arrived).astype(BF16),
-        ]
-    )
     d_kv_total = add_all(d_kv_half[:, 0], d_kv_arrived)
     kv_low_grad, d_gain_key = key_value_back(
         d_kv_total, kv_proj, gain_key[None], cosine_table[0], sine_table[0]
@@ -876,27 +873,29 @@
     key_value_own, key_value_arrived = scatter_blocks(key_value_blocks, "fsdp")
     plane = lax.axis_index("z")
     in_plane = ("y", "core", "fsdp")
-    big_mine, key_value_arrived, first_passed = lax.optimization_barrier(
-        (big_mine, key_value_arrived, first_passed)
+    big_mine, key_value_arrived, query_arrived = lax.optimization_barrier(
+        (big_mine, key_value_arrived, query_arrived)
     )
     big_gram = gram_blocks(big_mine)
-    from_query, down_far, first_passed, key_value_arrived = after(
-        (from_query, down_far, first_passed, key_value_arrived), big_gram
+    from_query, down_far, query_arrived, key_value_arrived = after(
+        (from_query, down_far, query_arrived, key_value_arrived), big_gram
     )
     down_half = (down_near.astype(F32) + swap(down_far).astype(F32)).reshape(
         ring, rows, MODEL_WIDTH
     )
     kept, arrived, attention_passed = halves_over_y(
-        [add_all(key_value_own.astype(F32), key_value_arrived).astype(BF16)]
-    )
-    first_own, first_chunks, first_chunks_sent = chunks_over_z(first_kept, first_passed)
-    from_kv = times_rows(
-        after(both_kv_low, attention_passed, first_chunks_sent), attention_rows, 0
+        [
+            add_all(query_own.astype(F32), query_arrived).astype(BF16),
+            add_all(key_value_own.astype(F32), key_value_arrived).astype(BF16),
+        ]
+    )
+    first_own, first_chunks, first_chunks_sent = chunks_over_z(
+        first_kept, after(first_passed, attention_passed)
     )
     big_gram = lax.psum(big_gram, in_plane)
-    arrived, first_chunks = after((arrived, first_chunks), from_kv)
+    arrived = after(arrived, first_chunks_sent)
     last_own, last_chunks, last_chunks_sent = chunks_over_z(kept, arrived)
-    from_kv = after(from_kv, last_chunks_sent)
+    from_kv = dot_nt(after(both_kv_low, last_chunks_sent), key_value_rows).astype(BF16)
 
     from_query = from_query[:rows].astype(F32) + swap(from_query[rows:]).astype(F32)
     kv_here = from_kv[:rows].reshape(rows, -1, HEAD_SIZE)
@@ -910,25 +909,28 @@
     input_grad = (d_middle + d_residual).reshape(inputs.shape)
     gain_grad = jnp.concatenate([d_gain_attn, d_gain_mlp, d_gain_query, d_gain_key])
 
-    first_total = add_all(first_own, first_chunks)
-    output_new = updated(first_total[:, :MODEL_WIDTH], 3)
-    query_new = updated(first_total[:, MODEL_WIDTH:], 0)
-    last_chunks, big_gram, gain_grad, down_half, output_new, query_new = after(
+    output_new = updated(add_all(first_own, first_chunks), 3)
+    big = [
+        updated(shard, idx)
+        for shard, idx in zip(after((gate_shard, up_shard, down_shard), last_chunks_sent), (4, 5, 6))
+    ]
+    big = [(grad, moment) for grad, moment, _ in big]
+    last_chunks, big_gram, gain_grad, down_half, output_new, big = after(
         (
             last_chunks,
             big_gram,
             butterfly(butterfly(gain_grad, "core"), "fsdp"),
             down_half,
             output_new,
-            query_new,
+            big,
         ),
         input_grad,
     )
-    key_value_shard = add_all(last_own, last_chunks)
+    last_total = add_all(last_own, last_chunks)
     small = [
-        query_new,
-        updated(key_value_shard[:, :KV_WIDTH], 1),
-        updated(key_value_shard[:, KV_WIDTH:], 2),
+        updated(last_total[:, :MODEL_WIDTH], 0),
+        updated(last_total[:, MODEL_WIDTH : MODEL_WIDTH + KV_WIDTH], 1),
+        updated(last_total[:, MODEL_WIDTH + KV_WIDTH :], 2),
         output_new,
     ]
     small_slots = jnp.stack(
@@ -980,8 +982,8 @@
     return (
         block_out,
         input_grad,
-        *(grad for grad, _, _ in small + big),
-        *(moment for _, moment, _ in small + big),
+        *(new[0] for new in small + big),
+        *(new[1] for new in small + big),
         *new_weights,
         first_new,
         second_new,

time: 1330 us -> 1370 us (1.030)
  starting transfers between devices: 99.7 us -> 128 us
    ppermute x22, waiting for transfers between devices: 60.9 us -> 92.6 us  [swap(): return lax.ppermute(value, axis_name, shifted(1, CORES))]
    ppermute x3, waiting for transfers between devices: 19.7 us -> 0.01 us  [ring_send(): lax.ppermute(blocks[step].astype(BF16), axis_name, shifted(-step, count))]
    ppermute x6, starting transfers between devices: 9.36 us -> 23.9 us  [to_planes(): lax.ppermute(pick(chunks, (here + step) % PLANES), 'z', shifted(step, PLA...]
    unnamed x271 -> x269, local copies, waits for them, and re-layouts: 57 us -> 62.8 us
  transfers between devices with their start and end apart: 70 -> 70, of which waited for: 31 -> 29; matrix products, arithmetic and copies ran while one was open for 16% -> 17% of each run, Pallas kernels for 28% -> 26%
where the time goes in v5:
time: 1370 us; the launch traced here: 1360 us
  waiting for transfers between devices  477 us (35%)
  Pallas kernels  413 us (30%)
  other arithmetic  157 us (11%)
  starting transfers between devices  128 us (9%)
  local copies, waits for them, and re-layouts  125 us (9%)
  matrix products  40.2 us (3%)
  between operations  16.1 us (1%)
    all_gather x5, waiting for transfers between devices, gather_rows(): return lax.all_gather(shard, axes, axis=0, tiled=True)  195 us
    pallas_call x2, Pallas kernels, muon(): pl.pallas_call(muon_kernel, grid=(), in_specs=[pl.BlockSpec(memory_space=...  109 us
    ppermute x22, waiting for transfers between devices, swap(): return lax.ppermute(value, axis_name, shifted(1, CORES))  92.6 us
    ppermute x15, waiting for transfers between devices, chunks_over_z(): lax.ppermute(value, 'z', shifted(step + 1, PLANES))  76.5 us
    ppermute x15, starting transfers between devices, chunks_over_z(): lax.ppermute(value, 'z', shifted(step + 1, PLANES))  69.4 us
    pallas_call x8, Pallas kernels, weight_grad(): pl.pallas_call(weight_grad_kernel, grid=(width // tile,), in_specs=[pl.Bl...  68.1 us
    pallas_call x4, Pallas kernels, back_to_width(): pl.pallas_call(functools.partial(back_to_width_kernel, len(lefts)), grid=...  63.4 us
    ppermute x6, waiting for transfers between devices, to_planes(): lax.ppermute(pick(chunks, (here + step) % PLANES), 'z', shifted(step, PLA...  62.8 us
  transfers between devices with their start and end apart: 70, of which 29 were waited for; matrix products, arithmetic and copies ran while one was open for 17% of the time, Pallas kernels for 26%

profile of v5, /device:TPU:0, one launch (start us, length us, event | category | flops | bytes accessed | tf_op | source)
XLA Modules:
  0.0 1356.8 jit_solution(12819236044315392806)
XLA Ops:
  24.3 7.7 reshape.411
  32.0 8.5 constant_dynamic-slice_fusion.13
  40.4 9.0 copy.59
  50.8 116.6 %all-gather.6.cloned.1.call-done.right_ref = bf16[1024,6144]{1,0:T(8,128)(2,1)} async-done(((bf16[64,6144]{1,0:T(8,128)(2,1)}), bf16[1024,6144]{1,0:T(8,128)(2,1)}) %all-gather.6.cloned.1.call-update) | async-done | bytes 12582928 | tf_op jit(solution)/shard_map/all_gather | solution.py:573
  167.4 5.9 fusion.28
  194.1 9.4 fusion.11.q_ref
  203.6 27.7 %all-gather.8.cloned.1.call-done.gate_ref.refs_4_ = bf16[768,2048]{1,0:T(8,128)(2,1)} async-done(((bf16[192,2048]{1,0:T(8,128)(2,1)}), bf16[768,2048]{1,0:T(8,128)(2,1)}) %all-gather.8.cloned.1.call-update) | async-done | bytes 3145744 | tf_op jit(solution)/shard_map/all_gather | solution.py:573
  231.3 9.6 collective-permute-done.3
  253.5 8.5 pad_maximum_fusion
  262.0 19.7 %attention.1 = (bf16[1024,1024]{1,0:T(8,128)(2,1)S(1)}, bf16[1024,1024]{1,0:T(8,128)(2,1)S(1)}) custom-call(f32[1024,1024]{1,0:T(8,128)S(1)} %copy-done.2, bf16[2,1024,2048]{2,1,0:T(8,128)(2,1)} %bitcast.313, bf16[2,1024,2048]{2,1,0:T(8,128)(2,1)} %bitcast.314, bf16[2,1024,512]{2,1,0:T(8,128)(2,1)S(1)} %and_convert_fusion.mask_ref, ...), custom_call_target="tpu_custom_call" | custom-call | flops 1 | bytes 1 | tf_op jit(solution)/shard_map/attention/pallas_call | solution.py:337
  281.7 13.3 collective-permute-done.5
  303.1 5.7 all-gather.10.cloned.1.call-done.up_ref.refs_5_
  308.8 9.9 collective-permute-done.6.gate_ref.refs_6_
  338.7 44.6 %all-gather.12.cloned.1.call-done.down_ref.refs_2_ = bf16[768,2048]{1,0:T(8,128)(2,1)} async-done(((bf16[192,2048]{1,0:T(8,128)(2,1)}), bf16[768,2048]{1,0:T(8,128)(2,1)}) %all-gather.12.cloned.1.call-update) | async-done | bytes 3145744 | tf_op jit(solution)/shard_map/all_gather | solution.py:573
  383.3 11.8 collective-permute-done.9.up_ref.refs_7_
  406.7 29.9 %swiglu_both_ways.2 = (bf16[2048,768]{1,0:T(8,128)(2,1)}, bf16[2048,768]{1,0:T(8,128)(2,1)}, bf16[2048,768]{1,0:T(8,128)(2,1)}, bf16[768,2048]{1,0:T(8,128)(2,1)...) custom-call(bf16[2048,2048]{1,0:T(8,128)(2,1)} %constant_dynamic-update-slice_fusion.5.two_ref.right_ref, ...), custom_call_target="tpu_custom_call" | custom-call | flops 1 | bytes 1 | tf_op jit(solution)/shard_map/swiglu_both_ways/pallas_call | solution.py:390
  438.5 9.1 weight_grad.8
  449.3 9.1 weight_grad.9
  458.4 10.1 weight_grad.10
  468.6 30.0 %swiglu_both_ways.3 = (bf16[2048,768]{1,0:T(8,128)(2,1)}, bf16[2048,768]{1,0:T(8,128)(2,1)}, bf16[2048,768]{1,0:T(8,128)(2,1)}, bf16[768,2048]{1,0:T(8,128)(2,1)...) custom-call(bf16[2048,2048]{1,0:T(8,128)(2,1)} %constant_dynamic-update-slice_fusion.5.two_ref.right_ref, ...), custom_call_target="tpu_custom_call" | custom-call | flops 1 | bytes 1 | tf_op jit(solution)/shard_map/swiglu_both_ways/pallas_call | solution.py:390
  500.5 9.8 weight_grad.11
  512.8 9.0 weight_grad.12
  523.3 20.0 %back_to_width.4 = bf16[1024,2048]{1,0:T(8,128)(2,1)} custom-call(bf16[2048,768]{1,0:T(8,128)(2,1)} %get-tuple-element.183.refs_0_, bf16[2048,768]{1,0:T(8,128)(2,1)} %get-tuple-element.184.refs_1_, bf16[2048,768]{1,0:T(8,128)(2,1)} %get-tuple-element.185.refs_2_, bf16[2048,768]{1,0:T(8,128)(2,1)} %get-tuple-element.186.refs_3_, ...), custom_call_target="tpu_custom_call" | custom-call | flops 1 | bytes 1 | tf_op jit(solution)/shard_map/back_to_width/pallas_call | solution.py:407
  543.4 20.5 %back_to_width.5 = bf16[1024,2048]{1,0:T(8,128)(2,1)} custom-call(bf16[2048,768]{1,0:T(8,128)(2,1)} %get-tuple-element.183.refs_0_, bf16[2048,768]{1,0:T(8,128)(2,1)} %get-tuple-element.184.refs_1_, bf16[2048,768]{1,0:T(8,128)(2,1)} %get-tuple-element.185.refs_2_, bf16[2048,768]{1,0:T(8,128)(2,1)} %get-tuple-element.186.refs_3_, ...), custom_call_target="tpu_custom_call" | custom-call | flops 1 | bytes 1 | tf_op jit(solution)/shard_map/back_to_width/pallas_call | solution.py:407
  563.8 16.9 %collective-permute-done.13 = bf16[4,192,2048]{2,1,0:T(8,128)(2,1)} collective-permute-done((bf16[4,192,2048]{2,1,0:T(8,128)(2,1)}, bf16[4,192,2048]{2,1,0:T(8,128)(2,1)}, u32[]{:S(2)}, u32[]{:S(2)}) %collective-permute-start.13) | collective-permute-done | bytes 3145760 | tf_op jit(solution)/shard_map/ppermute | solution.py:542
  584.3 7.3 collective-permute-done.14
  591.6 5.5 convert_add_fusion.3
  605.3 9.8 weight_grad.13
  617.9 5.5 collective-permute-done.16
  623.5 32.4 %collective-permute-done.17 = bf16[192,2048]{1,0:T(8,128)(2,1)} collective-permute-done((bf16[192,2048]{1,0:T(8,128)(2,1)S(1)}, bf16[192,2048]{1,0:T(8,128)(2,1)}, u32[]{:S(2)}, u32[]{:S(2)}) %collective-permute-start.17) | collective-permute-done | bytes 786464 | tf_op jit(solution)/shard_map/ppermute | solution.py:609
  679.5 5.6 weight_grad.14
  687.5 11.7 collective-permute-start.22
  701.6 6.8 times_rows.1.grad_ref
  709.7 21.8 %attention_back.2 = (bf16[1024,1024]{1,0:T(8,128)(2,1)S(1)}, bf16[1024,1024]{1,0:T(8,128)(2,1)S(1)}, bf16[2,1024,1024]{2,1,0:T(8,128)(2,1)}, f32[1,128]{1,0:T(1,128)S(1)}) custom-call(f32[1024,1024]{1,0:T(8,128)} %fusion.11.q_ref, bf16[2,1024,2048]{2,1,0:T(8,128)(2,1)} %bitcast.315, bf16[2,1024,2048]{2,1,0:T(8,128)(2,1)} %bitcast.316, ...), custom_call_target="tpu_custom_call" | custom-call | flops 1 | bytes 1 | tf_op jit(solution)/shard_map/attention_back/pallas_call | solution.py:361
  731.5 22.1 %attention_back.3 = (bf16[1024,1024]{1,0:T(8,128)(2,1)S(1)}, bf16[1024,1024]{1,0:T(8,128)(2,1)S(1)}, bf16[2,1024,1024]{2,1,0:T(8,128)(2,1)}, f32[1,128]{1,0:T(1,128)S(1)}) custom-call(f32[1024,1024]{1,0:T(8,128)} %fusion.11.q_ref, bf16[2,1024,2048]{2,1,0:T(8,128)(2,1)} %bitcast.317, ...), custom_call_target="tpu_custom_call", output_to_operand_aliasing={{0}: (8, {}), {1}: (9, {})} | custom-call | flops 1 | bytes 1 | tf_op jit(solution)/shard_map/attention_back/pallas_call | solution.py:361
  753.7 5.6 weight_grad.15
  761.2 6.7 times_columns.1
  768.0 5.7 fusion.66
  773.8 7.1 collective-permute-done.29
  798.7 11.5 back_to_width.6
  810.2 11.3 back_to_width.7
  821.6 27.6 %collective-permute-done.27 = bf16[192,2048]{1,0:T(8,128)(2,1)} collective-permute-done((bf16[192,2048]{1,0:T(8,128)(2,1)S(1)}, bf16[192,2048]{1,0:T(8,128)(2,1)}, u32[]{:S(2)}, u32[]{:S(2)}) %collective-permute-start.27) | collective-permute-done | bytes 786464 | tf_op jit(solution)/shard_map/ppermute | solution.py:609
  853.2 7.7 key_value_back.1
  886.5 17.4 %collective-permute-start.32 = (bf16[192,2048]{1,0:T(8,128)(2,1)S(1)}, bf16[192,2048]{1,0:T(8,128)(2,1)S(1)}, u32[]{:S(2)}, u32[]{:S(2)}) collective-permute-start(bf16[192,2048]{1,0:T(8,128)(2,1)S(1)} %get-tuple-element.322), channel_id=1, source_target_pairs={{0,8},{8,16},{16,24},{24,0},{1,9},{9,17},{17,25},{25,1},{2,10},{10... | collective-permute-start | bytes 2359304 | tf_op jit(solution)/shard_map/ppermute | solution.py:636
  906.3 16.2 %collective-permute-done.32 = bf16[192,2048]{1,0:T(8,128)(2,1)S(1)} collective-permute-done((bf16[192,2048]{1,0:T(8,128)(2,1)S(1)}, bf16[192,2048]{1,0:T(8,128)(2,1)S(1)}, u32[]{:S(2)}, u32[]{:S(2)}) %collective-permute-start.32) | collective-permute-done | bytes 786464 | tf_op jit(solution)/shard_map/ppermute | solution.py:636
  922.5 33.3 %collective-permute-done.33 = bf16[192,2048]{1,0:T(8,128)(2,1)S(1)} collective-permute-done((bf16[192,2048]{1,0:T(8,128)(2,1)S(1)}, bf16[192,2048]{1,0:T(8,128)(2,1)S(1)}, u32[]{:S(2)}, u32[]{:S(2)}) %collective-permute-start.33) | collective-permute-done | bytes 786464 | tf_op jit(solution)/shard_map/ppermute | solution.py:636
  956.7 6.4 collective-permute-done.36
  964.4 7.5 gram_blocks.2
  983.9 17.4 %collective-permute-start.47 = (bf16[64,2048]{1,0:T(8,128)(2,1)S(1)}, bf16[64,2048]{1,0:T(8,128)(2,1)S(1)}, u32[]{:S(2)}, u32[]{:S(2)}) collective-permute-start(bf16[64,2048]{1,0:T(8,128)(2,1)S(1)} %get-tuple-element.318), channel_id=1, source_target_pairs={{0,8},{8,16},{16,24},{24,0},{1,9},{9,17},{17,25},{25,1},{2,10},{10... | collective-permute-start | bytes 786440 | tf_op jit(solution)/shard_map/ppermute | solution.py:609
  1008.6 10.3 collective-permute-done.48
  1020.9 29.5 %collective-permute-done.38 = bf16[4,64,4096]{2,1,0:T(8,128)(2,1)} collective-permute-done((bf16[4,64,4096]{2,1,0:T(8,128)(2,1)}, bf16[4,64,4096]{2,1,0:T(8,128)(2,1)}, u32[]{:S(2)}, u32[]{:S(2)}) %collective-permute-start.38) | collective-permute-done | bytes 2097184 | tf_op jit(solution)/shard_map/ppermute | solution.py:542
  1053.2 24.3 %collective-permute-start.39 = (bf16[64,4096]{1,0:T(8,128)(2,1)}, bf16[64,4096]{1,0:T(8,128)(2,1)}, u32[]{:S(2)}, u32[]{:S(2)}) collective-permute-start(bf16[64,4096]{1,0:T(8,128)(2,1)} %get-tuple-element.333), channel_id=1, source_target_pairs={{0,8},{8,16},{16,24},{24,0},{1,9},{9,17},{17,25},{25,1},{2,10},{10... | collective-permute-start | bytes 1572872 | tf_op jit(solution)/shard_map/ppermute | solution.py:609
  1078.1 7.2 fusion.37
  1103.8 8.5 maximum_convert_fusion
  1112.3 6.6 reshape.451
  1118.9 5.8 fusion.9
  1126.5 5.7 fusion.6
  1132.3 7.3 convert_add_fusion.1
  1155.1 10.1 collective-permute-done.51
  1166.3 5.6 collective-permute-start.54
  1174.4 71.5 %muon.2 = bf16[768,2048]{1,0:T(8,128)(2,1)} custom-call(s32[1]{0:T(128)} %constant.615.clone.1.halves_ref, bf16[768,2048]{1,0:T(8,128)(2,1)} %bitcast.299, bf16[10,512,512]{2,1,0:T(8,128)(2,1)} %all-reduce.3.cloned.1.call-done.packed_ref), custom_call_target="tpu_custom_call" | custom-call | flops 1 | bytes 1 | tf_op jit(solution)/shard_map/muon/pallas_call | solution.py:514
  1258.0 15.8 %gram_blocks.3.packed_ref = bf16[10,512,512]{2,1,0:T(8,128)(2,1)S(1)} custom-call(s32[10]{0:T(128)S(1)} %copy-done.41, s32[10]{0:T(128)S(1)} %copy-done.42, bf16[2048,2048]{1,0:T(8,128)(2,1)S(1)} %copy-done.3, bf16[2048,2048]{1,0:T(8,128)(2,1)S(1)} %copy-done.3), custom_call_target="tpu_custom_call" | custom-call | flops 1 | bytes 1 | tf_op jit(solution)/shard_map/gram_blocks/pallas_call | solution.py:493
  1276.1 37.2 %muon.3 = bf16[256,2048]{1,0:T(8,128)(2,1)} custom-call(s32[1]{0:T(128)} %bitcast.91.halves_ref, bf16[256,2048]{1,0:T(8,128)(2,1)} %bitcast.331, bf16[10,512,512]{2,1,0:T(8,128)(2,1)} %copy-done.9), custom_call_target="tpu_custom_call" | custom-call | flops 1 | bytes 1 | tf_op jit(solution)/shard_map/muon/pallas_call | solution.py:514
  1335.3 11.6 collective-permute-done.62
  (515 shorter events, 301.6 us)
Async XLA Ops:
  7.2 160.2 %all-gather.6.cloned.1.call-start = ((), (), s32[]{:S(2)}) async-start(), calls=%async_computation | async-start | bytes 13369344 | tf_op jit(solution)/shard_map/all_gather | solution.py:573
  12.5 218.8 %all-gather.8.cloned.1.call-start = ((), (), s32[]{:S(2)}) async-start(), calls=%async_computation.1 | async-start | bytes 3932160 | tf_op jit(solution)/shard_map/all_gather | solution.py:573
  15.4 157.9 %collective-permute-start.2 = (s32[1,1024]{1,0:T(1,128)S(1)}, s32[1,1024]{1,0:T(1,128)S(1)}, u32[]{:S(2)}, u32[]{:S(2)}) collective-permute-start(s32[1,1024]{1,0:T(1,128)S(1)} %copy-done.123), channel_id=1, source_target_pairs={{0,2},{2,0},{1,3},{3,1},{4,6},{6,4},{5,7},{7,5},{8,10},{10,8},{9,1... | collective-permute-start | bytes 12296 | tf_op jit(solution)/shard_map/ppermute | solution.py:542
  16.5 292.3 %all-gather.10.cloned.1.call-start = ((), (), s32[]{:S(2)}) async-start(), calls=%async_computation.2 | async-start | bytes 3932160 | tf_op jit(solution)/shard_map/all_gather | solution.py:573
  173.3 9.6 collective-permute-start.1
  192.7 48.2 %collective-permute-start.3 = (bf16[512,2048]{1,0:T(8,128)(2,1)S(1)}, bf16[512,2048]{1,0:T(8,128)(2,1)}, u32[]{:S(2)}, u32[]{:S(2)}) collective-permute-start(bf16[512,2048]{1,0:T(8,128)(2,1)S(1)} %get-tuple-element.150), channel_id=1, source_target_pairs={{0,1},{1,0},{2,3},{3,2},{4,5},{5,4},{6,7},{7,6},{8,9},{9,8},{10,11... | collective-permute-start | bytes 6291464 | tf_op jit(solution)/shard_map/ppermute | solution.py:551
  245.6 7.9 collective-permute-start.4
  246.6 136.7 %all-gather.12.cloned.1.call-start = ((), (), s32[]{:S(2)}) async-start(), calls=%async_computation.3 | async-start | bytes 3932160 | tf_op jit(solution)/shard_map/all_gather | solution.py:573
  246.6 48.4 %collective-permute-start.5 = (bf16[512,2048]{1,0:T(8,128)(2,1)}, bf16[512,2048]{1,0:T(8,128)(2,1)}, u32[]{:S(2)}, u32[]{:S(2)}) collective-permute-start(bf16[512,2048]{1,0:T(8,128)(2,1)} %bitcast.327), channel_id=1, source_target_pairs={{0,1},{1,0},{2,3},{3,2},{4,5},{5,4},{6,7},{7,6},{8,9},{9,8},{10,11... | collective-permute-start | bytes 6291464 | tf_op jit(solution)/shard_map/ppermute | solution.py:551
  248.1 70.5 %collective-permute-start.6 = (bf16[768,2048]{1,0:T(8,128)(2,1)}, bf16[768,2048]{1,0:T(8,128)(2,1)}, u32[]{:S(2)}, u32[]{:S(2)}) collective-permute-start(bf16[768,2048]{1,0:T(8,128)(2,1)} %all-gather.8.cloned.1.call-done.gate_ref.refs_4_), channel_id=1, source_target_pairs={{0,4},{4,0},{1,5},{5,1},{2,6},{6,2},{3,7},{7,3},{8,12},{12,8},{9,1... | collective-permute-start | bytes 9437192 | tf_op jit(solution)/shard_map/ppermute | solution.py:542
  318.7 6.6 collective-permute-start.7
  321.1 818.5 %all-reduce.3.cloned.1.call-start = ((), (), s32[]{:S(2)}) async-start(), calls=%async_computation.4 | async-start | bytes 10485760 | tf_op jit(solution)/shard_map/psum | solution.py:895
  324.1 12.1 collective-permute-start.10
  324.7 70.4 %collective-permute-start.9 = (bf16[768,2048]{1,0:T(8,128)(2,1)}, bf16[768,2048]{1,0:T(8,128)(2,1)}, u32[]{:S(2)}, u32[]{:S(2)}) collective-permute-start(bf16[768,2048]{1,0:T(8,128)(2,1)} %all-gather.10.cloned.1.call-done.up_ref.refs_5_), channel_id=1, source_target_pairs={{0,4},{4,0},{1,5},{5,1},{2,6},{6,2},{3,7},{7,3},{8,12},{12,8},{9,1... | collective-permute-start | bytes 9437192 | tf_op jit(solution)/shard_map/ppermute | solution.py:542
  330.2 64.9 %collective-permute-start.8 = (bf16[512,2048]{1,0:T(8,128)(2,1)S(1)}, bf16[512,2048]{1,0:T(8,128)(2,1)}, u32[]{:S(2)}, u32[]{:S(2)}) collective-permute-start(bf16[512,2048]{1,0:T(8,128)(2,1)S(1)} %multiply_convert_fusion), channel_id=1, source_target_pairs={{0,1},{1,0},{2,3},{3,2},{4,5},{5,4},{6,7},{7,6},{8,9},{9,8},{10,11... | collective-permute-start | bytes 6291464 | tf_op jit(solution)/shard_map/ppermute | solution.py:551
  397.2 7.2 collective-permute-start.11
  397.3 71.3 %collective-permute-start.12 = (bf16[768,2048]{1,0:T(8,128)(2,1)}, bf16[768,2048]{1,0:T(8,128)(2,1)}, u32[]{:S(2)}, u32[]{:S(2)}) collective-permute-start(bf16[768,2048]{1,0:T(8,128)(2,1)} %all-gather.12.cloned.1.call-done.down_ref.refs_2_), channel_id=1, source_target_pairs={{0,4},{4,0},{1,5},{5,1},{2,6},{6,2},{3,7},{7,3},{8,12},{12,8},{9,1... | collective-permute-start | bytes 9437192 | tf_op jit(solution)/shard_map/ppermute | solution.py:542
  510.3 70.5 %collective-permute-start.13 = (bf16[4,192,2048]{2,1,0:T(8,128)(2,1)}, bf16[4,192,2048]{2,1,0:T(8,128)(2,1)}, u32[]{:S(2)}, u32[]{:S(2)}) collective-permute-start(bf16[4,192,2048]{2,1,0:T(8,128)(2,1)} %bitcast.16), channel_id=1, source_target_pairs={{0,4},{4,0},{1,5},{5,1},{2,6},{6,2},{3,7},{7,3},{8,12},{12,8},{9,1... | collective-permute-start | bytes 9437192 | tf_op jit(solution)/shard_map/ppermute | solution.py:542
  584.3 7.3 collective-permute-start.14
  598.7 57.1 %collective-permute-start.15 = (bf16[512,2048]{1,0:T(8,128)(2,1)}, bf16[512,2048]{1,0:T(8,128)(2,1)S(1)}, u32[]{:S(2)}, u32[]{:S(2)}) collective-permute-start(bf16[512,2048]{1,0:T(8,128)(2,1)} %slice.293), channel_id=1, source_target_pairs={{0,1},{1,0},{2,3},{3,2},{4,5},{5,4},{6,7},{7,6},{8,9},{9,8},{10,11... | collective-permute-start | bytes 6291464 | tf_op jit(solution)/shard_map/ppermute | solution.py:557
  599.3 70.0 %collective-permute-start.19 = (bf16[4,192,2048]{2,1,0:T(8,128)(2,1)S(1)}, bf16[4,192,2048]{2,1,0:T(8,128)(2,1)}, u32[]{:S(2)}, u32[]{:S(2)}) collective-permute-start(bf16[4,192,2048]{2,1,0:T(8,128)(2,1)S(1)} %bitcast.310), channel_id=1, source_target_pairs={{0,4},{4,0},{1,5},{5,1},{2,6},{6,2},{3,7},{7,3},{8,12},{12,8},{9,1... | collective-permute-start | bytes 9437192 | tf_op jit(solution)/shard_map/ppermute | solution.py:542
  600.8 22.7 %collective-permute-start.16 = (bf16[192,2048]{1,0:T(8,128)(2,1)}, bf16[192,2048]{1,0:T(8,128)(2,1)}, u32[]{:S(2)}, u32[]{:S(2)}) collective-permute-start(bf16[192,2048]{1,0:T(8,128)(2,1)} %get-tuple-element.306), channel_id=1, source_target_pairs={{0,8},{8,16},{16,24},{24,0},{1,9},{9,17},{17,25},{25,1},{2,10},{10... | collective-permute-start | bytes 2359304 | tf_op jit(solution)/shard_map/ppermute | solution.py:609
  600.8 55.0 %collective-permute-start.17 = (bf16[192,2048]{1,0:T(8,128)(2,1)S(1)}, bf16[192,2048]{1,0:T(8,128)(2,1)}, u32[]{:S(2)}, u32[]{:S(2)}) collective-permute-start(bf16[192,2048]{1,0:T(8,128)(2,1)S(1)} %get-tuple-element.305), channel_id=1, source_target_pairs={{0,16},{8,24},{16,0},{24,8},{1,17},{9,25},{17,1},{25,9},{2,18},{10... | collective-permute-start | bytes 2359304 | tf_op jit(solution)/shard_map/ppermute | solution.py:609
  603.0 52.8 %collective-permute-start.18 = (bf16[192,2048]{1,0:T(8,128)(2,1)S(1)}, bf16[192,2048]{1,0:T(8,128)(2,1)}, u32[]{:S(2)}, u32[]{:S(2)}) collective-permute-start(bf16[192,2048]{1,0:T(8,128)(2,1)S(1)} %get-tuple-element.304), channel_id=1, source_target_pairs={{0,24},{8,0},{16,8},{24,16},{1,25},{9,1},{17,9},{25,17},{2,26},{10... | collective-permute-start | bytes 2359304 | tf_op jit(solution)/shard_map/ppermute | solution.py:609
  670.9 97.0 %collective-permute-start.21 = (bf16[4,192,2048]{2,1,0:T(8,128)(2,1)}, bf16[4,192,2048]{2,1,0:T(8,128)(2,1)}, u32[]{:S(2)}, u32[]{:S(2)}) collective-permute-start(bf16[4,192,2048]{2,1,0:T(8,128)(2,1)} %bitcast.21), channel_id=1, source_target_pairs={{0,4},{4,0},{1,5},{5,1},{2,6},{6,2},{3,7},{7,3},{8,12},{12,8},{9,1... | collective-permute-start | bytes 9437192 | tf_op jit(solution)/shard_map/ppermute | solution.py:542
  687.0 81.0 %collective-permute-start.25 = (bf16[8,64,2048]{2,1,0:T(8,128)(2,1)}, bf16[8,64,2048]{2,1,0:T(8,128)(2,1)S(1)}, u32[]{:S(2)}, u32[]{:S(2)}) collective-permute-start(bf16[8,64,2048]{2,1,0:T(8,128)(2,1)} %dynamic-slice_bitcast_fusion.2), channel_id=1, source_target_pairs={{0,1},{1,0},{2,3},{3,2},{4,5},{5,4},{6,7},{7,6},{8,9},{9,8},{10,11... | collective-permute-start | bytes 6291464 | tf_op jit(solution)/shard_map/ppermute | solution.py:580
  687.5 80.4 %collective-permute-start.22 = (bf16[192,2048]{1,0:T(8,128)(2,1)}, bf16[192,2048]{1,0:T(8,128)(2,1)}, u32[]{:S(2)}, u32[]{:S(2)}) collective-permute-start(bf16[192,2048]{1,0:T(8,128)(2,1)} %get-tuple-element.303), channel_id=1, source_target_pairs={{0,8},{8,16},{16,24},{24,0},{1,9},{9,17},{17,25},{25,1},{2,10},{10... | collective-permute-start | bytes 2359304 | tf_op jit(solution)/shard_map/ppermute | solution.py:609
  699.2 68.7 %collective-permute-start.23 = (bf16[192,2048]{1,0:T(8,128)(2,1)S(1)}, bf16[192,2048]{1,0:T(8,128)(2,1)}, u32[]{:S(2)}, u32[]{:S(2)}) collective-permute-start(bf16[192,2048]{1,0:T(8,128)(2,1)S(1)} %get-tuple-element.302), channel_id=1, source_target_pairs={{0,16},{8,24},{16,0},{24,8},{1,17},{9,25},{17,1},{25,9},{2,18},{10... | collective-permute-start | bytes 2359304 | tf_op jit(solution)/shard_map/ppermute | solution.py:609
  701.0 67.0 %collective-permute-start.24 = (bf16[192,2048]{1,0:T(8,128)(2,1)S(1)}, bf16[192,2048]{1,0:T(8,128)(2,1)}, u32[]{:S(2)}, u32[]{:S(2)}) collective-permute-start(bf16[192,2048]{1,0:T(8,128)(2,1)S(1)} %get-tuple-element.301), channel_id=1, source_target_pairs={{0,24},{8,0},{16,8},{24,16},{1,25},{9,1},{17,9},{25,17},{2,26},{10... | collective-permute-start | bytes 2359304 | tf_op jit(solution)/shard_map/ppermute | solution.py:609
  773.7 7.2 collective-permute-start.29
  787.8 61.4 %collective-permute-start.30 = (bf16[2,512,1024]{2,1,0:T(8,128)(2,1)}, bf16[2,512,1024]{2,1,0:T(8,128)(2,1)}, u32[]{:S(2)}, u32[]{:S(2)}) collective-permute-start(bf16[2,512,1024]{2,1,0:T(8,128)(2,1)} %fusion.36), channel_id=1, source_target_pairs={{0,1},{1,0},{2,3},{3,2},{4,5},{5,4},{6,7},{7,6},{8,9},{9,8},{10,11... | collective-permute-start | bytes 6291464 | tf_op jit(solution)/shard_map/ppermute | solution.py:557
  793.0 56.3 %collective-permute-start.31 = (bf16[4,64,2048]{2,1,0:T(8,128)(2,1)S(1)}, bf16[4,64,2048]{2,1,0:T(8,128)(2,1)S(1)}, u32[]{:S(2)}, u32[]{:S(2)}) collective-permute-start(bf16[4,64,2048]{2,1,0:T(8,128)(2,1)S(1)} %dynamic-slice_bitcast_fusion.5), channel_id=1, source_target_pairs={{0,4},{4,0},{1,5},{5,1},{2,6},{6,2},{3,7},{7,3},{8,12},{12,8},{9,1... | collective-permute-start | bytes 3145736 | tf_op jit(solution)/shard_map/ppermute | solution.py:542
  794.5 27.1 %collective-permute-start.26 = (bf16[192,2048]{1,0:T(8,128)(2,1)S(1)}, bf16[192,2048]{1,0:T(8,128)(2,1)}, u32[]{:S(2)}, u32[]{:S(2)}) collective-permute-start(bf16[192,2048]{1,0:T(8,128)(2,1)S(1)} %copy-done.109), channel_id=1, source_target_pairs={{0,8},{8,16},{16,24},{24,0},{1,9},{9,17},{17,25},{25,1},{2,10},{10... | collective-permute-start | bytes 2359304 | tf_op jit(solution)/shard_map/ppermute | solution.py:609
  796.3 53.0 %collective-permute-start.27 = (bf16[192,2048]{1,0:T(8,128)(2,1)S(1)}, bf16[192,2048]{1,0:T(8,128)(2,1)}, u32[]{:S(2)}, u32[]{:S(2)}) collective-permute-start(bf16[192,2048]{1,0:T(8,128)(2,1)S(1)} %copy-done.108), channel_id=1, source_target_pairs={{0,16},{8,24},{16,0},{24,8},{1,17},{9,25},{17,1},{25,9},{2,18},{10... | collective-permute-start | bytes 2359304 | tf_op jit(solution)/shard_map/ppermute | solution.py:609
  797.4 51.9 %collective-permute-start.28 = (bf16[192,2048]{1,0:T(8,128)(2,1)S(1)}, bf16[192,2048]{1,0:T(8,128)(2,1)}, u32[]{:S(2)}, u32[]{:S(2)}) collective-permute-start(bf16[192,2048]{1,0:T(8,128)(2,1)S(1)} %copy-done.107), channel_id=1, source_target_pairs={{0,24},{8,0},{16,8},{24,16},{1,25},{9,1},{17,9},{25,17},{2,26},{10... | collective-permute-start | bytes 2359304 | tf_op jit(solution)/shard_map/ppermute | solution.py:609
  861.0 11.5 collective-permute-start.35
  870.0 86.7 %collective-permute-start.37 = (bf16[8,64,2048]{2,1,0:T(8,128)(2,1)S(1)}, bf16[8,64,2048]{2,1,0:T(8,128)(2,1)S(1)}, u32[]{:S(2)}, u32[]{:S(2)}) collective-permute-start(bf16[8,64,2048]{2,1,0:T(8,128)(2,1)S(1)} %dynamic-slice_bitcast_fusion), channel_id=1, source_target_pairs={{0,1},{1,0},{2,3},{3,2},{4,5},{5,4},{6,7},{7,6},{8,9},{9,8},{10,11... | collective-permute-start | bytes 6291464 | tf_op jit(solution)/shard_map/ppermute | solution.py:580
  879.6 83.4 %collective-permute-start.36 = (bf16[8,64,2048]{2,1,0:T(8,128)(2,1)S(1)}, bf16[8,64,2048]{2,1,0:T(8,128)(2,1)S(1)}, u32[]{:S(2)}, u32[]{:S(2)}) collective-permute-start(bf16[8,64,2048]{2,1,0:T(8,128)(2,1)S(1)} %dynamic-slice_bitcast_fusion.1), channel_id=1, source_target_pairs={{0,1},{1,0},{2,3},{3,2},{4,5},{5,4},{6,7},{7,6},{8,9},{9,8},{10,11... | collective-permute-start | bytes 6291464 | tf_op jit(solution)/shard_map/ppermute | solution.py:580
  886.5 36.0 %collective-permute-start.32 = (bf16[192,2048]{1,0:T(8,128)(2,1)S(1)}, bf16[192,2048]{1,0:T(8,128)(2,1)S(1)}, u32[]{:S(2)}, u32[]{:S(2)}) collective-permute-start(bf16[192,2048]{1,0:T(8,128)(2,1)S(1)} %get-tuple-element.322), channel_id=1, source_target_pairs={{0,8},{8,16},{16,24},{24,0},{1,9},{9,17},{17,25},{25,1},{2,10},{10... | collective-permute-start | bytes 2359304 | tf_op jit(solution)/shard_map/ppermute | solution.py:636
  903.9 51.9 %collective-permute-start.33 = (bf16[192,2048]{1,0:T(8,128)(2,1)S(1)}, bf16[192,2048]{1,0:T(8,128)(2,1)S(1)}, u32[]{:S(2)}, u32[]{:S(2)}) collective-permute-start(bf16[192,2048]{1,0:T(8,128)(2,1)S(1)} %get-tuple-element.321), channel_id=1, source_target_pairs={{0,16},{8,24},{16,0},{24,8},{1,17},{9,25},{17,1},{25,9},{2,18},{10... | collective-permute-start | bytes 2359304 | tf_op jit(solution)/shard_map/ppermute | solution.py:636
  904.6 51.2 %collective-permute-start.34 = (bf16[192,2048]{1,0:T(8,128)(2,1)S(1)}, bf16[192,2048]{1,0:T(8,128)(2,1)S(1)}, u32[]{:S(2)}, u32[]{:S(2)}) collective-permute-start(bf16[192,2048]{1,0:T(8,128)(2,1)S(1)} %get-tuple-element.320), channel_id=1, source_target_pairs={{0,24},{8,0},{16,8},{24,16},{1,25},{9,1},{17,9},{25,17},{2,26},{10... | collective-permute-start | bytes 2359304 | tf_op jit(solution)/shard_map/ppermute | solution.py:636
  981.8 68.6 %collective-permute-start.38 = (bf16[4,64,4096]{2,1,0:T(8,128)(2,1)}, bf16[4,64,4096]{2,1,0:T(8,128)(2,1)}, u32[]{:S(2)}, u32[]{:S(2)}) collective-permute-start(bf16[4,64,4096]{2,1,0:T(8,128)(2,1)} %pad_maximum_fusion.7), channel_id=1, source_target_pairs={{0,4},{4,0},{1,5},{5,1},{2,6},{6,2},{3,7},{7,3},{8,12},{12,8},{9,1... | collective-permute-start | bytes 6291464 | tf_op jit(solution)/shard_map/ppermute | solution.py:542
  982.4 263.4 %all-gather.14.cloned.1.call-start = ((), (), s32[]{:S(2)}) async-start(), calls=%async_computation.5 | async-start | bytes 9437184 | tf_op jit(solution)/shard_map/all_gather | solution.py:573
  983.9 24.6 %collective-permute-start.47 = (bf16[64,2048]{1,0:T(8,128)(2,1)S(1)}, bf16[64,2048]{1,0:T(8,128)(2,1)S(1)}, u32[]{:S(2)}, u32[]{:S(2)}) collective-permute-start(bf16[64,2048]{1,0:T(8,128)(2,1)S(1)} %get-tuple-element.318), channel_id=1, source_target_pairs={{0,8},{8,16},{16,24},{24,0},{1,9},{9,17},{17,25},{25,1},{2,10},{10... | collective-permute-start | bytes 786440 | tf_op jit(solution)/shard_map/ppermute | solution.py:609
  1001.3 17.6 %collective-permute-start.48 = (bf16[64,2048]{1,0:T(8,128)(2,1)S(1)}, bf16[64,2048]{1,0:T(8,128)(2,1)S(1)}, u32[]{:S(2)}, u32[]{:S(2)}) collective-permute-start(bf16[64,2048]{1,0:T(8,128)(2,1)S(1)} %get-tuple-element.317), channel_id=1, source_target_pairs={{0,16},{8,24},{16,0},{24,8},{1,17},{9,25},{17,1},{25,9},{2,18},{10... | collective-permute-start | bytes 786440 | tf_op jit(solution)/shard_map/ppermute | solution.py:609
  1001.9 17.0 %collective-permute-start.49 = (bf16[64,2048]{1,0:T(8,128)(2,1)S(1)}, bf16[64,2048]{1,0:T(8,128)(2,1)S(1)}, u32[]{:S(2)}, u32[]{:S(2)}) collective-permute-start(bf16[64,2048]{1,0:T(8,128)(2,1)S(1)} %get-tuple-element.316), channel_id=1, source_target_pairs={{0,24},{8,0},{16,8},{24,16},{1,25},{9,1},{17,9},{25,17},{2,26},{10... | collective-permute-start | bytes 786440 | tf_op jit(solution)/shard_map/ppermute | solution.py:609
  1007.1 111.7 %collective-permute-start.42 = (bf16[512,2048]{1,0:T(8,128)(2,1)}, bf16[512,2048]{1,0:T(8,128)(2,1)}, u32[]{:S(2)}, u32[]{:S(2)}) collective-permute-start(bf16[512,2048]{1,0:T(8,128)(2,1)} %slice.169), channel_id=1, source_target_pairs={{0,2},{2,0},{1,3},{3,1},{4,6},{6,4},{5,7},{7,5},{8,10},{10,8},{9,1... | collective-permute-start | bytes 6291464 | tf_op jit(solution)/shard_map/ppermute | solution.py:542
  1008.6 123.7 %collective-permute-start.46 = (bf16[1024,2048]{1,0:T(8,128)(2,1)}, bf16[1024,2048]{1,0:T(8,128)(2,1)}, u32[]{:S(2)}, u32[]{:S(2)}) collective-permute-start(bf16[1024,2048]{1,0:T(8,128)(2,1)} %back_to_width.6), channel_id=1, source_target_pairs={{0,2},{2,0},{1,3},{3,1},{4,6},{6,4},{5,7},{7,5},{8,10},{10,8},{9,1... | collective-permute-start | bytes 12582920 | tf_op jit(solution)/shard_map/ppermute | solution.py:542
  1053.2 86.4 %collective-permute-start.39 = (bf16[64,4096]{1,0:T(8,128)(2,1)}, bf16[64,4096]{1,0:T(8,128)(2,1)}, u32[]{:S(2)}, u32[]{:S(2)}) collective-permute-start(bf16[64,4096]{1,0:T(8,128)(2,1)} %get-tuple-element.333), channel_id=1, source_target_pairs={{0,8},{8,16},{16,24},{24,0},{1,9},{9,17},{17,25},{25,1},{2,10},{10... | collective-permute-start | bytes 1572872 | tf_op jit(solution)/shard_map/ppermute | solution.py:609
  1077.5 62.1 %collective-permute-start.40 = (bf16[64,4096]{1,0:T(8,128)(2,1)}, bf16[64,4096]{1,0:T(8,128)(2,1)}, u32[]{:S(2)}, u32[]{:S(2)}) collective-permute-start(bf16[64,4096]{1,0:T(8,128)(2,1)} %get-tuple-element.332), channel_id=1, source_target_pairs={{0,16},{8,24},{16,0},{24,8},{1,17},{9,25},{17,1},{25,9},{2,18},{10... | collective-permute-start | bytes 1572872 | tf_op jit(solution)/shard_map/ppermute | solution.py:609
  1091.9 47.7 %collective-permute-start.41 = (bf16[64,4096]{1,0:T(8,128)(2,1)}, bf16[64,4096]{1,0:T(8,128)(2,1)}, u32[]{:S(2)}, u32[]{:S(2)}) collective-permute-start(bf16[64,4096]{1,0:T(8,128)(2,1)} %get-tuple-element.331), channel_id=1, source_target_pairs={{0,24},{8,0},{16,8},{24,16},{1,25},{9,1},{17,9},{25,17},{2,26},{10... | collective-permute-start | bytes 1572872 | tf_op jit(solution)/shard_map/ppermute | solution.py:609
  1144.0 11.2 collective-permute-start.50
  1144.5 20.7 %collective-permute-start.51 = (bf16[64,2048]{1,0:T(8,128)(2,1)S(1)}, bf16[64,2048]{1,0:T(8,128)(2,1)S(1)}, u32[]{:S(2)}, u32[]{:S(2)}) collective-permute-start(bf16[64,2048]{1,0:T(8,128)(2,1)S(1)} %get-tuple-element.342), channel_id=1, source_target_pairs={{0,16},{8,24},{16,0},{24,8},{1,17},{9,25},{17,1},{25,9},{2,18},{10... | collective-permute-start | bytes 786440 | tf_op jit(solution)/shard_map/ppermute | solution.py:636
  1146.8 18.4 %collective-permute-start.52 = (bf16[64,2048]{1,0:T(8,128)(2,1)S(1)}, bf16[64,2048]{1,0:T(8,128)(2,1)S(1)}, u32[]{:S(2)}, u32[]{:S(2)}) collective-permute-start(bf16[64,2048]{1,0:T(8,128)(2,1)S(1)} %get-tuple-element.341), channel_id=1, source_target_pairs={{0,24},{8,0},{16,8},{24,16},{1,25},{9,1},{17,9},{25,17},{2,26},{10... | collective-permute-start | bytes 786440 | tf_op jit(solution)/shard_map/ppermute | solution.py:636
  1166.3 79.5 %collective-permute-start.54 = (f32[4352]{0:T(1024)S(1)}, f32[4352]{0:T(1024)S(1)}, u32[]{:S(2)}, u32[]{:S(2)}) collective-permute-start(f32[4352]{0:T(1024)S(1)} %add.688), channel_id=1, source_target_pairs={{0,8},{8,16},{16,24},{24,0},{1,9},{9,17},{17,25},{25,1},{2,10},{10... | collective-permute-start | bytes 52232 | tf_op jit(solution)/shard_map/ppermute | solution.py:551
  1171.9 73.9 %collective-permute-start.55 = (f32[4352]{0:T(1024)S(1)}, f32[4352]{0:T(1024)S(1)}, u32[]{:S(2)}, u32[]{:S(2)}) collective-permute-start(f32[4352]{0:T(1024)S(1)} %add.688), channel_id=1, source_target_pairs={{0,16},{8,24},{16,0},{24,8},{1,17},{9,25},{17,1},{25,9},{2,18},{10... | collective-permute-start | bytes 52232 | tf_op jit(solution)/shard_map/ppermute | solution.py:551
  1172.2 73.6 %collective-permute-start.56 = (f32[4352]{0:T(1024)S(1)}, f32[4352]{0:T(1024)S(1)}, u32[]{:S(2)}, u32[]{:S(2)}) collective-permute-start(f32[4352]{0:T(1024)S(1)} %add.688), channel_id=1, source_target_pairs={{0,24},{8,0},{16,8},{24,16},{1,25},{9,1},{17,9},{25,17},{2,26},{10... | collective-permute-start | bytes 52232 | tf_op jit(solution)/shard_map/ppermute | solution.py:551
  1249.9 71.8 %collective-permute-start.60 = (bf16[512,2048]{1,0:T(8,128)(2,1)}, bf16[512,2048]{1,0:T(8,128)(2,1)}, u32[]{:S(2)}, u32[]{:S(2)}) collective-permute-start(bf16[512,2048]{1,0:T(8,128)(2,1)} %fusion.35), channel_id=1, source_target_pairs={{0,1},{1,0},{2,3},{3,2},{4,5},{5,4},{6,7},{7,6},{8,9},{9,8},{10,11... | collective-permute-start | bytes 6291464 | tf_op jit(solution)/shard_map/ppermute | solution.py:557
  1252.6 61.6 %collective-permute-start.57 = (bf16[192,2048]{1,0:T(8,128)(2,1)}, bf16[192,2048]{1,0:T(8,128)(2,1)S(1)}, u32[]{:S(2)}, u32[]{:S(2)}) collective-permute-start(bf16[192,2048]{1,0:T(8,128)(2,1)} %get-tuple-element.313), channel_id=1, source_target_pairs={{0,24},{8,0},{16,8},{24,16},{1,25},{9,1},{17,9},{25,17},{2,26},{10... | collective-permute-start | bytes 2359304 | tf_op jit(solution)/shard_map/ppermute | solution.py:645
  1254.1 65.5 %collective-permute-start.58 = (bf16[192,2048]{1,0:T(8,128)(2,1)}, bf16[192,2048]{1,0:T(8,128)(2,1)}, u32[]{:S(2)}, u32[]{:S(2)}) collective-permute-start(bf16[192,2048]{1,0:T(8,128)(2,1)} %get-tuple-element.312), channel_id=1, source_target_pairs={{0,16},{8,24},{16,0},{24,8},{1,17},{9,25},{17,1},{25,9},{2,18},{10... | collective-permute-start | bytes 2359304 | tf_op jit(solution)/shard_map/ppermute | solution.py:645
  1254.1 65.5 %collective-permute-start.59 = (bf16[192,2048]{1,0:T(8,128)(2,1)}, bf16[192,2048]{1,0:T(8,128)(2,1)}, u32[]{:S(2)}, u32[]{:S(2)}) collective-permute-start(bf16[192,2048]{1,0:T(8,128)(2,1)} %get-tuple-element.311), channel_id=1, source_target_pairs={{0,8},{8,16},{16,24},{24,0},{1,9},{9,17},{17,25},{25,1},{2,10},{10... | collective-permute-start | bytes 2359304 | tf_op jit(solution)/shard_map/ppermute | solution.py:645
  1321.7 13.6 %collective-permute-start.61 = (bf16[64,2048]{1,0:T(8,128)(2,1)S(1)}, bf16[64,2048]{1,0:T(8,128)(2,1)S(1)}, u32[]{:S(2)}, u32[]{:S(2)}) collective-permute-start(bf16[64,2048]{1,0:T(8,128)(2,1)S(1)} %get-tuple-element.339), channel_id=1, source_target_pairs={{0,24},{8,0},{16,8},{24,16},{1,25},{9,1},{17,9},{25,17},{2,26},{10... | collective-permute-start | bytes 786440 | tf_op jit(solution)/shard_map/ppermute | solution.py:645
  1321.8 25.1 %collective-permute-start.62 = (bf16[64,2048]{1,0:T(8,128)(2,1)S(1)}, bf16[64,2048]{1,0:T(8,128)(2,1)S(1)}, u32[]{:S(2)}, u32[]{:S(2)}) collective-permute-start(bf16[64,2048]{1,0:T(8,128)(2,1)S(1)} %get-tuple-element.338), channel_id=1, source_target_pairs={{0,16},{8,24},{16,0},{24,8},{1,17},{9,25},{17,1},{25,9},{2,18},{10... | collective-permute-start | bytes 786440 | tf_op jit(solution)/shard_map/ppermute | solution.py:645
  1324.5 22.4 %collective-permute-start.63 = (bf16[64,2048]{1,0:T(8,128)(2,1)S(1)}, bf16[64,2048]{1,0:T(8,128)(2,1)S(1)}, u32[]{:S(2)}, u32[]{:S(2)}) collective-permute-start(bf16[64,2048]{1,0:T(8,128)(2,1)S(1)} %get-tuple-element.337), channel_id=1, source_target_pairs={{0,8},{8,16},{16,24},{24,0},{1,9},{9,17},{17,25},{25,1},{2,10},{10... | collective-permute-start | bytes 786440 | tf_op jit(solution)/shard_map/ppermute | solution.py:645
  (136 other events, 1510.0 us)
Sparse Core Ops, SparseCore 0:
  12.6 154.7 all-gather.5
  169.5 61.6 all-gather.7
  246.7 62.0 all-gather.9
  321.2 62.0 all-gather.11
  982.5 134.8 all-reduce.2
  1166.5 56.2 all-gather.13
